TPU v7x, 32 devices: a whole 2x2x4 slice. The times are simulated.
32 devices in a mesh: shot: 4 (over y, core), band: 8 (over z, x).
Axes of the slice: x: 2, y: 2, z: 4, core: 2. Of those that a mesh axis runs over, the one named last changes fastest.
Arguments:
- sensitivity: bfloat16 [2048, 128, 128], P(('shot', 'band')), may hold values from -0.0625 to 0.0625
- bundle_of: int32 [2048], P(('shot', 'band')), may hold values from 0 to 7
- cellblock_of: int32 [2048], P(('shot', 'band')), may hold values from 0 to 15
- state: float32 [16384, 128], P('band'), may hold values from -6 to 6
- prior_velocity: float32 [16384, 128], P('band'), may hold values from -6 to 6
- observed: float32 [32, 128], P(('shot', 'band')), may hold values from -6 to 6
- pick_weight: float32 [32, 128], P(('shot', 'band')), may hold values from 0.3 to 3
Outputs:
- new_state: float32 [16384, 128], P('band')
- weighted_residual: float32 [32, 128, 128], P(('shot', 'band'))
Inputs may be any that keep to these rules, and one draw needn't show every extreme that they name: bundle_of names a bundle of the block's own source group. cellblock_of names a cell block of the block's own depth band.
All inputs are finite; a program needn't handle non-finite values.
Results may differ from a plain program's by a relative error of at most 0.0059.
Values may be sent and summed in bfloat16 or wider, within the bound.
No kernel may reach another device: no remote copies, remote signals or barrier semaphores. Data moves between devices by JAX's collectives and lax.ppermute only.
A program may use at most 64 MiB of HBM per device.

v0:
```python
import functools

import jax
import jax.numpy as jnp
from jax import lax
from jax.experimental import pallas as pl
from jax.experimental.pallas import tpu as pltpu
from jax.sharding import PartitionSpec as P

CBLK = 128
GROUP = 16
CHUNKS = 4
FIRST_VMEM = 57 << 20

VMEM = pl.BlockSpec(memory_space=pltpu.VMEM)
SMEM = pl.BlockSpec(memory_space=pltpu.SMEM)
HBM = pl.BlockSpec(memory_space=pltpu.HBM)

bf16, f32 = jnp.bfloat16, jnp.float32
arr = jax.ShapeDtypeStruct


def call(body, outs, scratch, in_specs, name, flops=0, bytes_accessed=0, vmem=32 << 20):
    return pl.pallas_call(
        body,
        out_shape=outs,
        in_specs=in_specs,
        out_specs=jax.tree.map(lambda _: VMEM, outs),
        scratch_shapes=scratch,
        compiler_params=pltpu.CompilerParams(vmem_limit_bytes=vmem),
        cost_estimate=pl.CostEstimate(
            flops=flops, bytes_accessed=bytes_accessed, transcendentals=0
        ),
        name=name,
    )


def products(first, count, lhs_of, rhs_of, slot_of, acc_ref):
    def group(g, carry):
        ks = [first + g * GROUP + j for j in range(GROUP)]
        prods = [jnp.dot(lhs_of(k), rhs_of(k), preferred_element_type=f32) for k in ks]
        for k, prod in zip(ks, prods):
            acc_ref[slot_of(k)] += prod
        return carry

    if count == GROUP:
        group(0, 0)
    else:
        lax.fori_loop(0, count // GROUP, group, 0)


def first_forward_kernel(
    bund_hbm, cblk_hbm, sens_hbm, state_hbm, prior_hbm, out_ref, acc, probe, bund, cblk, sens, state, prior, sems
):
    nblk = sens.shape[0]
    step = nblk // CHUNKS
    half = state.shape[0] // 2
    small = [
        pltpu.make_async_copy(bund_hbm, bund, sems.at[0]),
        pltpu.make_async_copy(cblk_hbm, cblk, sems.at[1]),
    ]
    fields = []
    for h in range(2):
        part = pl.ds(h * half, half)
        fields.append(
            [
                pltpu.make_async_copy(state_hbm.at[part], state.at[part], sems.at[2 + 2 * h]),
                pltpu.make_async_copy(prior_hbm.at[part], prior.at[part], sems.at[3 + 2 * h]),
            ]
        )

    def block_copy(c):
        part = pl.ds(c * step, step)
        return pltpu.make_async_copy(sens_hbm.at[part], sens.at[part], sems.at[6 + c])

    for copy in small + fields[0] + fields[1] + [block_copy(c) for c in range(CHUNKS)]:
        copy.start()
    acc[...] = jnp.zeros_like(acc)
    for h in range(2):
        part = pl.ds(h * half, half)
        for copy in fields[h]:
            copy.wait()
        probe[part] = (state[part] + 0.5 * prior[part]).astype(bf16)
    for copy in small:
        copy.wait()

    def chunk(c, carry):
        block_copy(c).wait()
        products(
            c * step,
            step,
            lambda k: sens[k],
            lambda k: probe[cblk[k]],
            lambda k: bund[k],
            acc,
        )
        return carry

    lax.fori_loop(0, CHUNKS, chunk, 0)
    out_ref[...] = acc[...].astype(bf16)


def forward_kernel(shot_ref, bund, cblk, sens, own_ref, mate_ref, out_ref, acc, probe):
    half = own_ref.shape[0]
    core = shot_ref[0] % 2
    probe[pl.ds(core * half, half)] = own_ref[...]
    probe[pl.ds((1 - core) * half, half)] = mate_ref[...]
    acc[...] = jnp.zeros_like(acc)
    products(
        0,
        sens.shape[0],
        lambda k: sens[k],
        lambda k: probe[cblk[k]],
        lambda k: bund[k],
        acc,
    )
    out_ref[...] = acc[...].astype(bf16)


def adjoint_kernel(shot_ref, bund, cblk, sens, resid, keep_ref, give_ref, acc):
    acc[...] = jnp.zeros_like(acc)
    products(
        0,
        sens.shape[0],
        lambda k: resid[bund[k]],
        lambda k: sens[k],
        lambda k: cblk[k],
        acc,
    )
    half = keep_ref.shape[0]
    core = shot_ref[0] % 2
    keep_ref[...] = acc[pl.ds(core * half, half)]
    give_ref[...] = acc[pl.ds((1 - core) * half, half)].astype(bf16)


def pair_kernel(keep_ref, got_ref, out_ref):
    out_ref[...] = (keep_ref[...] + got_ref[...].astype(f32)).astype(bf16)


def residual_kernel(parts_ref, obs_ref, wt_ref, out_ref, *resid_ref):
    for i in range(parts_ref.shape[1]):
        total = parts_ref[0, i].astype(f32)
        for d in range(1, parts_ref.shape[0]):
            total += parts_ref[d, i].astype(f32)
        resid = wt_ref[pl.ds(i, 1), :] * (total.T - obs_ref[pl.ds(i, 1), :])
        if resid_ref:
            resid_ref[0][i] = resid
        rounded = resid.astype(bf16)
        for d in range(parts_ref.shape[0]):
            out_ref[d, i] = rounded


def turn_kernel(in_ref, out_ref):
    for i in range(in_ref.shape[0]):
        out_ref[i] = in_ref[i].T


def sum_over_y(chip_y, part_refs, order, i):
    if len(part_refs) > 2:
        for d, part_ref in enumerate(part_refs):
            order[chip_y ^ d] = part_ref[i]
        part_refs = [order.at[y] for y in range(len(part_refs))]
        read = lambda ref: ref[...]
    else:
        read = lambda ref: ref[i]
    total = read(part_refs[0]).astype(f32)
    for part_ref in part_refs[1:]:
        total += read(part_ref).astype(f32)
    return total


def probe_kernel(ny, shot_ref, state_hbm, prior_hbm, *rest):
    part_refs, (out_ref, grad_ref, state, prior, order, sems) = rest[:ny], rest[ny:]
    half = out_ref.shape[0]
    core = shot_ref[0] % 2
    part = pl.ds(core * half, half)
    copies = [
        pltpu.make_async_copy(state_hbm.at[part], state, sems.at[0]),
        pltpu.make_async_copy(prior_hbm.at[part], prior, sems.at[1]),
    ]
    for copy in copies:
        copy.start()
    for i in range(half):
        grad_ref[i] = sum_over_y(shot_ref[0] // 2, part_refs, order, i).T
    for copy in copies:
        copy.wait()
    middle = state[...] + 0.5 * (prior[...] - 0.5 * grad_ref[...])
    out_ref[...] = (middle + 0.5 * prior[...]).astype(bf16)


def total_kernel(ny, shot_ref, grad_ref, *rest):
    part_refs, (out_ref, order) = rest[:ny], rest[ny:]
    for i in range(out_ref.shape[0]):
        grad2 = sum_over_y(shot_ref[0] // 2, part_refs, order, i).T
        out_ref[i] = (grad_ref[i] + grad2).astype(bf16)


def last_kernel(shot_ref, state, prior, own_ref, mate_ref, out_ref):
    half = own_ref.shape[0]
    core = shot_ref[0] % 2
    for at, part_ref in ((core * half, own_ref), ((1 - core) * half, mate_ref)):
        part = pl.ds(at, half)
        out_ref[part] = state[part] + 0.5 * (prior[part] - 0.25 * part_ref[...].astype(f32))


def per_device(nshot, nband, sens, bund, cblk, state, prior, observed, pick_weight):
    nblk = sens.shape[0]
    samples = state.shape[1]
    owned, rays = observed.shape
    bundles = owned * nband
    cells = state.shape[0] // CBLK
    half = cells // 2
    ny = nshot // 2
    flops = 2 * nblk * rays * CBLK * samples
    sens_bytes = nblk * rays * CBLK * 2

    state_b = state.reshape(cells, CBLK, samples)
    prior_b = prior.reshape(cells, CBLK, samples)
    shot = lax.axis_index("shot").reshape(1)

    def other_core(array):
        return lax.ppermute(array, "shot", [(i, i ^ 1) for i in range(nshot)])

    def other_chips(array):
        return [array] + [
            lax.ppermute(array, "shot", [(i, i ^ (2 * d)) for i in range(nshot)])
            for d in range(1, ny)
        ]

    def over_band(array):
        return lax.all_to_all(array, "band", split_axis=0, concat_axis=0, tiled=True)

    part_out = arr((bundles, rays, samples), bf16)
    part_acc = pltpu.VMEM((bundles, rays, samples), f32)
    whole_field = pltpu.VMEM((cells, CBLK, samples), bf16)
    half_bf16 = arr((half, CBLK, samples), bf16)
    half_f32 = arr((half, CBLK, samples), f32)
    half_scratch = pltpu.VMEM((half, CBLK, samples), f32)
    order = pltpu.VMEM((ny, samples, CBLK), bf16)

    def residual(part, name, keep):
        parts = over_band(part).reshape(nband, owned, rays, samples)
        outs = (arr((nband, owned, samples, rays), bf16),)
        if keep:
            outs += (arr((owned, samples, rays), f32),)
        copies, *resid = call(
            residual_kernel, outs, [], [VMEM] * 3, name, bytes_accessed=1 << 20
        )(parts, observed, pick_weight)
        return resid, over_band(copies).reshape(bundles, samples, rays)

    def adjoint(resid_all, name):
        keep, give = call(
            adjoint_kernel,
            (half_f32, half_bf16),
            [pltpu.VMEM((cells, samples, CBLK), f32)],
            [SMEM] * 3 + [VMEM] * 2,
            name,
            flops,
            sens_bytes,
        )(shot, bund, cblk, sens, resid_all)
        pair = call(
            pair_kernel, half_bf16, [], [VMEM] * 2, name + "_pair", bytes_accessed=1 << 20
        )(keep, other_core(give))
        return other_chips(pair)

    part1 = call(
        first_forward_kernel,
        part_out,
        [
            part_acc,
            whole_field,
            pltpu.SMEM((nblk,), jnp.int32),
            pltpu.SMEM((nblk,), jnp.int32),
            pltpu.VMEM(sens.shape, bf16),
            pltpu.VMEM(state_b.shape, f32),
            pltpu.VMEM(state_b.shape, f32),
            pltpu.SemaphoreType.DMA((6 + CHUNKS,)),
        ],
        [HBM] * 5,
        "forward1",
        flops,
        sens_bytes,
        vmem=FIRST_VMEM,
    )(bund, cblk, sens, state_b, prior_b)
    _, resid_all1 = residual(part1, "residual1", False)
    gparts1 = adjoint(resid_all1, "adjoint1")
    probe_own, grad1 = call(
        functools.partial(probe_kernel, ny),
        (half_bf16, half_f32),
        [half_scratch, half_scratch, order, pltpu.SemaphoreType.DMA((2,))],
        [SMEM, HBM, HBM] + [VMEM] * ny,
        "probe2",
        bytes_accessed=1 << 20,
    )(shot, state_b, prior_b, *gparts1)
    part2 = call(
        forward_kernel,
        part_out,
        [part_acc, whole_field],
        [SMEM] * 3 + [VMEM] * 3,
        "forward2",
        flops,
        sens_bytes,
    )(shot, bund, cblk, sens, probe_own, other_core(probe_own))
    (resid2_t,), resid_all2 = residual(part2, "residual2", True)
    resid2 = call(
        turn_kernel,
        arr((owned, rays, samples), f32),
        [],
        [VMEM],
        "turn",
        bytes_accessed=1 << 20,
    )(resid2_t)
    gparts2 = adjoint(resid_all2, "adjoint2")
    total = call(
        functools.partial(total_kernel, ny),
        half_bf16,
        [order],
        [SMEM] + [VMEM] * (1 + ny),
        "total",
        bytes_accessed=1 << 20,
    )(shot, grad1, *gparts2)
    new_state = call(
        last_kernel,
        arr((cells, CBLK, samples), f32),
        [],
        [SMEM] + [VMEM] * 4,
        "new_state",
        bytes_accessed=4 << 20,
    )(shot, state_b, prior_b, total, other_core(total))
    return new_state.reshape(state.shape), resid2


def solution(mesh):
    in_specs = (
        P(("shot", "band"), None, None),
        P(("shot", "band")),
        P(("shot", "band")),
        P("band", None),
        P("band", None),
        P(("shot", "band"), None),
        P(("shot", "band"), None),
    )
    out_specs = (P("band", None), P(("shot", "band"), None, None))
    return jax.shard_map(
        functools.partial(per_device, mesh.shape["shot"], mesh.shape["band"]),
        mesh=mesh,
        in_specs=in_specs,
        out_specs=out_specs,
        check_vma=False,
    )
```

profile of v0, /device:TPU:0, one launch (start us, length us, event | category | flops | bytes accessed | tf_op | source)
XLA Modules:
  0.0 89.6 jit_solution(16091486026002006565)
XLA Ops:
  0.6 0.0 copy-start.6
  0.7 4.0 %forward1.1 = bf16[8,128,128]{2,1,0:T(8,128)(2,1)} custom-call(s32[64]{0:T(128)} %bund.5, s32[64]{0:T(128)} %cblk.5, bf16[64,128,128]{2,1,0:T(8,128)(2,1)} %sens.5, f32[16,128,128]{2,1,0:T(8,128)} %bitcast.8, f32[16,128,128]{2,1,0:T(8,128)} %bitcast.11), custom_call_target="tpu_custom_call" | custom-call | flops 268435456 | bytes 2097152 | tf_op jit(solution)/shard_map/forward1/pallas_call | solution.py:266
  4.7 16.2 %all_to_all.20 = bf16[8,128,128]{2,1,0:T(8,128)(2,1)S(1)} all-to-all(bf16[8,128,128]{2,1,0:T(8,128)(2,1)} %forward1.1), channel_id=1, replica_groups=mesh['shot'=4,'band'=8] {'band'}, dimensions={0} | all-to-all | bytes 524288 | tf_op jit(solution)/shard_map/all_to_all | solution.py:231
  20.9 0.1 residual1.1
  21.0 0.0 copy-start.3
  21.0 0.7 copy-done.3
  21.7 3.7 %all-to-all-start.1 = ((bf16[8,1,128,128]{3,2,1,0:T(8,128)(2,1)}), bf16[8,1,128,128]{3,2,1,0:T(8,128)(2,1)S(1)}, u32[]{:S(2)}, u32[]{:S(2)}) async-start(bf16[8,1,128,128]{3,2,1,0:T(8,128)(2,1)} %copy-done.3), calls=%async_computation.1 | async-start | bytes 524288 | tf_op jit(solution)/shard_map/all_to_all | solution.py:231
  25.4 8.6 %all-to-all-done.1 = bf16[8,1,128,128]{3,2,1,0:T(8,128)(2,1)S(1)} async-done(((bf16[8,1,128,128]{3,2,1,0:T(8,128)(2,1)}), bf16[8,1,128,128]{3,2,1,0:T(8,128)(2,1)S(1)}, u32[]{:S(2)}, u32[]{:S(2)}) %all-to-all-start.1) | async-done | bytes 262176 | tf_op jit(solution)/shard_map/all_to_all | solution.py:231
  34.0 0.0 copy-done
  34.0 1.9 %adjoint1.1 = (f32[8,128,128]{2,1,0:T(8,128)S(1)}, bf16[8,128,128]{2,1,0:T(8,128)(2,1)S(1)}) custom-call(s32[1]{0:T(128)} %bitcast.shot_ref, s32[64]{0:T(128)S(1)} %copy-done.4, s32[64]{0:T(128)S(1)} %copy-done.5, bf16[64,128,128]{2,1,0:T(8,128)(2,1)S(1)} %copy-done, bf16[8,128,128]{2,1,0:T(8,128)(2,1)S(1)} %bitcast.14), custom_call_target="tpu_custom_call" | custom-call | flops 268435456 | bytes 2097152 | tf_op jit(solution)/shard_map/adjoint1/pallas_call | solution.py:252
  35.9 0.1 collective-permute-start
  36.0 1.5 %collective-permute-done.got_ref = bf16[8,128,128]{2,1,0:T(8,128)(2,1)S(1)} collective-permute-done((bf16[8,128,128]{2,1,0:T(8,128)(2,1)S(1)}, bf16[8,128,128]{2,1,0:T(8,128)(2,1)S(1)}, u32[]{:S(2)}, u32[]{:S(2)}) %collective-permute-start) | collective-permute-done | bytes 262176 | tf_op jit(solution)/shard_map/ppermute | solution.py:222
  37.5 0.1 adjoint1_pair.1.rest_0_
  37.6 1.6 %collective-permute-start.1 = (bf16[8,128,128]{2,1,0:T(8,128)(2,1)S(1)}, bf16[8,128,128]{2,1,0:T(8,128)(2,1)S(1)}, u32[]{:S(2)}, u32[]{:S(2)}) collective-permute-start(bf16[8,128,128]{2,1,0:T(8,128)(2,1)S(1)} %adjoint1_pair.1.rest_0_), channel_id=1, source_target_pairs={{0,16},{8,24},{16,0},{24,8},{1,17},{9,25},{17,1},{25,9},{2,18},{10... | collective-permute-start | bytes 786440 | tf_op jit(solution)/shard_map/ppermute | solution.py:226
  39.2 6.8 %collective-permute-done.1.rest_1_ = bf16[8,128,128]{2,1,0:T(8,128)(2,1)S(1)} collective-permute-done((bf16[8,128,128]{2,1,0:T(8,128)(2,1)S(1)}, bf16[8,128,128]{2,1,0:T(8,128)(2,1)S(1)}, u32[]{:S(2)}, u32[]{:S(2)}) %collective-permute-start.1) | collective-permute-done | bytes 262176 | tf_op jit(solution)/shard_map/ppermute | solution.py:226
  46.0 0.4 probe2.1
  46.4 0.1 collective-permute-start.2
  46.5 1.5 %collective-permute-done.2.mate_ref = bf16[8,128,128]{2,1,0:T(8,128)(2,1)S(1)} collective-permute-done((bf16[8,128,128]{2,1,0:T(8,128)(2,1)S(1)}, bf16[8,128,128]{2,1,0:T(8,128)(2,1)S(1)}, u32[]{:S(2)}, u32[]{:S(2)}) %collective-permute-start.2) | collective-permute-done | bytes 262176 | tf_op jit(solution)/shard_map/ppermute | solution.py:222
  48.1 1.9 %forward2.1 = bf16[8,128,128]{2,1,0:T(8,128)(2,1)S(1)} custom-call(s32[1]{0:T(128)} %bitcast.shot_ref, s32[64]{0:T(128)S(1)} %copy-done.4, s32[64]{0:T(128)S(1)} %copy-done.5, bf16[64,128,128]{2,1,0:T(8,128)(2,1)S(1)} %copy-done, bf16[8,128,128]{2,1,0:T(8,128)(2,1)S(1)} %get-tuple-element.13.own_ref, bf16[8,128,128]{2,1,0:T(8,128)(2,1)S(1)} %collective-permute-done.2.mate_ref), custom_call_target="tpu_custom_call" | custom-call | flops 268435456 | bytes 2097152 | tf_op jit(solution)/shard_map/forward2/pallas_call | solution.py:295
  49.9 12.6 %all_to_all.21 = bf16[8,128,128]{2,1,0:T(8,128)(2,1)S(1)} all-to-all(bf16[8,128,128]{2,1,0:T(8,128)(2,1)S(1)} %forward2.1), channel_id=1, replica_groups=mesh['shot'=4,'band'=8] {'band'}, dimensions={0} | all-to-all | bytes 524288 | tf_op jit(solution)/shard_map/all_to_all | solution.py:231
  62.5 0.1 residual2.1
  62.6 12.0 %all_to_all.22 = bf16[8,1,128,128]{3,2,1,0:T(8,128)(2,1)S(1)} all-to-all(bf16[8,1,128,128]{3,2,1,0:T(8,128)(2,1)S(1)} %get-tuple-element.14), channel_id=1, replica_groups=mesh['shot'=4,'band'=8] {'band'}, dimensions={0} | all-to-all | bytes 524288 | tf_op jit(solution)/shard_map/all_to_all | solution.py:231
  74.6 1.9 %adjoint2.1 = (f32[8,128,128]{2,1,0:T(8,128)S(1)}, bf16[8,128,128]{2,1,0:T(8,128)(2,1)S(1)}) custom-call(s32[1]{0:T(128)} %bitcast.shot_ref, s32[64]{0:T(128)S(1)} %copy-done.4, s32[64]{0:T(128)S(1)} %copy-done.5, bf16[64,128,128]{2,1,0:T(8,128)(2,1)S(1)} %copy-done, bf16[8,128,128]{2,1,0:T(8,128)(2,1)S(1)} %bitcast.15), custom_call_target="tpu_custom_call" | custom-call | flops 268435456 | bytes 2097152 | tf_op jit(solution)/shard_map/adjoint2/pallas_call | solution.py:252
  76.5 0.1 collective-permute-start.3
  76.6 1.5 %collective-permute-done.3.got_ref = bf16[8,128,128]{2,1,0:T(8,128)(2,1)S(1)} collective-permute-done((bf16[8,128,128]{2,1,0:T(8,128)(2,1)S(1)}, bf16[8,128,128]{2,1,0:T(8,128)(2,1)S(1)}, u32[]{:S(2)}, u32[]{:S(2)}) %collective-permute-start.3) | collective-permute-done | bytes 262176 | tf_op jit(solution)/shard_map/ppermute | solution.py:222
  78.2 1.6 %collective-permute-start.4 = (bf16[8,128,128]{2,1,0:T(8,128)(2,1)S(1)}, bf16[8,128,128]{2,1,0:T(8,128)(2,1)S(1)}, u32[]{:S(2)}, u32[]{:S(2)}) collective-permute-start(bf16[8,128,128]{2,1,0:T(8,128)(2,1)S(1)} %adjoint2_pair.1.rest_0_), channel_id=1, source_target_pairs={{0,16},{8,24},{16,0},{24,8},{1,17},{9,25},{17,1},{25,9},{2,18},{10... | collective-permute-start | bytes 786440 | tf_op jit(solution)/shard_map/ppermute | solution.py:226
  79.7 6.8 %collective-permute-done.4.rest_1_ = bf16[8,128,128]{2,1,0:T(8,128)(2,1)S(1)} collective-permute-done((bf16[8,128,128]{2,1,0:T(8,128)(2,1)S(1)}, bf16[8,128,128]{2,1,0:T(8,128)(2,1)S(1)}, u32[]{:S(2)}, u32[]{:S(2)}) %collective-permute-start.4) | collective-permute-done | bytes 262176 | tf_op jit(solution)/shard_map/ppermute | solution.py:226
  86.6 0.2 total.1.own_ref
  86.8 0.1 collective-permute-start.5
  86.9 0.7 turn.1
  87.6 0.8 collective-permute-done.5.mate_ref
  88.4 1.2 %new_state.1 = f32[16,128,128]{2,1,0:T(8,128)} custom-call(s32[1]{0:T(128)} %bitcast.shot_ref, f32[16,128,128]{2,1,0:T(8,128)S(1)} %bitcast.10, f32[16,128,128]{2,1,0:T(8,128)S(1)} %bitcast.13, bf16[8,128,128]{2,1,0:T(8,128)(2,1)S(1)} %total.1.own_ref, bf16[8,128,128]{2,1,0:T(8,128)(2,1)S(1)} %collective-permute-done.5.mate_ref), custom_call_target="tpu_custom_call" | custom-call | bytes 4194304 | tf_op jit(solution)/shard_map/new_state/pallas_call | solution.py:322
  (13 shorter events, 0.1 us)
Async XLA Ops:
  0.6 20.3 %copy-start.6 = (f32[1,128]{1,0:T(1,128)S(1)}, f32[1,128]{1,0:T(1,128)}, u32[]{:S(2)}) copy-start(f32[1,128]{1,0:T(1,128)} %obs_ref.3) | copy-start | bytes 1540
  0.6 20.3 %copy-start.7 = (f32[1,128]{1,0:T(1,128)S(1)}, f32[1,128]{1,0:T(1,128)}, u32[]{:S(2)}) copy-start(f32[1,128]{1,0:T(1,128)} %wt_ref.3) | copy-start | bytes 1540
  0.7 33.4 %copy-start = (bf16[64,128,128]{2,1,0:T(8,128)(2,1)S(1)}, bf16[64,128,128]{2,1,0:T(8,128)(2,1)}, u32[]{:S(2)}) copy-start(bf16[64,128,128]{2,1,0:T(8,128)(2,1)} %sens.5) | copy-start | bytes 6291460
  0.7 33.4 %copy-start.4 = (s32[64]{0:T(128)S(1)}, s32[64]{0:T(128)}, u32[]{:S(2)}) copy-start(s32[64]{0:T(128)} %bund.5) | copy-start | bytes 772
  0.7 33.4 %copy-start.5 = (s32[64]{0:T(128)S(1)}, s32[64]{0:T(128)}, u32[]{:S(2)}) copy-start(s32[64]{0:T(128)} %cblk.5) | copy-start | bytes 772
  21.0 0.7 copy-start.3
  21.7 24.3 %copy-start.1 = (f32[2048,128]{1,0:T(8,128)S(1)}, f32[2048,128]{1,0:T(8,128)}, u32[]{:S(2)}) copy-start(f32[2048,128]{1,0:T(8,128)} %param.10) | copy-start | bytes 3145732
  21.7 12.3 %all-to-all-start.1 = ((bf16[8,1,128,128]{3,2,1,0:T(8,128)(2,1)}), bf16[8,1,128,128]{3,2,1,0:T(8,128)(2,1)S(1)}, u32[]{:S(2)}, u32[]{:S(2)}) async-start(bf16[8,1,128,128]{3,2,1,0:T(8,128)(2,1)} %copy-done.3), calls=%async_computation.1 | async-start | bytes 524288 | tf_op jit(solution)/shard_map/all_to_all | solution.py:231
  34.0 12.0 %copy-start.2 = (f32[2048,128]{1,0:T(8,128)S(1)}, f32[2048,128]{1,0:T(8,128)}, u32[]{:S(2)}) copy-start(f32[2048,128]{1,0:T(8,128)} %param.11) | copy-start | bytes 3145732
  35.9 1.6 %collective-permute-start = (bf16[8,128,128]{2,1,0:T(8,128)(2,1)S(1)}, bf16[8,128,128]{2,1,0:T(8,128)(2,1)S(1)}, u32[]{:S(2)}, u32[]{:S(2)}) collective-permute-start(bf16[8,128,128]{2,1,0:T(8,128)(2,1)S(1)} %get-tuple-element.11), channel_id=1, source_target_pairs={{0,8},{8,0},{16,24},{24,16},{1,9},{9,1},{17,25},{25,17},{2,10},{10... | collective-permute-start | bytes 786440 | tf_op jit(solution)/shard_map/ppermute | solution.py:222
  37.6 8.4 %collective-permute-start.1 = (bf16[8,128,128]{2,1,0:T(8,128)(2,1)S(1)}, bf16[8,128,128]{2,1,0:T(8,128)(2,1)S(1)}, u32[]{:S(2)}, u32[]{:S(2)}) collective-permute-start(bf16[8,128,128]{2,1,0:T(8,128)(2,1)S(1)} %adjoint1_pair.1.rest_0_), channel_id=1, source_target_pairs={{0,16},{8,24},{16,0},{24,8},{1,17},{9,25},{17,1},{25,9},{2,18},{10... | collective-permute-start | bytes 786440 | tf_op jit(solution)/shard_map/ppermute | solution.py:226
  46.4 1.6 %collective-permute-start.2 = (bf16[8,128,128]{2,1,0:T(8,128)(2,1)S(1)}, bf16[8,128,128]{2,1,0:T(8,128)(2,1)S(1)}, u32[]{:S(2)}, u32[]{:S(2)}) collective-permute-start(bf16[8,128,128]{2,1,0:T(8,128)(2,1)S(1)} %get-tuple-element.13.own_ref), channel_id=1, source_target_pairs={{0,8},{8,0},{16,24},{24,16},{1,9},{9,1},{17,25},{25,17},{2,10},{10... | collective-permute-start | bytes 786440 | tf_op jit(solution)/shard_map/ppermute | solution.py:222
  76.5 1.6 %collective-permute-start.3 = (bf16[8,128,128]{2,1,0:T(8,128)(2,1)S(1)}, bf16[8,128,128]{2,1,0:T(8,128)(2,1)S(1)}, u32[]{:S(2)}, u32[]{:S(2)}) collective-permute-start(bf16[8,128,128]{2,1,0:T(8,128)(2,1)S(1)} %get-tuple-element.16), channel_id=1, source_target_pairs={{0,8},{8,0},{16,24},{24,16},{1,9},{9,1},{17,25},{25,17},{2,10},{10... | collective-permute-start | bytes 786440 | tf_op jit(solution)/shard_map/ppermute | solution.py:222
  78.2 8.4 %collective-permute-start.4 = (bf16[8,128,128]{2,1,0:T(8,128)(2,1)S(1)}, bf16[8,128,128]{2,1,0:T(8,128)(2,1)S(1)}, u32[]{:S(2)}, u32[]{:S(2)}) collective-permute-start(bf16[8,128,128]{2,1,0:T(8,128)(2,1)S(1)} %adjoint2_pair.1.rest_0_), channel_id=1, source_target_pairs={{0,16},{8,24},{16,0},{24,8},{1,17},{9,25},{17,1},{25,9},{2,18},{10... | collective-permute-start | bytes 786440 | tf_op jit(solution)/shard_map/ppermute | solution.py:226
  86.8 1.6 %collective-permute-start.5 = (bf16[8,128,128]{2,1,0:T(8,128)(2,1)S(1)}, bf16[8,128,128]{2,1,0:T(8,128)(2,1)S(1)}, u32[]{:S(2)}, u32[]{:S(2)}) collective-permute-start(bf16[8,128,128]{2,1,0:T(8,128)(2,1)S(1)} %total.1.own_ref), channel_id=1, source_target_pairs={{0,8},{8,0},{16,24},{24,16},{1,9},{9,1},{17,25},{25,17},{2,10},{10... | collective-permute-start | bytes 786440 | tf_op jit(solution)/shard_map/ppermute | solution.py:222
where the time goes:
time: 90 us; the launch traced here: 89.6 us
  blocking collectives  40.7 us (45%)
  waiting for transfers between devices  27.6 us (31%)
  Pallas kernels  12.6 us (14%)
  starting transfers between devices  7.18 us (8%)
    all_to_all x3, blocking collectives, over_band(): lax.all_to_all(array, 'band', split_axis=0, concat_axis=0, tiled=True)  40.7 us
    ppermute x2, waiting for transfers between devices, other_chips(): lax.ppermute(array, 'shot', [(i, i ^ 2 * d) for i in range(nshot)])  13.6 us
    all_to_all x1, waiting for transfers between devices, over_band(): lax.all_to_all(array, 'band', split_axis=0, concat_axis=0, tiled=True)  8.57 us
    ppermute x4, waiting for transfers between devices, other_core(): return lax.ppermute(array, 'shot', [(i, i ^ 1) for i in range(nshot)])  5.36 us
    pallas_call x1, Pallas kernels, per_device(): call(first_forward_kernel, part_out, [part_acc, whole_field, pltpu.SMEM((...  4.03 us
    pallas_call x2, Pallas kernels, adjoint(): call(adjoint_kernel, (half_f32, half_bf16), [pltpu.VMEM((cells, samples,...  3.81 us
    all_to_all x1, starting transfers between devices, over_band(): lax.all_to_all(array, 'band', split_axis=0, concat_axis=0, tiled=True)  3.72 us
    ppermute x2, starting transfers between devices, other_chips(): lax.ppermute(array, 'shot', [(i, i ^ 2 * d) for i in range(nshot)])  3.18 us
  transfers between devices with their start and end apart: 7, of which 7 were waited for; matrix products, arithmetic and copies ran while one was open for 0% of the time, Pallas kernels for 1%

commit v1 on v0

v1 whole, which is shorter than its diff:
```python
import functools

import jax
import jax.numpy as jnp
from jax import lax
from jax.experimental import pallas as pl
from jax.experimental.pallas import tpu as pltpu
from jax.sharding import PartitionSpec as P

CBLK = 128
GROUP = 16
CHUNKS = 4
CHAINS = 2
FIRST_VMEM = 57 << 20

VMEM = pl.BlockSpec(memory_space=pltpu.VMEM)
SMEM = pl.BlockSpec(memory_space=pltpu.SMEM)
HBM = pl.BlockSpec(memory_space=pltpu.HBM)

bf16, f32 = jnp.bfloat16, jnp.float32
arr = jax.ShapeDtypeStruct


def call(body, outs, scratch, in_specs, name, flops=0, bytes_accessed=0, vmem=32 << 20):
    return pl.pallas_call(
        body,
        out_shape=outs,
        in_specs=in_specs,
        out_specs=jax.tree.map(lambda _: VMEM, outs),
        scratch_shapes=scratch,
        compiler_params=pltpu.CompilerParams(vmem_limit_bytes=vmem),
        cost_estimate=pl.CostEstimate(
            flops=flops, bytes_accessed=bytes_accessed, transcendentals=0
        ),
        name=name,
    )


def products(first, count, product_of, slot_of, acc_ref):
    def group(g, carry):
        ks = [first + g * GROUP + j for j in range(GROUP)]
        prods = [product_of(k) for k in ks]
        for k, prod in zip(ks, prods):
            acc_ref[slot_of(k)] += prod
        return carry

    if count == GROUP:
        group(0, 0)
    else:
        lax.fori_loop(0, count // GROUP, group, 0)


def first_forward_kernel(
    bund_hbm, cblk_hbm, sens_hbm, state_hbm, prior_hbm, *rest
):
    out_refs, (acc, probe, bund, cblk, sens, state, prior, sems) = rest[:CHAINS], rest[CHAINS:]
    nblk = sens.shape[0]
    step = nblk // CHUNKS
    half = state.shape[0] // 2
    small = [
        pltpu.make_async_copy(bund_hbm, bund, sems.at[0]),
        pltpu.make_async_copy(cblk_hbm, cblk, sems.at[1]),
    ]
    fields = []
    for h in range(2):
        part = pl.ds(h * half, half)
        fields.append(
            [
                pltpu.make_async_copy(state_hbm.at[part], state.at[part], sems.at[2 + 2 * h]),
                pltpu.make_async_copy(prior_hbm.at[part], prior.at[part], sems.at[3 + 2 * h]),
            ]
        )

    def block_copy(c):
        part = pl.ds(c * step, step)
        return pltpu.make_async_copy(sens_hbm.at[part], sens.at[part], sems.at[6 + c])

    for copy in small + fields[0] + fields[1] + [block_copy(c) for c in range(CHUNKS)]:
        copy.start()
    acc[...] = jnp.zeros_like(acc)
    for h in range(2):
        part = pl.ds(h * half, half)
        for copy in fields[h]:
            copy.wait()
        probe[part] = (state[part] + 0.5 * prior[part]).astype(bf16)
    for copy in small:
        copy.wait()

    def chunk(c, carry):
        block_copy(c).wait()
        products(
            c * step,
            step,
            lambda k: jnp.dot(sens[k], probe[cblk[k]], preferred_element_type=f32),
            lambda k: bund[k],
            acc,
        )
        return carry

    lax.fori_loop(0, CHUNKS, chunk, 0)
    for m in range(acc.shape[0]):
        turned = acc[m].T.astype(bf16)
        rows = turned.shape[0] // CHAINS
        for h, out_ref in enumerate(out_refs):
            out_ref[m] = turned[h * rows : (h + 1) * rows]


def turn_field_kernel(shot_ref, state_hbm, prior_hbm, *rest):
    out_refs, (state, prior, sems) = rest[:CHAINS], rest[CHAINS:]
    half = state.shape[0]
    part = pl.ds(shot_ref[0] % 2 * half, half)
    copies = [
        pltpu.make_async_copy(state_hbm.at[part], state, sems.at[0]),
        pltpu.make_async_copy(prior_hbm.at[part], prior, sems.at[1]),
    ]
    for copy in copies:
        copy.start()
    for copy in copies:
        copy.wait()
    for i in range(half):
        turned = (state[i] + prior[i]).T
        rows = turned.shape[0] // CHAINS
        for h, out_ref in enumerate(out_refs):
            out_ref[i] = turned[h * rows : (h + 1) * rows]


def forward_kernel(shot_ref, bund, cblk, sens, own_ref, mate_ref, out_ref, acc, probe):
    half = own_ref.shape[0]
    core = shot_ref[0] % 2
    probe[pl.ds(core * half, half)] = own_ref[...]
    probe[pl.ds((1 - core) * half, half)] = mate_ref[...]
    acc[...] = jnp.zeros_like(acc)
    products(
        0,
        sens.shape[0],
        lambda k: lax.dot_general(
            probe[cblk[k]], sens[k], (((1,), (1,)), ((), ())), preferred_element_type=f32
        ),
        lambda k: bund[k],
        acc,
    )
    out_ref[...] = acc[...].astype(bf16)


def adjoint_kernel(shot_ref, bund, cblk, sens, resid, keep_ref, give_ref, acc):
    acc[...] = jnp.zeros_like(acc)
    products(
        0,
        sens.shape[0],
        lambda k: jnp.dot(resid[bund[k]], sens[k], preferred_element_type=f32),
        lambda k: cblk[k],
        acc,
    )
    half = keep_ref.shape[0]
    core = shot_ref[0] % 2
    keep_ref[...] = acc[pl.ds(core * half, half)]
    give_ref[...] = acc[pl.ds((1 - core) * half, half)].astype(bf16)


def pair_kernel(keep_ref, got_ref, out_ref):
    out_ref[...] = (keep_ref[...] + got_ref[...].astype(f32)).astype(bf16)


def residual_kernel(parts_ref, obs_ref, wt_ref, out_ref, *resid_ref):
    for i in range(parts_ref.shape[1]):
        total = parts_ref[0, i].astype(f32)
        for d in range(1, parts_ref.shape[0]):
            total += parts_ref[d, i].astype(f32)
        resid = wt_ref[pl.ds(i, 1), :] * (total - obs_ref[pl.ds(i, 1), :])
        if resid_ref:
            resid_ref[0][i] = resid
        rounded = resid.astype(bf16)
        for d in range(parts_ref.shape[0]):
            out_ref[d, i] = rounded


def turn_residual_kernel(*refs):
    in_refs, out_ref = refs[:-1], refs[-1]
    for i in range(out_ref.shape[0]):
        out_ref[i] = jnp.concatenate([in_ref[i] for in_ref in in_refs], axis=0).T


def sum_over_y(chip_y, part_refs, order, i):
    if len(part_refs) > 2:
        for d, part_ref in enumerate(part_refs):
            order[chip_y ^ d] = part_ref[i]
        parts = [order[y] for y in range(len(part_refs))]
    else:
        parts = [part_ref[i] for part_ref in part_refs]
    total = parts[0].astype(f32)
    for part in parts[1:]:
        total += part.astype(f32)
    return total


def probe_kernel(ny, shot_ref, field_ref, *rest):
    part_refs, (out_ref, grad_ref, order) = rest[:ny], rest[ny:]
    for i in range(out_ref.shape[0]):
        grad = sum_over_y(shot_ref[0] // 2, part_refs, order, i)
        grad_ref[i] = grad
        out_ref[i] = (field_ref[i] - 0.25 * grad).astype(bf16)


def total_kernel(ny, shot_ref, grad_ref, *rest):
    part_refs, (out_ref, order) = rest[:ny], rest[ny:]
    for i in range(out_ref.shape[0]):
        grad2 = sum_over_y(shot_ref[0] // 2, part_refs, order, i)
        out_ref[i] = (grad_ref[i] + grad2).astype(bf16)


def last_kernel(shot_ref, state, prior, *rest):
    own_refs, mate_refs, out_ref = rest[:CHAINS], rest[CHAINS : 2 * CHAINS], rest[2 * CHAINS]
    half = own_refs[0].shape[0]
    core = shot_ref[0] % 2
    for at, part_refs in ((core * half, own_refs), ((1 - core) * half, mate_refs)):
        for i in range(half):
            both = jnp.concatenate([part_ref[i] for part_ref in part_refs], axis=0)
            both = both.astype(f32).T
            out_ref[at + i] = state[at + i] + 0.5 * (prior[at + i] - 0.25 * both)


def per_device(nshot, nband, sens, bund, cblk, state, prior, observed, pick_weight):
    nblk = sens.shape[0]
    samples = state.shape[1]
    rows = samples // CHAINS
    owned, rays = observed.shape
    bundles = owned * nband
    cells = state.shape[0] // CBLK
    half = cells // 2
    ny = nshot // 2
    flops = 2 * nblk * rays * CBLK * samples
    sens_bytes = nblk * rays * CBLK * 2

    state_b = state.reshape(cells, CBLK, samples)
    prior_b = prior.reshape(cells, CBLK, samples)
    shot = lax.axis_index("shot").reshape(1)

    def other_core(array):
        return lax.ppermute(array, "shot", [(i, i ^ 1) for i in range(nshot)])

    def other_chips(array):
        return [array] + [
            lax.ppermute(array, "shot", [(i, i ^ (2 * d)) for i in range(nshot)])
            for d in range(1, ny)
        ]

    def over_band(array):
        return lax.all_to_all(array, "band", split_axis=0, concat_axis=0, tiled=True)

    both = range(CHAINS)
    half_bf16 = arr((half, rows, CBLK), bf16)
    half_f32 = arr((half, rows, CBLK), f32)
    half_field = pltpu.VMEM((half, CBLK, samples), f32)
    order = pltpu.VMEM((ny, rows, CBLK), bf16)

    def residual(part, name, keep):
        parts = over_band(part).reshape(nband, owned, rows, rays)
        outs = (arr((nband, owned, rows, rays), bf16),)
        if keep:
            outs += (arr((owned, rows, rays), f32),)
        copies, *resid = call(
            residual_kernel, outs, [], [VMEM] * 3, name, bytes_accessed=1 << 19
        )(parts, observed, pick_weight)
        return resid, over_band(copies).reshape(bundles, rows, rays)

    def adjoint(resid_all, name):
        keep, give = call(
            adjoint_kernel,
            (half_f32, half_bf16),
            [pltpu.VMEM((cells, rows, CBLK), f32)],
            [SMEM] * 3 + [VMEM] * 2,
            name,
            flops,
            sens_bytes,
        )(shot, bund, cblk, sens, resid_all)
        pair = call(
            pair_kernel, half_bf16, [], [VMEM] * 2, name + "_pair", bytes_accessed=1 << 19
        )(keep, other_core(give))
        return other_chips(pair)

    part1 = call(
        first_forward_kernel,
        tuple(arr((bundles, rows, rays), bf16) for _ in both),
        [
            pltpu.VMEM((bundles, rays, samples), f32),
            pltpu.VMEM((cells, CBLK, samples), bf16),
            pltpu.SMEM((nblk,), jnp.int32),
            pltpu.SMEM((nblk,), jnp.int32),
            pltpu.VMEM(sens.shape, bf16),
            pltpu.VMEM(state_b.shape, f32),
            pltpu.VMEM(state_b.shape, f32),
            pltpu.SemaphoreType.DMA((6 + CHUNKS,)),
        ],
        [HBM] * 5,
        "forward1",
        flops,
        sens_bytes,
        vmem=FIRST_VMEM,
    )(bund, cblk, sens, state_b, prior_b)
    field = call(
        turn_field_kernel,
        tuple(half_f32 for _ in both),
        [half_field, half_field, pltpu.SemaphoreType.DMA((2,))],
        [SMEM, HBM, HBM],
        "turn_field",
        bytes_accessed=2 << 20,
    )(shot, state_b, prior_b)

    resid2, total, grad1, part2, resid_all2 = [], [], [], [], []
    gparts1 = [adjoint(residual(part1[h], "residual1", False)[1], "adjoint1") for h in both]
    for h in both:
        probe_own, grad = call(
            functools.partial(probe_kernel, ny),
            (half_bf16, half_f32),
            [order],
            [SMEM] + [VMEM] * (1 + ny),
            "probe2",
            bytes_accessed=1 << 19,
        )(shot, field[h], *gparts1[h])
        grad1.append(grad)
        part2.append(
            call(
                forward_kernel,
                arr((bundles, rows, rays), bf16),
                [
                    pltpu.VMEM((bundles, rows, rays), f32),
                    pltpu.VMEM((cells, rows, CBLK), bf16),
                ],
                [SMEM] * 3 + [VMEM] * 3,
                "forward2",
                flops,
                sens_bytes,
            )(shot, bund, cblk, sens, probe_own, other_core(probe_own))
        )
    for h in both:
        (resid,), resid_all = residual(part2[h], "residual2", True)
        resid2.append(resid)
        gparts2 = adjoint(resid_all, "adjoint2")
        total.append(
            call(
                functools.partial(total_kernel, ny),
                half_bf16,
                [order],
                [SMEM] + [VMEM] * (1 + ny),
                "total",
                bytes_accessed=1 << 19,
            )(shot, grad1[h], *gparts2)
        )
    resid2 = call(
        turn_residual_kernel,
        arr((owned, rays, samples), f32),
        [],
        [VMEM] * CHAINS,
        "turn_residual",
        bytes_accessed=1 << 20,
    )(*resid2)
    new_state = call(
        last_kernel,
        arr((cells, CBLK, samples), f32),
        [],
        [SMEM] + [VMEM] * (2 + 2 * CHAINS),
        "new_state",
        bytes_accessed=4 << 20,
    )(shot, state_b, prior_b, *total, *[other_core(t) for t in total])
    return new_state.reshape(state.shape), resid2


def solution(mesh):
    in_specs = (
        P(("shot", "band"), None, None),
        P(("shot", "band")),
        P(("shot", "band")),
        P("band", None),
        P("band", None),
        P(("shot", "band"), None),
        P(("shot", "band"), None),
    )
    out_specs = (P("band", None), P(("shot", "band"), None, None))
    return jax.shard_map(
        functools.partial(per_device, mesh.shape["shot"], mesh.shape["band"]),
        mesh=mesh,
        in_specs=in_specs,
        out_specs=out_specs,
        check_vma=False,
    )
```

time: 90 us -> 121 us (1.34)
  blocking collectives: 40.7 us -> 14.6 us
  starting transfers between devices: 7.18 us -> 33.1 us
  waiting for transfers between devices: 27.6 us -> 42.7 us
  Pallas kernels: 12.6 us -> 23.1 us
  local copies, waits for them, and re-layouts: 0.73 us -> 4.97 us
    all_to_all x3 -> x1, blocking collectives: 40.7 us -> 14.6 us  [over_band(): lax.all_to_all(array, 'band', split_axis=0, concat_axis=0, tiled=True)]
    all_to_all x1 -> x7, waiting for transfers between devices: 8.57 us -> 34.3 us  [over_band(): lax.all_to_all(array, 'band', split_axis=0, concat_axis=0, tiled=True)]
    all_to_all x1 -> x7, starting transfers between devices: 3.72 us -> 26.5 us  [over_band(): lax.all_to_all(array, 'band', split_axis=0, concat_axis=0, tiled=True)]
    pallas_call x8 -> x15, Pallas kernels: 11.1 us -> 21.7 us  [the longest x4 7.5 us: adjoint(): call(adjoint_kernel, (half_f32, half_bf16), [pltpu.VMEM((cells, rows, CBL...]
    ppermute x2 -> x4, waiting for transfers between devices: 13.6 us -> 5.07 us  [other_chips(): lax.ppermute(array, 'shot', [(i, i ^ 2 * d) for i in range(nshot)])]
    unnamed x16 -> x32, local copies, waits for them, and re-layouts: 0.73 us -> 4.97 us
    ppermute x2 -> x4, starting transfers between devices: 3.18 us -> 5.81 us  [other_chips(): lax.ppermute(array, 'shot', [(i, i ^ 2 * d) for i in range(nshot)])]
    ppermute x4 -> x8, waiting for transfers between devices: 5.36 us -> 3.29 us  [other_core(): return lax.ppermute(array, 'shot', [(i, i ^ 1) for i in range(nshot)])]
  transfers between devices with their start and end apart: 7 -> 19, of which waited for: 7 -> 12; matrix products, arithmetic and copies ran while one was open for 0% -> 0% of each run, Pallas kernels for 1% -> 15%
where the time goes in v1:
time: 121 us; the launch traced here: 119 us
  waiting for transfers between devices  42.7 us (35%)
  starting transfers between devices  33.1 us (27%)
  Pallas kernels  23.1 us (19%)
  blocking collectives  14.6 us (12%)
  local copies, waits for them, and re-layouts  4.97 us (4%)
    all_to_all x7, waiting for transfers between devices, over_band(): lax.all_to_all(array, 'band', split_axis=0, concat_axis=0, tiled=True)  34.3 us
    all_to_all x7, starting transfers between devices, over_band(): lax.all_to_all(array, 'band', split_axis=0, concat_axis=0, tiled=True)  26.5 us
    all_to_all x1, blocking collectives, over_band(): lax.all_to_all(array, 'band', split_axis=0, concat_axis=0, tiled=True)  14.6 us
    pallas_call x4, Pallas kernels, adjoint(): call(adjoint_kernel, (half_f32, half_bf16), [pltpu.VMEM((cells, rows, CBL...  7.5 us
    pallas_call x2, Pallas kernels, per_device(): call(forward_kernel, arr((bundles, rows, rays), bf16), [pltpu.VMEM((bundl...  6.16 us
    ppermute x4, starting transfers between devices, other_chips(): lax.ppermute(array, 'shot', [(i, i ^ 2 * d) for i in range(nshot)])  5.81 us
    ppermute x4, waiting for transfers between devices, other_chips(): lax.ppermute(array, 'shot', [(i, i ^ 2 * d) for i in range(nshot)])  5.07 us
    unnamed x32, local copies, waits for them, and re-layouts  4.97 us
  transfers between devices with their start and end apart: 19, of which 12 were waited for; matrix products, arithmetic and copies ran while one was open for 0% of the time, Pallas kernels for 15%

profile of v1, /device:TPU:0, one launch (start us, length us, event | category | flops | bytes accessed | tf_op | source)
XLA Modules:
  0.0 119.4 jit_solution(16097897364634251290)
XLA Ops:
  0.7 4.1 %forward1.1 = (bf16[8,64,128]{2,1,0:T(8,128)(2,1)}, bf16[8,64,128]{2,1,0:T(8,128)(2,1)}) custom-call(s32[64]{0:T(128)} %bund.11, s32[64]{0:T(128)} %cblk.11, bf16[64,128,128]{2,1,0:T(8,128)(2,1)} %sens.11, f32[16,128,128]{2,1,0:T(8,128)} %bitcast.12, f32[16,128,128]{2,1,0:T(8,128)} %bitcast.15), custom_call_target="tpu_custom_call" | custom-call | flops 268435456 | bytes 2097152 | tf_op jit(solution)/shard_map/forward1/pallas_call | solution.py:281
  4.8 14.6 %all_to_all.40 = bf16[8,64,128]{2,1,0:T(8,128)(2,1)S(1)} all-to-all(bf16[8,64,128]{2,1,0:T(8,128)(2,1)} %get-tuple-element.23), channel_id=1, replica_groups=mesh['shot'=4,'band'=8] {'band'}, dimensions={0} | all-to-all | bytes 262144 | tf_op jit(solution)/shard_map/all_to_all | solution.py:248
  19.4 3.4 %all-to-all-start.4 = ((bf16[8,64,128]{2,1,0:T(8,128)(2,1)}), bf16[8,64,128]{2,1,0:T(8,128)(2,1)S(1)}, u32[]{:S(2)}, u32[]{:S(2)}) async-start(bf16[8,64,128]{2,1,0:T(8,128)(2,1)} %get-tuple-element.32), calls=%async_computation.4 | async-start | bytes 262144 | tf_op jit(solution)/shard_map/all_to_all | solution.py:248
  23.5 6.6 %all-to-all-done.4 = bf16[8,64,128]{2,1,0:T(8,128)(2,1)S(1)} async-done(((bf16[8,64,128]{2,1,0:T(8,128)(2,1)}), bf16[8,64,128]{2,1,0:T(8,128)(2,1)S(1)}, u32[]{:S(2)}, u32[]{:S(2)}) %all-to-all-start.4) | async-done | bytes 131104 | tf_op jit(solution)/shard_map/all_to_all | solution.py:248
  30.0 3.4 %all-to-all-start.1 = ((bf16[8,1,64,128]{3,2,1,0:T(8,128)(2,1)}), bf16[8,1,64,128]{3,2,1,0:T(8,128)(2,1)S(1)}, u32[]{:S(2)}, u32[]{:S(2)}) async-start(bf16[8,1,64,128]{3,2,1,0:T(8,128)(2,1)} %residual1.2), calls=%async_computation.1 | async-start | bytes 262144 | tf_op jit(solution)/shard_map/all_to_all | solution.py:248
  34.1 6.6 %all-to-all-done.1 = bf16[8,1,64,128]{3,2,1,0:T(8,128)(2,1)S(1)} async-done(((bf16[8,1,64,128]{3,2,1,0:T(8,128)(2,1)}), bf16[8,1,64,128]{3,2,1,0:T(8,128)(2,1)S(1)}, u32[]{:S(2)}, u32[]{:S(2)}) %all-to-all-start.1) | async-done | bytes 131104 | tf_op jit(solution)/shard_map/all_to_all | solution.py:248
  40.7 3.4 %all-to-all-start.5 = ((bf16[8,1,64,128]{3,2,1,0:T(8,128)(2,1)}), bf16[8,1,64,128]{3,2,1,0:T(8,128)(2,1)S(1)}, u32[]{:S(2)}, u32[]{:S(2)}) async-start(bf16[8,1,64,128]{3,2,1,0:T(8,128)(2,1)} %residual1.3), calls=%async_computation.5 | async-start | bytes 262144 | tf_op jit(solution)/shard_map/all_to_all | solution.py:248
  44.1 1.7 %adjoint1.2 = (f32[8,64,128]{2,1,0:T(8,128)S(1)}, bf16[8,64,128]{2,1,0:T(8,128)(2,1)S(1)}) custom-call(s32[1]{0:T(128)} %bitcast.shot_ref, s32[64]{0:T(128)S(1)} %copy-done.12, s32[64]{0:T(128)S(1)} %copy-done.13, bf16[64,128,128]{2,1,0:T(8,128)(2,1)S(1)} %copy-done, bf16[8,64,128]{2,1,0:T(8,128)(2,1)S(1)} %bitcast.19), custom_call_target="tpu_custom_call" | custom-call | flops 268435456 | bytes 2097152 | tf_op jit(solution)/shard_map/adjoint1/pallas_call | solution.py:267
  45.9 1.3 %collective-permute-done.got_ref = bf16[8,64,128]{2,1,0:T(8,128)(2,1)S(1)} collective-permute-done((bf16[8,64,128]{2,1,0:T(8,128)(2,1)S(1)}, bf16[8,64,128]{2,1,0:T(8,128)(2,1)S(1)}, u32[]{:S(2)}, u32[]{:S(2)}) %collective-permute-start) | collective-permute-done | bytes 131104 | tf_op jit(solution)/shard_map/ppermute | solution.py:239
  47.3 1.6 %collective-permute-start.1 = (bf16[8,64,128]{2,1,0:T(8,128)(2,1)S(1)}, bf16[8,64,128]{2,1,0:T(8,128)(2,1)S(1)}, u32[]{:S(2)}, u32[]{:S(2)}) collective-permute-start(bf16[8,64,128]{2,1,0:T(8,128)(2,1)S(1)} %adjoint1_pair.2.rest_0_), channel_id=1, source_target_pairs={{0,16},{8,24},{16,0},{24,8},{1,17},{9,25},{17,1},{25,9},{2,18},{10... | collective-permute-start | bytes 393224 | tf_op jit(solution)/shard_map/ppermute | solution.py:243
  48.9 2.5 %all-to-all-done.5 = bf16[8,1,64,128]{3,2,1,0:T(8,128)(2,1)S(1)} async-done(((bf16[8,1,64,128]{3,2,1,0:T(8,128)(2,1)}), bf16[8,1,64,128]{3,2,1,0:T(8,128)(2,1)S(1)}, u32[]{:S(2)}, u32[]{:S(2)}) %all-to-all-start.5) | async-done | bytes 131104 | tf_op jit(solution)/shard_map/all_to_all | solution.py:248
  51.4 1.7 %adjoint1.3 = (f32[8,64,128]{2,1,0:T(8,128)S(1)}, bf16[8,64,128]{2,1,0:T(8,128)(2,1)S(1)}) custom-call(s32[1]{0:T(128)} %bitcast.shot_ref, s32[64]{0:T(128)S(1)} %copy-done.12, s32[64]{0:T(128)S(1)} %copy-done.13, bf16[64,128,128]{2,1,0:T(8,128)(2,1)S(1)} %copy-done, bf16[8,64,128]{2,1,0:T(8,128)(2,1)S(1)} %bitcast.18), custom_call_target="tpu_custom_call" | custom-call | flops 268435456 | bytes 2097152 | tf_op jit(solution)/shard_map/adjoint1/pallas_call | solution.py:267
  54.8 1.6 %collective-permute-start.6 = (bf16[8,64,128]{2,1,0:T(8,128)(2,1)S(1)}, bf16[8,64,128]{2,1,0:T(8,128)(2,1)S(1)}, u32[]{:S(2)}, u32[]{:S(2)}) collective-permute-start(bf16[8,64,128]{2,1,0:T(8,128)(2,1)S(1)} %adjoint1_pair.3.rest_0_), channel_id=1, source_target_pairs={{0,16},{8,24},{16,0},{24,8},{1,17},{9,25},{17,1},{25,9},{2,18},{10... | collective-permute-start | bytes 393224 | tf_op jit(solution)/shard_map/ppermute | solution.py:243
  56.4 3.1 %forward2.2 = bf16[8,64,128]{2,1,0:T(8,128)(2,1)} custom-call(s32[1]{0:T(128)} %bitcast.shot_ref, s32[64]{0:T(128)S(1)} %copy-done.12, s32[64]{0:T(128)S(1)} %copy-done.13, bf16[64,128,128]{2,1,0:T(8,128)(2,1)S(1)} %copy-done, bf16[8,64,128]{2,1,0:T(8,128)(2,1)S(1)} %get-tuple-element.27.own_ref, bf16[8,64,128]{2,1,0:T(8,128)(2,1)S(1)} %collective-permute-done.2.mate_ref), custom_call_target="tpu_custom_call" | custom-call | flops 268435456 | bytes 2097152 | tf_op jit(solution)/shard_map/forward2/pallas_call | solution.py:322
  59.5 4.9 %all-to-all-start.2 = ((bf16[8,64,128]{2,1,0:T(8,128)(2,1)}), bf16[8,64,128]{2,1,0:T(8,128)(2,1)S(1)}, u32[]{:S(2)}, u32[]{:S(2)}) async-start(bf16[8,64,128]{2,1,0:T(8,128)(2,1)} %forward2.2), calls=%async_computation.2 | async-start | bytes 262144 | tf_op jit(solution)/shard_map/all_to_all | solution.py:248
  66.1 1.3 %collective-permute-done.7.mate_ref = bf16[8,64,128]{2,1,0:T(8,128)(2,1)S(1)} collective-permute-done((bf16[8,64,128]{2,1,0:T(8,128)(2,1)S(1)}, bf16[8,64,128]{2,1,0:T(8,128)(2,1)S(1)}, u32[]{:S(2)}, u32[]{:S(2)}) %collective-permute-start.7) | collective-permute-done | bytes 131104 | tf_op jit(solution)/shard_map/ppermute | solution.py:239
  67.4 3.1 %forward2.3 = bf16[8,64,128]{2,1,0:T(8,128)(2,1)} custom-call(s32[1]{0:T(128)} %bitcast.shot_ref, s32[64]{0:T(128)S(1)} %copy-done.12, s32[64]{0:T(128)S(1)} %copy-done.13, bf16[64,128,128]{2,1,0:T(8,128)(2,1)S(1)} %copy-done, bf16[8,64,128]{2,1,0:T(8,128)(2,1)S(1)} %get-tuple-element.36.own_ref, bf16[8,64,128]{2,1,0:T(8,128)(2,1)S(1)} %collective-permute-done.7.mate_ref), custom_call_target="tpu_custom_call" | custom-call | flops 268435456 | bytes 2097152 | tf_op jit(solution)/shard_map/forward2/pallas_call | solution.py:322
  70.5 1.2 %all-to-all-done.2 = bf16[8,64,128]{2,1,0:T(8,128)(2,1)S(1)} async-done(((bf16[8,64,128]{2,1,0:T(8,128)(2,1)}), bf16[8,64,128]{2,1,0:T(8,128)(2,1)S(1)}, u32[]{:S(2)}, u32[]{:S(2)}) %all-to-all-start.2) | async-done | bytes 131104 | tf_op jit(solution)/shard_map/all_to_all | solution.py:248
  71.7 4.8 %all-to-all-start.6 = ((bf16[8,64,128]{2,1,0:T(8,128)(2,1)}), bf16[8,64,128]{2,1,0:T(8,128)(2,1)S(1)}, u32[]{:S(2)}, u32[]{:S(2)}) async-start(bf16[8,64,128]{2,1,0:T(8,128)(2,1)} %forward2.3), calls=%async_computation.6 | async-start | bytes 262144 | tf_op jit(solution)/shard_map/all_to_all | solution.py:248
  77.2 6.7 %all-to-all-done.6 = bf16[8,64,128]{2,1,0:T(8,128)(2,1)S(1)} async-done(((bf16[8,64,128]{2,1,0:T(8,128)(2,1)}), bf16[8,64,128]{2,1,0:T(8,128)(2,1)S(1)}, u32[]{:S(2)}, u32[]{:S(2)}) %all-to-all-start.6) | async-done | bytes 131104 | tf_op jit(solution)/shard_map/all_to_all | solution.py:248
  83.8 3.4 %all-to-all-start.3 = ((bf16[8,1,64,128]{3,2,1,0:T(8,128)(2,1)}), bf16[8,1,64,128]{3,2,1,0:T(8,128)(2,1)S(1)}, u32[]{:S(2)}, u32[]{:S(2)}) async-start(bf16[8,1,64,128]{3,2,1,0:T(8,128)(2,1)} %get-tuple-element.28), calls=%async_computation.3 | async-start | bytes 262144 | tf_op jit(solution)/shard_map/all_to_all | solution.py:248
  87.9 6.6 %all-to-all-done.3 = bf16[8,1,64,128]{3,2,1,0:T(8,128)(2,1)S(1)} async-done(((bf16[8,1,64,128]{3,2,1,0:T(8,128)(2,1)}), bf16[8,1,64,128]{3,2,1,0:T(8,128)(2,1)S(1)}, u32[]{:S(2)}, u32[]{:S(2)}) %all-to-all-start.3) | async-done | bytes 131104 | tf_op jit(solution)/shard_map/all_to_all | solution.py:248
  94.5 3.4 %all-to-all-start.7 = ((bf16[8,1,64,128]{3,2,1,0:T(8,128)(2,1)}), bf16[8,1,64,128]{3,2,1,0:T(8,128)(2,1)S(1)}, u32[]{:S(2)}, u32[]{:S(2)}) async-start(bf16[8,1,64,128]{3,2,1,0:T(8,128)(2,1)} %get-tuple-element.37), calls=%async_computation.7 | async-start | bytes 262144 | tf_op jit(solution)/shard_map/all_to_all | solution.py:248
  97.9 2.4 %adjoint2.2 = (f32[8,64,128]{2,1,0:T(8,128)S(1)}, bf16[8,64,128]{2,1,0:T(8,128)(2,1)}) custom-call(s32[1]{0:T(128)} %bitcast.shot_ref, s32[64]{0:T(128)S(1)} %copy-done.12, s32[64]{0:T(128)S(1)} %copy-done.13, bf16[64,128,128]{2,1,0:T(8,128)(2,1)S(1)} %copy-done, bf16[8,64,128]{2,1,0:T(8,128)(2,1)S(1)} %bitcast.20), custom_call_target="tpu_custom_call" | custom-call | flops 268435456 | bytes 2097152 | tf_op jit(solution)/shard_map/adjoint2/pallas_call | solution.py:267
  100.9 4.2 %all-to-all-done.7 = bf16[8,1,64,128]{3,2,1,0:T(8,128)(2,1)S(1)} async-done(((bf16[8,1,64,128]{3,2,1,0:T(8,128)(2,1)}), bf16[8,1,64,128]{3,2,1,0:T(8,128)(2,1)S(1)}, u32[]{:S(2)}, u32[]{:S(2)}) %all-to-all-start.7) | async-done | bytes 131104 | tf_op jit(solution)/shard_map/all_to_all | solution.py:248
  105.2 1.7 %adjoint2.3 = (f32[8,64,128]{2,1,0:T(8,128)S(1)}, bf16[8,64,128]{2,1,0:T(8,128)(2,1)S(1)}) custom-call(s32[1]{0:T(128)} %bitcast.shot_ref, s32[64]{0:T(128)S(1)} %copy-done.12, s32[64]{0:T(128)S(1)} %copy-done.13, bf16[64,128,128]{2,1,0:T(8,128)(2,1)S(1)} %copy-done, bf16[8,64,128]{2,1,0:T(8,128)(2,1)S(1)} %bitcast.21), custom_call_target="tpu_custom_call" | custom-call | flops 268435456 | bytes 2097152 | tf_op jit(solution)/shard_map/adjoint2/pallas_call | solution.py:267
  107.0 1.3 %collective-permute-start.4 = (bf16[8,64,128]{2,1,0:T(8,128)(2,1)S(1)}, bf16[8,64,128]{2,1,0:T(8,128)(2,1)S(1)}, u32[]{:S(2)}, u32[]{:S(2)}) collective-permute-start(bf16[8,64,128]{2,1,0:T(8,128)(2,1)S(1)} %adjoint2_pair.2.rest_0_), channel_id=1, source_target_pairs={{0,16},{8,24},{16,0},{24,8},{1,17},{9,25},{17,1},{25,9},{2,18},{10... | collective-permute-start | bytes 393224 | tf_op jit(solution)/shard_map/ppermute | solution.py:243
  108.4 1.3 %collective-permute-start.9 = (bf16[8,64,128]{2,1,0:T(8,128)(2,1)S(1)}, bf16[8,64,128]{2,1,0:T(8,128)(2,1)S(1)}, u32[]{:S(2)}, u32[]{:S(2)}) collective-permute-start(bf16[8,64,128]{2,1,0:T(8,128)(2,1)S(1)} %adjoint2_pair.3.rest_0_), channel_id=1, source_target_pairs={{0,16},{8,24},{16,0},{24,8},{1,17},{9,25},{17,1},{25,9},{2,18},{10... | collective-permute-start | bytes 393224 | tf_op jit(solution)/shard_map/ppermute | solution.py:243
  109.6 3.7 %collective-permute-done.4.rest_1_ = bf16[8,64,128]{2,1,0:T(8,128)(2,1)S(1)} collective-permute-done((bf16[8,64,128]{2,1,0:T(8,128)(2,1)S(1)}, bf16[8,64,128]{2,1,0:T(8,128)(2,1)S(1)}, u32[]{:S(2)}, u32[]{:S(2)}) %collective-permute-start.4) | collective-permute-done | bytes 131104 | tf_op jit(solution)/shard_map/ppermute | solution.py:243
  113.4 0.9 copy-done.7
  114.5 1.3 %collective-permute-done.9.rest_1_ = bf16[8,64,128]{2,1,0:T(8,128)(2,1)S(1)} collective-permute-done((bf16[8,64,128]{2,1,0:T(8,128)(2,1)S(1)}, bf16[8,64,128]{2,1,0:T(8,128)(2,1)S(1)}, u32[]{:S(2)}, u32[]{:S(2)}) %collective-permute-start.9) | collective-permute-done | bytes 131104 | tf_op jit(solution)/shard_map/ppermute | solution.py:243
  118.2 1.2 %new_state.1 = f32[16,128,128]{2,1,0:T(8,128)} custom-call(s32[1]{0:T(128)} %bitcast.shot_ref, f32[16,128,128]{2,1,0:T(8,128)S(1)} %bitcast.14, f32[16,128,128]{2,1,0:T(8,128)S(1)} %bitcast.17, bf16[8,64,128]{2,1,0:T(8,128)(2,1)S(1)} %total.2.rest_0_, bf16[8,64,128]{2,1,0:T(8,128)(2,1)S(1)} %total.3.rest_1_, ...), custom_call_target="tpu_custom_call" | custom-call | bytes 4194304 | tf_op jit(solution)/shard_map/new_state/pallas_call | solution.py:357
  (61 shorter events, 9.5 us)
Async XLA Ops:
  0.6 22.1 %copy-start.14 = (f32[1,128]{1,0:T(1,128)S(1)}, f32[1,128]{1,0:T(1,128)}, u32[]{:S(2)}) copy-start(f32[1,128]{1,0:T(1,128)} %obs_ref.7) | copy-start | bytes 1540
  0.6 22.1 %copy-start.15 = (f32[1,128]{1,0:T(1,128)S(1)}, f32[1,128]{1,0:T(1,128)}, u32[]{:S(2)}) copy-start(f32[1,128]{1,0:T(1,128)} %wt_ref.7) | copy-start | bytes 1540
  0.7 43.4 %copy-start = (bf16[64,128,128]{2,1,0:T(8,128)(2,1)S(1)}, bf16[64,128,128]{2,1,0:T(8,128)(2,1)}, u32[]{:S(2)}) copy-start(bf16[64,128,128]{2,1,0:T(8,128)(2,1)} %sens.11) | copy-start | bytes 6291460
  0.7 43.4 %copy-start.12 = (s32[64]{0:T(128)S(1)}, s32[64]{0:T(128)}, u32[]{:S(2)}) copy-start(s32[64]{0:T(128)} %bund.11) | copy-start | bytes 772
  0.7 43.4 %copy-start.13 = (s32[64]{0:T(128)S(1)}, s32[64]{0:T(128)}, u32[]{:S(2)}) copy-start(s32[64]{0:T(128)} %cblk.11) | copy-start | bytes 772
  19.4 10.7 %all-to-all-start.4 = ((bf16[8,64,128]{2,1,0:T(8,128)(2,1)}), bf16[8,64,128]{2,1,0:T(8,128)(2,1)S(1)}, u32[]{:S(2)}, u32[]{:S(2)}) async-start(bf16[8,64,128]{2,1,0:T(8,128)(2,1)} %get-tuple-element.32), calls=%async_computation.4 | async-start | bytes 262144 | tf_op jit(solution)/shard_map/all_to_all | solution.py:248
  30.0 10.7 %all-to-all-start.1 = ((bf16[8,1,64,128]{3,2,1,0:T(8,128)(2,1)}), bf16[8,1,64,128]{3,2,1,0:T(8,128)(2,1)S(1)}, u32[]{:S(2)}, u32[]{:S(2)}) async-start(bf16[8,1,64,128]{3,2,1,0:T(8,128)(2,1)} %residual1.2), calls=%async_computation.1 | async-start | bytes 262144 | tf_op jit(solution)/shard_map/all_to_all | solution.py:248
  40.7 10.7 %all-to-all-start.5 = ((bf16[8,1,64,128]{3,2,1,0:T(8,128)(2,1)}), bf16[8,1,64,128]{3,2,1,0:T(8,128)(2,1)S(1)}, u32[]{:S(2)}, u32[]{:S(2)}) async-start(bf16[8,1,64,128]{3,2,1,0:T(8,128)(2,1)} %residual1.3), calls=%async_computation.5 | async-start | bytes 262144 | tf_op jit(solution)/shard_map/all_to_all | solution.py:248
  44.1 9.1 %copy-start.1 = (f32[2048,128]{1,0:T(8,128)S(1)}, f32[2048,128]{1,0:T(8,128)}, u32[]{:S(2)}) copy-start(f32[2048,128]{1,0:T(8,128)} %param.10) | copy-start | bytes 3145732
  45.8 1.4 %collective-permute-start = (bf16[8,64,128]{2,1,0:T(8,128)(2,1)S(1)}, bf16[8,64,128]{2,1,0:T(8,128)(2,1)S(1)}, u32[]{:S(2)}, u32[]{:S(2)}) collective-permute-start(bf16[8,64,128]{2,1,0:T(8,128)(2,1)S(1)} %get-tuple-element.25), channel_id=1, source_target_pairs={{0,8},{8,0},{16,24},{24,16},{1,9},{9,1},{17,25},{25,17},{2,10},{10... | collective-permute-start | bytes 393224 | tf_op jit(solution)/shard_map/ppermute | solution.py:239
  47.3 6.2 %collective-permute-start.1 = (bf16[8,64,128]{2,1,0:T(8,128)(2,1)S(1)}, bf16[8,64,128]{2,1,0:T(8,128)(2,1)S(1)}, u32[]{:S(2)}, u32[]{:S(2)}) collective-permute-start(bf16[8,64,128]{2,1,0:T(8,128)(2,1)S(1)} %adjoint1_pair.2.rest_0_), channel_id=1, source_target_pairs={{0,16},{8,24},{16,0},{24,8},{1,17},{9,25},{17,1},{25,9},{2,18},{10... | collective-permute-start | bytes 393224 | tf_op jit(solution)/shard_map/ppermute | solution.py:243
  51.4 1.8 %copy-start.2 = (f32[2048,128]{1,0:T(8,128)S(1)}, f32[2048,128]{1,0:T(8,128)}, u32[]{:S(2)}) copy-start(f32[2048,128]{1,0:T(8,128)} %param.11) | copy-start | bytes 3145732
  53.1 1.7 %collective-permute-start.5 = (bf16[8,64,128]{2,1,0:T(8,128)(2,1)S(1)}, bf16[8,64,128]{2,1,0:T(8,128)(2,1)S(1)}, u32[]{:S(2)}, u32[]{:S(2)}) collective-permute-start(bf16[8,64,128]{2,1,0:T(8,128)(2,1)S(1)} %get-tuple-element.34), channel_id=1, source_target_pairs={{0,8},{8,0},{16,24},{24,16},{1,9},{9,1},{17,25},{25,17},{2,10},{10... | collective-permute-start | bytes 393224 | tf_op jit(solution)/shard_map/ppermute | solution.py:239
  53.5 1.3 %copy-start.4 = (f32[8,64,128]{2,1,0:T(8,128)}, f32[8,64,128]{2,1,0:T(8,128)S(1)}, u32[]{:S(2)}) copy-start(f32[8,64,128]{2,1,0:T(8,128)S(1)} %get-tuple-element.31.field_ref) | copy-start | bytes 786436
  54.3 2.1 %collective-permute-start.2 = (bf16[8,64,128]{2,1,0:T(8,128)(2,1)S(1)}, bf16[8,64,128]{2,1,0:T(8,128)(2,1)S(1)}, u32[]{:S(2)}, u32[]{:S(2)}) collective-permute-start(bf16[8,64,128]{2,1,0:T(8,128)(2,1)S(1)} %get-tuple-element.27.own_ref), channel_id=1, source_target_pairs={{0,8},{8,0},{16,24},{24,16},{1,9},{9,1},{17,25},{25,17},{2,10},{10... | collective-permute-start | bytes 393224 | tf_op jit(solution)/shard_map/ppermute | solution.py:239
  54.8 9.6 %collective-permute-start.6 = (bf16[8,64,128]{2,1,0:T(8,128)(2,1)S(1)}, bf16[8,64,128]{2,1,0:T(8,128)(2,1)S(1)}, u32[]{:S(2)}, u32[]{:S(2)}) collective-permute-start(bf16[8,64,128]{2,1,0:T(8,128)(2,1)S(1)} %adjoint1_pair.3.rest_0_), channel_id=1, source_target_pairs={{0,16},{8,24},{16,0},{24,8},{1,17},{9,25},{17,1},{25,9},{2,18},{10... | collective-permute-start | bytes 393224 | tf_op jit(solution)/shard_map/ppermute | solution.py:243
  59.5 12.2 %all-to-all-start.2 = ((bf16[8,64,128]{2,1,0:T(8,128)(2,1)}), bf16[8,64,128]{2,1,0:T(8,128)(2,1)S(1)}, u32[]{:S(2)}, u32[]{:S(2)}) async-start(bf16[8,64,128]{2,1,0:T(8,128)(2,1)} %forward2.2), calls=%async_computation.2 | async-start | bytes 262144 | tf_op jit(solution)/shard_map/all_to_all | solution.py:248
  64.4 1.0 copy-start.5
  66.1 1.3 %collective-permute-start.7 = (bf16[8,64,128]{2,1,0:T(8,128)(2,1)S(1)}, bf16[8,64,128]{2,1,0:T(8,128)(2,1)S(1)}, u32[]{:S(2)}, u32[]{:S(2)}) collective-permute-start(bf16[8,64,128]{2,1,0:T(8,128)(2,1)S(1)} %get-tuple-element.36.own_ref), channel_id=1, source_target_pairs={{0,8},{8,0},{16,24},{24,16},{1,9},{9,1},{17,25},{25,17},{2,10},{10... | collective-permute-start | bytes 393224 | tf_op jit(solution)/shard_map/ppermute | solution.py:239
  71.7 12.1 %all-to-all-start.6 = ((bf16[8,64,128]{2,1,0:T(8,128)(2,1)}), bf16[8,64,128]{2,1,0:T(8,128)(2,1)S(1)}, u32[]{:S(2)}, u32[]{:S(2)}) async-start(bf16[8,64,128]{2,1,0:T(8,128)(2,1)} %forward2.3), calls=%async_computation.6 | async-start | bytes 262144 | tf_op jit(solution)/shard_map/all_to_all | solution.py:248
  83.8 10.7 %all-to-all-start.3 = ((bf16[8,1,64,128]{3,2,1,0:T(8,128)(2,1)}), bf16[8,1,64,128]{3,2,1,0:T(8,128)(2,1)S(1)}, u32[]{:S(2)}, u32[]{:S(2)}) async-start(bf16[8,1,64,128]{3,2,1,0:T(8,128)(2,1)} %get-tuple-element.28), calls=%async_computation.3 | async-start | bytes 262144 | tf_op jit(solution)/shard_map/all_to_all | solution.py:248
  94.5 10.7 %all-to-all-start.7 = ((bf16[8,1,64,128]{3,2,1,0:T(8,128)(2,1)}), bf16[8,1,64,128]{3,2,1,0:T(8,128)(2,1)S(1)}, u32[]{:S(2)}, u32[]{:S(2)}) async-start(bf16[8,1,64,128]{3,2,1,0:T(8,128)(2,1)} %get-tuple-element.37), calls=%async_computation.7 | async-start | bytes 262144 | tf_op jit(solution)/shard_map/all_to_all | solution.py:248
  100.9 6.0 %collective-permute-start.3 = (bf16[8,64,128]{2,1,0:T(8,128)(2,1)}, bf16[8,64,128]{2,1,0:T(8,128)(2,1)S(1)}, u32[]{:S(2)}, u32[]{:S(2)}) collective-permute-start(bf16[8,64,128]{2,1,0:T(8,128)(2,1)} %get-tuple-element.30), channel_id=1, source_target_pairs={{0,8},{8,0},{16,24},{24,16},{1,9},{9,1},{17,25},{25,17},{2,10},{10... | collective-permute-start | bytes 393224 | tf_op jit(solution)/shard_map/ppermute | solution.py:239
  105.2 1.8 %copy-start.11 = (f32[8,64,128]{2,1,0:T(8,128)S(1)}, f32[8,64,128]{2,1,0:T(8,128)}, u32[]{:S(2)}) copy-start(f32[8,64,128]{2,1,0:T(8,128)} %copy-done.10) | copy-start | bytes 786436
  105.2 13.0 %copy-start.3 = (f32[2048,128]{1,0:T(8,128)S(1)}, f32[2048,128]{1,0:T(8,128)}, u32[]{:S(2)}) copy-start(f32[2048,128]{1,0:T(8,128)} %param.11) | copy-start | bytes 3145732
  106.9 1.4 %collective-permute-start.8 = (bf16[8,64,128]{2,1,0:T(8,128)(2,1)S(1)}, bf16[8,64,128]{2,1,0:T(8,128)(2,1)S(1)}, u32[]{:S(2)}, u32[]{:S(2)}) collective-permute-start(bf16[8,64,128]{2,1,0:T(8,128)(2,1)S(1)} %get-tuple-element.39), channel_id=1, source_target_pairs={{0,8},{8,0},{16,24},{24,16},{1,9},{9,1},{17,25},{25,17},{2,10},{10... | collective-permute-start | bytes 393224 | tf_op jit(solution)/shard_map/ppermute | solution.py:239
  107.0 6.4 %collective-permute-start.4 = (bf16[8,64,128]{2,1,0:T(8,128)(2,1)S(1)}, bf16[8,64,128]{2,1,0:T(8,128)(2,1)S(1)}, u32[]{:S(2)}, u32[]{:S(2)}) collective-permute-start(bf16[8,64,128]{2,1,0:T(8,128)(2,1)S(1)} %adjoint2_pair.2.rest_0_), channel_id=1, source_target_pairs={{0,16},{8,24},{16,0},{24,8},{1,17},{9,25},{17,1},{25,9},{2,18},{10... | collective-permute-start | bytes 393224 | tf_op jit(solution)/shard_map/ppermute | solution.py:243
  108.4 7.4 %collective-permute-start.9 = (bf16[8,64,128]{2,1,0:T(8,128)(2,1)S(1)}, bf16[8,64,128]{2,1,0:T(8,128)(2,1)S(1)}, u32[]{:S(2)}, u32[]{:S(2)}) collective-permute-start(bf16[8,64,128]{2,1,0:T(8,128)(2,1)S(1)} %adjoint2_pair.3.rest_0_), channel_id=1, source_target_pairs={{0,16},{8,24},{16,0},{24,8},{1,17},{9,25},{17,1},{25,9},{2,18},{10... | collective-permute-start | bytes 393224 | tf_op jit(solution)/shard_map/ppermute | solution.py:243
  113.4 1.0 copy-start.7
  114.4 3.2 %collective-permute-start.10 = (bf16[8,64,128]{2,1,0:T(8,128)(2,1)S(1)}, bf16[8,64,128]{2,1,0:T(8,128)(2,1)S(1)}, u32[]{:S(2)}, u32[]{:S(2)}) collective-permute-start(bf16[8,64,128]{2,1,0:T(8,128)(2,1)S(1)} %total.2.rest_0_), channel_id=1, source_target_pairs={{0,8},{8,0},{16,24},{24,16},{1,9},{9,1},{17,25},{25,17},{2,10},{10... | collective-permute-start | bytes 393224 | tf_op jit(solution)/shard_map/ppermute | solution.py:239
  115.8 1.0 copy-start.9
  116.8 1.4 %collective-permute-start.11 = (bf16[8,64,128]{2,1,0:T(8,128)(2,1)S(1)}, bf16[8,64,128]{2,1,0:T(8,128)(2,1)S(1)}, u32[]{:S(2)}, u32[]{:S(2)}) collective-permute-start(bf16[8,64,128]{2,1,0:T(8,128)(2,1)S(1)} %total.3.rest_1_), channel_id=1, source_target_pairs={{0,8},{8,0},{16,24},{24,16},{1,9},{9,1},{17,25},{25,17},{2,10},{10... | collective-permute-start | bytes 393224 | tf_op jit(solution)/shard_map/ppermute | solution.py:239
  (3 other events, 2.1 us)

commit v2 on v0

v2 whole, which is shorter than its diff:
```python
import functools

import jax
import jax.numpy as jnp
from jax import lax
from jax.experimental import pallas as pl
from jax.experimental.pallas import tpu as pltpu
from jax.sharding import PartitionSpec as P

CBLK = 128
GROUP = 16
PAIRS = 4
CHUNKS = 4
FIRST_VMEM = 57 << 20

VMEM = pl.BlockSpec(memory_space=pltpu.VMEM)
SMEM = pl.BlockSpec(memory_space=pltpu.SMEM)
HBM = pl.BlockSpec(memory_space=pltpu.HBM)
ANY = pl.BlockSpec(memory_space=pl.ANY)

bf16, f32, i32 = jnp.bfloat16, jnp.float32, jnp.int32
arr = jax.ShapeDtypeStruct

BLOCK, OPERAND, TARGET, STEPS = range(4)


def call(body, outs, scratch, in_specs, name, flops=0, bytes_accessed=0, vmem=32 << 20, **more):
    if "out_specs" not in more:
        more["out_specs"] = jax.tree.map(lambda _: VMEM, outs)
    return pl.pallas_call(
        body,
        out_shape=outs,
        in_specs=in_specs,
        scratch_shapes=scratch,
        compiler_params=pltpu.CompilerParams(vmem_limit_bytes=vmem),
        cost_estimate=pl.CostEstimate(
            flops=flops, bytes_accessed=bytes_accessed, transcendentals=0
        ),
        name=name,
        **more,
    )


def region_of(nblk, bins):
    step = 2 * PAIRS
    return -(-(nblk + bins) // step) * step


def column(row):
    n = row.shape[1]
    eye = lax.broadcasted_iota(i32, (n, n), 0) == lax.broadcasted_iota(i32, (n, n), 1)
    return jnp.sum(jnp.where(eye, row, 0.0), axis=1, keepdims=True)


def make_plan(cls, bins, target, operand, empty, region, plan_ref):
    n, classes = cls.shape[1], len(empty)
    key = cls * bins + target
    key_c, cls_c = column(key), column(cls)
    row = lax.broadcasted_iota(i32, (n, n), 0)
    col = lax.broadcasted_iota(i32, (n, n), 1)
    before = jnp.sum(
        jnp.where((key_c == key) & (col < row), 1.0, 0.0), axis=1, keepdims=True
    )
    bin_of = lax.broadcasted_iota(i32, (n, classes * bins), 1).astype(f32)
    count = jnp.sum(jnp.where(bin_of == key_c, 1.0, 0.0), axis=0, keepdims=True)
    padded = 2.0 * jnp.floor((count + 1.0) * 0.5)
    start = jnp.sum(
        jnp.where((bin_of < key_c) & (bin_of >= cls_c * bins), padded, 0.0),
        axis=1,
        keepdims=True,
    )
    position = cls_c * region + start + before
    width = plan_ref.shape[1]
    entry = lax.broadcasted_iota(i32, (n, width), 1).astype(f32)
    hit = entry == position

    def placed(values):
        return jnp.sum(jnp.where(hit, values, 0.0), axis=0, keepdims=True)

    block = lax.broadcasted_iota(i32, (n, 1), 0).astype(f32)
    at = entry[0:1]
    vacant = jnp.zeros((1, width), f32)
    steps = jnp.zeros((1, width), f32)
    for c in range(classes):
        mine = (bin_of[0:1] >= c * bins) & (bin_of[0:1] < (c + 1) * bins)
        size = jnp.sum(jnp.where(mine, padded, 0.0), axis=1, keepdims=True)
        step = 2 * PAIRS
        vacant += jnp.where((at >= c * region) & (at < (c + 1) * region), float(empty[c]), 0.0)
        steps += jnp.where(at == c, jnp.floor((size + (step - 1)) * (1.0 / step)), 0.0)
    filled = placed(1.0)
    plan_ref[BLOCK : BLOCK + 1, :] = placed(block).astype(i32)
    plan_ref[OPERAND : OPERAND + 1, :] = (
        placed(column(operand)) + (1.0 - filled) * vacant
    ).astype(i32)
    plan_ref[TARGET : TARGET + 1, :] = placed(column(target)).astype(i32)
    plan_ref[STEPS : STEPS + 1, :] = steps.astype(i32)


def paired_products(plan, c, region, product_of, acc_ref):
    def group(g, carry):
        first = c * region + g * (2 * PAIRS)
        at = [first + 2 * j for j in range(PAIRS)]
        prods = [
            product_of(
                plan[BLOCK, p], plan[BLOCK, p + 1], plan[OPERAND, p], plan[OPERAND, p + 1]
            )
            for p in at
        ]
        for p, prod in zip(at, prods):
            acc_ref[plan[TARGET, p]] += prod
        return carry

    lax.fori_loop(0, plan[STEPS, c], group, 0)


def first_forward_kernel(
    shot_ref,
    bund_row,
    cblk_row,
    bund_hbm,
    cblk_hbm,
    sens_hbm,
    state_hbm,
    prior_hbm,
    out_ref,
    adjoint_plan,
    forward_plan,
    acc,
    probe,
    bund,
    cblk,
    sens,
    state,
    prior,
    sems,
):
    nblk = sens.shape[0]
    step = nblk // CHUNKS
    cells = state.shape[0]
    half, quarter = cells // 2, cells // 4
    bundles = acc.shape[0]
    small = [
        pltpu.make_async_copy(bund_hbm, bund, sems.at[0]),
        pltpu.make_async_copy(cblk_hbm, cblk, sems.at[1]),
    ]
    fields = []
    for h in range(2):
        part = pl.ds(h * half, half)
        fields.append(
            [
                pltpu.make_async_copy(state_hbm.at[part], state.at[part], sems.at[2 + 2 * h]),
                pltpu.make_async_copy(prior_hbm.at[part], prior.at[part], sems.at[3 + 2 * h]),
            ]
        )

    def block_copy(c):
        part = pl.ds(c * step, step)
        return pltpu.make_async_copy(sens_hbm.at[part], sens.at[part], sems.at[6 + c])

    for copy in small + fields[0] + fields[1] + [block_copy(c) for c in range(CHUNKS)]:
        copy.start()
    acc[...] = jnp.zeros_like(acc)

    core = (shot_ref[0] % 2).astype(f32)
    bundle, cell = bund_row[...].astype(f32), cblk_row[...].astype(f32)
    upper = jnp.where(cell >= half, 1.0, 0.0)
    kept = jnp.where(upper == core, 1.0, 0.0)
    in_half = cell - upper * half
    second = jnp.where(in_half >= quarter, 1.0, 0.0)
    in_quarter = in_half - second * quarter
    make_plan(
        2.0 * second + kept,
        quarter,
        in_quarter,
        bundle,
        [bundles] * 4,
        region_of(nblk, quarter),
        adjoint_plan,
    )
    late = (1.0 - kept) * second
    make_plan(
        late,
        bundles,
        bundle,
        jnp.where(late > 0.5, in_quarter, cell),
        [cells, quarter],
        region_of(nblk, bundles),
        forward_plan,
    )

    for h in range(2):
        part = pl.ds(h * half, half)
        for copy in fields[h]:
            copy.wait()
        probe[part] = (state[part] + 0.5 * prior[part]).astype(bf16)
    for copy in small:
        copy.wait()

    def chunk(c, carry):
        block_copy(c).wait()
        for g in range(step // GROUP):
            ks = [c * step + g * GROUP + j for j in range(GROUP)]
            prods = [
                jnp.dot(sens[k], probe[cblk[k]], preferred_element_type=f32) for k in ks
            ]
            for k, prod in zip(ks, prods):
                acc[bund[k]] += prod
        return carry

    lax.fori_loop(0, CHUNKS, chunk, 0)
    out_ref[...] = acc[...].astype(bf16)


def forward_pair(sens, probe):
    def product(k1, k2, c1, c2):
        return jnp.dot(
            jnp.concatenate([sens[k1], sens[k2]], axis=1),
            jnp.concatenate([probe[c1], probe[c2]], axis=0),
            preferred_element_type=f32,
        )

    return product


def early_forward_kernel(shot_ref, plan, sens, own_a, own_b, mate_a, acc, probe):
    cells = probe.shape[0] - 1
    half, quarter = cells // 2, cells // 4
    core = shot_ref[0] % 2
    own, mate = core * half, (1 - core) * half
    probe[pl.ds(own, quarter)] = own_a[...]
    probe[pl.ds(own + quarter, quarter)] = own_b[...]
    probe[pl.ds(mate, quarter)] = mate_a[...]
    probe[cells] = jnp.zeros_like(probe[cells])
    acc[...] = jnp.zeros_like(acc)
    region = region_of(sens.shape[0], acc.shape[0])
    paired_products(plan, 0, region, forward_pair(sens, probe), acc)


def late_forward_kernel(plan, sens, mate_b, early, out_ref, acc, probe):
    quarter = mate_b.shape[0]
    probe[pl.ds(0, quarter)] = mate_b[...]
    probe[quarter] = jnp.zeros_like(probe[quarter])
    acc[...] = early[...]
    region = region_of(sens.shape[0], acc.shape[0])
    paired_products(plan, 1, region, forward_pair(sens, probe), acc)
    out_ref[...] = acc[...].astype(bf16)


def adjoint_kernel(classes, plan, sens, resid_ref, *rest):
    out_refs, (acc, resid) = rest[: len(classes)], rest[len(classes) :]
    bundles = resid_ref.shape[0]
    resid[pl.ds(0, bundles)] = resid_ref[...]
    resid[bundles] = jnp.zeros_like(resid[bundles])
    region = region_of(sens.shape[0], acc.shape[0])

    def product(k1, k2, b1, b2):
        return jnp.dot(
            jnp.concatenate([resid[b1], resid[b2]], axis=1),
            jnp.concatenate([sens[k1], sens[k2]], axis=0),
            preferred_element_type=f32,
        )

    for c, out_ref in zip(classes, out_refs):
        acc[...] = jnp.zeros_like(acc)
        paired_products(plan, c, region, product, acc)
        out_ref[...] = acc[...].astype(out_ref.dtype)


def pair_kernel(keep_ref, got_ref, out_ref):
    out_ref[...] = (keep_ref[...] + got_ref[...].astype(f32)).astype(bf16)


def residual_kernel(parts_ref, obs_ref, wt_ref, out_ref, *resid_ref):
    for i in range(parts_ref.shape[1]):
        total = parts_ref[0, i].astype(f32)
        for d in range(1, parts_ref.shape[0]):
            total += parts_ref[d, i].astype(f32)
        resid = wt_ref[pl.ds(i, 1), :] * (total.T - obs_ref[pl.ds(i, 1), :])
        if resid_ref:
            resid_ref[0][i] = resid
        rounded = resid.astype(bf16)
        for d in range(parts_ref.shape[0]):
            out_ref[d, i] = rounded


def turn_kernel(in_ref, out_ref):
    for i in range(in_ref.shape[0]):
        out_ref[i] = in_ref[i].T


def prepare_kernel(shot_ref, state, prior, after_ref, field_a, field_b, base_ref):
    quarter = field_a.shape[0]
    own = shot_ref[0] % 2 * (2 * quarter)
    for at, field_ref in ((own, field_a), (own + quarter, field_b)):
        part = pl.ds(at, quarter)
        field_ref[...] = state[part] + prior[part]
    base_ref[...] = state[...] + 0.5 * prior[...]


def sum_over_y(chip_y, part_refs, order, i):
    if len(part_refs) > 2:
        for d, part_ref in enumerate(part_refs):
            order[chip_y ^ d] = part_ref[i]
        parts = [order[y] for y in range(len(part_refs))]
    else:
        parts = [part_ref[i] for part_ref in part_refs]
    total = parts[0].astype(f32)
    for part in parts[1:]:
        total += part.astype(f32)
    return total.T


def probe_kernel(ny, shot_ref, field_ref, *rest):
    part_refs, (out_ref, grad_ref, order) = rest[:ny], rest[ny:]
    for i in range(out_ref.shape[0]):
        grad = sum_over_y(shot_ref[0] // 2, part_refs, order, i)
        grad_ref[i] = grad
        out_ref[i] = (field_ref[i] - 0.25 * grad).astype(bf16)


def total_kernel(ny, shot_ref, grad_ref, *rest):
    part_refs, (out_ref, order) = rest[:ny], rest[ny:]
    for i in range(out_ref.shape[0]):
        grad2 = sum_over_y(shot_ref[0] // 2, part_refs, order, i)
        out_ref[i] = (grad_ref[i] + grad2).astype(bf16)


def early_update_kernel(shot_ref, base, own_a, own_b, mate_a, out_hbm, rest_ref, new, sems):
    quarter = own_a.shape[0]
    core = shot_ref[0] % 2
    own, mate = core * (2 * quarter), (1 - core) * (2 * quarter)
    copies = []
    for n, (at, part_ref) in enumerate(((own, own_a), (own + quarter, own_b), (mate, mate_a))):
        new[n] = base[pl.ds(at, quarter)] - 0.125 * part_ref[...].astype(f32)
        copies.append(
            pltpu.make_async_copy(new.at[n], out_hbm.at[pl.ds(at, quarter)], sems.at[n])
        )
        copies[-1].start()
    rest_ref[...] = base[pl.ds(mate + quarter, quarter)]
    for copy in copies:
        copy.wait()


def late_update_kernel(shot_ref, rest_ref, mate_b, so_far_hbm, out_hbm, new, sem):
    quarter = mate_b.shape[0]
    at = (1 - shot_ref[0] % 2) * (2 * quarter) + quarter
    new[...] = rest_ref[...] - 0.125 * mate_b[...].astype(f32)
    copy = pltpu.make_async_copy(new, out_hbm.at[pl.ds(at, quarter)], sem)
    copy.start()
    copy.wait()


def per_device(nshot, nband, sens, bund, cblk, state, prior, observed, pick_weight):
    nblk = sens.shape[0]
    samples = state.shape[1]
    owned, rays = observed.shape
    bundles = owned * nband
    cells = state.shape[0] // CBLK
    quarter = cells // 4
    ny = nshot // 2
    flops = 2 * nblk * rays * CBLK * samples
    sens_bytes = nblk * rays * CBLK * 2

    state_b = state.reshape(cells, CBLK, samples)
    prior_b = prior.reshape(cells, CBLK, samples)
    shot = lax.axis_index("shot").reshape(1)

    def other_core(array):
        return lax.ppermute(array, "shot", [(i, i ^ 1) for i in range(nshot)])

    def other_chips(array):
        return [array] + [
            lax.ppermute(array, "shot", [(i, i ^ (2 * d)) for i in range(nshot)])
            for d in range(1, ny)
        ]

    def over_band(array):
        return lax.all_to_all(array, "band", split_axis=0, concat_axis=0, tiled=True)

    part_out = arr((bundles, rays, samples), bf16)
    part_f32 = arr((bundles, rays, samples), f32)
    part_acc = pltpu.VMEM((bundles, rays, samples), f32)
    quarter_bf16 = arr((quarter, CBLK, samples), bf16)
    quarter_f32 = arr((quarter, CBLK, samples), f32)
    order = pltpu.VMEM((ny, samples, CBLK), bf16)

    def residual(part, name, keep):
        parts = over_band(part).reshape(nband, owned, rays, samples)
        outs = (arr((nband, owned, samples, rays), bf16),)
        if keep:
            outs += (arr((owned, samples, rays), f32),)
        copies, *resid = call(
            residual_kernel, outs, [], [VMEM] * 3, name, bytes_accessed=1 << 20
        )(parts, observed, pick_weight)
        return resid, over_band(copies).reshape(bundles, samples, rays)

    def adjoint(plan, resid_all, name):
        def kernel(classes, part):
            return call(
                functools.partial(adjoint_kernel, classes),
                tuple(quarter_f32 if c % 2 else quarter_bf16 for c in classes),
                [
                    pltpu.VMEM((quarter, samples, CBLK), f32),
                    pltpu.VMEM((bundles + 1, samples, rays), bf16),
                ],
                [SMEM] + [VMEM] * 2,
                name + part,
                flops * len(classes) // 4,
                sens_bytes * len(classes) // 4,
            )(plan, sens, resid_all)

        def pair(keep, got, part):
            return call(
                pair_kernel,
                quarter_bf16,
                [],
                [VMEM] * 2,
                name + "_pair" + part,
                bytes_accessed=1 << 19,
            )(keep, got)

        (give_a,) = kernel((0,), "_give_a")
        got_a = other_core(give_a)
        keep_a, give_b = kernel((1, 2), "_keep_a")
        got_b = other_core(give_b)
        sums_a = other_chips(pair(keep_a, got_a, "_a"))
        (keep_b,) = kernel((3,), "_keep_b")
        sums_b = other_chips(pair(keep_b, got_b, "_b"))
        return sums_a, sums_b, keep_b

    part1, adjoint_plan, forward_plan = call(
        first_forward_kernel,
        (
            part_out,
            arr((4, 4 * region_of(nblk, quarter)), i32),
            arr((4, 2 * region_of(nblk, bundles)), i32),
        ),
        [
            part_acc,
            pltpu.VMEM((cells, CBLK, samples), bf16),
            pltpu.SMEM((nblk,), i32),
            pltpu.SMEM((nblk,), i32),
            pltpu.VMEM(sens.shape, bf16),
            pltpu.VMEM(state_b.shape, f32),
            pltpu.VMEM(state_b.shape, f32),
            pltpu.SemaphoreType.DMA((6 + CHUNKS,)),
        ],
        [SMEM, VMEM, VMEM] + [HBM] * 5,
        "forward1",
        flops,
        sens_bytes,
        vmem=FIRST_VMEM,
    )(shot, bund.reshape(1, nblk), cblk.reshape(1, nblk), bund, cblk, sens, state_b, prior_b)
    _, resid_all1 = residual(part1, "residual1", False)
    *sums1, after = adjoint(adjoint_plan, resid_all1, "adjoint1")

    *fields, base = call(
        prepare_kernel,
        (quarter_f32, quarter_f32, arr((cells, CBLK, samples), f32)),
        [],
        [SMEM, VMEM, VMEM, ANY],
        "prepare",
        bytes_accessed=4 << 20,
    )(shot, state_b, prior_b, after)
    own, grad1, mate = [], [], []
    for field, sums, part in zip(fields, sums1, "ab"):
        probe, grad = call(
            functools.partial(probe_kernel, ny),
            (quarter_bf16, quarter_f32),
            [order],
            [SMEM] + [VMEM] * (1 + ny),
            "probe2_" + part,
            bytes_accessed=1 << 19,
        )(shot, field, *sums)
        own.append(probe)
        grad1.append(grad)
        mate.append(other_core(probe))

    early = call(
        early_forward_kernel,
        part_f32,
        [pltpu.VMEM((cells + 1, CBLK, samples), bf16)],
        [SMEM] * 2 + [VMEM] * 4,
        "forward2_early",
        flops * 3 // 4,
        sens_bytes * 3 // 4,
    )(shot, forward_plan, sens, own[0], own[1], mate[0])
    part2 = call(
        late_forward_kernel,
        part_out,
        [part_acc, pltpu.VMEM((quarter + 1, CBLK, samples), bf16)],
        [SMEM] + [VMEM] * 3,
        "forward2_late",
        flops // 4,
        sens_bytes // 4,
    )(forward_plan, sens, mate[1], early)

    (resid2_t,), resid_all2 = residual(part2, "residual2", True)
    *sums2, _ = adjoint(adjoint_plan, resid_all2, "adjoint2")
    resid2 = call(
        turn_kernel,
        arr((owned, rays, samples), f32),
        [],
        [VMEM],
        "turn",
        bytes_accessed=1 << 20,
    )(resid2_t)
    own, mate = [], []
    for grad, sums, part in zip(grad1, sums2, "ab"):
        total = call(
            functools.partial(total_kernel, ny),
            quarter_bf16,
            [order],
            [SMEM] + [VMEM] * (1 + ny),
            "total_" + part,
            bytes_accessed=1 << 19,
        )(shot, grad, *sums)
        own.append(total)
        mate.append(other_core(total))
    whole = arr((cells, CBLK, samples), f32)
    so_far, rest = call(
        early_update_kernel,
        (whole, quarter_f32),
        [pltpu.VMEM((3, quarter, CBLK, samples), f32), pltpu.SemaphoreType.DMA((3,))],
        [SMEM] + [VMEM] * 4,
        "new_state_early",
        bytes_accessed=3 << 20,
        out_specs=(HBM, VMEM),
    )(shot, base, own[0], own[1], mate[0])
    new_state = call(
        late_update_kernel,
        whole,
        [pltpu.VMEM((quarter, CBLK, samples), f32), pltpu.SemaphoreType.DMA],
        [SMEM, VMEM, VMEM, HBM],
        "new_state_late",
        bytes_accessed=1 << 20,
        out_specs=HBM,
        input_output_aliases={3: 0},
    )(shot, rest, mate[1], so_far)
    return new_state.reshape(state.shape), resid2


def solution(mesh):
    in_specs = (
        P(("shot", "band"), None, None),
        P(("shot", "band")),
        P(("shot", "band")),
        P("band", None),
        P("band", None),
        P(("shot", "band"), None),
        P(("shot", "band"), None),
    )
    out_specs = (P("band", None), P(("shot", "band"), None, None))
    return jax.shard_map(
        functools.partial(per_device, mesh.shape["shot"], mesh.shape["band"]),
        mesh=mesh,
        in_specs=in_specs,
        out_specs=out_specs,
        check_vma=False,
    )
```

time: 90 us -> 91.6 us (1.018)
  waiting for transfers between devices: 27.6 us -> 10.2 us
  blocking collectives: 40.7 us -> 53.1 us
  Pallas kernels: 12.6 us -> 20.7 us
  starting transfers between devices: 7.18 us -> 5.35 us
    all_to_all x3 -> x4, blocking collectives: 40.7 us -> 53.1 us  [over_band(): lax.all_to_all(array, 'band', split_axis=0, concat_axis=0, tiled=True)]
    all_to_all x1 -> x0, waiting for transfers between devices: 8.57 us -> none  [over_band(): lax.all_to_all(array, 'band', split_axis=0, concat_axis=0, tiled=True)]
    pallas_call x9 -> x20, Pallas kernels: 11.6 us -> 19.7 us  [the longest x6 8.75 us: kernel(): call(functools.partial(adjoint_kernel, classes), tuple((quarter_f32 if c...]
    ppermute x4 -> x8, waiting for transfers between devices: 5.36 us -> 0.02 us  [other_core(): return lax.ppermute(array, 'shot', [(i, i ^ 1) for i in range(nshot)])]
    all_to_all x1 -> x0, starting transfers between devices: 3.72 us -> none  [over_band(): lax.all_to_all(array, 'band', split_axis=0, concat_axis=0, tiled=True)]
    ppermute x2 -> x4, waiting for transfers between devices: 13.6 us -> 10.2 us  [other_chips(): lax.ppermute(array, 'shot', [(i, i ^ 2 * d) for i in range(nshot)])]
    ppermute x2 -> x4, starting transfers between devices: 3.18 us -> 4.25 us  [other_chips(): lax.ppermute(array, 'shot', [(i, i ^ 2 * d) for i in range(nshot)])]
  transfers between devices with their start and end apart: 7 -> 12, of which waited for: 7 -> 4; matrix products, arithmetic and copies ran while one was open for 0% -> 0% of each run, Pallas kernels for 1% -> 12%
where the time goes in v2:
time: 91.6 us; the launch traced here: 91.1 us
  blocking collectives  53.1 us (58%)
  Pallas kernels  20.7 us (23%)
  waiting for transfers between devices  10.2 us (11%)
  starting transfers between devices  5.35 us (6%)
  between operations  0.95 us (1%)
    all_to_all x4, blocking collectives, over_band(): lax.all_to_all(array, 'band', split_axis=0, concat_axis=0, tiled=True)  53.1 us
    ppermute x4, waiting for transfers between devices, other_chips(): lax.ppermute(array, 'shot', [(i, i ^ 2 * d) for i in range(nshot)])  10.2 us
    pallas_call x6, Pallas kernels, kernel(): call(functools.partial(adjoint_kernel, classes), tuple((quarter_f32 if c...  8.75 us
    pallas_call x1, Pallas kernels, per_device(): call(first_forward_kernel, (part_out, arr((4, 4 * region_of(nblk, quarter...  4.85 us
    ppermute x4, starting transfers between devices, other_chips(): lax.ppermute(array, 'shot', [(i, i ^ 2 * d) for i in range(nshot)])  4.25 us
    pallas_call x1, Pallas kernels, per_device(): call(early_forward_kernel, part_f32, [pltpu.VMEM((cells + 1, CBLK, sample...  2.27 us
  transfers between devices with their start and end apart: 12, of which 4 were waited for; matrix products, arithmetic and copies ran while one was open for 0% of the time, Pallas kernels for 12%

profile of v2, /device:TPU:0, one launch (start us, length us, event | category | flops | bytes accessed | tf_op | source)
XLA Modules:
  0.0 91.1 jit_solution(10637689004232923971)
XLA Ops:
  0.7 4.9 %forward1.1 = (bf16[8,128,128]{2,1,0:T(8,128)(2,1)}, s32[4,288]{1,0:T(4,128)}, s32[4,144]{1,0:T(4,128)}) custom-call(s32[1]{0:T(128)} %bitcast.shot_ref, s32[1,64]{1,0:T(1,128)} %bitcast.23, s32[1,64]{1,0:T(1,128)} %bitcast.24, s32[64]{0:T(128)} %bund_hbm.1, s32[64]{0:T(128)} %cblk_hbm.1, bf16[64,128,128]{2,1,0:T(8,128)(2,1)} %sens.15, ...), custom_call_target="tpu_custom_call" | custom-call | flops 268435456 | bytes 2097152 | tf_op jit(solution)/shard_map/forward1/pallas_call | solution.py:431
  5.5 16.2 %all_to_all.20 = bf16[8,128,128]{2,1,0:T(8,128)(2,1)S(1)} all-to-all(bf16[8,128,128]{2,1,0:T(8,128)(2,1)} %get-tuple-element.21), channel_id=1, replica_groups=mesh['shot'=4,'band'=8] {'band'}, dimensions={0} | all-to-all | bytes 524288 | tf_op jit(solution)/shard_map/all_to_all | solution.py:378
  21.7 0.1 residual1.1
  21.8 12.0 %all_to_all.21 = bf16[8,1,128,128]{3,2,1,0:T(8,128)(2,1)S(1)} all-to-all(bf16[8,1,128,128]{3,2,1,0:T(8,128)(2,1)S(1)} %residual1.1), channel_id=1, replica_groups=mesh['shot'=4,'band'=8] {'band'}, dimensions={0} | all-to-all | bytes 524288 | tf_op jit(solution)/shard_map/all_to_all | solution.py:378
  33.8 0.7 copy-done.3
  34.5 1.1 %adjoint1_give_a.1 = bf16[4,128,128]{2,1,0:T(8,128)(2,1)S(1)} custom-call(s32[4,288]{1,0:T(4,128)S(1)} %copy-done.3, bf16[64,128,128]{2,1,0:T(8,128)(2,1)S(1)} %copy-done, bf16[8,128,128]{2,1,0:T(8,128)(2,1)S(1)} %bitcast.17), custom_call_target="tpu_custom_call" | custom-call | flops 67108864 | bytes 524288 | tf_op jit(solution)/shard_map/adjoint1_give_a/pallas_call | solution.py:399
  35.7 1.9 %adjoint1_keep_a.1 = (f32[4,128,128]{2,1,0:T(8,128)S(1)}, bf16[4,128,128]{2,1,0:T(8,128)(2,1)S(1)}) custom-call(s32[4,288]{1,0:T(4,128)S(1)} %copy-done.3, bf16[64,128,128]{2,1,0:T(8,128)(2,1)S(1)} %copy-done, bf16[8,128,128]{2,1,0:T(8,128)(2,1)S(1)} %bitcast.18), custom_call_target="tpu_custom_call" | custom-call | flops 134217728 | bytes 1048576 | tf_op jit(solution)/shard_map/adjoint1_keep_a/pallas_call | solution.py:399
  37.6 0.3 collective-permute-start.2
  38.0 1.8 %collective-permute-start.1 = (bf16[4,128,128]{2,1,0:T(8,128)(2,1)S(1)}, bf16[4,128,128]{2,1,0:T(8,128)(2,1)S(1)}, u32[]{:S(2)}, u32[]{:S(2)}) collective-permute-start(bf16[4,128,128]{2,1,0:T(8,128)(2,1)S(1)} %adjoint1_pair_a.1.rest_0_), channel_id=1, source_target_pairs={{0,16},{8,24},{16,0},{24,8},{1,17},{9,25},{17,1},{25,9},{2,18},{10... | collective-permute-start | bytes 393224 | tf_op jit(solution)/shard_map/ppermute | solution.py:373
  39.8 1.4 %adjoint1_keep_b.1.after_ref.keep_ref = f32[4,128,128]{2,1,0:T(8,128)S(1)} custom-call(s32[4,288]{1,0:T(4,128)S(1)} %copy-done.4, bf16[64,128,128]{2,1,0:T(8,128)(2,1)S(1)} %copy-done, bf16[8,128,128]{2,1,0:T(8,128)(2,1)S(1)} %bitcast.19), custom_call_target="tpu_custom_call" | custom-call | flops 67108864 | bytes 524288 | tf_op jit(solution)/shard_map/adjoint1_keep_b/pallas_call | solution.py:399
  41.2 0.1 collective-permute-start.3
  41.4 0.2 prepare.1
  41.5 2.4 %collective-permute-done.1.rest_1_ = bf16[4,128,128]{2,1,0:T(8,128)(2,1)S(1)} collective-permute-done((bf16[4,128,128]{2,1,0:T(8,128)(2,1)S(1)}, bf16[4,128,128]{2,1,0:T(8,128)(2,1)S(1)}, u32[]{:S(2)}, u32[]{:S(2)}) %collective-permute-start.1) | collective-permute-done | bytes 131104 | tf_op jit(solution)/shard_map/ppermute | solution.py:373
  43.9 0.1 probe2_a.1
  44.2 2.6 %collective-permute-done.3.rest_1_ = bf16[4,128,128]{2,1,0:T(8,128)(2,1)S(1)} collective-permute-done((bf16[4,128,128]{2,1,0:T(8,128)(2,1)S(1)}, bf16[4,128,128]{2,1,0:T(8,128)(2,1)S(1)}, u32[]{:S(2)}, u32[]{:S(2)}) %collective-permute-start.3) | collective-permute-done | bytes 131104 | tf_op jit(solution)/shard_map/ppermute | solution.py:373
  46.7 0.1 probe2_b.1
  47.0 2.3 %forward2_early.1.early = f32[8,128,128]{2,1,0:T(8,128)S(1)} custom-call(s32[1]{0:T(128)} %bitcast.shot_ref, s32[4,144]{1,0:T(4,128)S(1)} %copy-done.5, bf16[64,128,128]{2,1,0:T(8,128)(2,1)S(1)} %copy-done, bf16[4,128,128]{2,1,0:T(8,128)(2,1)S(1)} %get-tuple-element.30.own_a, bf16[4,128,128]{2,1,0:T(8,128)(2,1)S(1)} %get-tuple-element.29.own_b, ...), custom_call_target="tpu_custom_call" | custom-call | flops 201326592 | bytes 1572864 | tf_op jit(solution)/shard_map/forward2_early/pallas_call | solution.py:479
  49.3 1.4 %forward2_late.1 = bf16[8,128,128]{2,1,0:T(8,128)(2,1)S(1)} custom-call(s32[4,144]{1,0:T(4,128)S(1)} %copy-done.5, bf16[64,128,128]{2,1,0:T(8,128)(2,1)S(1)} %copy-done, bf16[4,128,128]{2,1,0:T(8,128)(2,1)S(1)} %collective-permute-done.4.mate_b, f32[8,128,128]{2,1,0:T(8,128)S(1)} %forward2_early.1.early), custom_call_target="tpu_custom_call" | custom-call | flops 67108864 | bytes 524288 | tf_op jit(solution)/shard_map/forward2_late/pallas_call | solution.py:488
  50.7 12.7 %all_to_all.22 = bf16[8,128,128]{2,1,0:T(8,128)(2,1)S(1)} all-to-all(bf16[8,128,128]{2,1,0:T(8,128)(2,1)S(1)} %forward2_late.1), channel_id=1, replica_groups=mesh['shot'=4,'band'=8] {'band'}, dimensions={0} | all-to-all | bytes 524288 | tf_op jit(solution)/shard_map/all_to_all | solution.py:378
  63.5 12.3 %all_to_all.23 = bf16[8,1,128,128]{3,2,1,0:T(8,128)(2,1)S(1)} all-to-all(bf16[8,1,128,128]{3,2,1,0:T(8,128)(2,1)S(1)} %get-tuple-element.31), channel_id=1, replica_groups=mesh['shot'=4,'band'=8] {'band'}, dimensions={0} | all-to-all | bytes 524288 | tf_op jit(solution)/shard_map/all_to_all | solution.py:378
  75.8 1.1 %adjoint2_give_a.1 = bf16[4,128,128]{2,1,0:T(8,128)(2,1)S(1)} custom-call(s32[4,288]{1,0:T(4,128)S(1)} %copy-done.4, bf16[64,128,128]{2,1,0:T(8,128)(2,1)S(1)} %copy-done, bf16[8,128,128]{2,1,0:T(8,128)(2,1)S(1)} %bitcast.14), custom_call_target="tpu_custom_call" | custom-call | flops 67108864 | bytes 524288 | tf_op jit(solution)/shard_map/adjoint2_give_a/pallas_call | solution.py:399
  77.0 1.9 %adjoint2_keep_a.1 = (f32[4,128,128]{2,1,0:T(8,128)S(1)}, bf16[4,128,128]{2,1,0:T(8,128)(2,1)S(1)}) custom-call(s32[4,288]{1,0:T(4,128)S(1)} %copy-done.4, bf16[64,128,128]{2,1,0:T(8,128)(2,1)S(1)} %copy-done, bf16[8,128,128]{2,1,0:T(8,128)(2,1)S(1)} %bitcast.15), custom_call_target="tpu_custom_call" | custom-call | flops 134217728 | bytes 1048576 | tf_op jit(solution)/shard_map/adjoint2_keep_a/pallas_call | solution.py:399
  78.9 0.3 collective-permute-start.8
  79.2 2.2 %collective-permute-start.7 = (bf16[4,128,128]{2,1,0:T(8,128)(2,1)S(1)}, bf16[4,128,128]{2,1,0:T(8,128)(2,1)S(1)}, u32[]{:S(2)}, u32[]{:S(2)}) collective-permute-start(bf16[4,128,128]{2,1,0:T(8,128)(2,1)S(1)} %adjoint2_pair_a.1.rest_0_), channel_id=1, source_target_pairs={{0,16},{8,24},{16,0},{24,8},{1,17},{9,25},{17,1},{25,9},{2,18},{10... | collective-permute-start | bytes 393224 | tf_op jit(solution)/shard_map/ppermute | solution.py:373
  81.5 1.4 %adjoint2_keep_b.1.keep_ref = f32[4,128,128]{2,1,0:T(8,128)S(1)} custom-call(s32[4,288]{1,0:T(4,128)S(1)} %copy-done.4, bf16[64,128,128]{2,1,0:T(8,128)(2,1)S(1)} %copy-done, bf16[8,128,128]{2,1,0:T(8,128)(2,1)S(1)} %bitcast.16), custom_call_target="tpu_custom_call" | custom-call | flops 67108864 | bytes 524288 | tf_op jit(solution)/shard_map/adjoint2_keep_b/pallas_call | solution.py:399
  83.0 2.7 %collective-permute-done.7.rest_1_ = bf16[4,128,128]{2,1,0:T(8,128)(2,1)S(1)} collective-permute-done((bf16[4,128,128]{2,1,0:T(8,128)(2,1)S(1)}, bf16[4,128,128]{2,1,0:T(8,128)(2,1)S(1)}, u32[]{:S(2)}, u32[]{:S(2)}) %collective-permute-start.7) | collective-permute-done | bytes 131104 | tf_op jit(solution)/shard_map/ppermute | solution.py:373
  85.6 0.1 total_a.1.own_a
  85.9 2.6 %collective-permute-done.9.rest_1_ = bf16[4,128,128]{2,1,0:T(8,128)(2,1)S(1)} collective-permute-done((bf16[4,128,128]{2,1,0:T(8,128)(2,1)S(1)}, bf16[4,128,128]{2,1,0:T(8,128)(2,1)S(1)}, u32[]{:S(2)}, u32[]{:S(2)}) %collective-permute-start.9) | collective-permute-done | bytes 131104 | tf_op jit(solution)/shard_map/ppermute | solution.py:373
  88.4 0.1 total_b.1.own_b
  88.7 0.7 turn.1
  89.4 0.9 %new_state_early.1 = (f32[16,128,128]{2,1,0:T(8,128)}, f32[4,128,128]{2,1,0:T(8,128)S(1)}) custom-call(s32[1]{0:T(128)} %bitcast.shot_ref, f32[16,128,128]{2,1,0:T(8,128)S(1)} %get-tuple-element.22.base, bf16[4,128,128]{2,1,0:T(8,128)(2,1)S(1)} %total_a.1.own_a, bf16[4,128,128]{2,1,0:T(8,128)(2,1)S(1)} %total_b.1.own_b, ...), custom_call_target="tpu_custom_call" | custom-call | bytes 3145728 | tf_op jit(solution)/shard_map/new_state_early/pallas_call | solution.py:521
  90.3 0.7 new_state_late.1
  (35 shorter events, 0.8 us)
Async XLA Ops:
  0.6 21.1 %copy-start.6 = (f32[1,128]{1,0:T(1,128)S(1)}, f32[1,128]{1,0:T(1,128)}, u32[]{:S(2)}) copy-start(f32[1,128]{1,0:T(1,128)} %obs_ref.3) | copy-start | bytes 1540
  0.6 21.1 %copy-start.7 = (f32[1,128]{1,0:T(1,128)S(1)}, f32[1,128]{1,0:T(1,128)}, u32[]{:S(2)}) copy-start(f32[1,128]{1,0:T(1,128)} %wt_ref.3) | copy-start | bytes 1540
  0.7 33.1 %copy-start = (bf16[64,128,128]{2,1,0:T(8,128)(2,1)S(1)}, bf16[64,128,128]{2,1,0:T(8,128)(2,1)}, u32[]{:S(2)}) copy-start(bf16[64,128,128]{2,1,0:T(8,128)(2,1)} %sens.15) | copy-start | bytes 6291460
  33.8 0.7 copy-start.3
  34.5 5.3 %copy-start.4 = (s32[4,288]{1,0:T(4,128)S(1)}, s32[4,288]{1,0:T(4,128)}, u32[]{:S(2)}) copy-start(s32[4,288]{1,0:T(4,128)} %get-tuple-element.20.plan) | copy-start | bytes 13828
  35.6 2.3 %collective-permute-start = (bf16[4,128,128]{2,1,0:T(8,128)(2,1)S(1)}, bf16[4,128,128]{2,1,0:T(8,128)(2,1)S(1)}, u32[]{:S(2)}, u32[]{:S(2)}) collective-permute-start(bf16[4,128,128]{2,1,0:T(8,128)(2,1)S(1)} %adjoint1_give_a.1), channel_id=1, source_target_pairs={{0,8},{8,0},{16,24},{24,16},{1,9},{9,1},{17,25},{25,17},{2,10},{10... | collective-permute-start | bytes 393224 | tf_op jit(solution)/shard_map/ppermute | solution.py:369
  37.6 3.8 %copy-start.1 = (f32[2048,128]{1,0:T(8,128)S(1)}, f32[2048,128]{1,0:T(8,128)}, u32[]{:S(2)}) copy-start(f32[2048,128]{1,0:T(8,128)} %param.10) | copy-start | bytes 3145732
  37.6 3.8 %copy-start.2 = (f32[2048,128]{1,0:T(8,128)S(1)}, f32[2048,128]{1,0:T(8,128)}, u32[]{:S(2)}) copy-start(f32[2048,128]{1,0:T(8,128)} %param.11) | copy-start | bytes 3145732
  37.6 3.6 %collective-permute-start.2 = (bf16[4,128,128]{2,1,0:T(8,128)(2,1)S(1)}, bf16[4,128,128]{2,1,0:T(8,128)(2,1)S(1)}, u32[]{:S(2)}, u32[]{:S(2)}) collective-permute-start(bf16[4,128,128]{2,1,0:T(8,128)(2,1)S(1)} %get-tuple-element.28), channel_id=1, source_target_pairs={{0,8},{8,0},{16,24},{24,16},{1,9},{9,1},{17,25},{25,17},{2,10},{10... | collective-permute-start | bytes 393224 | tf_op jit(solution)/shard_map/ppermute | solution.py:369
  38.0 5.9 %collective-permute-start.1 = (bf16[4,128,128]{2,1,0:T(8,128)(2,1)S(1)}, bf16[4,128,128]{2,1,0:T(8,128)(2,1)S(1)}, u32[]{:S(2)}, u32[]{:S(2)}) collective-permute-start(bf16[4,128,128]{2,1,0:T(8,128)(2,1)S(1)} %adjoint1_pair_a.1.rest_0_), channel_id=1, source_target_pairs={{0,16},{8,24},{16,0},{24,8},{1,17},{9,25},{17,1},{25,9},{2,18},{10... | collective-permute-start | bytes 393224 | tf_op jit(solution)/shard_map/ppermute | solution.py:373
  41.2 5.8 %copy-start.5 = (s32[4,144]{1,0:T(4,128)S(1)}, s32[4,144]{1,0:T(4,128)}, u32[]{:S(2)}) copy-start(s32[4,144]{1,0:T(4,128)} %get-tuple-element.26.plan) | copy-start | bytes 6916
  41.2 5.5 %collective-permute-start.3 = (bf16[4,128,128]{2,1,0:T(8,128)(2,1)S(1)}, bf16[4,128,128]{2,1,0:T(8,128)(2,1)S(1)}, u32[]{:S(2)}, u32[]{:S(2)}) collective-permute-start(bf16[4,128,128]{2,1,0:T(8,128)(2,1)S(1)} %adjoint1_pair_b.1.rest_0_), channel_id=1, source_target_pairs={{0,16},{8,24},{16,0},{24,8},{1,17},{9,25},{17,1},{25,9},{2,18},{10... | collective-permute-start | bytes 393224 | tf_op jit(solution)/shard_map/ppermute | solution.py:373
  44.1 2.9 %collective-permute-start.5 = (bf16[4,128,128]{2,1,0:T(8,128)(2,1)S(1)}, bf16[4,128,128]{2,1,0:T(8,128)(2,1)S(1)}, u32[]{:S(2)}, u32[]{:S(2)}) collective-permute-start(bf16[4,128,128]{2,1,0:T(8,128)(2,1)S(1)} %get-tuple-element.30.own_a), channel_id=1, source_target_pairs={{0,8},{8,0},{16,24},{24,16},{1,9},{9,1},{17,25},{25,17},{2,10},{10... | collective-permute-start | bytes 393224 | tf_op jit(solution)/shard_map/ppermute | solution.py:369
  46.9 2.4 %collective-permute-start.4 = (bf16[4,128,128]{2,1,0:T(8,128)(2,1)S(1)}, bf16[4,128,128]{2,1,0:T(8,128)(2,1)S(1)}, u32[]{:S(2)}, u32[]{:S(2)}) collective-permute-start(bf16[4,128,128]{2,1,0:T(8,128)(2,1)S(1)} %get-tuple-element.29.own_b), channel_id=1, source_target_pairs={{0,8},{8,0},{16,24},{24,16},{1,9},{9,1},{17,25},{25,17},{2,10},{10... | collective-permute-start | bytes 393224 | tf_op jit(solution)/shard_map/ppermute | solution.py:369
  76.9 2.3 %collective-permute-start.6 = (bf16[4,128,128]{2,1,0:T(8,128)(2,1)S(1)}, bf16[4,128,128]{2,1,0:T(8,128)(2,1)S(1)}, u32[]{:S(2)}, u32[]{:S(2)}) collective-permute-start(bf16[4,128,128]{2,1,0:T(8,128)(2,1)S(1)} %adjoint2_give_a.1), channel_id=1, source_target_pairs={{0,8},{8,0},{16,24},{24,16},{1,9},{9,1},{17,25},{25,17},{2,10},{10... | collective-permute-start | bytes 393224 | tf_op jit(solution)/shard_map/ppermute | solution.py:369
  78.9 4.0 %collective-permute-start.8 = (bf16[4,128,128]{2,1,0:T(8,128)(2,1)S(1)}, bf16[4,128,128]{2,1,0:T(8,128)(2,1)S(1)}, u32[]{:S(2)}, u32[]{:S(2)}) collective-permute-start(bf16[4,128,128]{2,1,0:T(8,128)(2,1)S(1)} %get-tuple-element.34), channel_id=1, source_target_pairs={{0,8},{8,0},{16,24},{24,16},{1,9},{9,1},{17,25},{25,17},{2,10},{10... | collective-permute-start | bytes 393224 | tf_op jit(solution)/shard_map/ppermute | solution.py:369
  79.2 6.4 %collective-permute-start.7 = (bf16[4,128,128]{2,1,0:T(8,128)(2,1)S(1)}, bf16[4,128,128]{2,1,0:T(8,128)(2,1)S(1)}, u32[]{:S(2)}, u32[]{:S(2)}) collective-permute-start(bf16[4,128,128]{2,1,0:T(8,128)(2,1)S(1)} %adjoint2_pair_a.1.rest_0_), channel_id=1, source_target_pairs={{0,16},{8,24},{16,0},{24,8},{1,17},{9,25},{17,1},{25,9},{2,18},{10... | collective-permute-start | bytes 393224 | tf_op jit(solution)/shard_map/ppermute | solution.py:373
  82.9 5.5 %collective-permute-start.9 = (bf16[4,128,128]{2,1,0:T(8,128)(2,1)S(1)}, bf16[4,128,128]{2,1,0:T(8,128)(2,1)S(1)}, u32[]{:S(2)}, u32[]{:S(2)}) collective-permute-start(bf16[4,128,128]{2,1,0:T(8,128)(2,1)S(1)} %adjoint2_pair_b.1.rest_0_), channel_id=1, source_target_pairs={{0,16},{8,24},{16,0},{24,8},{1,17},{9,25},{17,1},{25,9},{2,18},{10... | collective-permute-start | bytes 393224 | tf_op jit(solution)/shard_map/ppermute | solution.py:373
  85.8 3.6 %collective-permute-start.10 = (bf16[4,128,128]{2,1,0:T(8,128)(2,1)S(1)}, bf16[4,128,128]{2,1,0:T(8,128)(2,1)S(1)}, u32[]{:S(2)}, u32[]{:S(2)}) collective-permute-start(bf16[4,128,128]{2,1,0:T(8,128)(2,1)S(1)} %total_a.1.own_a), channel_id=1, source_target_pairs={{0,8},{8,0},{16,24},{24,16},{1,9},{9,1},{17,25},{25,17},{2,10},{10... | collective-permute-start | bytes 393224 | tf_op jit(solution)/shard_map/ppermute | solution.py:369
  88.6 1.8 %collective-permute-start.11 = (bf16[4,128,128]{2,1,0:T(8,128)(2,1)S(1)}, bf16[4,128,128]{2,1,0:T(8,128)(2,1)S(1)}, u32[]{:S(2)}, u32[]{:S(2)}) collective-permute-start(bf16[4,128,128]{2,1,0:T(8,128)(2,1)S(1)} %total_b.1.own_b), channel_id=1, source_target_pairs={{0,8},{8,0},{16,24},{24,16},{1,9},{9,1},{17,25},{25,17},{2,10},{10... | collective-permute-start | bytes 393224 | tf_op jit(solution)/shard_map/ppermute | solution.py:369

commit v3 on v2

--- a/solution.py
+++ b/solution.py
@@ -9,9 +9,9 @@
 
 CBLK = 128
 GROUP = 16
-PAIRS = 4
+PAIRS = 16
 CHUNKS = 4
-FIRST_VMEM = 57 << 20
+FIRST_VMEM = 55 << 20
 
 VMEM = pl.BlockSpec(memory_space=pltpu.VMEM)
 SMEM = pl.BlockSpec(memory_space=pltpu.SMEM)
@@ -21,7 +21,7 @@
 bf16, f32, i32 = jnp.bfloat16, jnp.float32, jnp.int32
 arr = jax.ShapeDtypeStruct
 
-BLOCK, OPERAND, TARGET, STEPS = range(4)
+BASE = 256
 
 
 def call(body, outs, scratch, in_specs, name, flops=0, bytes_accessed=0, vmem=32 << 20, **more):
@@ -86,37 +86,32 @@
         size = jnp.sum(jnp.where(mine, padded, 0.0), axis=1, keepdims=True)
         step = 2 * PAIRS
         vacant += jnp.where((at >= c * region) & (at < (c + 1) * region), float(empty[c]), 0.0)
-        steps += jnp.where(at == c, jnp.floor((size + (step - 1)) * (1.0 / step)), 0.0)
-    filled = placed(1.0)
-    plan_ref[BLOCK : BLOCK + 1, :] = placed(block).astype(i32)
-    plan_ref[OPERAND : OPERAND + 1, :] = (
-        placed(column(operand)) + (1.0 - filled) * vacant
-    ).astype(i32)
-    plan_ref[TARGET : TARGET + 1, :] = placed(column(target)).astype(i32)
-    plan_ref[STEPS : STEPS + 1, :] = steps.astype(i32)
-
-
-def paired_products(plan, c, region, product_of, acc_ref):
+        steps += jnp.where(at == classes * region + c, jnp.floor((size + (step - 1)) * (1.0 / step)), 0.0)
+    word = block + BASE * (column(operand) + BASE * column(target))
+    plan = placed(word) + (1.0 - placed(1.0)) * (BASE * vacant) + steps
+    plan_ref[...] = plan.astype(i32)
+
+
+def paired_products(plan, classes, c, region, product_of, acc_ref):
     def group(g, carry):
         first = c * region + g * (2 * PAIRS)
-        at = [first + 2 * j for j in range(PAIRS)]
-        prods = [
-            product_of(
-                plan[BLOCK, p], plan[BLOCK, p + 1], plan[OPERAND, p], plan[OPERAND, p + 1]
-            )
-            for p in at
-        ]
-        for p, prod in zip(at, prods):
-            acc_ref[plan[TARGET, p]] += prod
+        prods, targets = [], []
+        for j in range(PAIRS):
+            one, two = plan[0, first + 2 * j], plan[0, first + 2 * j + 1]
+            k1, k2 = one & (BASE - 1), two & (BASE - 1)
+            rest1, rest2 = one // BASE, two // BASE
+            prods.append(product_of(k1, k2, rest1 & (BASE - 1), rest2 & (BASE - 1)))
+            targets.append(rest1 // BASE)
+        for target, prod in zip(targets, prods):
+            acc_ref[target] += prod
         return carry
 
-    lax.fori_loop(0, plan[STEPS, c], group, 0)
+    lax.fori_loop(0, plan[0, classes * region + c], group, 0)
 
 
 def first_forward_kernel(
-    shot_ref,
-    bund_row,
-    cblk_row,
+    bund_row_hbm,
+    cblk_row_hbm,
     bund_hbm,
     cblk_hbm,
     sens_hbm,
@@ -132,6 +127,8 @@
     sens,
     state,
     prior,
+    bund_row,
+    cblk_row,
     sems,
 ):
     nblk = sens.shape[0]
@@ -143,6 +140,10 @@
         pltpu.make_async_copy(bund_hbm, bund, sems.at[0]),
         pltpu.make_async_copy(cblk_hbm, cblk, sems.at[1]),
     ]
+    rows = [
+        pltpu.make_async_copy(bund_row_hbm, bund_row, sems.at[6 + CHUNKS]),
+        pltpu.make_async_copy(cblk_row_hbm, cblk_row, sems.at[7 + CHUNKS]),
+    ]
     fields = []
     for h in range(2):
         part = pl.ds(h * half, half)
@@ -157,11 +158,13 @@
         part = pl.ds(c * step, step)
         return pltpu.make_async_copy(sens_hbm.at[part], sens.at[part], sems.at[6 + c])
 
-    for copy in small + fields[0] + fields[1] + [block_copy(c) for c in range(CHUNKS)]:
+    for copy in rows + small + fields[0] + fields[1] + [block_copy(c) for c in range(CHUNKS)]:
         copy.start()
     acc[...] = jnp.zeros_like(acc)
 
-    core = (shot_ref[0] % 2).astype(f32)
+    for copy in rows:
+        copy.wait()
+    core = (lax.axis_index("shot") % 2).astype(f32)
     bundle, cell = bund_row[...].astype(f32), cblk_row[...].astype(f32)
     upper = jnp.where(cell >= half, 1.0, 0.0)
     kept = jnp.where(upper == core, 1.0, 0.0)
@@ -222,10 +225,10 @@
     return product
 
 
-def early_forward_kernel(shot_ref, plan, sens, own_a, own_b, mate_a, acc, probe):
+def early_forward_kernel(plan, sens, own_a, own_b, mate_a, acc, probe):
     cells = probe.shape[0] - 1
     half, quarter = cells // 2, cells // 4
-    core = shot_ref[0] % 2
+    core = lax.axis_index("shot") % 2
     own, mate = core * half, (1 - core) * half
     probe[pl.ds(own, quarter)] = own_a[...]
     probe[pl.ds(own + quarter, quarter)] = own_b[...]
@@ -233,7 +236,7 @@
     probe[cells] = jnp.zeros_like(probe[cells])
     acc[...] = jnp.zeros_like(acc)
     region = region_of(sens.shape[0], acc.shape[0])
-    paired_products(plan, 0, region, forward_pair(sens, probe), acc)
+    paired_products(plan, 2, 0, region, forward_pair(sens, probe), acc)
 
 
 def late_forward_kernel(plan, sens, mate_b, early, out_ref, acc, probe):
@@ -242,7 +245,7 @@
     probe[quarter] = jnp.zeros_like(probe[quarter])
     acc[...] = early[...]
     region = region_of(sens.shape[0], acc.shape[0])
-    paired_products(plan, 1, region, forward_pair(sens, probe), acc)
+    paired_products(plan, 2, 1, region, forward_pair(sens, probe), acc)
     out_ref[...] = acc[...].astype(bf16)
 
 
@@ -262,7 +265,7 @@
 
     for c, out_ref in zip(classes, out_refs):
         acc[...] = jnp.zeros_like(acc)
-        paired_products(plan, c, region, product, acc)
+        paired_products(plan, 4, c, region, product, acc)
         out_ref[...] = acc[...].astype(out_ref.dtype)
 
 
@@ -288,9 +291,9 @@
         out_ref[i] = in_ref[i].T
 
 
-def prepare_kernel(shot_ref, state, prior, after_ref, field_a, field_b, base_ref):
+def prepare_kernel(state, prior, after_ref, field_a, field_b, base_ref):
     quarter = field_a.shape[0]
-    own = shot_ref[0] % 2 * (2 * quarter)
+    own = lax.axis_index("shot") % 2 * (2 * quarter)
     for at, field_ref in ((own, field_a), (own + quarter, field_b)):
         part = pl.ds(at, quarter)
         field_ref[...] = state[part] + prior[part]
@@ -310,24 +313,24 @@
     return total.T
 
 
-def probe_kernel(ny, shot_ref, field_ref, *rest):
+def probe_kernel(ny, field_ref, *rest):
     part_refs, (out_ref, grad_ref, order) = rest[:ny], rest[ny:]
     for i in range(out_ref.shape[0]):
-        grad = sum_over_y(shot_ref[0] // 2, part_refs, order, i)
+        grad = sum_over_y(lax.axis_index("shot") // 2, part_refs, order, i)
         grad_ref[i] = grad
         out_ref[i] = (field_ref[i] - 0.25 * grad).astype(bf16)
 
 
-def total_kernel(ny, shot_ref, grad_ref, *rest):
+def total_kernel(ny, grad_ref, after_ref, *rest):
     part_refs, (out_ref, order) = rest[:ny], rest[ny:]
     for i in range(out_ref.shape[0]):
-        grad2 = sum_over_y(shot_ref[0] // 2, part_refs, order, i)
+        grad2 = sum_over_y(lax.axis_index("shot") // 2, part_refs, order, i)
         out_ref[i] = (grad_ref[i] + grad2).astype(bf16)
 
 
-def early_update_kernel(shot_ref, base, own_a, own_b, mate_a, out_hbm, rest_ref, new, sems):
+def early_update_kernel(base, own_a, own_b, mate_a, out_hbm, rest_ref, new, sems):
     quarter = own_a.shape[0]
-    core = shot_ref[0] % 2
+    core = lax.axis_index("shot") % 2
     own, mate = core * (2 * quarter), (1 - core) * (2 * quarter)
     copies = []
     for n, (at, part_ref) in enumerate(((own, own_a), (own + quarter, own_b), (mate, mate_a))):
@@ -341,9 +344,9 @@
         copy.wait()
 
 
-def late_update_kernel(shot_ref, rest_ref, mate_b, so_far_hbm, out_hbm, new, sem):
+def late_update_kernel(rest_ref, mate_b, so_far_hbm, out_hbm, new, sem):
     quarter = mate_b.shape[0]
-    at = (1 - shot_ref[0] % 2) * (2 * quarter) + quarter
+    at = (1 - lax.axis_index("shot") % 2) * (2 * quarter) + quarter
     new[...] = rest_ref[...] - 0.125 * mate_b[...].astype(f32)
     copy = pltpu.make_async_copy(new, out_hbm.at[pl.ds(at, quarter)], sem)
     copy.start()
@@ -363,7 +366,6 @@
 
     state_b = state.reshape(cells, CBLK, samples)
     prior_b = prior.reshape(cells, CBLK, samples)
-    shot = lax.axis_index("shot").reshape(1)
 
     def other_core(array):
         return lax.ppermute(array, "shot", [(i, i ^ 1) for i in range(nshot)])
@@ -432,8 +434,8 @@
         first_forward_kernel,
         (
             part_out,
-            arr((4, 4 * region_of(nblk, quarter)), i32),
-            arr((4, 2 * region_of(nblk, bundles)), i32),
+            arr((1, 4 * region_of(nblk, quarter) + 4), i32),
+            arr((1, 2 * region_of(nblk, bundles) + 2), i32),
         ),
         [
             part_acc,
@@ -443,14 +445,16 @@
             pltpu.VMEM(sens.shape, bf16),
             pltpu.VMEM(state_b.shape, f32),
             pltpu.VMEM(state_b.shape, f32),
-            pltpu.SemaphoreType.DMA((6 + CHUNKS,)),
+            pltpu.VMEM((1, nblk), i32),
+            pltpu.VMEM((1, nblk), i32),
+            pltpu.SemaphoreType.DMA((8 + CHUNKS,)),
         ],
-        [SMEM, VMEM, VMEM] + [HBM] * 5,
+        [HBM] * 7,
         "forward1",
         flops,
         sens_bytes,
         vmem=FIRST_VMEM,
-    )(shot, bund.reshape(1, nblk), cblk.reshape(1, nblk), bund, cblk, sens, state_b, prior_b)
+    )(bund.reshape(1, nblk), cblk.reshape(1, nblk), bund, cblk, sens, state_b, prior_b)
     _, resid_all1 = residual(part1, "residual1", False)
     *sums1, after = adjoint(adjoint_plan, resid_all1, "adjoint1")
 
@@ -458,20 +462,20 @@
         prepare_kernel,
         (quarter_f32, quarter_f32, arr((cells, CBLK, samples), f32)),
         [],
-        [SMEM, VMEM, VMEM, ANY],
+        [VMEM, VMEM, ANY],
         "prepare",
         bytes_accessed=4 << 20,
-    )(shot, state_b, prior_b, after)
+    )(state_b, prior_b, after)
     own, grad1, mate = [], [], []
     for field, sums, part in zip(fields, sums1, "ab"):
         probe, grad = call(
             functools.partial(probe_kernel, ny),
             (quarter_bf16, quarter_f32),
             [order],
-            [SMEM] + [VMEM] * (1 + ny),
+            [VMEM] * (1 + ny),
             "probe2_" + part,
             bytes_accessed=1 << 19,
-        )(shot, field, *sums)
+        )(field, *sums)
         own.append(probe)
         grad1.append(grad)
         mate.append(other_core(probe))
@@ -480,11 +484,11 @@
         early_forward_kernel,
         part_f32,
         [pltpu.VMEM((cells + 1, CBLK, samples), bf16)],
-        [SMEM] * 2 + [VMEM] * 4,
+        [SMEM] + [VMEM] * 4,
         "forward2_early",
         flops * 3 // 4,
         sens_bytes * 3 // 4,
-    )(shot, forward_plan, sens, own[0], own[1], mate[0])
+    )(forward_plan, sens, own[0], own[1], mate[0])
     part2 = call(
         late_forward_kernel,
         part_out,
@@ -505,38 +509,39 @@
         "turn",
         bytes_accessed=1 << 20,
     )(resid2_t)
-    own, mate = [], []
+    own, mate, after = [], [], resid2
     for grad, sums, part in zip(grad1, sums2, "ab"):
         total = call(
             functools.partial(total_kernel, ny),
             quarter_bf16,
             [order],
-            [SMEM] + [VMEM] * (1 + ny),
+            [VMEM, ANY] + [VMEM] * ny,
             "total_" + part,
             bytes_accessed=1 << 19,
-        )(shot, grad, *sums)
+        )(grad, after, *sums)
         own.append(total)
+        after = grad
         mate.append(other_core(total))
     whole = arr((cells, CBLK, samples), f32)
     so_far, rest = call(
         early_update_kernel,
         (whole, quarter_f32),
         [pltpu.VMEM((3, quarter, CBLK, samples), f32), pltpu.SemaphoreType.DMA((3,))],
-        [SMEM] + [VMEM] * 4,
+        [VMEM] * 4,
         "new_state_early",
         bytes_accessed=3 << 20,
         out_specs=(HBM, VMEM),
-    )(shot, base, own[0], own[1], mate[0])
+    )(base, own[0], own[1], mate[0])
     new_state = call(
         late_update_kernel,
         whole,
         [pltpu.VMEM((quarter, CBLK, samples), f32), pltpu.SemaphoreType.DMA],
-        [SMEM, VMEM, VMEM, HBM],
+        [VMEM, VMEM, HBM],
         "new_state_late",
         bytes_accessed=1 << 20,
         out_specs=HBM,
-        input_output_aliases={3: 0},
-    )(shot, rest, mate[1], so_far)
+        input_output_aliases={2: 0},
+    )(rest, mate[1], so_far)
     return new_state.reshape(state.shape), resid2
 
 

time: 91.6 us -> 88.6 us (0.967)
  Pallas kernels: 20.7 us -> 18.1 us
  waiting for transfers between devices: 10.2 us -> 8.13 us
    ppermute x4, waiting for transfers between devices: 10.2 us -> 7.74 us  [other_chips(): lax.ppermute(array, 'shot', [(i, i ^ 2 * d) for i in range(nshot)])]
  transfers between devices with their start and end apart: 12 -> 12, of which waited for: 4 -> 5; matrix products, arithmetic and copies ran while one was open for 0% -> 0% of each run, Pallas kernels for 12% -> 11%
where the time goes in v3:
time: 88.6 us; the launch traced here: 88.2 us
  blocking collectives  53.6 us (60%)
  Pallas kernels  18.1 us (20%)
  waiting for transfers between devices  8.13 us (9%)
  starting transfers between devices  5.85 us (7%)
  local copies, waits for them, and re-layouts  1.56 us (2%)
  between operations  0.95 us (1%)
    all_to_all x4, blocking collectives, over_band(): lax.all_to_all(array, 'band', split_axis=0, concat_axis=0, tiled=True)  53.6 us
    pallas_call x6, Pallas kernels, kernel(): call(functools.partial(adjoint_kernel, classes), tuple((quarter_f32 if c...  7.88 us
    ppermute x4, waiting for transfers between devices, other_chips(): lax.ppermute(array, 'shot', [(i, i ^ 2 * d) for i in range(nshot)])  7.74 us
    ppermute x4, starting transfers between devices, other_chips(): lax.ppermute(array, 'shot', [(i, i ^ 2 * d) for i in range(nshot)])  4.31 us
    pallas_call x1, Pallas kernels, per_device(): call(first_forward_kernel, (part_out, arr((1, 4 * region_of(nblk, quarter...  4.04 us
  transfers between devices with their start and end apart: 12, of which 5 were waited for; matrix products, arithmetic and copies ran while one was open for 0% of the time, Pallas kernels for 11%

profile of v3, /device:TPU:0, one launch (start us, length us, event | category | flops | bytes accessed | tf_op | source)
XLA Modules:
  0.0 88.2 jit_solution(12563637800663295031)
XLA Ops:
  0.7 4.0 %forward1.1 = (bf16[8,128,128]{2,1,0:T(8,128)(2,1)}, s32[1,388]{1,0:T(1,128)}, s32[1,194]{1,0:T(1,128)}) custom-call(s32[1,64]{1,0:T(1,128)} %bitcast.22, s32[1,64]{1,0:T(1,128)} %bitcast.23, s32[64]{0:T(128)} %bund_hbm.1, s32[64]{0:T(128)} %cblk_hbm.1, bf16[64,128,128]{2,1,0:T(8,128)(2,1)} %sens.15, f32[16,128,128]{2,1,0:T(8,128)} %bitcast.9, ...), custom_call_target="tpu_custom_call" | custom-call | flops 268435456 | bytes 2097152 | tf_op jit(solution)/shard_map/forward1/pallas_call | solution.py:433
  4.7 16.2 %all_to_all.20 = bf16[8,128,128]{2,1,0:T(8,128)(2,1)S(1)} all-to-all(bf16[8,128,128]{2,1,0:T(8,128)(2,1)} %get-tuple-element.21), channel_id=1, replica_groups=mesh['shot'=4,'band'=8] {'band'}, dimensions={0} | all-to-all | bytes 524288 | tf_op jit(solution)/shard_map/all_to_all | solution.py:380
  21.0 12.0 %all_to_all.21 = bf16[8,1,128,128]{3,2,1,0:T(8,128)(2,1)S(1)} all-to-all(bf16[8,1,128,128]{3,2,1,0:T(8,128)(2,1)S(1)} %residual1.1), channel_id=1, replica_groups=mesh['shot'=4,'band'=8] {'band'}, dimensions={0} | all-to-all | bytes 524288 | tf_op jit(solution)/shard_map/all_to_all | solution.py:380
  33.0 0.7 copy-done.4
  33.7 1.1 %adjoint1_give_a.1 = bf16[4,128,128]{2,1,0:T(8,128)(2,1)S(1)} custom-call(s32[1,388]{1,0:T(1,128)S(1)} %copy-done.4, bf16[64,128,128]{2,1,0:T(8,128)(2,1)S(1)} %copy-done, bf16[8,128,128]{2,1,0:T(8,128)(2,1)S(1)} %bitcast.16), custom_call_target="tpu_custom_call" | custom-call | flops 67108864 | bytes 524288 | tf_op jit(solution)/shard_map/adjoint1_give_a/pallas_call | solution.py:401
  34.9 1.7 %adjoint1_keep_a.1 = (f32[4,128,128]{2,1,0:T(8,128)S(1)}, bf16[4,128,128]{2,1,0:T(8,128)(2,1)S(1)}) custom-call(s32[1,388]{1,0:T(1,128)S(1)} %copy-done.5, bf16[64,128,128]{2,1,0:T(8,128)(2,1)S(1)} %copy-done, bf16[8,128,128]{2,1,0:T(8,128)(2,1)S(1)} %bitcast.17), custom_call_target="tpu_custom_call" | custom-call | flops 134217728 | bytes 1048576 | tf_op jit(solution)/shard_map/adjoint1_keep_a/pallas_call | solution.py:401
  36.6 0.6 collective-permute-start.2
  37.2 1.6 %collective-permute-start.1 = (bf16[4,128,128]{2,1,0:T(8,128)(2,1)S(1)}, bf16[4,128,128]{2,1,0:T(8,128)(2,1)S(1)}, u32[]{:S(2)}, u32[]{:S(2)}) collective-permute-start(bf16[4,128,128]{2,1,0:T(8,128)(2,1)S(1)} %adjoint1_pair_a.1.rest_0_), channel_id=1, source_target_pairs={{0,16},{8,24},{16,0},{24,8},{1,17},{9,25},{17,1},{25,9},{2,18},{10... | collective-permute-start | bytes 393224 | tf_op jit(solution)/shard_map/ppermute | solution.py:375
  38.8 1.1 %adjoint1_keep_b.1.after_ref.keep_ref = f32[4,128,128]{2,1,0:T(8,128)S(1)} custom-call(s32[1,388]{1,0:T(1,128)S(1)} %copy-done.5, bf16[64,128,128]{2,1,0:T(8,128)(2,1)S(1)} %copy-done, bf16[8,128,128]{2,1,0:T(8,128)(2,1)S(1)} %bitcast.18), custom_call_target="tpu_custom_call" | custom-call | flops 67108864 | bytes 524288 | tf_op jit(solution)/shard_map/adjoint1_keep_b/pallas_call | solution.py:401
  40.0 0.6 collective-permute-start.3
  40.6 0.2 prepare.1
  40.7 2.2 %collective-permute-done.1.rest_1_ = bf16[4,128,128]{2,1,0:T(8,128)(2,1)S(1)} collective-permute-done((bf16[4,128,128]{2,1,0:T(8,128)(2,1)S(1)}, bf16[4,128,128]{2,1,0:T(8,128)(2,1)S(1)}, u32[]{:S(2)}, u32[]{:S(2)}) %collective-permute-start.1) | collective-permute-done | bytes 131104 | tf_op jit(solution)/shard_map/ppermute | solution.py:375
  43.0 0.1 probe2_a.1
  43.2 2.3 %collective-permute-done.3.rest_1_ = bf16[4,128,128]{2,1,0:T(8,128)(2,1)S(1)} collective-permute-done((bf16[4,128,128]{2,1,0:T(8,128)(2,1)S(1)}, bf16[4,128,128]{2,1,0:T(8,128)(2,1)S(1)}, u32[]{:S(2)}, u32[]{:S(2)}) %collective-permute-start.3) | collective-permute-done | bytes 131104 | tf_op jit(solution)/shard_map/ppermute | solution.py:375
  45.5 0.1 probe2_b.1
  45.8 1.6 %forward2_early.1.early = f32[8,128,128]{2,1,0:T(8,128)S(1)} custom-call(s32[1,194]{1,0:T(1,128)S(1)} %copy-done.6, bf16[64,128,128]{2,1,0:T(8,128)(2,1)S(1)} %copy-done, bf16[4,128,128]{2,1,0:T(8,128)(2,1)S(1)} %get-tuple-element.30.own_a, bf16[4,128,128]{2,1,0:T(8,128)(2,1)S(1)} %get-tuple-element.29.own_b, ...), custom_call_target="tpu_custom_call" | custom-call | flops 201326592 | bytes 1572864 | tf_op jit(solution)/shard_map/forward2_early/pallas_call | solution.py:483
  47.4 1.1 %forward2_late.1 = bf16[8,128,128]{2,1,0:T(8,128)(2,1)S(1)} custom-call(s32[1,194]{1,0:T(1,128)S(1)} %copy-done.6, bf16[64,128,128]{2,1,0:T(8,128)(2,1)S(1)} %copy-done, bf16[4,128,128]{2,1,0:T(8,128)(2,1)S(1)} %collective-permute-done.4.mate_b, f32[8,128,128]{2,1,0:T(8,128)S(1)} %forward2_early.1.early), custom_call_target="tpu_custom_call" | custom-call | flops 67108864 | bytes 524288 | tf_op jit(solution)/shard_map/forward2_late/pallas_call | solution.py:492
  48.5 12.9 %all_to_all.22 = bf16[8,128,128]{2,1,0:T(8,128)(2,1)S(1)} all-to-all(bf16[8,128,128]{2,1,0:T(8,128)(2,1)S(1)} %forward2_late.1), channel_id=1, replica_groups=mesh['shot'=4,'band'=8] {'band'}, dimensions={0} | all-to-all | bytes 524288 | tf_op jit(solution)/shard_map/all_to_all | solution.py:380
  61.6 12.5 %all_to_all.23 = bf16[8,1,128,128]{3,2,1,0:T(8,128)(2,1)S(1)} all-to-all(bf16[8,1,128,128]{3,2,1,0:T(8,128)(2,1)S(1)} %get-tuple-element.32), channel_id=1, replica_groups=mesh['shot'=4,'band'=8] {'band'}, dimensions={0} | all-to-all | bytes 524288 | tf_op jit(solution)/shard_map/all_to_all | solution.py:380
  74.1 1.1 %adjoint2_give_a.1 = bf16[4,128,128]{2,1,0:T(8,128)(2,1)S(1)} custom-call(s32[1,388]{1,0:T(1,128)S(1)} %copy-done.5, bf16[64,128,128]{2,1,0:T(8,128)(2,1)S(1)} %copy-done, bf16[8,128,128]{2,1,0:T(8,128)(2,1)S(1)} %bitcast.13), custom_call_target="tpu_custom_call" | custom-call | flops 67108864 | bytes 524288 | tf_op jit(solution)/shard_map/adjoint2_give_a/pallas_call | solution.py:401
  75.3 1.7 %adjoint2_keep_a.1 = (f32[4,128,128]{2,1,0:T(8,128)S(1)}, bf16[4,128,128]{2,1,0:T(8,128)(2,1)S(1)}) custom-call(s32[1,388]{1,0:T(1,128)S(1)} %copy-done.5, bf16[64,128,128]{2,1,0:T(8,128)(2,1)S(1)} %copy-done, bf16[8,128,128]{2,1,0:T(8,128)(2,1)S(1)} %bitcast.14), custom_call_target="tpu_custom_call" | custom-call | flops 134217728 | bytes 1048576 | tf_op jit(solution)/shard_map/adjoint2_keep_a/pallas_call | solution.py:401
  77.0 0.6 collective-permute-start.8
  77.6 1.6 %collective-permute-start.7 = (bf16[4,128,128]{2,1,0:T(8,128)(2,1)S(1)}, bf16[4,128,128]{2,1,0:T(8,128)(2,1)S(1)}, u32[]{:S(2)}, u32[]{:S(2)}) collective-permute-start(bf16[4,128,128]{2,1,0:T(8,128)(2,1)S(1)} %adjoint2_pair_a.1.rest_0_), channel_id=1, source_target_pairs={{0,16},{8,24},{16,0},{24,8},{1,17},{9,25},{17,1},{25,9},{2,18},{10... | collective-permute-start | bytes 393224 | tf_op jit(solution)/shard_map/ppermute | solution.py:375
  79.2 1.1 %adjoint2_keep_b.1.keep_ref = f32[4,128,128]{2,1,0:T(8,128)S(1)} custom-call(s32[1,388]{1,0:T(1,128)S(1)} %copy-done.5, bf16[64,128,128]{2,1,0:T(8,128)(2,1)S(1)} %copy-done, bf16[8,128,128]{2,1,0:T(8,128)(2,1)S(1)} %bitcast.15), custom_call_target="tpu_custom_call" | custom-call | flops 67108864 | bytes 524288 | tf_op jit(solution)/shard_map/adjoint2_keep_b/pallas_call | solution.py:401
  80.3 0.6 collective-permute-start.9
  80.9 0.7 turn.1.after_ref
  81.7 1.7 %collective-permute-done.7.rest_1_ = bf16[4,128,128]{2,1,0:T(8,128)(2,1)S(1)} collective-permute-done((bf16[4,128,128]{2,1,0:T(8,128)(2,1)S(1)}, bf16[4,128,128]{2,1,0:T(8,128)(2,1)S(1)}, u32[]{:S(2)}, u32[]{:S(2)}) %collective-permute-start.7) | collective-permute-done | bytes 131104 | tf_op jit(solution)/shard_map/ppermute | solution.py:375
  83.3 0.8 copy-done.3
  84.4 1.5 %collective-permute-done.9.rest_1_ = bf16[4,128,128]{2,1,0:T(8,128)(2,1)S(1)} collective-permute-done((bf16[4,128,128]{2,1,0:T(8,128)(2,1)S(1)}, bf16[4,128,128]{2,1,0:T(8,128)(2,1)S(1)}, u32[]{:S(2)}, u32[]{:S(2)}) %collective-permute-start.9) | collective-permute-done | bytes 131104 | tf_op jit(solution)/shard_map/ppermute | solution.py:375
  86.1 0.9 %new_state_early.1 = (f32[16,128,128]{2,1,0:T(8,128)}, f32[4,128,128]{2,1,0:T(8,128)S(1)}) custom-call(f32[16,128,128]{2,1,0:T(8,128)S(1)} %get-tuple-element.22.base, bf16[4,128,128]{2,1,0:T(8,128)(2,1)S(1)} %total_a.1.own_a, bf16[4,128,128]{2,1,0:T(8,128)(2,1)S(1)} %total_b.1.own_b, bf16[4,128,128]{2,1,0:T(8,128)(2,1)S(1)} %collective-permute-done.10.mate_a), custom_call_target="tpu_custom_call" | custom-call | bytes 3145728 | tf_op jit(solution)/shard_map/new_state_early/pallas_call | solution.py:526
  87.1 0.4 collective-permute-done.11.mate_b
  87.4 0.7 new_state_late.1
  (37 shorter events, 1.1 us)
Async XLA Ops:
  0.6 20.3 %copy-start.7 = (f32[1,128]{1,0:T(1,128)S(1)}, f32[1,128]{1,0:T(1,128)}, u32[]{:S(2)}) copy-start(f32[1,128]{1,0:T(1,128)} %obs_ref.3) | copy-start | bytes 1540
  0.6 20.3 %copy-start.8 = (f32[1,128]{1,0:T(1,128)S(1)}, f32[1,128]{1,0:T(1,128)}, u32[]{:S(2)}) copy-start(f32[1,128]{1,0:T(1,128)} %wt_ref.3) | copy-start | bytes 1540
  0.7 32.3 %copy-start = (bf16[64,128,128]{2,1,0:T(8,128)(2,1)S(1)}, bf16[64,128,128]{2,1,0:T(8,128)(2,1)}, u32[]{:S(2)}) copy-start(bf16[64,128,128]{2,1,0:T(8,128)(2,1)} %sens.15) | copy-start | bytes 6291460
  4.7 30.2 %copy-start.5 = (s32[1,388]{1,0:T(1,128)S(1)}, s32[1,388]{1,0:T(1,128)}, u32[]{:S(2)}) copy-start(s32[1,388]{1,0:T(1,128)} %get-tuple-element.20.plan) | copy-start | bytes 4660
  33.0 0.7 copy-start.4
  34.8 2.4 %collective-permute-start = (bf16[4,128,128]{2,1,0:T(8,128)(2,1)S(1)}, bf16[4,128,128]{2,1,0:T(8,128)(2,1)S(1)}, u32[]{:S(2)}, u32[]{:S(2)}) collective-permute-start(bf16[4,128,128]{2,1,0:T(8,128)(2,1)S(1)} %adjoint1_give_a.1), channel_id=1, source_target_pairs={{0,8},{8,0},{16,24},{24,16},{1,9},{9,1},{17,25},{25,17},{2,10},{10... | collective-permute-start | bytes 393224 | tf_op jit(solution)/shard_map/ppermute | solution.py:371
  36.6 4.0 %copy-start.1 = (f32[2048,128]{1,0:T(8,128)S(1)}, f32[2048,128]{1,0:T(8,128)}, u32[]{:S(2)}) copy-start(f32[2048,128]{1,0:T(8,128)} %param.10) | copy-start | bytes 3145732
  36.6 4.0 %copy-start.2 = (f32[2048,128]{1,0:T(8,128)S(1)}, f32[2048,128]{1,0:T(8,128)}, u32[]{:S(2)}) copy-start(f32[2048,128]{1,0:T(8,128)} %param.11) | copy-start | bytes 3145732
  36.6 3.3 %collective-permute-start.2 = (bf16[4,128,128]{2,1,0:T(8,128)(2,1)S(1)}, bf16[4,128,128]{2,1,0:T(8,128)(2,1)S(1)}, u32[]{:S(2)}, u32[]{:S(2)}) collective-permute-start(bf16[4,128,128]{2,1,0:T(8,128)(2,1)S(1)} %get-tuple-element.28), channel_id=1, source_target_pairs={{0,8},{8,0},{16,24},{24,16},{1,9},{9,1},{17,25},{25,17},{2,10},{10... | collective-permute-start | bytes 393224 | tf_op jit(solution)/shard_map/ppermute | solution.py:371
  37.2 5.8 %collective-permute-start.1 = (bf16[4,128,128]{2,1,0:T(8,128)(2,1)S(1)}, bf16[4,128,128]{2,1,0:T(8,128)(2,1)S(1)}, u32[]{:S(2)}, u32[]{:S(2)}) collective-permute-start(bf16[4,128,128]{2,1,0:T(8,128)(2,1)S(1)} %adjoint1_pair_a.1.rest_0_), channel_id=1, source_target_pairs={{0,16},{8,24},{16,0},{24,8},{1,17},{9,25},{17,1},{25,9},{2,18},{10... | collective-permute-start | bytes 393224 | tf_op jit(solution)/shard_map/ppermute | solution.py:375
  39.9 5.8 %copy-start.6 = (s32[1,194]{1,0:T(1,128)S(1)}, s32[1,194]{1,0:T(1,128)}, u32[]{:S(2)}) copy-start(s32[1,194]{1,0:T(1,128)} %get-tuple-element.26.plan) | copy-start | bytes 2332
  40.0 5.5 %collective-permute-start.3 = (bf16[4,128,128]{2,1,0:T(8,128)(2,1)S(1)}, bf16[4,128,128]{2,1,0:T(8,128)(2,1)S(1)}, u32[]{:S(2)}, u32[]{:S(2)}) collective-permute-start(bf16[4,128,128]{2,1,0:T(8,128)(2,1)S(1)} %adjoint1_pair_b.1.rest_0_), channel_id=1, source_target_pairs={{0,16},{8,24},{16,0},{24,8},{1,17},{9,25},{17,1},{25,9},{2,18},{10... | collective-permute-start | bytes 393224 | tf_op jit(solution)/shard_map/ppermute | solution.py:375
  43.1 2.6 %collective-permute-start.5 = (bf16[4,128,128]{2,1,0:T(8,128)(2,1)S(1)}, bf16[4,128,128]{2,1,0:T(8,128)(2,1)S(1)}, u32[]{:S(2)}, u32[]{:S(2)}) collective-permute-start(bf16[4,128,128]{2,1,0:T(8,128)(2,1)S(1)} %get-tuple-element.30.own_a), channel_id=1, source_target_pairs={{0,8},{8,0},{16,24},{24,16},{1,9},{9,1},{17,25},{25,17},{2,10},{10... | collective-permute-start | bytes 393224 | tf_op jit(solution)/shard_map/ppermute | solution.py:371
  45.7 1.7 %collective-permute-start.4 = (bf16[4,128,128]{2,1,0:T(8,128)(2,1)S(1)}, bf16[4,128,128]{2,1,0:T(8,128)(2,1)S(1)}, u32[]{:S(2)}, u32[]{:S(2)}) collective-permute-start(bf16[4,128,128]{2,1,0:T(8,128)(2,1)S(1)} %get-tuple-element.29.own_b), channel_id=1, source_target_pairs={{0,8},{8,0},{16,24},{24,16},{1,9},{9,1},{17,25},{25,17},{2,10},{10... | collective-permute-start | bytes 393224 | tf_op jit(solution)/shard_map/ppermute | solution.py:371
  75.2 2.3 %collective-permute-start.6 = (bf16[4,128,128]{2,1,0:T(8,128)(2,1)S(1)}, bf16[4,128,128]{2,1,0:T(8,128)(2,1)S(1)}, u32[]{:S(2)}, u32[]{:S(2)}) collective-permute-start(bf16[4,128,128]{2,1,0:T(8,128)(2,1)S(1)} %adjoint2_give_a.1), channel_id=1, source_target_pairs={{0,8},{8,0},{16,24},{24,16},{1,9},{9,1},{17,25},{25,17},{2,10},{10... | collective-permute-start | bytes 393224 | tf_op jit(solution)/shard_map/ppermute | solution.py:371
  77.0 3.3 %collective-permute-start.8 = (bf16[4,128,128]{2,1,0:T(8,128)(2,1)S(1)}, bf16[4,128,128]{2,1,0:T(8,128)(2,1)S(1)}, u32[]{:S(2)}, u32[]{:S(2)}) collective-permute-start(bf16[4,128,128]{2,1,0:T(8,128)(2,1)S(1)} %get-tuple-element.35), channel_id=1, source_target_pairs={{0,8},{8,0},{16,24},{24,16},{1,9},{9,1},{17,25},{25,17},{2,10},{10... | collective-permute-start | bytes 393224 | tf_op jit(solution)/shard_map/ppermute | solution.py:371
  77.6 5.8 %collective-permute-start.7 = (bf16[4,128,128]{2,1,0:T(8,128)(2,1)S(1)}, bf16[4,128,128]{2,1,0:T(8,128)(2,1)S(1)}, u32[]{:S(2)}, u32[]{:S(2)}) collective-permute-start(bf16[4,128,128]{2,1,0:T(8,128)(2,1)S(1)} %adjoint2_pair_a.1.rest_0_), channel_id=1, source_target_pairs={{0,16},{8,24},{16,0},{24,8},{1,17},{9,25},{17,1},{25,9},{2,18},{10... | collective-permute-start | bytes 393224 | tf_op jit(solution)/shard_map/ppermute | solution.py:375
  80.3 5.5 %collective-permute-start.9 = (bf16[4,128,128]{2,1,0:T(8,128)(2,1)S(1)}, bf16[4,128,128]{2,1,0:T(8,128)(2,1)S(1)}, u32[]{:S(2)}, u32[]{:S(2)}) collective-permute-start(bf16[4,128,128]{2,1,0:T(8,128)(2,1)S(1)} %adjoint2_pair_b.1.rest_0_), channel_id=1, source_target_pairs={{0,16},{8,24},{16,0},{24,8},{1,17},{9,25},{17,1},{25,9},{2,18},{10... | collective-permute-start | bytes 393224 | tf_op jit(solution)/shard_map/ppermute | solution.py:375
  83.3 0.8 copy-start.3
  84.3 1.8 %collective-permute-start.10 = (bf16[4,128,128]{2,1,0:T(8,128)(2,1)S(1)}, bf16[4,128,128]{2,1,0:T(8,128)(2,1)S(1)}, u32[]{:S(2)}, u32[]{:S(2)}) collective-permute-start(bf16[4,128,128]{2,1,0:T(8,128)(2,1)S(1)} %total_a.1.own_a), channel_id=1, source_target_pairs={{0,8},{8,0},{16,24},{24,16},{1,9},{9,1},{17,25},{25,17},{2,10},{10... | collective-permute-start | bytes 393224 | tf_op jit(solution)/shard_map/ppermute | solution.py:371
  86.0 1.4 %collective-permute-start.11 = (bf16[4,128,128]{2,1,0:T(8,128)(2,1)S(1)}, bf16[4,128,128]{2,1,0:T(8,128)(2,1)S(1)}, u32[]{:S(2)}, u32[]{:S(2)}) collective-permute-start(bf16[4,128,128]{2,1,0:T(8,128)(2,1)S(1)} %total_b.1.own_b), channel_id=1, source_target_pairs={{0,8},{8,0},{16,24},{24,16},{1,9},{9,1},{17,25},{25,17},{2,10},{10... | collective-permute-start | bytes 393224 | tf_op jit(solution)/shard_map/ppermute | solution.py:371

commit v4 on v3

v4 whole, which is shorter than its diff:
```python
import functools

import jax
import jax.numpy as jnp
from jax import lax
from jax.experimental import pallas as pl
from jax.experimental.pallas import tpu as pltpu
from jax.sharding import PartitionSpec as P

CBLK = 128
GROUP = 16
CHUNKS = 4
FIRST_VMEM = 55 << 20

VMEM = pl.BlockSpec(memory_space=pltpu.VMEM)
SMEM = pl.BlockSpec(memory_space=pltpu.SMEM)
HBM = pl.BlockSpec(memory_space=pltpu.HBM)
ANY = pl.BlockSpec(memory_space=pl.ANY)

bf16, f32, i32 = jnp.bfloat16, jnp.float32, jnp.int32
arr = jax.ShapeDtypeStruct

def call(body, outs, scratch, in_specs, name, flops=0, bytes_accessed=0, vmem=32 << 20, **more):
    if "out_specs" not in more:
        more["out_specs"] = jax.tree.map(lambda _: VMEM, outs)
    return pl.pallas_call(
        body,
        out_shape=outs,
        in_specs=in_specs,
        scratch_shapes=scratch,
        compiler_params=pltpu.CompilerParams(vmem_limit_bytes=vmem),
        cost_estimate=pl.CostEstimate(
            flops=flops, bytes_accessed=bytes_accessed, transcendentals=0
        ),
        name=name,
        **more,
    )


def first_forward_kernel(
    bund_hbm,
    cblk_hbm,
    sens_hbm,
    state_hbm,
    prior_hbm,
    out_ref,
    acc,
    probe,
    bund,
    cblk,
    sens,
    state,
    prior,
    sems,
):
    nblk = sens.shape[0]
    step = nblk // CHUNKS
    cells = state.shape[0]
    half = cells // 2
    small = [
        pltpu.make_async_copy(bund_hbm, bund, sems.at[0]),
        pltpu.make_async_copy(cblk_hbm, cblk, sems.at[1]),
    ]
    fields = []
    for h in range(2):
        part = pl.ds(h * half, half)
        fields.append(
            [
                pltpu.make_async_copy(state_hbm.at[part], state.at[part], sems.at[2 + 2 * h]),
                pltpu.make_async_copy(prior_hbm.at[part], prior.at[part], sems.at[3 + 2 * h]),
            ]
        )

    def block_copy(c):
        part = pl.ds(c * step, step)
        return pltpu.make_async_copy(sens_hbm.at[part], sens.at[part], sems.at[6 + c])

    for copy in small + fields[0] + fields[1] + [block_copy(c) for c in range(CHUNKS)]:
        copy.start()
    acc[...] = jnp.zeros_like(acc)

    for h in range(2):
        part = pl.ds(h * half, half)
        for copy in fields[h]:
            copy.wait()
        probe[part] = (state[part] + 0.5 * prior[part]).astype(bf16)
    for copy in small:
        copy.wait()

    def chunk(c, carry):
        block_copy(c).wait()
        for g in range(step // GROUP):
            ks = [c * step + g * GROUP + j for j in range(GROUP)]
            prods = [
                jnp.dot(sens[k], probe[cblk[k]], preferred_element_type=f32) for k in ks
            ]
            for k, prod in zip(ks, prods):
                acc[bund[k]] += prod
        return carry

    lax.fori_loop(0, CHUNKS, chunk, 0)
    out_ref[...] = acc[...].astype(bf16)


def dense_kernel(bund, cblk, sens, after_ref, out_ref, token_ref, total):
    rays = sens.shape[1]
    total[...] = jnp.zeros_like(total)

    def place(k, carry):
        rows = pl.ds(pl.multiple_of(bund[k] * rays, rays), rays)
        lanes = pl.ds(pl.multiple_of(cblk[k] % 2 * CBLK, CBLK), CBLK)
        total[cblk[k] // 2, rows, lanes] += sens[k].astype(f32)
        return carry

    lax.fori_loop(0, sens.shape[0], place, 0)
    for i in range(total.shape[0]):
        out_ref[i] = total[i].astype(bf16)
    token_ref[...] = jnp.zeros_like(token_ref)


def dense_forward(dense, columns, start_of, store):
    step = 2 * CBLK
    probe = jnp.concatenate([part for _, part in columns], axis=0)
    for m in range(dense.shape[1] // step):
        rows = pl.ds(m * step, step)
        lhs = jnp.concatenate([dense[pair, rows, :] for pair, _ in columns], axis=1)
        total = jnp.dot(lhs, probe, preferred_element_type=f32)
        store(m, start_of(m, total.reshape(2, CBLK, -1)))


def columns_of(first, part_ref):
    return [
        (first + j, part_ref[pl.ds(2 * j, 2)].reshape(2 * CBLK, -1))
        for j in range(part_ref.shape[0] // 2)
    ]


def early_forward_kernel(dense, own_a, own_b, mate_a, acc):
    half, quarter = dense.shape[0] // 2, dense.shape[0] // 4
    core = lax.axis_index("shot") % 2
    own, mate = core * half, (1 - core) * half
    columns = columns_of(own, own_a) + columns_of(own + quarter, own_b) + columns_of(mate, mate_a)

    def store(m, value):
        acc[pl.ds(2 * m, 2)] = value

    dense_forward(dense, columns, lambda m, value: value, store)


def late_forward_kernel(dense, mate_b, early, out_ref):
    half, quarter = dense.shape[0] // 2, dense.shape[0] // 4
    core = lax.axis_index("shot") % 2

    def store(m, value):
        out_ref[pl.ds(2 * m, 2)] = value.astype(bf16)

    dense_forward(
        dense,
        columns_of((1 - core) * half + quarter, mate_b),
        lambda m, value: early[pl.ds(2 * m, 2)] + value,
        store,
    )


def adjoint_kernel(parts, dense, resid, *out_refs):
    half, quarter = dense.shape[0] // 2, dense.shape[0] // 4
    core = lax.axis_index("shot") % 2
    lhs = jnp.concatenate([resid[m] for m in range(resid.shape[0])], axis=1)
    for (keep, second), out_ref in zip(parts, out_refs):
        first = (core if keep else 1 - core) * half + second * quarter
        for j in range(quarter):
            both = jnp.dot(lhs, dense[first + j], preferred_element_type=f32)
            both = both.astype(out_ref.dtype)
            out_ref[2 * j] = both[:, :CBLK]
            out_ref[2 * j + 1] = both[:, CBLK:]


def pair_kernel(keep_ref, got_ref, out_ref):
    out_ref[...] = (keep_ref[...] + got_ref[...].astype(f32)).astype(bf16)


def residual_kernel(parts_ref, obs_ref, wt_ref, after_ref, out_ref, *resid_ref):
    for i in range(parts_ref.shape[1]):
        total = parts_ref[0, i].astype(f32)
        for d in range(1, parts_ref.shape[0]):
            total += parts_ref[d, i].astype(f32)
        resid = wt_ref[pl.ds(i, 1), :] * (total.T - obs_ref[pl.ds(i, 1), :])
        if resid_ref:
            resid_ref[0][i] = resid
        rounded = resid.astype(bf16)
        for d in range(parts_ref.shape[0]):
            out_ref[d, i] = rounded


def turn_kernel(in_ref, out_ref):
    for i in range(in_ref.shape[0]):
        out_ref[i] = in_ref[i].T


def prepare_kernel(state, prior, after_ref, field_a, field_b, base_ref):
    quarter = field_a.shape[0]
    own = lax.axis_index("shot") % 2 * (2 * quarter)
    for at, field_ref in ((own, field_a), (own + quarter, field_b)):
        part = pl.ds(at, quarter)
        field_ref[...] = state[part] + prior[part]
    base_ref[...] = state[...] + 0.5 * prior[...]


def sum_over_y(chip_y, part_refs, order, i):
    if len(part_refs) > 2:
        for d, part_ref in enumerate(part_refs):
            order[chip_y ^ d] = part_ref[i]
        parts = [order[y] for y in range(len(part_refs))]
    else:
        parts = [part_ref[i] for part_ref in part_refs]
    total = parts[0].astype(f32)
    for part in parts[1:]:
        total += part.astype(f32)
    return total.T


def probe_kernel(ny, field_ref, *rest):
    part_refs, (out_ref, grad_ref, order) = rest[:ny], rest[ny:]
    for i in range(out_ref.shape[0]):
        grad = sum_over_y(lax.axis_index("shot") // 2, part_refs, order, i)
        grad_ref[i] = grad
        out_ref[i] = (field_ref[i] - 0.25 * grad).astype(bf16)


def total_kernel(ny, grad_ref, after_ref, *rest):
    part_refs, (out_ref, order) = rest[:ny], rest[ny:]
    for i in range(out_ref.shape[0]):
        grad2 = sum_over_y(lax.axis_index("shot") // 2, part_refs, order, i)
        out_ref[i] = (grad_ref[i] + grad2).astype(bf16)


def early_update_kernel(base, own_a, own_b, mate_a, out_hbm, rest_ref, new, sems):
    quarter = own_a.shape[0]
    core = lax.axis_index("shot") % 2
    own, mate = core * (2 * quarter), (1 - core) * (2 * quarter)
    copies = []
    for n, (at, part_ref) in enumerate(((own, own_a), (own + quarter, own_b), (mate, mate_a))):
        new[n] = base[pl.ds(at, quarter)] - 0.125 * part_ref[...].astype(f32)
        copies.append(
            pltpu.make_async_copy(new.at[n], out_hbm.at[pl.ds(at, quarter)], sems.at[n])
        )
        copies[-1].start()
    rest_ref[...] = base[pl.ds(mate + quarter, quarter)]
    for copy in copies:
        copy.wait()


def late_update_kernel(rest_ref, mate_b, so_far_hbm, out_hbm, new, sem):
    quarter = mate_b.shape[0]
    at = (1 - lax.axis_index("shot") % 2) * (2 * quarter) + quarter
    new[...] = rest_ref[...] - 0.125 * mate_b[...].astype(f32)
    copy = pltpu.make_async_copy(new, out_hbm.at[pl.ds(at, quarter)], sem)
    copy.start()
    copy.wait()


def per_device(nshot, nband, sens, bund, cblk, state, prior, observed, pick_weight):
    nblk = sens.shape[0]
    samples = state.shape[1]
    owned, rays = observed.shape
    bundles = owned * nband
    cells = state.shape[0] // CBLK
    quarter = cells // 4
    ny = nshot // 2
    flops = 2 * nblk * rays * CBLK * samples
    sens_bytes = nblk * rays * CBLK * 2

    state_b = state.reshape(cells, CBLK, samples)
    prior_b = prior.reshape(cells, CBLK, samples)

    def other_core(array):
        return lax.ppermute(array, "shot", [(i, i ^ 1) for i in range(nshot)])

    def other_chips(array):
        return [array] + [
            lax.ppermute(array, "shot", [(i, i ^ (2 * d)) for i in range(nshot)])
            for d in range(1, ny)
        ]

    def over_band(array):
        return lax.all_to_all(array, "band", split_axis=0, concat_axis=0, tiled=True)

    part_out = arr((bundles, rays, samples), bf16)
    dense_shape = (cells // 2, bundles * rays, 2 * CBLK)
    dense_flops = 2 * bundles * rays * cells * CBLK * samples
    dense_bytes = 2 * bundles * rays * cells * CBLK
    quarter_bf16 = arr((quarter, CBLK, samples), bf16)
    quarter_f32 = arr((quarter, CBLK, samples), f32)
    order = pltpu.VMEM((ny, samples, CBLK), bf16)

    def residual(part, after, name, keep):
        parts = over_band(part).reshape(nband, owned, rays, samples)
        outs = (arr((nband, owned, samples, rays), bf16),)
        if keep:
            outs += (arr((owned, samples, rays), f32),)
        copies, *resid = call(
            residual_kernel, outs, [], [VMEM] * 3 + [ANY], name, bytes_accessed=1 << 20
        )(parts, observed, pick_weight, after)
        return resid, over_band(copies).reshape(bundles, samples, rays)

    def adjoint(dense, resid_all, name):
        def kernel(parts, part):
            return call(
                functools.partial(adjoint_kernel, parts),
                tuple(quarter_f32 if keep else quarter_bf16 for keep, _ in parts),
                [],
                [VMEM] * 2,
                name + part,
                dense_flops * len(parts) // 4,
                dense_bytes * len(parts) // 4,
            )(dense, resid_all)

        def pair(keep, got, part):
            return call(
                pair_kernel,
                quarter_bf16,
                [],
                [VMEM] * 2,
                name + "_pair" + part,
                bytes_accessed=1 << 19,
            )(keep, got)

        (give_a,) = kernel(((False, 0),), "_give_a")
        got_a = other_core(give_a)
        keep_a, give_b = kernel(((True, 0), (False, 1)), "_keep_a")
        got_b = other_core(give_b)
        sums_a = other_chips(pair(keep_a, got_a, "_a"))
        (keep_b,) = kernel(((True, 1),), "_keep_b")
        sums_b = other_chips(pair(keep_b, got_b, "_b"))
        return sums_a, sums_b, keep_b

    part1 = call(
        first_forward_kernel,
        part_out,
        [
            pltpu.VMEM((bundles, rays, samples), f32),
            pltpu.VMEM((cells, CBLK, samples), bf16),
            pltpu.SMEM((nblk,), i32),
            pltpu.SMEM((nblk,), i32),
            pltpu.VMEM(sens.shape, bf16),
            pltpu.VMEM(state_b.shape, f32),
            pltpu.VMEM(state_b.shape, f32),
            pltpu.SemaphoreType.DMA((6 + CHUNKS,)),
        ],
        [HBM] * 5,
        "forward1",
        flops,
        sens_bytes,
        vmem=FIRST_VMEM,
    )(bund, cblk, sens, state_b, prior_b)
    dense, token = call(
        dense_kernel,
        (arr(dense_shape, bf16), arr((8, CBLK), f32)),
        [pltpu.VMEM(dense_shape, f32)],
        [SMEM, SMEM, VMEM, ANY],
        "dense",
        0,
        16 << 20,
        vmem=3 * dense_bytes + 2 * sens_bytes + (2 << 20),
    )(bund, cblk, sens, part1)
    _, resid_all1 = residual(part1, token, "residual1", False)
    *sums1, after = adjoint(dense, resid_all1, "adjoint1")

    *fields, base = call(
        prepare_kernel,
        (quarter_f32, quarter_f32, arr((cells, CBLK, samples), f32)),
        [],
        [VMEM, VMEM, ANY],
        "prepare",
        bytes_accessed=4 << 20,
    )(state_b, prior_b, after)
    own, grad1, mate = [], [], []
    for field, sums, part in zip(fields, sums1, "ab"):
        probe, grad = call(
            functools.partial(probe_kernel, ny),
            (quarter_bf16, quarter_f32),
            [order],
            [VMEM] * (1 + ny),
            "probe2_" + part,
            bytes_accessed=1 << 19,
        )(field, *sums)
        own.append(probe)
        grad1.append(grad)
        mate.append(other_core(probe))

    early = call(
        early_forward_kernel,
        arr((bundles, rays, samples), f32),
        [],
        [VMEM] * 4,
        "forward2_early",
        dense_flops * 3 // 4,
        dense_bytes * 3 // 4,
    )(dense, own[0], own[1], mate[0])
    part2 = call(
        late_forward_kernel,
        part_out,
        [],
        [VMEM] * 3,
        "forward2_late",
        dense_flops // 4,
        dense_bytes // 4,
    )(dense, mate[1], early)

    (resid2_t,), resid_all2 = residual(part2, token, "residual2", True)
    *sums2, _ = adjoint(dense, resid_all2, "adjoint2")
    resid2 = call(
        turn_kernel,
        arr((owned, rays, samples), f32),
        [],
        [VMEM],
        "turn",
        bytes_accessed=1 << 20,
    )(resid2_t)
    own, mate, after = [], [], resid2
    for grad, sums, part in zip(grad1, sums2, "ab"):
        total = call(
            functools.partial(total_kernel, ny),
            quarter_bf16,
            [order],
            [VMEM, ANY] + [VMEM] * ny,
            "total_" + part,
            bytes_accessed=1 << 19,
        )(grad, after, *sums)
        own.append(total)
        after = grad
        mate.append(other_core(total))
    whole = arr((cells, CBLK, samples), f32)
    so_far, rest = call(
        early_update_kernel,
        (whole, quarter_f32),
        [pltpu.VMEM((3, quarter, CBLK, samples), f32), pltpu.SemaphoreType.DMA((3,))],
        [VMEM] * 4,
        "new_state_early",
        bytes_accessed=3 << 20,
        out_specs=(HBM, VMEM),
    )(base, own[0], own[1], mate[0])
    new_state = call(
        late_update_kernel,
        whole,
        [pltpu.VMEM((quarter, CBLK, samples), f32), pltpu.SemaphoreType.DMA],
        [VMEM, VMEM, HBM],
        "new_state_late",
        bytes_accessed=1 << 20,
        out_specs=HBM,
        input_output_aliases={2: 0},
    )(rest, mate[1], so_far)
    return new_state.reshape(state.shape), resid2


def solution(mesh):
    in_specs = (
        P(("shot", "band"), None, None),
        P(("shot", "band")),
        P(("shot", "band")),
        P("band", None),
        P("band", None),
        P(("shot", "band"), None),
        P(("shot", "band"), None),
    )
    out_specs = (P("band", None), P(("shot", "band"), None, None))
    return jax.shard_map(
        functools.partial(per_device, mesh.shape["shot"], mesh.shape["band"]),
        mesh=mesh,
        in_specs=in_specs,
        out_specs=out_specs,
        check_vma=False,
    )
```

time: 88.6 us -> 85 us (0.959)
  blocking collectives: 53.6 us -> 36.5 us
  starting transfers between devices: 5.85 us -> 13.1 us
  waiting for transfers between devices: 8.13 us -> 14.4 us
  Pallas kernels: 18.1 us -> 13.6 us
  local copies, waits for them, and re-layouts: 1.56 us -> 5.97 us
    all_to_all x4 -> x3, blocking collectives: 53.6 us -> 36.5 us  [over_band(): lax.all_to_all(array, 'band', split_axis=0, concat_axis=0, tiled=True)]
    all_to_all x0 -> x1, starting transfers between devices: none -> 7.28 us  [over_band(): lax.all_to_all(array, 'band', split_axis=0, concat_axis=0, tiled=True)]
    pallas_call x11 -> x12, Pallas kernels: 14.9 us -> 10.4 us  [the longest x1 4.01 us: per_device(): call(first_forward_kernel, part_out, [pltpu.VMEM((bundles, rays, samples)...]
    unnamed x18 -> x24, local copies, waits for them, and re-layouts: 1.56 us -> 5.97 us
    all_to_all x0 -> x1, waiting for transfers between devices: none -> 3.35 us  [over_band(): lax.all_to_all(array, 'band', split_axis=0, concat_axis=0, tiled=True)]
    ppermute x4, waiting for transfers between devices: 7.74 us -> 9.63 us  [other_chips(): lax.ppermute(array, 'shot', [(i, i ^ 2 * d) for i in range(nshot)])]
    ppermute x8, waiting for transfers between devices: 0.4 us -> 1.39 us  [other_core(): return lax.ppermute(array, 'shot', [(i, i ^ 1) for i in range(nshot)])]
  transfers between devices with their start and end apart: 12 -> 13, of which waited for: 5 -> 10; matrix products, arithmetic and copies ran while one was open for 0% -> 0% of each run, Pallas kernels for 11% -> 9%
where the time goes in v4:
time: 85 us; the launch traced here: 84.5 us
  blocking collectives  36.5 us (43%)
  waiting for transfers between devices  14.4 us (17%)
  Pallas kernels  13.6 us (16%)
  starting transfers between devices  13.1 us (15%)
  local copies, waits for them, and re-layouts  5.97 us (7%)
  between operations  0.96 us (1%)
    all_to_all x3, blocking collectives, over_band(): lax.all_to_all(array, 'band', split_axis=0, concat_axis=0, tiled=True)  36.5 us
    ppermute x4, waiting for transfers between devices, other_chips(): lax.ppermute(array, 'shot', [(i, i ^ 2 * d) for i in range(nshot)])  9.63 us
    all_to_all x1, starting transfers between devices, over_band(): lax.all_to_all(array, 'band', split_axis=0, concat_axis=0, tiled=True)  7.28 us
    unnamed x24, local copies, waits for them, and re-layouts  5.97 us
    ppermute x4, starting transfers between devices, other_chips(): lax.ppermute(array, 'shot', [(i, i ^ 2 * d) for i in range(nshot)])  4.32 us
    pallas_call x1, Pallas kernels, per_device(): call(first_forward_kernel, part_out, [pltpu.VMEM((bundles, rays, samples)...  4.01 us
    all_to_all x1, waiting for transfers between devices, over_band(): lax.all_to_all(array, 'band', split_axis=0, concat_axis=0, tiled=True)  3.35 us
    pallas_call x1, Pallas kernels, per_device(): call(dense_kernel, (arr(dense_shape, bf16), arr((8, CBLK), f32)), [pltpu....  2.63 us
  transfers between devices with their start and end apart: 13, of which 10 were waited for; matrix products, arithmetic and copies ran while one was open for 0% of the time, Pallas kernels for 9%

profile of v4, /device:TPU:0, one launch (start us, length us, event | category | flops | bytes accessed | tf_op | source)
XLA Modules:
  0.0 84.5 jit_solution(709295870719389542)
XLA Ops:
  0.7 4.0 %forward1.1.after_ref = bf16[8,128,128]{2,1,0:T(8,128)(2,1)} custom-call(s32[64]{0:T(128)} %bund.1, s32[64]{0:T(128)} %cblk.1, bf16[64,128,128]{2,1,0:T(8,128)(2,1)} %sens.1, f32[16,128,128]{2,1,0:T(8,128)} %bitcast.13, f32[16,128,128]{2,1,0:T(8,128)} %bitcast.15), custom_call_target="tpu_custom_call" | custom-call | flops 268435456 | bytes 2097152 | tf_op jit(solution)/shard_map/forward1/pallas_call | solution.py:337
  4.7 7.3 %all-to-all-start = ((bf16[8,128,128]{2,1,0:T(8,128)(2,1)}), bf16[8,128,128]{2,1,0:T(8,128)(2,1)S(1)}, u32[]{:S(2)}, u32[]{:S(2)}) async-start(bf16[8,128,128]{2,1,0:T(8,128)(2,1)} %forward1.1.after_ref), calls=%async_computation | async-start | bytes 524288 | tf_op jit(solution)/shard_map/all_to_all | solution.py:286
  12.0 0.9 %copy-done.6 = bf16[8,128,128]{2,1,0:T(8,128)(2,1)S(1)} copy-done((bf16[8,128,128]{2,1,0:T(8,128)(2,1)S(1)}, bf16[8,128,128]{2,1,0:T(8,128)(2,1)}, u32[]{:S(2)}) %copy-start.6) | copy-done | bytes 262168
  13.0 2.6 %dense.1 = (bf16[8,1024,256]{2,1,0:T(8,128)(2,1)S(1)}, f32[8,128]{1,0:T(8,128)S(1)}) custom-call(s32[64]{0:T(128)S(1)} %copy-done.10, s32[64]{0:T(128)S(1)} %copy-done.11, bf16[64,128,128]{2,1,0:T(8,128)(2,1)S(1)} %copy-done.3, bf16[8,128,128]{2,1,0:T(8,128)(2,1)S(1)} %copy-done.6), custom_call_target="tpu_custom_call" | custom-call | bytes 16777216 | tf_op jit(solution)/shard_map/dense/pallas_call | solution.py:356
  15.6 1.9 %copy-done = bf16[8,1024,256]{2,1,0:T(8,128)(2,1)} copy-done((bf16[8,1024,256]{2,1,0:T(8,128)(2,1)}, bf16[8,1024,256]{2,1,0:T(8,128)(2,1)S(1)}, u32[]{:S(2)}) %copy-start) | copy-done | bytes 4194328
  17.6 3.4 %all-to-all-done = bf16[8,128,128]{2,1,0:T(8,128)(2,1)S(1)} async-done(((bf16[8,128,128]{2,1,0:T(8,128)(2,1)}), bf16[8,128,128]{2,1,0:T(8,128)(2,1)S(1)}, u32[]{:S(2)}, u32[]{:S(2)}) %all-to-all-start) | async-done | bytes 262176 | tf_op jit(solution)/shard_map/all_to_all | solution.py:286
  21.0 12.0 %all_to_all.20 = bf16[8,1,128,128]{3,2,1,0:T(8,128)(2,1)S(1)} all-to-all(bf16[8,1,128,128]{3,2,1,0:T(8,128)(2,1)S(1)} %residual1.1), channel_id=1, replica_groups=mesh['shot'=4,'band'=8] {'band'}, dimensions={0} | all-to-all | bytes 524288 | tf_op jit(solution)/shard_map/all_to_all | solution.py:286
  33.0 2.2 %copy-done.1 = bf16[8,1024,256]{2,1,0:T(8,128)(2,1)S(1)} copy-done((bf16[8,1024,256]{2,1,0:T(8,128)(2,1)S(1)}, bf16[8,1024,256]{2,1,0:T(8,128)(2,1)}, u32[]{:S(2)}) %copy-start.1) | copy-done | bytes 4194328
  35.2 0.3 adjoint1_give_a.1
  35.6 0.5 adjoint1_keep_a.1
  36.1 0.5 collective-permute-start.2
  36.6 0.3 collective-permute-done.got_ref
  37.0 1.6 %collective-permute-start.1 = (bf16[4,128,128]{2,1,0:T(8,128)(2,1)S(1)}, bf16[4,128,128]{2,1,0:T(8,128)(2,1)S(1)}, u32[]{:S(2)}, u32[]{:S(2)}) collective-permute-start(bf16[4,128,128]{2,1,0:T(8,128)(2,1)S(1)} %adjoint1_pair_a.1.rest_0_), channel_id=1, source_target_pairs={{0,16},{8,24},{16,0},{24,8},{1,17},{9,25},{17,1},{25,9},{2,18},{10... | collective-permute-start | bytes 393224 | tf_op jit(solution)/shard_map/ppermute | solution.py:281
  38.9 0.6 collective-permute-start.3
  39.7 3.7 %collective-permute-done.1.rest_1_ = bf16[4,128,128]{2,1,0:T(8,128)(2,1)S(1)} collective-permute-done((bf16[4,128,128]{2,1,0:T(8,128)(2,1)S(1)}, bf16[4,128,128]{2,1,0:T(8,128)(2,1)S(1)}, u32[]{:S(2)}, u32[]{:S(2)}) %collective-permute-start.1) | collective-permute-done | bytes 131104 | tf_op jit(solution)/shard_map/ppermute | solution.py:281
  43.6 1.8 %collective-permute-done.3.rest_1_ = bf16[4,128,128]{2,1,0:T(8,128)(2,1)S(1)} collective-permute-done((bf16[4,128,128]{2,1,0:T(8,128)(2,1)S(1)}, bf16[4,128,128]{2,1,0:T(8,128)(2,1)S(1)}, u32[]{:S(2)}, u32[]{:S(2)}) %collective-permute-start.3) | collective-permute-done | bytes 131104 | tf_op jit(solution)/shard_map/ppermute | solution.py:281
  45.6 1.0 %forward2_early.1.early = f32[8,128,128]{2,1,0:T(8,128)S(1)} custom-call(bf16[8,1024,256]{2,1,0:T(8,128)(2,1)S(1)} %copy-done.2, bf16[4,128,128]{2,1,0:T(8,128)(2,1)S(1)} %get-tuple-element.28.own_a, bf16[4,128,128]{2,1,0:T(8,128)(2,1)S(1)} %get-tuple-element.27.own_b, bf16[4,128,128]{2,1,0:T(8,128)(2,1)S(1)} %collective-permute-done.5.mate_a), custom_call_target="tpu_custom_call" | custom-call | flops 402653184 | bytes 3145728 | tf_op jit(solution)/shard_map/forward2_early/pallas_call | solution.py:391
  46.6 0.4 collective-permute-done.4.mate_b
  47.0 0.4 forward2_late.1
  47.4 12.6 %all_to_all.21 = bf16[8,128,128]{2,1,0:T(8,128)(2,1)S(1)} all-to-all(bf16[8,128,128]{2,1,0:T(8,128)(2,1)S(1)} %forward2_late.1), channel_id=1, replica_groups=mesh['shot'=4,'band'=8] {'band'}, dimensions={0} | all-to-all | bytes 524288 | tf_op jit(solution)/shard_map/all_to_all | solution.py:286
  60.1 12.0 %all_to_all.22 = bf16[8,1,128,128]{3,2,1,0:T(8,128)(2,1)S(1)} all-to-all(bf16[8,1,128,128]{3,2,1,0:T(8,128)(2,1)S(1)} %get-tuple-element.30), channel_id=1, replica_groups=mesh['shot'=4,'band'=8] {'band'}, dimensions={0} | all-to-all | bytes 524288 | tf_op jit(solution)/shard_map/all_to_all | solution.py:286
  72.5 0.5 adjoint2_keep_a.1
  72.9 0.5 collective-permute-start.8
  73.5 0.3 collective-permute-done.6.got_ref
  73.8 1.6 %collective-permute-start.7 = (bf16[4,128,128]{2,1,0:T(8,128)(2,1)S(1)}, bf16[4,128,128]{2,1,0:T(8,128)(2,1)S(1)}, u32[]{:S(2)}, u32[]{:S(2)}) collective-permute-start(bf16[4,128,128]{2,1,0:T(8,128)(2,1)S(1)} %adjoint2_pair_a.1.rest_0_), channel_id=1, source_target_pairs={{0,16},{8,24},{16,0},{24,8},{1,17},{9,25},{17,1},{25,9},{2,18},{10... | collective-permute-start | bytes 393224 | tf_op jit(solution)/shard_map/ppermute | solution.py:281
  75.7 0.6 collective-permute-start.9
  76.3 0.7 turn.1.after_ref
  77.1 3.2 %collective-permute-done.7.rest_1_ = bf16[4,128,128]{2,1,0:T(8,128)(2,1)S(1)} collective-permute-done((bf16[4,128,128]{2,1,0:T(8,128)(2,1)S(1)}, bf16[4,128,128]{2,1,0:T(8,128)(2,1)S(1)}, u32[]{:S(2)}, u32[]{:S(2)}) %collective-permute-start.7) | collective-permute-done | bytes 131104 | tf_op jit(solution)/shard_map/ppermute | solution.py:281
  80.2 0.8 copy-done.7
  81.3 1.0 %collective-permute-done.9.rest_1_ = bf16[4,128,128]{2,1,0:T(8,128)(2,1)S(1)} collective-permute-done((bf16[4,128,128]{2,1,0:T(8,128)(2,1)S(1)}, bf16[4,128,128]{2,1,0:T(8,128)(2,1)S(1)}, u32[]{:S(2)}, u32[]{:S(2)}) %collective-permute-start.9) | collective-permute-done | bytes 131104 | tf_op jit(solution)/shard_map/ppermute | solution.py:281
  82.6 0.9 %new_state_early.1 = (f32[16,128,128]{2,1,0:T(8,128)}, f32[4,128,128]{2,1,0:T(8,128)S(1)}) custom-call(f32[16,128,128]{2,1,0:T(8,128)S(1)} %get-tuple-element.21.base, bf16[4,128,128]{2,1,0:T(8,128)(2,1)S(1)} %total_a.1.own_a, bf16[4,128,128]{2,1,0:T(8,128)(2,1)S(1)} %total_b.1.own_b, bf16[4,128,128]{2,1,0:T(8,128)(2,1)S(1)} %collective-permute-done.10.mate_a), custom_call_target="tpu_custom_call" | custom-call | bytes 3145728 | tf_op jit(solution)/shard_map/new_state_early/pallas_call | solution.py:434
  83.8 0.7 new_state_late.1
  (45 shorter events, 2.8 us)
Async XLA Ops:
  0.6 11.4 %copy-start.10 = (s32[64]{0:T(128)S(1)}, s32[64]{0:T(128)}, u32[]{:S(2)}) copy-start(s32[64]{0:T(128)} %bund.1) | copy-start | bytes 772
  0.6 11.3 %copy-start.11 = (s32[64]{0:T(128)S(1)}, s32[64]{0:T(128)}, u32[]{:S(2)}) copy-start(s32[64]{0:T(128)} %cblk.1) | copy-start | bytes 772
  0.7 11.3 %copy-start.3 = (bf16[64,128,128]{2,1,0:T(8,128)(2,1)S(1)}, bf16[64,128,128]{2,1,0:T(8,128)(2,1)}, u32[]{:S(2)}) copy-start(bf16[64,128,128]{2,1,0:T(8,128)(2,1)} %sens.1) | copy-start | bytes 6291460
  0.7 20.3 %copy-start.8 = (f32[1,128]{1,0:T(1,128)S(1)}, f32[1,128]{1,0:T(1,128)}, u32[]{:S(2)}) copy-start(f32[1,128]{1,0:T(1,128)} %obs_ref.3) | copy-start | bytes 1540
  0.7 20.3 %copy-start.9 = (f32[1,128]{1,0:T(1,128)S(1)}, f32[1,128]{1,0:T(1,128)}, u32[]{:S(2)}) copy-start(f32[1,128]{1,0:T(1,128)} %wt_ref.3) | copy-start | bytes 1540
  4.7 16.2 %all-to-all-start = ((bf16[8,128,128]{2,1,0:T(8,128)(2,1)}), bf16[8,128,128]{2,1,0:T(8,128)(2,1)S(1)}, u32[]{:S(2)}, u32[]{:S(2)}) async-start(bf16[8,128,128]{2,1,0:T(8,128)(2,1)} %forward1.1.after_ref), calls=%async_computation | async-start | bytes 524288 | tf_op jit(solution)/shard_map/all_to_all | solution.py:286
  12.0 1.0 %copy-start.6 = (bf16[8,128,128]{2,1,0:T(8,128)(2,1)S(1)}, bf16[8,128,128]{2,1,0:T(8,128)(2,1)}, u32[]{:S(2)}) copy-start(bf16[8,128,128]{2,1,0:T(8,128)(2,1)} %forward1.1.after_ref) | copy-start | bytes 786436
  15.6 2.0 %copy-start = (bf16[8,1024,256]{2,1,0:T(8,128)(2,1)}, bf16[8,1024,256]{2,1,0:T(8,128)(2,1)S(1)}, u32[]{:S(2)}) copy-start(bf16[8,1024,256]{2,1,0:T(8,128)(2,1)S(1)} %get-tuple-element.19.dense) | copy-start | bytes 12582916
  33.0 2.2 %copy-start.1 = (bf16[8,1024,256]{2,1,0:T(8,128)(2,1)S(1)}, bf16[8,1024,256]{2,1,0:T(8,128)(2,1)}, u32[]{:S(2)}) copy-start(bf16[8,1024,256]{2,1,0:T(8,128)(2,1)} %copy-done) | copy-start | bytes 12582916
  35.2 3.3 %copy-start.2 = (bf16[8,1024,256]{2,1,0:T(8,128)(2,1)S(1)}, bf16[8,1024,256]{2,1,0:T(8,128)(2,1)}, u32[]{:S(2)}) copy-start(bf16[8,1024,256]{2,1,0:T(8,128)(2,1)} %copy-done) | copy-start | bytes 12582916
  35.5 4.0 %copy-start.4 = (f32[2048,128]{1,0:T(8,128)S(1)}, f32[2048,128]{1,0:T(8,128)}, u32[]{:S(2)}) copy-start(f32[2048,128]{1,0:T(8,128)} %param.10) | copy-start | bytes 3145732
  35.5 4.0 %copy-start.5 = (f32[2048,128]{1,0:T(8,128)S(1)}, f32[2048,128]{1,0:T(8,128)}, u32[]{:S(2)}) copy-start(f32[2048,128]{1,0:T(8,128)} %param.11) | copy-start | bytes 3145732
  35.5 1.4 %collective-permute-start = (bf16[4,128,128]{2,1,0:T(8,128)(2,1)S(1)}, bf16[4,128,128]{2,1,0:T(8,128)(2,1)S(1)}, u32[]{:S(2)}, u32[]{:S(2)}) collective-permute-start(bf16[4,128,128]{2,1,0:T(8,128)(2,1)S(1)} %adjoint1_give_a.1), channel_id=1, source_target_pairs={{0,8},{8,0},{16,24},{24,16},{1,9},{9,1},{17,25},{25,17},{2,10},{10... | collective-permute-start | bytes 393224 | tf_op jit(solution)/shard_map/ppermute | solution.py:277
  36.1 2.8 %collective-permute-start.2 = (bf16[4,128,128]{2,1,0:T(8,128)(2,1)S(1)}, bf16[4,128,128]{2,1,0:T(8,128)(2,1)S(1)}, u32[]{:S(2)}, u32[]{:S(2)}) collective-permute-start(bf16[4,128,128]{2,1,0:T(8,128)(2,1)S(1)} %get-tuple-element.26), channel_id=1, source_target_pairs={{0,8},{8,0},{16,24},{24,16},{1,9},{9,1},{17,25},{25,17},{2,10},{10... | collective-permute-start | bytes 393224 | tf_op jit(solution)/shard_map/ppermute | solution.py:277
  37.0 6.4 %collective-permute-start.1 = (bf16[4,128,128]{2,1,0:T(8,128)(2,1)S(1)}, bf16[4,128,128]{2,1,0:T(8,128)(2,1)S(1)}, u32[]{:S(2)}, u32[]{:S(2)}) collective-permute-start(bf16[4,128,128]{2,1,0:T(8,128)(2,1)S(1)} %adjoint1_pair_a.1.rest_0_), channel_id=1, source_target_pairs={{0,16},{8,24},{16,0},{24,8},{1,17},{9,25},{17,1},{25,9},{2,18},{10... | collective-permute-start | bytes 393224 | tf_op jit(solution)/shard_map/ppermute | solution.py:281
  38.9 6.5 %collective-permute-start.3 = (bf16[4,128,128]{2,1,0:T(8,128)(2,1)S(1)}, bf16[4,128,128]{2,1,0:T(8,128)(2,1)S(1)}, u32[]{:S(2)}, u32[]{:S(2)}) collective-permute-start(bf16[4,128,128]{2,1,0:T(8,128)(2,1)S(1)} %adjoint1_pair_b.1.rest_0_), channel_id=1, source_target_pairs={{0,16},{8,24},{16,0},{24,8},{1,17},{9,25},{17,1},{25,9},{2,18},{10... | collective-permute-start | bytes 393224 | tf_op jit(solution)/shard_map/ppermute | solution.py:281
  43.5 2.1 %collective-permute-start.5 = (bf16[4,128,128]{2,1,0:T(8,128)(2,1)S(1)}, bf16[4,128,128]{2,1,0:T(8,128)(2,1)S(1)}, u32[]{:S(2)}, u32[]{:S(2)}) collective-permute-start(bf16[4,128,128]{2,1,0:T(8,128)(2,1)S(1)} %get-tuple-element.28.own_a), channel_id=1, source_target_pairs={{0,8},{8,0},{16,24},{24,16},{1,9},{9,1},{17,25},{25,17},{2,10},{10... | collective-permute-start | bytes 393224 | tf_op jit(solution)/shard_map/ppermute | solution.py:277
  45.5 1.4 %collective-permute-start.4 = (bf16[4,128,128]{2,1,0:T(8,128)(2,1)S(1)}, bf16[4,128,128]{2,1,0:T(8,128)(2,1)S(1)}, u32[]{:S(2)}, u32[]{:S(2)}) collective-permute-start(bf16[4,128,128]{2,1,0:T(8,128)(2,1)S(1)} %get-tuple-element.27.own_b), channel_id=1, source_target_pairs={{0,8},{8,0},{16,24},{24,16},{1,9},{9,1},{17,25},{25,17},{2,10},{10... | collective-permute-start | bytes 393224 | tf_op jit(solution)/shard_map/ppermute | solution.py:277
  72.4 1.4 %collective-permute-start.6 = (bf16[4,128,128]{2,1,0:T(8,128)(2,1)S(1)}, bf16[4,128,128]{2,1,0:T(8,128)(2,1)S(1)}, u32[]{:S(2)}, u32[]{:S(2)}) collective-permute-start(bf16[4,128,128]{2,1,0:T(8,128)(2,1)S(1)} %adjoint2_give_a.1), channel_id=1, source_target_pairs={{0,8},{8,0},{16,24},{24,16},{1,9},{9,1},{17,25},{25,17},{2,10},{10... | collective-permute-start | bytes 393224 | tf_op jit(solution)/shard_map/ppermute | solution.py:277
  72.9 2.8 %collective-permute-start.8 = (bf16[4,128,128]{2,1,0:T(8,128)(2,1)S(1)}, bf16[4,128,128]{2,1,0:T(8,128)(2,1)S(1)}, u32[]{:S(2)}, u32[]{:S(2)}) collective-permute-start(bf16[4,128,128]{2,1,0:T(8,128)(2,1)S(1)} %get-tuple-element.33), channel_id=1, source_target_pairs={{0,8},{8,0},{16,24},{24,16},{1,9},{9,1},{17,25},{25,17},{2,10},{10... | collective-permute-start | bytes 393224 | tf_op jit(solution)/shard_map/ppermute | solution.py:277
  73.8 6.4 %collective-permute-start.7 = (bf16[4,128,128]{2,1,0:T(8,128)(2,1)S(1)}, bf16[4,128,128]{2,1,0:T(8,128)(2,1)S(1)}, u32[]{:S(2)}, u32[]{:S(2)}) collective-permute-start(bf16[4,128,128]{2,1,0:T(8,128)(2,1)S(1)} %adjoint2_pair_a.1.rest_0_), channel_id=1, source_target_pairs={{0,16},{8,24},{16,0},{24,8},{1,17},{9,25},{17,1},{25,9},{2,18},{10... | collective-permute-start | bytes 393224 | tf_op jit(solution)/shard_map/ppermute | solution.py:281
  75.7 6.5 %collective-permute-start.9 = (bf16[4,128,128]{2,1,0:T(8,128)(2,1)S(1)}, bf16[4,128,128]{2,1,0:T(8,128)(2,1)S(1)}, u32[]{:S(2)}, u32[]{:S(2)}) collective-permute-start(bf16[4,128,128]{2,1,0:T(8,128)(2,1)S(1)} %adjoint2_pair_b.1.rest_0_), channel_id=1, source_target_pairs={{0,16},{8,24},{16,0},{24,8},{1,17},{9,25},{17,1},{25,9},{2,18},{10... | collective-permute-start | bytes 393224 | tf_op jit(solution)/shard_map/ppermute | solution.py:281
  80.2 0.8 copy-start.7
  81.2 1.4 %collective-permute-start.10 = (bf16[4,128,128]{2,1,0:T(8,128)(2,1)S(1)}, bf16[4,128,128]{2,1,0:T(8,128)(2,1)S(1)}, u32[]{:S(2)}, u32[]{:S(2)}) collective-permute-start(bf16[4,128,128]{2,1,0:T(8,128)(2,1)S(1)} %total_a.1.own_a), channel_id=1, source_target_pairs={{0,8},{8,0},{16,24},{24,16},{1,9},{9,1},{17,25},{25,17},{2,10},{10... | collective-permute-start | bytes 393224 | tf_op jit(solution)/shard_map/ppermute | solution.py:277
  82.4 1.4 %collective-permute-start.11 = (bf16[4,128,128]{2,1,0:T(8,128)(2,1)S(1)}, bf16[4,128,128]{2,1,0:T(8,128)(2,1)S(1)}, u32[]{:S(2)}, u32[]{:S(2)}) collective-permute-start(bf16[4,128,128]{2,1,0:T(8,128)(2,1)S(1)} %total_b.1.own_b), channel_id=1, source_target_pairs={{0,8},{8,0},{16,24},{24,16},{1,9},{9,1},{17,25},{25,17},{2,10},{10... | collective-permute-start | bytes 393224 | tf_op jit(solution)/shard_map/ppermute | solution.py:277

commit v5 on v4

--- a/solution.py
+++ b/solution.py
@@ -8,9 +8,10 @@
 from jax.sharding import PartitionSpec as P
 
 CBLK = 128
-GROUP = 16
-CHUNKS = 4
+GROUP = 32
+CHUNKS = 2
 FIRST_VMEM = 55 << 20
+GIVE_A, KEEP_A, GIVE_B, KEEP_B = range(4)
 
 VMEM = pl.BlockSpec(memory_space=pltpu.VMEM)
 SMEM = pl.BlockSpec(memory_space=pltpu.SMEM)
@@ -102,77 +103,67 @@
     out_ref[...] = acc[...].astype(bf16)
 
 
-def dense_kernel(bund, cblk, sens, after_ref, out_ref, token_ref, total):
+def dense_kernel(bund, cblk, sens, after_ref, *rest):
+    out_refs, (token_ref, total) = rest[:4], rest[4:]
     rays = sens.shape[1]
+    quarter = 2 * total.shape[1]
+    core = lax.axis_index("shot") % 2
     total[...] = jnp.zeros_like(total)
 
     def place(k, carry):
+        cell = cblk[k]
+        kept = jnp.where(cell // (2 * quarter) == core, 1, 0)
+        part = 2 * (cell // quarter % 2) + kept
         rows = pl.ds(pl.multiple_of(bund[k] * rays, rays), rays)
-        lanes = pl.ds(pl.multiple_of(cblk[k] % 2 * CBLK, CBLK), CBLK)
-        total[cblk[k] // 2, rows, lanes] += sens[k].astype(f32)
+        lanes = pl.ds(pl.multiple_of(cell % 2 * CBLK, CBLK), CBLK)
+        total[part, cell % quarter // 2, rows, lanes] += sens[k].astype(f32)
         return carry
 
     lax.fori_loop(0, sens.shape[0], place, 0)
-    for i in range(total.shape[0]):
-        out_ref[i] = total[i].astype(bf16)
+    for part, out_ref in enumerate(out_refs):
+        out_ref[...] = total[part].astype(bf16)
     token_ref[...] = jnp.zeros_like(token_ref)
 
 
-def dense_forward(dense, columns, start_of, store):
+def dense_forward(columns, store):
     step = 2 * CBLK
-    probe = jnp.concatenate([part for _, part in columns], axis=0)
-    for m in range(dense.shape[1] // step):
+    pairs = columns[0][0].shape[0]
+    probe = jnp.concatenate(
+        [part[...].reshape(2 * CBLK * pairs, -1) for _, part in columns], axis=0
+    )
+    for m in range(columns[0][0].shape[1] // step):
         rows = pl.ds(m * step, step)
-        lhs = jnp.concatenate([dense[pair, rows, :] for pair, _ in columns], axis=1)
+        lhs = jnp.concatenate(
+            [dense[pair, rows, :] for dense, _ in columns for pair in range(pairs)], axis=1
+        )
         total = jnp.dot(lhs, probe, preferred_element_type=f32)
-        store(m, start_of(m, total.reshape(2, CBLK, -1)))
-
-
-def columns_of(first, part_ref):
-    return [
-        (first + j, part_ref[pl.ds(2 * j, 2)].reshape(2 * CBLK, -1))
-        for j in range(part_ref.shape[0] // 2)
-    ]
-
-
-def early_forward_kernel(dense, own_a, own_b, mate_a, acc):
-    half, quarter = dense.shape[0] // 2, dense.shape[0] // 4
-    core = lax.axis_index("shot") % 2
-    own, mate = core * half, (1 - core) * half
-    columns = columns_of(own, own_a) + columns_of(own + quarter, own_b) + columns_of(mate, mate_a)
-
-    def store(m, value):
-        acc[pl.ds(2 * m, 2)] = value
-
-    dense_forward(dense, columns, lambda m, value: value, store)
-
-
-def late_forward_kernel(dense, mate_b, early, out_ref):
-    half, quarter = dense.shape[0] // 2, dense.shape[0] // 4
-    core = lax.axis_index("shot") % 2
-
-    def store(m, value):
-        out_ref[pl.ds(2 * m, 2)] = value.astype(bf16)
-
-    dense_forward(
-        dense,
-        columns_of((1 - core) * half + quarter, mate_b),
-        lambda m, value: early[pl.ds(2 * m, 2)] + value,
-        store,
-    )
-
-
-def adjoint_kernel(parts, dense, resid, *out_refs):
-    half, quarter = dense.shape[0] // 2, dense.shape[0] // 4
-    core = lax.axis_index("shot") % 2
+        store(pl.ds(2 * m, 2), total.reshape(2, CBLK, -1))
+
+
+def early_forward_kernel(dense_own_a, dense_own_b, dense_mate_a, own_a, own_b, mate_a, acc):
+    def store(rows, value):
+        acc[rows] = value
+
+    columns = [(dense_own_a, own_a), (dense_own_b, own_b), (dense_mate_a, mate_a)]
+    dense_forward(columns, store)
+
+
+def late_forward_kernel(dense_mate_b, mate_b, early, out_ref):
+    def store(rows, value):
+        out_ref[rows] = (early[rows] + value).astype(bf16)
+
+    dense_forward([(dense_mate_b, mate_b)], store)
+
+
+def adjoint_kernel(resid, *refs):
     lhs = jnp.concatenate([resid[m] for m in range(resid.shape[0])], axis=1)
-    for (keep, second), out_ref in zip(parts, out_refs):
-        first = (core if keep else 1 - core) * half + second * quarter
-        for j in range(quarter):
-            both = jnp.dot(lhs, dense[first + j], preferred_element_type=f32)
+    count = len(refs) // 2
+    for dense, out_ref in zip(refs[:count], refs[count:]):
+        for pair in range(dense.shape[0]):
+            both = jnp.dot(lhs, dense[pair], preferred_element_type=f32)
             both = both.astype(out_ref.dtype)
-            out_ref[2 * j] = both[:, :CBLK]
-            out_ref[2 * j + 1] = both[:, CBLK:]
+            out_ref[2 * pair] = both[:, :CBLK]
+            out_ref[2 * pair + 1] = both[:, CBLK:]
 
 
 def pair_kernel(keep_ref, got_ref, out_ref):
@@ -192,9 +183,10 @@
             out_ref[d, i] = rounded
 
 
-def turn_kernel(in_ref, out_ref):
+def turn_kernel(in_ref, out_ref, token_ref):
     for i in range(in_ref.shape[0]):
         out_ref[i] = in_ref[i].T
+    token_ref[...] = jnp.zeros_like(token_ref)
 
 
 def prepare_kernel(state, prior, after_ref, field_a, field_b, base_ref):
@@ -286,7 +278,8 @@
         return lax.all_to_all(array, "band", split_axis=0, concat_axis=0, tiled=True)
 
     part_out = arr((bundles, rays, samples), bf16)
-    dense_shape = (cells // 2, bundles * rays, 2 * CBLK)
+    dense_shape = (quarter // 2, bundles * rays, 2 * CBLK)
+    small_token = arr((8, CBLK), f32)
     dense_flops = 2 * bundles * rays * cells * CBLK * samples
     dense_bytes = 2 * bundles * rays * cells * CBLK
     quarter_bf16 = arr((quarter, CBLK, samples), bf16)
@@ -306,14 +299,14 @@
     def adjoint(dense, resid_all, name):
         def kernel(parts, part):
             return call(
-                functools.partial(adjoint_kernel, parts),
-                tuple(quarter_f32 if keep else quarter_bf16 for keep, _ in parts),
+                adjoint_kernel,
+                tuple(quarter_f32 if p % 2 else quarter_bf16 for p in parts),
                 [],
-                [VMEM] * 2,
+                [VMEM] * (1 + len(parts)),
                 name + part,
                 dense_flops * len(parts) // 4,
                 dense_bytes * len(parts) // 4,
-            )(dense, resid_all)
+            )(resid_all, *[dense[p] for p in parts])
 
         def pair(keep, got, part):
             return call(
@@ -325,12 +318,12 @@
                 bytes_accessed=1 << 19,
             )(keep, got)
 
-        (give_a,) = kernel(((False, 0),), "_give_a")
+        (give_a,) = kernel((GIVE_A,), "_give_a")
         got_a = other_core(give_a)
-        keep_a, give_b = kernel(((True, 0), (False, 1)), "_keep_a")
+        keep_a, give_b = kernel((KEEP_A, GIVE_B), "_keep_a")
         got_b = other_core(give_b)
         sums_a = other_chips(pair(keep_a, got_a, "_a"))
-        (keep_b,) = kernel(((True, 1),), "_keep_b")
+        (keep_b,) = kernel((KEEP_B,), "_keep_b")
         sums_b = other_chips(pair(keep_b, got_b, "_b"))
         return sums_a, sums_b, keep_b
 
@@ -353,10 +346,10 @@
         sens_bytes,
         vmem=FIRST_VMEM,
     )(bund, cblk, sens, state_b, prior_b)
-    dense, token = call(
+    *dense, token = call(
         dense_kernel,
-        (arr(dense_shape, bf16), arr((8, CBLK), f32)),
-        [pltpu.VMEM(dense_shape, f32)],
+        (arr(dense_shape, bf16),) * 4 + (small_token,),
+        [pltpu.VMEM((4,) + dense_shape, f32)],
         [SMEM, SMEM, VMEM, ANY],
         "dense",
         0,
@@ -392,11 +385,11 @@
         early_forward_kernel,
         arr((bundles, rays, samples), f32),
         [],
-        [VMEM] * 4,
+        [VMEM] * 6,
         "forward2_early",
         dense_flops * 3 // 4,
         dense_bytes * 3 // 4,
-    )(dense, own[0], own[1], mate[0])
+    )(dense[KEEP_A], dense[KEEP_B], dense[GIVE_A], own[0], own[1], mate[0])
     part2 = call(
         late_forward_kernel,
         part_out,
@@ -405,19 +398,19 @@
         "forward2_late",
         dense_flops // 4,
         dense_bytes // 4,
-    )(dense, mate[1], early)
+    )(dense[GIVE_B], mate[1], early)
 
     (resid2_t,), resid_all2 = residual(part2, token, "residual2", True)
     *sums2, _ = adjoint(dense, resid_all2, "adjoint2")
-    resid2 = call(
+    resid2, after = call(
         turn_kernel,
-        arr((owned, rays, samples), f32),
+        (arr((owned, rays, samples), f32), small_token),
         [],
         [VMEM],
         "turn",
         bytes_accessed=1 << 20,
     )(resid2_t)
-    own, mate, after = [], [], resid2
+    own, mate = [], []
     for grad, sums, part in zip(grad1, sums2, "ab"):
         total = call(
             functools.partial(total_kernel, ny),
@@ -428,7 +421,6 @@
             bytes_accessed=1 << 19,
         )(grad, after, *sums)
         own.append(total)
-        after = grad
         mate.append(other_core(total))
     whole = arr((cells, CBLK, samples), f32)
     so_far, rest = call(

time: 85 us -> 83.9 us (0.987)
  local copies, waits for them, and re-layouts: 5.97 us -> 4.77 us
    all_to_all x1, waiting for transfers between devices: 3.35 us -> 1.9 us  [over_band(): lax.all_to_all(array, 'band', split_axis=0, concat_axis=0, tiled=True)]
    unnamed x24 -> x22, local copies, waits for them, and re-layouts: 5.97 us -> 4.77 us
  transfers between devices with their start and end apart: 13 -> 13, of which waited for: 10 -> 9; matrix products, arithmetic and copies ran while one was open for 0% -> 0% of each run, Pallas kernels for 9% -> 10%
where the time goes in v5:
time: 83.9 us; the launch traced here: 83.4 us
  blocking collectives  36.8 us (44%)
  Pallas kernels  14 us (17%)
  waiting for transfers between devices  13.7 us (16%)
  starting transfers between devices  13.1 us (16%)
  local copies, waits for them, and re-layouts  4.77 us (6%)
  between operations  0.96 us (1%)
    all_to_all x3, blocking collectives, over_band(): lax.all_to_all(array, 'band', split_axis=0, concat_axis=0, tiled=True)  36.8 us
    ppermute x4, waiting for transfers between devices, other_chips(): lax.ppermute(array, 'shot', [(i, i ^ 2 * d) for i in range(nshot)])  10.5 us
    all_to_all x1, starting transfers between devices, over_band(): lax.all_to_all(array, 'band', split_axis=0, concat_axis=0, tiled=True)  7.27 us
    unnamed x22, local copies, waits for them, and re-layouts  4.77 us
    ppermute x4, starting transfers between devices, other_chips(): lax.ppermute(array, 'shot', [(i, i ^ 2 * d) for i in range(nshot)])  4.31 us
    pallas_call x1, Pallas kernels, per_device(): call(first_forward_kernel, part_out, [pltpu.VMEM((bundles, rays, samples)...  3.61 us
    pallas_call x1, Pallas kernels, per_device(): call(dense_kernel, (arr(dense_shape, bf16),) * 4 + (small_token,), [pltpu...  3.48 us
    pallas_call x6, Pallas kernels, kernel(): call(adjoint_kernel, tuple((quarter_f32 if p % 2 else quarter_bf16 for p...  2.11 us
  transfers between devices with their start and end apart: 13, of which 9 were waited for; matrix products, arithmetic and copies ran while one was open for 0% of the time, Pallas kernels for 10%

profile of v5, /device:TPU:0, one launch (start us, length us, event | category | flops | bytes accessed | tf_op | source)
XLA Modules:
  0.0 83.4 jit_solution(18392017730005325830)
XLA Ops:
  0.6 3.6 %forward1.1.after_ref = bf16[8,128,128]{2,1,0:T(8,128)(2,1)} custom-call(s32[64]{0:T(128)} %bund.1, s32[64]{0:T(128)} %cblk.1, bf16[64,128,128]{2,1,0:T(8,128)(2,1)} %sens.1, f32[16,128,128]{2,1,0:T(8,128)} %bitcast.7, f32[16,128,128]{2,1,0:T(8,128)} %bitcast.9), custom_call_target="tpu_custom_call" | custom-call | flops 268435456 | bytes 2097152 | tf_op jit(solution)/shard_map/forward1/pallas_call | solution.py:330
  4.3 7.3 %all-to-all-start = ((bf16[8,128,128]{2,1,0:T(8,128)(2,1)}), bf16[8,128,128]{2,1,0:T(8,128)(2,1)S(1)}, u32[]{:S(2)}, u32[]{:S(2)}) async-start(bf16[8,128,128]{2,1,0:T(8,128)(2,1)} %forward1.1.after_ref), calls=%async_computation | async-start | bytes 524288 | tf_op jit(solution)/shard_map/all_to_all | solution.py:278
  11.6 1.6 %copy-done.3 = bf16[64,128,128]{2,1,0:T(8,128)(2,1)S(1)} copy-done((bf16[64,128,128]{2,1,0:T(8,128)(2,1)S(1)}, bf16[64,128,128]{2,1,0:T(8,128)(2,1)}, u32[]{:S(2)}) %copy-start.3) | copy-done | bytes 2097176
  13.2 0.9 %copy-done.6 = bf16[8,128,128]{2,1,0:T(8,128)(2,1)S(1)} copy-done((bf16[8,128,128]{2,1,0:T(8,128)(2,1)S(1)}, bf16[8,128,128]{2,1,0:T(8,128)(2,1)}, u32[]{:S(2)}) %copy-start.6) | copy-done | bytes 262168
  14.1 3.5 %dense.1 = (bf16[2,1024,256]{2,1,0:T(8,128)(2,1)S(1)}, bf16[2,1024,256]{2,1,0:T(8,128)(2,1)S(1)}, bf16[2,1024,256]{2,1,0:T(8,128)(2,1)S(1)}, bf16[2,1024,256]{2,1,0:T(8,128)(2,1)S(1)}, f32[8,128]{1,0:T(8,128)S(1)}) custom-call(s32[64]{0:T(128)S(1)} %copy-done.9, s32[64]{0:T(128)S(1)} %copy-done.10, bf16[64,128,128]{2,1,0:T(8,128)(2,1)S(1)} %copy-done.3, ...), custom_call_target="tpu_custom_call" | custom-call | bytes 16777216 | tf_op jit(solution)/shard_map/dense/pallas_call | solution.py:349
  17.6 1.0 %copy-done = bf16[2,1024,256]{2,1,0:T(8,128)(2,1)} copy-done((bf16[2,1024,256]{2,1,0:T(8,128)(2,1)}, bf16[2,1024,256]{2,1,0:T(8,128)(2,1)S(1)}, u32[]{:S(2)}) %copy-start) | copy-done | bytes 1048600
  18.6 1.9 %all-to-all-done = bf16[8,128,128]{2,1,0:T(8,128)(2,1)S(1)} async-done(((bf16[8,128,128]{2,1,0:T(8,128)(2,1)}), bf16[8,128,128]{2,1,0:T(8,128)(2,1)S(1)}, u32[]{:S(2)}, u32[]{:S(2)}) %all-to-all-start) | async-done | bytes 262176 | tf_op jit(solution)/shard_map/all_to_all | solution.py:278
  20.6 12.4 %all_to_all.20 = bf16[8,1,128,128]{3,2,1,0:T(8,128)(2,1)S(1)} all-to-all(bf16[8,1,128,128]{3,2,1,0:T(8,128)(2,1)S(1)} %residual1.1), channel_id=1, replica_groups=mesh['shot'=4,'band'=8] {'band'}, dimensions={0} | all-to-all | bytes 524288 | tf_op jit(solution)/shard_map/all_to_all | solution.py:278
  33.0 1.2 %copy-done.1 = bf16[2,1024,256]{2,1,0:T(8,128)(2,1)S(1)} copy-done((bf16[2,1024,256]{2,1,0:T(8,128)(2,1)S(1)}, bf16[2,1024,256]{2,1,0:T(8,128)(2,1)}, u32[]{:S(2)}) %copy-start.1) | copy-done | bytes 1048600
  34.6 0.4 adjoint1_keep_a.1
  35.1 0.5 collective-permute-start.2
  35.6 0.3 collective-permute-done.got_ref
  36.0 1.6 %collective-permute-start.1 = (bf16[4,128,128]{2,1,0:T(8,128)(2,1)S(1)}, bf16[4,128,128]{2,1,0:T(8,128)(2,1)S(1)}, u32[]{:S(2)}, u32[]{:S(2)}) collective-permute-start(bf16[4,128,128]{2,1,0:T(8,128)(2,1)S(1)} %adjoint1_pair_a.1.rest_0_), channel_id=1, source_target_pairs={{0,16},{8,24},{16,0},{24,8},{1,17},{9,25},{17,1},{25,9},{2,18},{10... | collective-permute-start | bytes 393224 | tf_op jit(solution)/shard_map/ppermute | solution.py:273
  37.9 0.6 collective-permute-start.3
  38.7 3.7 %collective-permute-done.1.rest_1_ = bf16[4,128,128]{2,1,0:T(8,128)(2,1)S(1)} collective-permute-done((bf16[4,128,128]{2,1,0:T(8,128)(2,1)S(1)}, bf16[4,128,128]{2,1,0:T(8,128)(2,1)S(1)}, u32[]{:S(2)}, u32[]{:S(2)}) %collective-permute-start.1) | collective-permute-done | bytes 131104 | tf_op jit(solution)/shard_map/ppermute | solution.py:273
  42.6 1.8 %collective-permute-done.3.rest_1_ = bf16[4,128,128]{2,1,0:T(8,128)(2,1)S(1)} collective-permute-done((bf16[4,128,128]{2,1,0:T(8,128)(2,1)S(1)}, bf16[4,128,128]{2,1,0:T(8,128)(2,1)S(1)}, u32[]{:S(2)}, u32[]{:S(2)}) %collective-permute-start.3) | collective-permute-done | bytes 131104 | tf_op jit(solution)/shard_map/ppermute | solution.py:273
  44.7 1.0 %forward2_early.1.early = f32[8,128,128]{2,1,0:T(8,128)S(1)} custom-call(bf16[2,1024,256]{2,1,0:T(8,128)(2,1)S(1)} %get-tuple-element.28.refs_0_.dense_own_a, bf16[2,1024,256]{2,1,0:T(8,128)(2,1)S(1)} %get-tuple-element.25.refs_0_.dense_own_b, bf16[2,1024,256]{2,1,0:T(8,128)(2,1)S(1)} %copy-done.2, bf16[4,128,128]{2,1,0:T(8,128)(2,1)S(1)} %get-tuple-element.36.own_a, ...), custom_call_target="tpu_custom_call" | custom-call | flops 402653184 | bytes 3145728 | tf_op jit(solution)/shard_map/forward2_early/pallas_call | solution.py:384
  45.6 0.3 collective-permute-done.4.mate_b
  46.0 0.4 forward2_late.1
  46.4 12.5 %all_to_all.21 = bf16[8,128,128]{2,1,0:T(8,128)(2,1)S(1)} all-to-all(bf16[8,128,128]{2,1,0:T(8,128)(2,1)S(1)} %forward2_late.1), channel_id=1, replica_groups=mesh['shot'=4,'band'=8] {'band'}, dimensions={0} | all-to-all | bytes 524288 | tf_op jit(solution)/shard_map/all_to_all | solution.py:278
  59.0 12.0 %all_to_all.22 = bf16[8,1,128,128]{3,2,1,0:T(8,128)(2,1)S(1)} all-to-all(bf16[8,1,128,128]{3,2,1,0:T(8,128)(2,1)S(1)} %get-tuple-element.39), channel_id=1, replica_groups=mesh['shot'=4,'band'=8] {'band'}, dimensions={0} | all-to-all | bytes 524288 | tf_op jit(solution)/shard_map/all_to_all | solution.py:278
  71.3 0.4 adjoint2_keep_a.1
  71.8 0.6 collective-permute-start.8
  72.3 0.3 collective-permute-done.6.got_ref
  72.7 1.6 %collective-permute-start.7 = (bf16[4,128,128]{2,1,0:T(8,128)(2,1)S(1)}, bf16[4,128,128]{2,1,0:T(8,128)(2,1)S(1)}, u32[]{:S(2)}, u32[]{:S(2)}) collective-permute-start(bf16[4,128,128]{2,1,0:T(8,128)(2,1)S(1)} %adjoint2_pair_a.1.rest_0_), channel_id=1, source_target_pairs={{0,16},{8,24},{16,0},{24,8},{1,17},{9,25},{17,1},{25,9},{2,18},{10... | collective-permute-start | bytes 393224 | tf_op jit(solution)/shard_map/ppermute | solution.py:273
  74.6 0.6 collective-permute-start.9
  75.2 0.7 turn.1
  75.9 3.2 %collective-permute-done.7.rest_1_ = bf16[4,128,128]{2,1,0:T(8,128)(2,1)S(1)} collective-permute-done((bf16[4,128,128]{2,1,0:T(8,128)(2,1)S(1)}, bf16[4,128,128]{2,1,0:T(8,128)(2,1)S(1)}, u32[]{:S(2)}, u32[]{:S(2)}) %collective-permute-start.7) | collective-permute-done | bytes 131104 | tf_op jit(solution)/shard_map/ppermute | solution.py:273
  79.3 1.8 %collective-permute-done.9.rest_1_ = bf16[4,128,128]{2,1,0:T(8,128)(2,1)S(1)} collective-permute-done((bf16[4,128,128]{2,1,0:T(8,128)(2,1)S(1)}, bf16[4,128,128]{2,1,0:T(8,128)(2,1)S(1)}, u32[]{:S(2)}, u32[]{:S(2)}) %collective-permute-start.9) | collective-permute-done | bytes 131104 | tf_op jit(solution)/shard_map/ppermute | solution.py:273
  81.4 0.9 %new_state_early.1 = (f32[16,128,128]{2,1,0:T(8,128)}, f32[4,128,128]{2,1,0:T(8,128)S(1)}) custom-call(f32[16,128,128]{2,1,0:T(8,128)S(1)} %get-tuple-element.26.base, bf16[4,128,128]{2,1,0:T(8,128)(2,1)S(1)} %total_a.1.own_a, bf16[4,128,128]{2,1,0:T(8,128)(2,1)S(1)} %total_b.1.own_b, bf16[4,128,128]{2,1,0:T(8,128)(2,1)S(1)} %collective-permute-done.10.mate_a), custom_call_target="tpu_custom_call" | custom-call | bytes 3145728 | tf_op jit(solution)/shard_map/new_state_early/pallas_call | solution.py:426
  82.3 0.4 collective-permute-done.11.mate_b
  82.7 0.7 new_state_late.1
  (43 shorter events, 2.7 us)
Async XLA Ops:
  0.6 10.9 %copy-start.9 = (s32[64]{0:T(128)S(1)}, s32[64]{0:T(128)}, u32[]{:S(2)}) copy-start(s32[64]{0:T(128)} %bund.1) | copy-start | bytes 772
  0.6 10.9 %copy-start.10 = (s32[64]{0:T(128)S(1)}, s32[64]{0:T(128)}, u32[]{:S(2)}) copy-start(s32[64]{0:T(128)} %cblk.1) | copy-start | bytes 772
  4.3 16.2 %copy-start.7 = (f32[1,128]{1,0:T(1,128)S(1)}, f32[1,128]{1,0:T(1,128)}, u32[]{:S(2)}) copy-start(f32[1,128]{1,0:T(1,128)} %obs_ref.3) | copy-start | bytes 1540
  4.3 16.2 %copy-start.8 = (f32[1,128]{1,0:T(1,128)S(1)}, f32[1,128]{1,0:T(1,128)}, u32[]{:S(2)}) copy-start(f32[1,128]{1,0:T(1,128)} %wt_ref.3) | copy-start | bytes 1540
  4.3 16.2 %all-to-all-start = ((bf16[8,128,128]{2,1,0:T(8,128)(2,1)}), bf16[8,128,128]{2,1,0:T(8,128)(2,1)S(1)}, u32[]{:S(2)}, u32[]{:S(2)}) async-start(bf16[8,128,128]{2,1,0:T(8,128)(2,1)} %forward1.1.after_ref), calls=%async_computation | async-start | bytes 524288 | tf_op jit(solution)/shard_map/all_to_all | solution.py:278
  11.6 1.6 %copy-start.3 = (bf16[64,128,128]{2,1,0:T(8,128)(2,1)S(1)}, bf16[64,128,128]{2,1,0:T(8,128)(2,1)}, u32[]{:S(2)}) copy-start(bf16[64,128,128]{2,1,0:T(8,128)(2,1)} %sens.1) | copy-start | bytes 6291460
  13.2 0.9 %copy-start.6 = (bf16[8,128,128]{2,1,0:T(8,128)(2,1)S(1)}, bf16[8,128,128]{2,1,0:T(8,128)(2,1)}, u32[]{:S(2)}) copy-start(bf16[8,128,128]{2,1,0:T(8,128)(2,1)} %forward1.1.after_ref) | copy-start | bytes 786436
  17.6 1.0 %copy-start = (bf16[2,1024,256]{2,1,0:T(8,128)(2,1)}, bf16[2,1024,256]{2,1,0:T(8,128)(2,1)S(1)}, u32[]{:S(2)}) copy-start(bf16[2,1024,256]{2,1,0:T(8,128)(2,1)S(1)} %get-tuple-element.31.refs_0_.dense_mate_a) | copy-start | bytes 3145732
  33.0 1.2 %copy-start.1 = (bf16[2,1024,256]{2,1,0:T(8,128)(2,1)S(1)}, bf16[2,1024,256]{2,1,0:T(8,128)(2,1)}, u32[]{:S(2)}) copy-start(bf16[2,1024,256]{2,1,0:T(8,128)(2,1)} %copy-done) | copy-start | bytes 3145732
  34.5 1.4 %collective-permute-start = (bf16[4,128,128]{2,1,0:T(8,128)(2,1)S(1)}, bf16[4,128,128]{2,1,0:T(8,128)(2,1)S(1)}, u32[]{:S(2)}, u32[]{:S(2)}) collective-permute-start(bf16[4,128,128]{2,1,0:T(8,128)(2,1)S(1)} %adjoint1_give_a.1), channel_id=1, source_target_pairs={{0,8},{8,0},{16,24},{24,16},{1,9},{9,1},{17,25},{25,17},{2,10},{10... | collective-permute-start | bytes 393224 | tf_op jit(solution)/shard_map/ppermute | solution.py:269
  34.6 3.9 %copy-start.4 = (f32[2048,128]{1,0:T(8,128)S(1)}, f32[2048,128]{1,0:T(8,128)}, u32[]{:S(2)}) copy-start(f32[2048,128]{1,0:T(8,128)} %param.10) | copy-start | bytes 3145732
  34.6 3.9 %copy-start.5 = (f32[2048,128]{1,0:T(8,128)S(1)}, f32[2048,128]{1,0:T(8,128)}, u32[]{:S(2)}) copy-start(f32[2048,128]{1,0:T(8,128)} %param.11) | copy-start | bytes 3145732
  35.1 2.8 %collective-permute-start.2 = (bf16[4,128,128]{2,1,0:T(8,128)(2,1)S(1)}, bf16[4,128,128]{2,1,0:T(8,128)(2,1)S(1)}, u32[]{:S(2)}, u32[]{:S(2)}) collective-permute-start(bf16[4,128,128]{2,1,0:T(8,128)(2,1)S(1)} %get-tuple-element.34), channel_id=1, source_target_pairs={{0,8},{8,0},{16,24},{24,16},{1,9},{9,1},{17,25},{25,17},{2,10},{10... | collective-permute-start | bytes 393224 | tf_op jit(solution)/shard_map/ppermute | solution.py:269
  36.0 6.4 %collective-permute-start.1 = (bf16[4,128,128]{2,1,0:T(8,128)(2,1)S(1)}, bf16[4,128,128]{2,1,0:T(8,128)(2,1)S(1)}, u32[]{:S(2)}, u32[]{:S(2)}) collective-permute-start(bf16[4,128,128]{2,1,0:T(8,128)(2,1)S(1)} %adjoint1_pair_a.1.rest_0_), channel_id=1, source_target_pairs={{0,16},{8,24},{16,0},{24,8},{1,17},{9,25},{17,1},{25,9},{2,18},{10... | collective-permute-start | bytes 393224 | tf_op jit(solution)/shard_map/ppermute | solution.py:273
  37.9 6.8 %copy-start.2 = (bf16[2,1024,256]{2,1,0:T(8,128)(2,1)S(1)}, bf16[2,1024,256]{2,1,0:T(8,128)(2,1)}, u32[]{:S(2)}) copy-start(bf16[2,1024,256]{2,1,0:T(8,128)(2,1)} %copy-done) | copy-start | bytes 3145732
  37.9 6.5 %collective-permute-start.3 = (bf16[4,128,128]{2,1,0:T(8,128)(2,1)S(1)}, bf16[4,128,128]{2,1,0:T(8,128)(2,1)S(1)}, u32[]{:S(2)}, u32[]{:S(2)}) collective-permute-start(bf16[4,128,128]{2,1,0:T(8,128)(2,1)S(1)} %adjoint1_pair_b.1.rest_0_), channel_id=1, source_target_pairs={{0,16},{8,24},{16,0},{24,8},{1,17},{9,25},{17,1},{25,9},{2,18},{10... | collective-permute-start | bytes 393224 | tf_op jit(solution)/shard_map/ppermute | solution.py:273
  42.5 2.1 %collective-permute-start.5 = (bf16[4,128,128]{2,1,0:T(8,128)(2,1)S(1)}, bf16[4,128,128]{2,1,0:T(8,128)(2,1)S(1)}, u32[]{:S(2)}, u32[]{:S(2)}) collective-permute-start(bf16[4,128,128]{2,1,0:T(8,128)(2,1)S(1)} %get-tuple-element.36.own_a), channel_id=1, source_target_pairs={{0,8},{8,0},{16,24},{24,16},{1,9},{9,1},{17,25},{25,17},{2,10},{10... | collective-permute-start | bytes 393224 | tf_op jit(solution)/shard_map/ppermute | solution.py:269
  44.6 1.4 %collective-permute-start.4 = (bf16[4,128,128]{2,1,0:T(8,128)(2,1)S(1)}, bf16[4,128,128]{2,1,0:T(8,128)(2,1)S(1)}, u32[]{:S(2)}, u32[]{:S(2)}) collective-permute-start(bf16[4,128,128]{2,1,0:T(8,128)(2,1)S(1)} %get-tuple-element.35.own_b), channel_id=1, source_target_pairs={{0,8},{8,0},{16,24},{24,16},{1,9},{9,1},{17,25},{25,17},{2,10},{10... | collective-permute-start | bytes 393224 | tf_op jit(solution)/shard_map/ppermute | solution.py:269
  71.2 1.4 %collective-permute-start.6 = (bf16[4,128,128]{2,1,0:T(8,128)(2,1)S(1)}, bf16[4,128,128]{2,1,0:T(8,128)(2,1)S(1)}, u32[]{:S(2)}, u32[]{:S(2)}) collective-permute-start(bf16[4,128,128]{2,1,0:T(8,128)(2,1)S(1)} %adjoint2_give_a.1), channel_id=1, source_target_pairs={{0,8},{8,0},{16,24},{24,16},{1,9},{9,1},{17,25},{25,17},{2,10},{10... | collective-permute-start | bytes 393224 | tf_op jit(solution)/shard_map/ppermute | solution.py:269
  71.8 2.8 %collective-permute-start.8 = (bf16[4,128,128]{2,1,0:T(8,128)(2,1)S(1)}, bf16[4,128,128]{2,1,0:T(8,128)(2,1)S(1)}, u32[]{:S(2)}, u32[]{:S(2)}) collective-permute-start(bf16[4,128,128]{2,1,0:T(8,128)(2,1)S(1)} %get-tuple-element.42), channel_id=1, source_target_pairs={{0,8},{8,0},{16,24},{24,16},{1,9},{9,1},{17,25},{25,17},{2,10},{10... | collective-permute-start | bytes 393224 | tf_op jit(solution)/shard_map/ppermute | solution.py:269
  72.7 6.4 %collective-permute-start.7 = (bf16[4,128,128]{2,1,0:T(8,128)(2,1)S(1)}, bf16[4,128,128]{2,1,0:T(8,128)(2,1)S(1)}, u32[]{:S(2)}, u32[]{:S(2)}) collective-permute-start(bf16[4,128,128]{2,1,0:T(8,128)(2,1)S(1)} %adjoint2_pair_a.1.rest_0_), channel_id=1, source_target_pairs={{0,16},{8,24},{16,0},{24,8},{1,17},{9,25},{17,1},{25,9},{2,18},{10... | collective-permute-start | bytes 393224 | tf_op jit(solution)/shard_map/ppermute | solution.py:273
  74.6 6.5 %collective-permute-start.9 = (bf16[4,128,128]{2,1,0:T(8,128)(2,1)S(1)}, bf16[4,128,128]{2,1,0:T(8,128)(2,1)S(1)}, u32[]{:S(2)}, u32[]{:S(2)}) collective-permute-start(bf16[4,128,128]{2,1,0:T(8,128)(2,1)S(1)} %adjoint2_pair_b.1.rest_0_), channel_id=1, source_target_pairs={{0,16},{8,24},{16,0},{24,8},{1,17},{9,25},{17,1},{25,9},{2,18},{10... | collective-permute-start | bytes 393224 | tf_op jit(solution)/shard_map/ppermute | solution.py:273
  79.2 2.1 %collective-permute-start.10 = (bf16[4,128,128]{2,1,0:T(8,128)(2,1)S(1)}, bf16[4,128,128]{2,1,0:T(8,128)(2,1)S(1)}, u32[]{:S(2)}, u32[]{:S(2)}) collective-permute-start(bf16[4,128,128]{2,1,0:T(8,128)(2,1)S(1)} %total_a.1.own_a), channel_id=1, source_target_pairs={{0,8},{8,0},{16,24},{24,16},{1,9},{9,1},{17,25},{25,17},{2,10},{10... | collective-permute-start | bytes 393224 | tf_op jit(solution)/shard_map/ppermute | solution.py:269
  81.3 1.4 %collective-permute-start.11 = (bf16[4,128,128]{2,1,0:T(8,128)(2,1)S(1)}, bf16[4,128,128]{2,1,0:T(8,128)(2,1)S(1)}, u32[]{:S(2)}, u32[]{:S(2)}) collective-permute-start(bf16[4,128,128]{2,1,0:T(8,128)(2,1)S(1)} %total_b.1.own_b), channel_id=1, source_target_pairs={{0,8},{8,0},{16,24},{24,16},{1,9},{9,1},{17,25},{25,17},{2,10},{10... | collective-permute-start | bytes 393224 | tf_op jit(solution)/shard_map/ppermute | solution.py:269

commit v6 on v5

--- a/solution.py
+++ b/solution.py
@@ -104,7 +104,7 @@
 
 
 def dense_kernel(bund, cblk, sens, after_ref, *rest):
-    out_refs, (token_ref, total) = rest[:4], rest[4:]
+    out_refs, (token_ref, total, last, sem) = rest[:4], rest[4:]
     rays = sens.shape[1]
     quarter = 2 * total.shape[1]
     core = lax.axis_index("shot") % 2
@@ -120,8 +120,12 @@
         return carry
 
     lax.fori_loop(0, sens.shape[0], place, 0)
-    for part, out_ref in enumerate(out_refs):
-        out_ref[...] = total[part].astype(bf16)
+    last[...] = total[KEEP_B].astype(bf16)
+    copy = pltpu.make_async_copy(last, out_refs[KEEP_B], sem)
+    copy.start()
+    for part in (GIVE_A, KEEP_A, GIVE_B):
+        out_refs[part][...] = total[part].astype(bf16)
+    copy.wait()
     token_ref[...] = jnp.zeros_like(token_ref)
 
 
@@ -349,12 +353,17 @@
     *dense, token = call(
         dense_kernel,
         (arr(dense_shape, bf16),) * 4 + (small_token,),
-        [pltpu.VMEM((4,) + dense_shape, f32)],
+        [
+            pltpu.VMEM((4,) + dense_shape, f32),
+            pltpu.VMEM(dense_shape, bf16),
+            pltpu.SemaphoreType.DMA,
+        ],
         [SMEM, SMEM, VMEM, ANY],
         "dense",
         0,
         16 << 20,
         vmem=3 * dense_bytes + 2 * sens_bytes + (2 << 20),
+        out_specs=(VMEM, VMEM, VMEM, HBM, VMEM),
     )(bund, cblk, sens, part1)
     _, resid_all1 = residual(part1, token, "residual1", False)
     *sums1, after = adjoint(dense, resid_all1, "adjoint1")

time: 83.9 us -> 84 us (level)
  no operation moved by 1% of the time
where the time goes in v6:
time: 84 us; the launch traced here: 83.5 us
  blocking collectives  37 us (44%)
  Pallas kernels  14.2 us (17%)
  waiting for transfers between devices  13.6 us (16%)
  starting transfers between devices  13.1 us (16%)
  local copies, waits for them, and re-layouts  4.77 us (6%)
  between operations  0.96 us (1%)
    all_to_all x3, blocking collectives, over_band(): lax.all_to_all(array, 'band', split_axis=0, concat_axis=0, tiled=True)  37 us
    ppermute x4, waiting for transfers between devices, other_chips(): lax.ppermute(array, 'shot', [(i, i ^ 2 * d) for i in range(nshot)])  10.5 us
    all_to_all x1, starting transfers between devices, over_band(): lax.all_to_all(array, 'band', split_axis=0, concat_axis=0, tiled=True)  7.26 us
    unnamed x22, local copies, waits for them, and re-layouts  4.77 us
    ppermute x4, starting transfers between devices, other_chips(): lax.ppermute(array, 'shot', [(i, i ^ 2 * d) for i in range(nshot)])  4.31 us
    pallas_call x1, Pallas kernels, per_device(): call(first_forward_kernel, part_out, [pltpu.VMEM((bundles, rays, samples)...  3.62 us
    pallas_call x1, Pallas kernels, per_device(): call(dense_kernel, (arr(dense_shape, bf16),) * 4 + (small_token,), [pltpu...  3.6 us
    pallas_call x6, Pallas kernels, kernel(): call(adjoint_kernel, tuple((quarter_f32 if p % 2 else quarter_bf16 for p...  2.11 us
  transfers between devices with their start and end apart: 13, of which 9 were waited for; matrix products, arithmetic and copies ran while one was open for 0% of the time, Pallas kernels for 10%

profile of v6, /device:TPU:0, one launch (start us, length us, event | category | flops | bytes accessed | tf_op | source)
XLA Modules:
  0.0 83.5 jit_solution(8523523425163598190)
XLA Ops:
  0.6 3.6 %forward1.1.after_ref = bf16[8,128,128]{2,1,0:T(8,128)(2,1)} custom-call(s32[64]{0:T(128)} %bund.1, s32[64]{0:T(128)} %cblk.1, bf16[64,128,128]{2,1,0:T(8,128)(2,1)} %sens.1, f32[16,128,128]{2,1,0:T(8,128)} %bitcast.7, f32[16,128,128]{2,1,0:T(8,128)} %bitcast.9), custom_call_target="tpu_custom_call" | custom-call | flops 268435456 | bytes 2097152 | tf_op jit(solution)/shard_map/forward1/pallas_call | solution.py:334
  4.3 7.3 %all-to-all-start = ((bf16[8,128,128]{2,1,0:T(8,128)(2,1)}), bf16[8,128,128]{2,1,0:T(8,128)(2,1)S(1)}, u32[]{:S(2)}, u32[]{:S(2)}) async-start(bf16[8,128,128]{2,1,0:T(8,128)(2,1)} %forward1.1.after_ref), calls=%async_computation | async-start | bytes 524288 | tf_op jit(solution)/shard_map/all_to_all | solution.py:282
  11.6 1.6 %copy-done.3 = bf16[64,128,128]{2,1,0:T(8,128)(2,1)S(1)} copy-done((bf16[64,128,128]{2,1,0:T(8,128)(2,1)S(1)}, bf16[64,128,128]{2,1,0:T(8,128)(2,1)}, u32[]{:S(2)}) %copy-start.3) | copy-done | bytes 2097176
  13.2 0.9 %copy-done.6 = bf16[8,128,128]{2,1,0:T(8,128)(2,1)S(1)} copy-done((bf16[8,128,128]{2,1,0:T(8,128)(2,1)S(1)}, bf16[8,128,128]{2,1,0:T(8,128)(2,1)}, u32[]{:S(2)}) %copy-start.6) | copy-done | bytes 262168
  14.1 3.6 %dense.1 = (bf16[2,1024,256]{2,1,0:T(8,128)(2,1)S(1)}, bf16[2,1024,256]{2,1,0:T(8,128)(2,1)S(1)}, bf16[2,1024,256]{2,1,0:T(8,128)(2,1)S(1)}, bf16[2,1024,256]{2,1,0:T(8,128)(2,1)S(1)}, f32[8,128]{1,0:T(8,128)S(1)}) custom-call(s32[64]{0:T(128)S(1)} %copy-done.9, s32[64]{0:T(128)S(1)} %copy-done.10, bf16[64,128,128]{2,1,0:T(8,128)(2,1)S(1)} %copy-done.3, ...), custom_call_target="tpu_custom_call" | custom-call | bytes 16777216 | tf_op jit(solution)/shard_map/dense/pallas_call | solution.py:353
  17.7 1.0 %copy-done = bf16[2,1024,256]{2,1,0:T(8,128)(2,1)} copy-done((bf16[2,1024,256]{2,1,0:T(8,128)(2,1)}, bf16[2,1024,256]{2,1,0:T(8,128)(2,1)S(1)}, u32[]{:S(2)}) %copy-start) | copy-done | bytes 1048600
  18.7 1.8 %all-to-all-done = bf16[8,128,128]{2,1,0:T(8,128)(2,1)S(1)} async-done(((bf16[8,128,128]{2,1,0:T(8,128)(2,1)}), bf16[8,128,128]{2,1,0:T(8,128)(2,1)S(1)}, u32[]{:S(2)}, u32[]{:S(2)}) %all-to-all-start) | async-done | bytes 262176 | tf_op jit(solution)/shard_map/all_to_all | solution.py:282
  20.6 12.5 %all_to_all.20 = bf16[8,1,128,128]{3,2,1,0:T(8,128)(2,1)S(1)} all-to-all(bf16[8,1,128,128]{3,2,1,0:T(8,128)(2,1)S(1)} %residual1.1), channel_id=1, replica_groups=mesh['shot'=4,'band'=8] {'band'}, dimensions={0} | all-to-all | bytes 524288 | tf_op jit(solution)/shard_map/all_to_all | solution.py:282
  33.1 1.2 %copy-done.1 = bf16[2,1024,256]{2,1,0:T(8,128)(2,1)S(1)} copy-done((bf16[2,1024,256]{2,1,0:T(8,128)(2,1)S(1)}, bf16[2,1024,256]{2,1,0:T(8,128)(2,1)}, u32[]{:S(2)}) %copy-start.1) | copy-done | bytes 1048600
  34.8 0.4 adjoint1_keep_a.1
  35.2 0.5 collective-permute-start.2
  35.8 0.3 collective-permute-done.got_ref
  36.1 1.6 %collective-permute-start.1 = (bf16[4,128,128]{2,1,0:T(8,128)(2,1)S(1)}, bf16[4,128,128]{2,1,0:T(8,128)(2,1)S(1)}, u32[]{:S(2)}, u32[]{:S(2)}) collective-permute-start(bf16[4,128,128]{2,1,0:T(8,128)(2,1)S(1)} %adjoint1_pair_a.1.rest_0_), channel_id=1, source_target_pairs={{0,16},{8,24},{16,0},{24,8},{1,17},{9,25},{17,1},{25,9},{2,18},{10... | collective-permute-start | bytes 393224 | tf_op jit(solution)/shard_map/ppermute | solution.py:277
  38.1 0.6 collective-permute-start.3
  38.8 3.7 %collective-permute-done.1.rest_1_ = bf16[4,128,128]{2,1,0:T(8,128)(2,1)S(1)} collective-permute-done((bf16[4,128,128]{2,1,0:T(8,128)(2,1)S(1)}, bf16[4,128,128]{2,1,0:T(8,128)(2,1)S(1)}, u32[]{:S(2)}, u32[]{:S(2)}) %collective-permute-start.1) | collective-permute-done | bytes 131104 | tf_op jit(solution)/shard_map/ppermute | solution.py:277
  42.7 1.8 %collective-permute-done.3.rest_1_ = bf16[4,128,128]{2,1,0:T(8,128)(2,1)S(1)} collective-permute-done((bf16[4,128,128]{2,1,0:T(8,128)(2,1)S(1)}, bf16[4,128,128]{2,1,0:T(8,128)(2,1)S(1)}, u32[]{:S(2)}, u32[]{:S(2)}) %collective-permute-start.3) | collective-permute-done | bytes 131104 | tf_op jit(solution)/shard_map/ppermute | solution.py:277
  44.8 1.0 %forward2_early.1.early = f32[8,128,128]{2,1,0:T(8,128)S(1)} custom-call(bf16[2,1024,256]{2,1,0:T(8,128)(2,1)S(1)} %get-tuple-element.28.refs_0_.dense_own_a, bf16[2,1024,256]{2,1,0:T(8,128)(2,1)S(1)} %get-tuple-element.25.refs_0_.dense_own_b, bf16[2,1024,256]{2,1,0:T(8,128)(2,1)S(1)} %copy-done.2, bf16[4,128,128]{2,1,0:T(8,128)(2,1)S(1)} %get-tuple-element.36.own_a, ...), custom_call_target="tpu_custom_call" | custom-call | flops 402653184 | bytes 3145728 | tf_op jit(solution)/shard_map/forward2_early/pallas_call | solution.py:393
  45.8 0.3 collective-permute-done.4.mate_b
  46.1 0.4 forward2_late.1
  46.5 12.5 %all_to_all.21 = bf16[8,128,128]{2,1,0:T(8,128)(2,1)S(1)} all-to-all(bf16[8,128,128]{2,1,0:T(8,128)(2,1)S(1)} %forward2_late.1), channel_id=1, replica_groups=mesh['shot'=4,'band'=8] {'band'}, dimensions={0} | all-to-all | bytes 524288 | tf_op jit(solution)/shard_map/all_to_all | solution.py:282
  59.1 12.0 %all_to_all.22 = bf16[8,1,128,128]{3,2,1,0:T(8,128)(2,1)S(1)} all-to-all(bf16[8,1,128,128]{3,2,1,0:T(8,128)(2,1)S(1)} %get-tuple-element.39), channel_id=1, replica_groups=mesh['shot'=4,'band'=8] {'band'}, dimensions={0} | all-to-all | bytes 524288 | tf_op jit(solution)/shard_map/all_to_all | solution.py:282
  71.5 0.4 adjoint2_keep_a.1
  71.9 0.6 collective-permute-start.8
  72.5 0.3 collective-permute-done.6.got_ref
  72.8 1.6 %collective-permute-start.7 = (bf16[4,128,128]{2,1,0:T(8,128)(2,1)S(1)}, bf16[4,128,128]{2,1,0:T(8,128)(2,1)S(1)}, u32[]{:S(2)}, u32[]{:S(2)}) collective-permute-start(bf16[4,128,128]{2,1,0:T(8,128)(2,1)S(1)} %adjoint2_pair_a.1.rest_0_), channel_id=1, source_target_pairs={{0,16},{8,24},{16,0},{24,8},{1,17},{9,25},{17,1},{25,9},{2,18},{10... | collective-permute-start | bytes 393224 | tf_op jit(solution)/shard_map/ppermute | solution.py:277
  74.8 0.6 collective-permute-start.9
  75.3 0.7 turn.1
  76.1 3.2 %collective-permute-done.7.rest_1_ = bf16[4,128,128]{2,1,0:T(8,128)(2,1)S(1)} collective-permute-done((bf16[4,128,128]{2,1,0:T(8,128)(2,1)S(1)}, bf16[4,128,128]{2,1,0:T(8,128)(2,1)S(1)}, u32[]{:S(2)}, u32[]{:S(2)}) %collective-permute-start.7) | collective-permute-done | bytes 131104 | tf_op jit(solution)/shard_map/ppermute | solution.py:277
  79.4 1.8 %collective-permute-done.9.rest_1_ = bf16[4,128,128]{2,1,0:T(8,128)(2,1)S(1)} collective-permute-done((bf16[4,128,128]{2,1,0:T(8,128)(2,1)S(1)}, bf16[4,128,128]{2,1,0:T(8,128)(2,1)S(1)}, u32[]{:S(2)}, u32[]{:S(2)}) %collective-permute-start.9) | collective-permute-done | bytes 131104 | tf_op jit(solution)/shard_map/ppermute | solution.py:277
  81.5 0.9 %new_state_early.1 = (f32[16,128,128]{2,1,0:T(8,128)}, f32[4,128,128]{2,1,0:T(8,128)S(1)}) custom-call(f32[16,128,128]{2,1,0:T(8,128)S(1)} %get-tuple-element.26.base, bf16[4,128,128]{2,1,0:T(8,128)(2,1)S(1)} %total_a.1.own_a, bf16[4,128,128]{2,1,0:T(8,128)(2,1)S(1)} %total_b.1.own_b, bf16[4,128,128]{2,1,0:T(8,128)(2,1)S(1)} %collective-permute-done.10.mate_a), custom_call_target="tpu_custom_call" | custom-call | bytes 3145728 | tf_op jit(solution)/shard_map/new_state_early/pallas_call | solution.py:435
  82.4 0.4 collective-permute-done.11.mate_b
  82.8 0.7 new_state_late.1
  (43 shorter events, 2.7 us)
Async XLA Ops:
  0.6 10.9 %copy-start.9 = (s32[64]{0:T(128)S(1)}, s32[64]{0:T(128)}, u32[]{:S(2)}) copy-start(s32[64]{0:T(128)} %bund.1) | copy-start | bytes 772
  0.6 10.9 %copy-start.10 = (s32[64]{0:T(128)S(1)}, s32[64]{0:T(128)}, u32[]{:S(2)}) copy-start(s32[64]{0:T(128)} %cblk.1) | copy-start | bytes 772
  4.3 16.2 %copy-start.7 = (f32[1,128]{1,0:T(1,128)S(1)}, f32[1,128]{1,0:T(1,128)}, u32[]{:S(2)}) copy-start(f32[1,128]{1,0:T(1,128)} %obs_ref.3) | copy-start | bytes 1540
  4.3 16.2 %copy-start.8 = (f32[1,128]{1,0:T(1,128)S(1)}, f32[1,128]{1,0:T(1,128)}, u32[]{:S(2)}) copy-start(f32[1,128]{1,0:T(1,128)} %wt_ref.3) | copy-start | bytes 1540
  4.3 16.2 %all-to-all-start = ((bf16[8,128,128]{2,1,0:T(8,128)(2,1)}), bf16[8,128,128]{2,1,0:T(8,128)(2,1)S(1)}, u32[]{:S(2)}, u32[]{:S(2)}) async-start(bf16[8,128,128]{2,1,0:T(8,128)(2,1)} %forward1.1.after_ref), calls=%async_computation | async-start | bytes 524288 | tf_op jit(solution)/shard_map/all_to_all | solution.py:282
  11.6 1.6 %copy-start.3 = (bf16[64,128,128]{2,1,0:T(8,128)(2,1)S(1)}, bf16[64,128,128]{2,1,0:T(8,128)(2,1)}, u32[]{:S(2)}) copy-start(bf16[64,128,128]{2,1,0:T(8,128)(2,1)} %sens.1) | copy-start | bytes 6291460
  13.2 0.9 %copy-start.6 = (bf16[8,128,128]{2,1,0:T(8,128)(2,1)S(1)}, bf16[8,128,128]{2,1,0:T(8,128)(2,1)}, u32[]{:S(2)}) copy-start(bf16[8,128,128]{2,1,0:T(8,128)(2,1)} %forward1.1.after_ref) | copy-start | bytes 786436
  17.7 1.0 %copy-start = (bf16[2,1024,256]{2,1,0:T(8,128)(2,1)}, bf16[2,1024,256]{2,1,0:T(8,128)(2,1)S(1)}, u32[]{:S(2)}) copy-start(bf16[2,1024,256]{2,1,0:T(8,128)(2,1)S(1)} %get-tuple-element.31.refs_0_.dense_mate_a) | copy-start | bytes 3145732
  33.1 1.2 %copy-start.1 = (bf16[2,1024,256]{2,1,0:T(8,128)(2,1)S(1)}, bf16[2,1024,256]{2,1,0:T(8,128)(2,1)}, u32[]{:S(2)}) copy-start(bf16[2,1024,256]{2,1,0:T(8,128)(2,1)} %copy-done) | copy-start | bytes 3145732
  34.7 1.4 %collective-permute-start = (bf16[4,128,128]{2,1,0:T(8,128)(2,1)S(1)}, bf16[4,128,128]{2,1,0:T(8,128)(2,1)S(1)}, u32[]{:S(2)}, u32[]{:S(2)}) collective-permute-start(bf16[4,128,128]{2,1,0:T(8,128)(2,1)S(1)} %adjoint1_give_a.1), channel_id=1, source_target_pairs={{0,8},{8,0},{16,24},{24,16},{1,9},{9,1},{17,25},{25,17},{2,10},{10... | collective-permute-start | bytes 393224 | tf_op jit(solution)/shard_map/ppermute | solution.py:273
  34.7 3.9 %copy-start.4 = (f32[2048,128]{1,0:T(8,128)S(1)}, f32[2048,128]{1,0:T(8,128)}, u32[]{:S(2)}) copy-start(f32[2048,128]{1,0:T(8,128)} %param.10) | copy-start | bytes 3145732
  34.8 3.9 %copy-start.5 = (f32[2048,128]{1,0:T(8,128)S(1)}, f32[2048,128]{1,0:T(8,128)}, u32[]{:S(2)}) copy-start(f32[2048,128]{1,0:T(8,128)} %param.11) | copy-start | bytes 3145732
  35.2 2.8 %collective-permute-start.2 = (bf16[4,128,128]{2,1,0:T(8,128)(2,1)S(1)}, bf16[4,128,128]{2,1,0:T(8,128)(2,1)S(1)}, u32[]{:S(2)}, u32[]{:S(2)}) collective-permute-start(bf16[4,128,128]{2,1,0:T(8,128)(2,1)S(1)} %get-tuple-element.34), channel_id=1, source_target_pairs={{0,8},{8,0},{16,24},{24,16},{1,9},{9,1},{17,25},{25,17},{2,10},{10... | collective-permute-start | bytes 393224 | tf_op jit(solution)/shard_map/ppermute | solution.py:273
  36.1 6.4 %collective-permute-start.1 = (bf16[4,128,128]{2,1,0:T(8,128)(2,1)S(1)}, bf16[4,128,128]{2,1,0:T(8,128)(2,1)S(1)}, u32[]{:S(2)}, u32[]{:S(2)}) collective-permute-start(bf16[4,128,128]{2,1,0:T(8,128)(2,1)S(1)} %adjoint1_pair_a.1.rest_0_), channel_id=1, source_target_pairs={{0,16},{8,24},{16,0},{24,8},{1,17},{9,25},{17,1},{25,9},{2,18},{10... | collective-permute-start | bytes 393224 | tf_op jit(solution)/shard_map/ppermute | solution.py:277
  38.0 6.8 %copy-start.2 = (bf16[2,1024,256]{2,1,0:T(8,128)(2,1)S(1)}, bf16[2,1024,256]{2,1,0:T(8,128)(2,1)}, u32[]{:S(2)}) copy-start(bf16[2,1024,256]{2,1,0:T(8,128)(2,1)} %copy-done) | copy-start | bytes 3145732
  38.1 6.5 %collective-permute-start.3 = (bf16[4,128,128]{2,1,0:T(8,128)(2,1)S(1)}, bf16[4,128,128]{2,1,0:T(8,128)(2,1)S(1)}, u32[]{:S(2)}, u32[]{:S(2)}) collective-permute-start(bf16[4,128,128]{2,1,0:T(8,128)(2,1)S(1)} %adjoint1_pair_b.1.rest_0_), channel_id=1, source_target_pairs={{0,16},{8,24},{16,0},{24,8},{1,17},{9,25},{17,1},{25,9},{2,18},{10... | collective-permute-start | bytes 393224 | tf_op jit(solution)/shard_map/ppermute | solution.py:277
  42.7 2.1 %collective-permute-start.5 = (bf16[4,128,128]{2,1,0:T(8,128)(2,1)S(1)}, bf16[4,128,128]{2,1,0:T(8,128)(2,1)S(1)}, u32[]{:S(2)}, u32[]{:S(2)}) collective-permute-start(bf16[4,128,128]{2,1,0:T(8,128)(2,1)S(1)} %get-tuple-element.36.own_a), channel_id=1, source_target_pairs={{0,8},{8,0},{16,24},{24,16},{1,9},{9,1},{17,25},{25,17},{2,10},{10... | collective-permute-start | bytes 393224 | tf_op jit(solution)/shard_map/ppermute | solution.py:273
  44.7 1.4 %collective-permute-start.4 = (bf16[4,128,128]{2,1,0:T(8,128)(2,1)S(1)}, bf16[4,128,128]{2,1,0:T(8,128)(2,1)S(1)}, u32[]{:S(2)}, u32[]{:S(2)}) collective-permute-start(bf16[4,128,128]{2,1,0:T(8,128)(2,1)S(1)} %get-tuple-element.35.own_b), channel_id=1, source_target_pairs={{0,8},{8,0},{16,24},{24,16},{1,9},{9,1},{17,25},{25,17},{2,10},{10... | collective-permute-start | bytes 393224 | tf_op jit(solution)/shard_map/ppermute | solution.py:273
  71.4 1.4 %collective-permute-start.6 = (bf16[4,128,128]{2,1,0:T(8,128)(2,1)S(1)}, bf16[4,128,128]{2,1,0:T(8,128)(2,1)S(1)}, u32[]{:S(2)}, u32[]{:S(2)}) collective-permute-start(bf16[4,128,128]{2,1,0:T(8,128)(2,1)S(1)} %adjoint2_give_a.1), channel_id=1, source_target_pairs={{0,8},{8,0},{16,24},{24,16},{1,9},{9,1},{17,25},{25,17},{2,10},{10... | collective-permute-start | bytes 393224 | tf_op jit(solution)/shard_map/ppermute | solution.py:273
  71.9 2.8 %collective-permute-start.8 = (bf16[4,128,128]{2,1,0:T(8,128)(2,1)S(1)}, bf16[4,128,128]{2,1,0:T(8,128)(2,1)S(1)}, u32[]{:S(2)}, u32[]{:S(2)}) collective-permute-start(bf16[4,128,128]{2,1,0:T(8,128)(2,1)S(1)} %get-tuple-element.42), channel_id=1, source_target_pairs={{0,8},{8,0},{16,24},{24,16},{1,9},{9,1},{17,25},{25,17},{2,10},{10... | collective-permute-start | bytes 393224 | tf_op jit(solution)/shard_map/ppermute | solution.py:273
  72.8 6.4 %collective-permute-start.7 = (bf16[4,128,128]{2,1,0:T(8,128)(2,1)S(1)}, bf16[4,128,128]{2,1,0:T(8,128)(2,1)S(1)}, u32[]{:S(2)}, u32[]{:S(2)}) collective-permute-start(bf16[4,128,128]{2,1,0:T(8,128)(2,1)S(1)} %adjoint2_pair_a.1.rest_0_), channel_id=1, source_target_pairs={{0,16},{8,24},{16,0},{24,8},{1,17},{9,25},{17,1},{25,9},{2,18},{10... | collective-permute-start | bytes 393224 | tf_op jit(solution)/shard_map/ppermute | solution.py:277
  74.8 6.5 %collective-permute-start.9 = (bf16[4,128,128]{2,1,0:T(8,128)(2,1)S(1)}, bf16[4,128,128]{2,1,0:T(8,128)(2,1)S(1)}, u32[]{:S(2)}, u32[]{:S(2)}) collective-permute-start(bf16[4,128,128]{2,1,0:T(8,128)(2,1)S(1)} %adjoint2_pair_b.1.rest_0_), channel_id=1, source_target_pairs={{0,16},{8,24},{16,0},{24,8},{1,17},{9,25},{17,1},{25,9},{2,18},{10... | collective-permute-start | bytes 393224 | tf_op jit(solution)/shard_map/ppermute | solution.py:277
  79.4 2.1 %collective-permute-start.10 = (bf16[4,128,128]{2,1,0:T(8,128)(2,1)S(1)}, bf16[4,128,128]{2,1,0:T(8,128)(2,1)S(1)}, u32[]{:S(2)}, u32[]{:S(2)}) collective-permute-start(bf16[4,128,128]{2,1,0:T(8,128)(2,1)S(1)} %total_a.1.own_a), channel_id=1, source_target_pairs={{0,8},{8,0},{16,24},{24,16},{1,9},{9,1},{17,25},{25,17},{2,10},{10... | collective-permute-start | bytes 393224 | tf_op jit(solution)/shard_map/ppermute | solution.py:273
  81.4 1.4 %collective-permute-start.11 = (bf16[4,128,128]{2,1,0:T(8,128)(2,1)S(1)}, bf16[4,128,128]{2,1,0:T(8,128)(2,1)S(1)}, u32[]{:S(2)}, u32[]{:S(2)}) collective-permute-start(bf16[4,128,128]{2,1,0:T(8,128)(2,1)S(1)} %total_b.1.own_b), channel_id=1, source_target_pairs={{0,8},{8,0},{16,24},{24,16},{1,9},{9,1},{17,25},{25,17},{2,10},{10... | collective-permute-start | bytes 393224 | tf_op jit(solution)/shard_map/ppermute | solution.py:273

commit v7 on v5

--- a/solution.py
+++ b/solution.py
@@ -8,8 +8,8 @@
 from jax.sharding import PartitionSpec as P
 
 CBLK = 128
-GROUP = 32
-CHUNKS = 2
+GROUP = 64
+CHUNKS = 1
 FIRST_VMEM = 55 << 20
 GIVE_A, KEEP_A, GIVE_B, KEEP_B = range(4)
 
@@ -103,7 +103,7 @@
     out_ref[...] = acc[...].astype(bf16)
 
 
-def dense_kernel(bund, cblk, sens, after_ref, *rest):
+def dense_kernel(bund, cblk, sens, *rest):
     out_refs, (token_ref, total) = rest[:4], rest[4:]
     rays = sens.shape[1]
     quarter = 2 * total.shape[1]
@@ -120,7 +120,7 @@
         return carry
 
     lax.fori_loop(0, sens.shape[0], place, 0)
-    for part, out_ref in enumerate(out_refs):
+    for part, out_ref in zip((KEEP_B, GIVE_A, KEEP_A, GIVE_B), out_refs):
         out_ref[...] = total[part].astype(bf16)
     token_ref[...] = jnp.zeros_like(token_ref)
 
@@ -346,16 +346,17 @@
         sens_bytes,
         vmem=FIRST_VMEM,
     )(bund, cblk, sens, state_b, prior_b)
-    *dense, token = call(
+    dense_keep_b, *dense, token = call(
         dense_kernel,
         (arr(dense_shape, bf16),) * 4 + (small_token,),
         [pltpu.VMEM((4,) + dense_shape, f32)],
-        [SMEM, SMEM, VMEM, ANY],
+        [SMEM, SMEM, VMEM],
         "dense",
         0,
         16 << 20,
         vmem=3 * dense_bytes + 2 * sens_bytes + (2 << 20),
-    )(bund, cblk, sens, part1)
+    )(bund, cblk, sens)
+    dense.append(dense_keep_b)
     _, resid_all1 = residual(part1, token, "residual1", False)
     *sums1, after = adjoint(dense, resid_all1, "adjoint1")
 

time: 83.9 us -> 83.8 us (level)
  waiting for transfers between devices: 13.7 us -> 14.7 us
  local copies, waits for them, and re-layouts: 4.77 us -> 3.82 us
    all_to_all x1, waiting for transfers between devices: 1.9 us -> 2.85 us  [over_band(): lax.all_to_all(array, 'band', split_axis=0, concat_axis=0, tiled=True)]
    unnamed x22 -> x20, local copies, waits for them, and re-layouts: 4.77 us -> 3.82 us
where the time goes in v7:
time: 83.8 us; the launch traced here: 83.4 us
  blocking collectives  36.5 us (44%)
  waiting for transfers between devices  14.7 us (18%)
  Pallas kernels  14.3 us (17%)
  starting transfers between devices  13.1 us (16%)
  local copies, waits for them, and re-layouts  3.82 us (5%)
  between operations  0.96 us (1%)
    all_to_all x3, blocking collectives, over_band(): lax.all_to_all(array, 'band', split_axis=0, concat_axis=0, tiled=True)  36.5 us
    ppermute x4, waiting for transfers between devices, other_chips(): lax.ppermute(array, 'shot', [(i, i ^ 2 * d) for i in range(nshot)])  10.5 us
    all_to_all x1, starting transfers between devices, over_band(): lax.all_to_all(array, 'band', split_axis=0, concat_axis=0, tiled=True)  7.26 us
    ppermute x4, starting transfers between devices, other_chips(): lax.ppermute(array, 'shot', [(i, i ^ 2 * d) for i in range(nshot)])  4.31 us
    pallas_call x1, Pallas kernels, per_device(): call(first_forward_kernel, part_out, [pltpu.VMEM((bundles, rays, samples)...  3.87 us
    unnamed x20, local copies, waits for them, and re-layouts  3.82 us
    pallas_call x1, Pallas kernels, per_device(): call(dense_kernel, (arr(dense_shape, bf16),) * 4 + (small_token,), [pltpu...  3.48 us
    all_to_all x1, waiting for transfers between devices, over_band(): lax.all_to_all(array, 'band', split_axis=0, concat_axis=0, tiled=True)  2.85 us
  transfers between devices with their start and end apart: 13, of which 9 were waited for; matrix products, arithmetic and copies ran while one was open for 0% of the time, Pallas kernels for 10%

profile of v7, /device:TPU:0, one launch (start us, length us, event | category | flops | bytes accessed | tf_op | source)
XLA Modules:
  0.0 83.4 jit_solution(17385263281476210501)
XLA Ops:
  0.6 3.9 %forward1.1 = bf16[8,128,128]{2,1,0:T(8,128)(2,1)} custom-call(s32[64]{0:T(128)} %bund.1, s32[64]{0:T(128)} %cblk.1, bf16[64,128,128]{2,1,0:T(8,128)(2,1)} %sens.1, f32[16,128,128]{2,1,0:T(8,128)} %bitcast.7, f32[16,128,128]{2,1,0:T(8,128)} %bitcast.9), custom_call_target="tpu_custom_call" | custom-call | flops 268435456 | bytes 2097152 | tf_op jit(solution)/shard_map/forward1/pallas_call | solution.py:330
  4.6 7.3 %all-to-all-start = ((bf16[8,128,128]{2,1,0:T(8,128)(2,1)}), bf16[8,128,128]{2,1,0:T(8,128)(2,1)S(1)}, u32[]{:S(2)}, u32[]{:S(2)}) async-start(bf16[8,128,128]{2,1,0:T(8,128)(2,1)} %forward1.1), calls=%async_computation | async-start | bytes 524288 | tf_op jit(solution)/shard_map/all_to_all | solution.py:278
  11.8 1.6 %copy-done.3 = bf16[64,128,128]{2,1,0:T(8,128)(2,1)S(1)} copy-done((bf16[64,128,128]{2,1,0:T(8,128)(2,1)S(1)}, bf16[64,128,128]{2,1,0:T(8,128)(2,1)}, u32[]{:S(2)}) %copy-start.3) | copy-done | bytes 2097176
  13.4 3.5 %dense.1 = (bf16[2,1024,256]{2,1,0:T(8,128)(2,1)S(1)}, bf16[2,1024,256]{2,1,0:T(8,128)(2,1)S(1)}, bf16[2,1024,256]{2,1,0:T(8,128)(2,1)S(1)}, bf16[2,1024,256]{2,1,0:T(8,128)(2,1)S(1)}, f32[8,128]{1,0:T(8,128)S(1)}) custom-call(s32[64]{0:T(128)S(1)} %copy-done.8, s32[64]{0:T(128)S(1)} %copy-done.9, bf16[64,128,128]{2,1,0:T(8,128)(2,1)S(1)} %copy-done.3), custom_call_target="tpu_custom_call" | custom-call | bytes 16777216 | tf_op jit(solution)/shard_map/dense/pallas_call | solution.py:349
  16.9 1.0 %copy-done = bf16[2,1024,256]{2,1,0:T(8,128)(2,1)} copy-done((bf16[2,1024,256]{2,1,0:T(8,128)(2,1)}, bf16[2,1024,256]{2,1,0:T(8,128)(2,1)S(1)}, u32[]{:S(2)}) %copy-start) | copy-done | bytes 1048600
  17.9 2.9 %all-to-all-done = bf16[8,128,128]{2,1,0:T(8,128)(2,1)S(1)} async-done(((bf16[8,128,128]{2,1,0:T(8,128)(2,1)}), bf16[8,128,128]{2,1,0:T(8,128)(2,1)S(1)}, u32[]{:S(2)}, u32[]{:S(2)}) %all-to-all-start) | async-done | bytes 262176 | tf_op jit(solution)/shard_map/all_to_all | solution.py:278
  20.9 12.0 %all_to_all.20 = bf16[8,1,128,128]{3,2,1,0:T(8,128)(2,1)S(1)} all-to-all(bf16[8,1,128,128]{3,2,1,0:T(8,128)(2,1)S(1)} %residual1.1), channel_id=1, replica_groups=mesh['shot'=4,'band'=8] {'band'}, dimensions={0} | all-to-all | bytes 524288 | tf_op jit(solution)/shard_map/all_to_all | solution.py:278
  32.8 1.2 %copy-done.1 = bf16[2,1024,256]{2,1,0:T(8,128)(2,1)S(1)} copy-done((bf16[2,1024,256]{2,1,0:T(8,128)(2,1)S(1)}, bf16[2,1024,256]{2,1,0:T(8,128)(2,1)}, u32[]{:S(2)}) %copy-start.1) | copy-done | bytes 1048600
  34.5 0.4 adjoint1_keep_a.1
  34.9 0.5 collective-permute-start.2
  35.4 0.3 collective-permute-done.got_ref
  35.8 1.6 %collective-permute-start.1 = (bf16[4,128,128]{2,1,0:T(8,128)(2,1)S(1)}, bf16[4,128,128]{2,1,0:T(8,128)(2,1)S(1)}, u32[]{:S(2)}, u32[]{:S(2)}) collective-permute-start(bf16[4,128,128]{2,1,0:T(8,128)(2,1)S(1)} %adjoint1_pair_a.1.rest_0_), channel_id=1, source_target_pairs={{0,16},{8,24},{16,0},{24,8},{1,17},{9,25},{17,1},{25,9},{2,18},{10... | collective-permute-start | bytes 393224 | tf_op jit(solution)/shard_map/ppermute | solution.py:273
  37.7 0.6 collective-permute-start.3
  38.5 3.7 %collective-permute-done.1.rest_1_ = bf16[4,128,128]{2,1,0:T(8,128)(2,1)S(1)} collective-permute-done((bf16[4,128,128]{2,1,0:T(8,128)(2,1)S(1)}, bf16[4,128,128]{2,1,0:T(8,128)(2,1)S(1)}, u32[]{:S(2)}, u32[]{:S(2)}) %collective-permute-start.1) | collective-permute-done | bytes 131104 | tf_op jit(solution)/shard_map/ppermute | solution.py:273
  42.4 1.8 %collective-permute-done.3.rest_1_ = bf16[4,128,128]{2,1,0:T(8,128)(2,1)S(1)} collective-permute-done((bf16[4,128,128]{2,1,0:T(8,128)(2,1)S(1)}, bf16[4,128,128]{2,1,0:T(8,128)(2,1)S(1)}, u32[]{:S(2)}, u32[]{:S(2)}) %collective-permute-start.3) | collective-permute-done | bytes 131104 | tf_op jit(solution)/shard_map/ppermute | solution.py:273
  44.5 1.0 %forward2_early.1.early = f32[8,128,128]{2,1,0:T(8,128)S(1)} custom-call(bf16[2,1024,256]{2,1,0:T(8,128)(2,1)S(1)} %get-tuple-element.28.refs_0_.dense_own_a, bf16[2,1024,256]{2,1,0:T(8,128)(2,1)S(1)} %get-tuple-element.25.refs_0_.dense_own_b, bf16[2,1024,256]{2,1,0:T(8,128)(2,1)S(1)} %copy-done.2, bf16[4,128,128]{2,1,0:T(8,128)(2,1)S(1)} %get-tuple-element.36.own_a, ...), custom_call_target="tpu_custom_call" | custom-call | flops 402653184 | bytes 3145728 | tf_op jit(solution)/shard_map/forward2_early/pallas_call | solution.py:385
  45.4 0.3 collective-permute-done.4.mate_b
  45.8 0.4 forward2_late.1
  46.2 12.6 %all_to_all.21 = bf16[8,128,128]{2,1,0:T(8,128)(2,1)S(1)} all-to-all(bf16[8,128,128]{2,1,0:T(8,128)(2,1)S(1)} %forward2_late.1), channel_id=1, replica_groups=mesh['shot'=4,'band'=8] {'band'}, dimensions={0} | all-to-all | bytes 524288 | tf_op jit(solution)/shard_map/all_to_all | solution.py:278
  58.9 12.0 %all_to_all.22 = bf16[8,1,128,128]{3,2,1,0:T(8,128)(2,1)S(1)} all-to-all(bf16[8,1,128,128]{3,2,1,0:T(8,128)(2,1)S(1)} %get-tuple-element.39), channel_id=1, replica_groups=mesh['shot'=4,'band'=8] {'band'}, dimensions={0} | all-to-all | bytes 524288 | tf_op jit(solution)/shard_map/all_to_all | solution.py:278
  70.9 0.3 adjoint2_give_a.1
  71.3 0.4 adjoint2_keep_a.1
  71.7 0.6 collective-permute-start.8
  72.3 0.3 collective-permute-done.6.got_ref
  72.7 1.6 %collective-permute-start.7 = (bf16[4,128,128]{2,1,0:T(8,128)(2,1)S(1)}, bf16[4,128,128]{2,1,0:T(8,128)(2,1)S(1)}, u32[]{:S(2)}, u32[]{:S(2)}) collective-permute-start(bf16[4,128,128]{2,1,0:T(8,128)(2,1)S(1)} %adjoint2_pair_a.1.rest_0_), channel_id=1, source_target_pairs={{0,16},{8,24},{16,0},{24,8},{1,17},{9,25},{17,1},{25,9},{2,18},{10... | collective-permute-start | bytes 393224 | tf_op jit(solution)/shard_map/ppermute | solution.py:273
  74.6 0.6 collective-permute-start.9
  75.2 0.7 turn.1
  75.9 3.2 %collective-permute-done.7.rest_1_ = bf16[4,128,128]{2,1,0:T(8,128)(2,1)S(1)} collective-permute-done((bf16[4,128,128]{2,1,0:T(8,128)(2,1)S(1)}, bf16[4,128,128]{2,1,0:T(8,128)(2,1)S(1)}, u32[]{:S(2)}, u32[]{:S(2)}) %collective-permute-start.7) | collective-permute-done | bytes 131104 | tf_op jit(solution)/shard_map/ppermute | solution.py:273
  79.3 1.8 %collective-permute-done.9.rest_1_ = bf16[4,128,128]{2,1,0:T(8,128)(2,1)S(1)} collective-permute-done((bf16[4,128,128]{2,1,0:T(8,128)(2,1)S(1)}, bf16[4,128,128]{2,1,0:T(8,128)(2,1)S(1)}, u32[]{:S(2)}, u32[]{:S(2)}) %collective-permute-start.9) | collective-permute-done | bytes 131104 | tf_op jit(solution)/shard_map/ppermute | solution.py:273
  81.3 0.9 %new_state_early.1 = (f32[16,128,128]{2,1,0:T(8,128)}, f32[4,128,128]{2,1,0:T(8,128)S(1)}) custom-call(f32[16,128,128]{2,1,0:T(8,128)S(1)} %get-tuple-element.26.base, bf16[4,128,128]{2,1,0:T(8,128)(2,1)S(1)} %total_a.1.own_a, bf16[4,128,128]{2,1,0:T(8,128)(2,1)S(1)} %total_b.1.own_b, bf16[4,128,128]{2,1,0:T(8,128)(2,1)S(1)} %collective-permute-done.10.mate_a), custom_call_target="tpu_custom_call" | custom-call | bytes 3145728 | tf_op jit(solution)/shard_map/new_state_early/pallas_call | solution.py:427
  82.3 0.4 collective-permute-done.11.mate_b
  82.6 0.7 new_state_late.1
  (41 shorter events, 2.4 us)
Async XLA Ops:
  0.6 11.2 %copy-start.8 = (s32[64]{0:T(128)S(1)}, s32[64]{0:T(128)}, u32[]{:S(2)}) copy-start(s32[64]{0:T(128)} %bund.1) | copy-start | bytes 772
  0.6 11.2 %copy-start.9 = (s32[64]{0:T(128)S(1)}, s32[64]{0:T(128)}, u32[]{:S(2)}) copy-start(s32[64]{0:T(128)} %cblk.1) | copy-start | bytes 772
  4.5 16.2 %copy-start.6 = (f32[1,128]{1,0:T(1,128)S(1)}, f32[1,128]{1,0:T(1,128)}, u32[]{:S(2)}) copy-start(f32[1,128]{1,0:T(1,128)} %obs_ref.3) | copy-start | bytes 1540
  4.5 16.2 %copy-start.7 = (f32[1,128]{1,0:T(1,128)S(1)}, f32[1,128]{1,0:T(1,128)}, u32[]{:S(2)}) copy-start(f32[1,128]{1,0:T(1,128)} %wt_ref.3) | copy-start | bytes 1540
  4.6 16.2 %all-to-all-start = ((bf16[8,128,128]{2,1,0:T(8,128)(2,1)}), bf16[8,128,128]{2,1,0:T(8,128)(2,1)S(1)}, u32[]{:S(2)}, u32[]{:S(2)}) async-start(bf16[8,128,128]{2,1,0:T(8,128)(2,1)} %forward1.1), calls=%async_computation | async-start | bytes 524288 | tf_op jit(solution)/shard_map/all_to_all | solution.py:278
  11.8 1.6 %copy-start.3 = (bf16[64,128,128]{2,1,0:T(8,128)(2,1)S(1)}, bf16[64,128,128]{2,1,0:T(8,128)(2,1)}, u32[]{:S(2)}) copy-start(bf16[64,128,128]{2,1,0:T(8,128)(2,1)} %sens.1) | copy-start | bytes 6291460
  16.9 1.0 %copy-start = (bf16[2,1024,256]{2,1,0:T(8,128)(2,1)}, bf16[2,1024,256]{2,1,0:T(8,128)(2,1)S(1)}, u32[]{:S(2)}) copy-start(bf16[2,1024,256]{2,1,0:T(8,128)(2,1)S(1)} %get-tuple-element.31.refs_0_.dense_mate_a) | copy-start | bytes 3145732
  32.8 1.2 %copy-start.1 = (bf16[2,1024,256]{2,1,0:T(8,128)(2,1)S(1)}, bf16[2,1024,256]{2,1,0:T(8,128)(2,1)}, u32[]{:S(2)}) copy-start(bf16[2,1024,256]{2,1,0:T(8,128)(2,1)} %copy-done) | copy-start | bytes 3145732
  34.3 1.4 %collective-permute-start = (bf16[4,128,128]{2,1,0:T(8,128)(2,1)S(1)}, bf16[4,128,128]{2,1,0:T(8,128)(2,1)S(1)}, u32[]{:S(2)}, u32[]{:S(2)}) collective-permute-start(bf16[4,128,128]{2,1,0:T(8,128)(2,1)S(1)} %adjoint1_give_a.1), channel_id=1, source_target_pairs={{0,8},{8,0},{16,24},{24,16},{1,9},{9,1},{17,25},{25,17},{2,10},{10... | collective-permute-start | bytes 393224 | tf_op jit(solution)/shard_map/ppermute | solution.py:269
  34.4 3.9 %copy-start.4 = (f32[2048,128]{1,0:T(8,128)S(1)}, f32[2048,128]{1,0:T(8,128)}, u32[]{:S(2)}) copy-start(f32[2048,128]{1,0:T(8,128)} %param.10) | copy-start | bytes 3145732
  34.4 3.9 %copy-start.5 = (f32[2048,128]{1,0:T(8,128)S(1)}, f32[2048,128]{1,0:T(8,128)}, u32[]{:S(2)}) copy-start(f32[2048,128]{1,0:T(8,128)} %param.11) | copy-start | bytes 3145732
  34.9 2.8 %collective-permute-start.2 = (bf16[4,128,128]{2,1,0:T(8,128)(2,1)S(1)}, bf16[4,128,128]{2,1,0:T(8,128)(2,1)S(1)}, u32[]{:S(2)}, u32[]{:S(2)}) collective-permute-start(bf16[4,128,128]{2,1,0:T(8,128)(2,1)S(1)} %get-tuple-element.34), channel_id=1, source_target_pairs={{0,8},{8,0},{16,24},{24,16},{1,9},{9,1},{17,25},{25,17},{2,10},{10... | collective-permute-start | bytes 393224 | tf_op jit(solution)/shard_map/ppermute | solution.py:269
  35.8 6.4 %collective-permute-start.1 = (bf16[4,128,128]{2,1,0:T(8,128)(2,1)S(1)}, bf16[4,128,128]{2,1,0:T(8,128)(2,1)S(1)}, u32[]{:S(2)}, u32[]{:S(2)}) collective-permute-start(bf16[4,128,128]{2,1,0:T(8,128)(2,1)S(1)} %adjoint1_pair_a.1.rest_0_), channel_id=1, source_target_pairs={{0,16},{8,24},{16,0},{24,8},{1,17},{9,25},{17,1},{25,9},{2,18},{10... | collective-permute-start | bytes 393224 | tf_op jit(solution)/shard_map/ppermute | solution.py:273
  37.7 6.8 %copy-start.2 = (bf16[2,1024,256]{2,1,0:T(8,128)(2,1)S(1)}, bf16[2,1024,256]{2,1,0:T(8,128)(2,1)}, u32[]{:S(2)}) copy-start(bf16[2,1024,256]{2,1,0:T(8,128)(2,1)} %copy-done) | copy-start | bytes 3145732
  37.7 6.5 %collective-permute-start.3 = (bf16[4,128,128]{2,1,0:T(8,128)(2,1)S(1)}, bf16[4,128,128]{2,1,0:T(8,128)(2,1)S(1)}, u32[]{:S(2)}, u32[]{:S(2)}) collective-permute-start(bf16[4,128,128]{2,1,0:T(8,128)(2,1)S(1)} %adjoint1_pair_b.1.rest_0_), channel_id=1, source_target_pairs={{0,16},{8,24},{16,0},{24,8},{1,17},{9,25},{17,1},{25,9},{2,18},{10... | collective-permute-start | bytes 393224 | tf_op jit(solution)/shard_map/ppermute | solution.py:273
  42.3 2.1 %collective-permute-start.5 = (bf16[4,128,128]{2,1,0:T(8,128)(2,1)S(1)}, bf16[4,128,128]{2,1,0:T(8,128)(2,1)S(1)}, u32[]{:S(2)}, u32[]{:S(2)}) collective-permute-start(bf16[4,128,128]{2,1,0:T(8,128)(2,1)S(1)} %get-tuple-element.36.own_a), channel_id=1, source_target_pairs={{0,8},{8,0},{16,24},{24,16},{1,9},{9,1},{17,25},{25,17},{2,10},{10... | collective-permute-start | bytes 393224 | tf_op jit(solution)/shard_map/ppermute | solution.py:269
  44.4 1.4 %collective-permute-start.4 = (bf16[4,128,128]{2,1,0:T(8,128)(2,1)S(1)}, bf16[4,128,128]{2,1,0:T(8,128)(2,1)S(1)}, u32[]{:S(2)}, u32[]{:S(2)}) collective-permute-start(bf16[4,128,128]{2,1,0:T(8,128)(2,1)S(1)} %get-tuple-element.35.own_b), channel_id=1, source_target_pairs={{0,8},{8,0},{16,24},{24,16},{1,9},{9,1},{17,25},{25,17},{2,10},{10... | collective-permute-start | bytes 393224 | tf_op jit(solution)/shard_map/ppermute | solution.py:269
  71.2 1.4 %collective-permute-start.6 = (bf16[4,128,128]{2,1,0:T(8,128)(2,1)S(1)}, bf16[4,128,128]{2,1,0:T(8,128)(2,1)S(1)}, u32[]{:S(2)}, u32[]{:S(2)}) collective-permute-start(bf16[4,128,128]{2,1,0:T(8,128)(2,1)S(1)} %adjoint2_give_a.1), channel_id=1, source_target_pairs={{0,8},{8,0},{16,24},{24,16},{1,9},{9,1},{17,25},{25,17},{2,10},{10... | collective-permute-start | bytes 393224 | tf_op jit(solution)/shard_map/ppermute | solution.py:269
  71.7 2.8 %collective-permute-start.8 = (bf16[4,128,128]{2,1,0:T(8,128)(2,1)S(1)}, bf16[4,128,128]{2,1,0:T(8,128)(2,1)S(1)}, u32[]{:S(2)}, u32[]{:S(2)}) collective-permute-start(bf16[4,128,128]{2,1,0:T(8,128)(2,1)S(1)} %get-tuple-element.42), channel_id=1, source_target_pairs={{0,8},{8,0},{16,24},{24,16},{1,9},{9,1},{17,25},{25,17},{2,10},{10... | collective-permute-start | bytes 393224 | tf_op jit(solution)/shard_map/ppermute | solution.py:269
  72.7 6.4 %collective-permute-start.7 = (bf16[4,128,128]{2,1,0:T(8,128)(2,1)S(1)}, bf16[4,128,128]{2,1,0:T(8,128)(2,1)S(1)}, u32[]{:S(2)}, u32[]{:S(2)}) collective-permute-start(bf16[4,128,128]{2,1,0:T(8,128)(2,1)S(1)} %adjoint2_pair_a.1.rest_0_), channel_id=1, source_target_pairs={{0,16},{8,24},{16,0},{24,8},{1,17},{9,25},{17,1},{25,9},{2,18},{10... | collective-permute-start | bytes 393224 | tf_op jit(solution)/shard_map/ppermute | solution.py:273
  74.6 6.5 %collective-permute-start.9 = (bf16[4,128,128]{2,1,0:T(8,128)(2,1)S(1)}, bf16[4,128,128]{2,1,0:T(8,128)(2,1)S(1)}, u32[]{:S(2)}, u32[]{:S(2)}) collective-permute-start(bf16[4,128,128]{2,1,0:T(8,128)(2,1)S(1)} %adjoint2_pair_b.1.rest_0_), channel_id=1, source_target_pairs={{0,16},{8,24},{16,0},{24,8},{1,17},{9,25},{17,1},{25,9},{2,18},{10... | collective-permute-start | bytes 393224 | tf_op jit(solution)/shard_map/ppermute | solution.py:273
  79.2 2.1 %collective-permute-start.10 = (bf16[4,128,128]{2,1,0:T(8,128)(2,1)S(1)}, bf16[4,128,128]{2,1,0:T(8,128)(2,1)S(1)}, u32[]{:S(2)}, u32[]{:S(2)}) collective-permute-start(bf16[4,128,128]{2,1,0:T(8,128)(2,1)S(1)} %total_a.1.own_a), channel_id=1, source_target_pairs={{0,8},{8,0},{16,24},{24,16},{1,9},{9,1},{17,25},{25,17},{2,10},{10... | collective-permute-start | bytes 393224 | tf_op jit(solution)/shard_map/ppermute | solution.py:269
  81.2 1.4 %collective-permute-start.11 = (bf16[4,128,128]{2,1,0:T(8,128)(2,1)S(1)}, bf16[4,128,128]{2,1,0:T(8,128)(2,1)S(1)}, u32[]{:S(2)}, u32[]{:S(2)}) collective-permute-start(bf16[4,128,128]{2,1,0:T(8,128)(2,1)S(1)} %total_b.1.own_b), channel_id=1, source_target_pairs={{0,8},{8,0},{16,24},{24,16},{1,9},{9,1},{17,25},{25,17},{2,10},{10... | collective-permute-start | bytes 393224 | tf_op jit(solution)/shard_map/ppermute | solution.py:269

commit v8 on v7

--- a/solution.py
+++ b/solution.py
@@ -8,8 +8,8 @@
 from jax.sharding import PartitionSpec as P
 
 CBLK = 128
-GROUP = 64
-CHUNKS = 1
+GROUP = 32
+CHUNKS = 2
 FIRST_VMEM = 55 << 20
 GIVE_A, KEEP_A, GIVE_B, KEEP_B = range(4)
 
@@ -292,7 +292,7 @@
         if keep:
             outs += (arr((owned, samples, rays), f32),)
         copies, *resid = call(
-            residual_kernel, outs, [], [VMEM] * 3 + [ANY], name, bytes_accessed=1 << 20
+            residual_kernel, outs, [], [VMEM] * 3 + [ANY], name, bytes_accessed=64 << 20
         )(parts, observed, pick_weight, after)
         return resid, over_band(copies).reshape(bundles, samples, rays)
 

time: 83.8 us -> 83.5 us (level)
  no operation moved by 1% of the time
where the time goes in v8:
time: 83.5 us; the launch traced here: 83.1 us
  blocking collectives  36.5 us (44%)
  waiting for transfers between devices  14.7 us (18%)
  Pallas kernels  14 us (17%)
  starting transfers between devices  13.1 us (16%)
  local copies, waits for them, and re-layouts  3.82 us (5%)
  between operations  0.96 us (1%)
    all_to_all x3, blocking collectives, over_band(): lax.all_to_all(array, 'band', split_axis=0, concat_axis=0, tiled=True)  36.5 us
    ppermute x4, waiting for transfers between devices, other_chips(): lax.ppermute(array, 'shot', [(i, i ^ 2 * d) for i in range(nshot)])  10.5 us
    all_to_all x1, starting transfers between devices, over_band(): lax.all_to_all(array, 'band', split_axis=0, concat_axis=0, tiled=True)  7.27 us
    ppermute x4, starting transfers between devices, other_chips(): lax.ppermute(array, 'shot', [(i, i ^ 2 * d) for i in range(nshot)])  4.31 us
    unnamed x20, local copies, waits for them, and re-layouts  3.82 us
    pallas_call x1, Pallas kernels, per_device(): call(first_forward_kernel, part_out, [pltpu.VMEM((bundles, rays, samples)...  3.62 us
    pallas_call x1, Pallas kernels, per_device(): call(dense_kernel, (arr(dense_shape, bf16),) * 4 + (small_token,), [pltpu...  3.48 us
    all_to_all x1, waiting for transfers between devices, over_band(): lax.all_to_all(array, 'band', split_axis=0, concat_axis=0, tiled=True)  2.85 us
  transfers between devices with their start and end apart: 13, of which 9 were waited for; matrix products, arithmetic and copies ran while one was open for 0% of the time, Pallas kernels for 10%

profile of v8, /device:TPU:0, one launch (start us, length us, event | category | flops | bytes accessed | tf_op | source)
XLA Modules:
  0.0 83.1 jit_solution(14533382989103756798)
XLA Ops:
  0.6 3.6 %forward1.1 = bf16[8,128,128]{2,1,0:T(8,128)(2,1)} custom-call(s32[64]{0:T(128)} %bund.1, s32[64]{0:T(128)} %cblk.1, bf16[64,128,128]{2,1,0:T(8,128)(2,1)} %sens.1, f32[16,128,128]{2,1,0:T(8,128)} %bitcast.7, f32[16,128,128]{2,1,0:T(8,128)} %bitcast.9), custom_call_target="tpu_custom_call" | custom-call | flops 268435456 | bytes 2097152 | tf_op jit(solution)/shard_map/forward1/pallas_call | solution.py:330
  4.3 7.3 %all-to-all-start = ((bf16[8,128,128]{2,1,0:T(8,128)(2,1)}), bf16[8,128,128]{2,1,0:T(8,128)(2,1)S(1)}, u32[]{:S(2)}, u32[]{:S(2)}) async-start(bf16[8,128,128]{2,1,0:T(8,128)(2,1)} %forward1.1), calls=%async_computation | async-start | bytes 524288 | tf_op jit(solution)/shard_map/all_to_all | solution.py:278
  11.6 1.6 %copy-done.3 = bf16[64,128,128]{2,1,0:T(8,128)(2,1)S(1)} copy-done((bf16[64,128,128]{2,1,0:T(8,128)(2,1)S(1)}, bf16[64,128,128]{2,1,0:T(8,128)(2,1)}, u32[]{:S(2)}) %copy-start.3) | copy-done | bytes 2097176
  13.2 3.5 %dense.1 = (bf16[2,1024,256]{2,1,0:T(8,128)(2,1)S(1)}, bf16[2,1024,256]{2,1,0:T(8,128)(2,1)S(1)}, bf16[2,1024,256]{2,1,0:T(8,128)(2,1)S(1)}, bf16[2,1024,256]{2,1,0:T(8,128)(2,1)S(1)}, f32[8,128]{1,0:T(8,128)S(1)}) custom-call(s32[64]{0:T(128)S(1)} %copy-done.8, s32[64]{0:T(128)S(1)} %copy-done.9, bf16[64,128,128]{2,1,0:T(8,128)(2,1)S(1)} %copy-done.3), custom_call_target="tpu_custom_call" | custom-call | bytes 16777216 | tf_op jit(solution)/shard_map/dense/pallas_call | solution.py:349
  16.7 1.0 %copy-done = bf16[2,1024,256]{2,1,0:T(8,128)(2,1)} copy-done((bf16[2,1024,256]{2,1,0:T(8,128)(2,1)}, bf16[2,1024,256]{2,1,0:T(8,128)(2,1)S(1)}, u32[]{:S(2)}) %copy-start) | copy-done | bytes 1048600
  17.6 2.9 %all-to-all-done = bf16[8,128,128]{2,1,0:T(8,128)(2,1)S(1)} async-done(((bf16[8,128,128]{2,1,0:T(8,128)(2,1)}), bf16[8,128,128]{2,1,0:T(8,128)(2,1)S(1)}, u32[]{:S(2)}, u32[]{:S(2)}) %all-to-all-start) | async-done | bytes 262176 | tf_op jit(solution)/shard_map/all_to_all | solution.py:278
  20.6 12.0 %all_to_all.20 = bf16[8,1,128,128]{3,2,1,0:T(8,128)(2,1)S(1)} all-to-all(bf16[8,1,128,128]{3,2,1,0:T(8,128)(2,1)S(1)} %residual1.1), channel_id=1, replica_groups=mesh['shot'=4,'band'=8] {'band'}, dimensions={0} | all-to-all | bytes 524288 | tf_op jit(solution)/shard_map/all_to_all | solution.py:278
  32.6 1.2 %copy-done.1 = bf16[2,1024,256]{2,1,0:T(8,128)(2,1)S(1)} copy-done((bf16[2,1024,256]{2,1,0:T(8,128)(2,1)S(1)}, bf16[2,1024,256]{2,1,0:T(8,128)(2,1)}, u32[]{:S(2)}) %copy-start.1) | copy-done | bytes 1048600
  34.2 0.4 adjoint1_keep_a.1
  34.7 0.5 collective-permute-start.2
  35.2 0.3 collective-permute-done.got_ref
  35.5 1.6 %collective-permute-start.1 = (bf16[4,128,128]{2,1,0:T(8,128)(2,1)S(1)}, bf16[4,128,128]{2,1,0:T(8,128)(2,1)S(1)}, u32[]{:S(2)}, u32[]{:S(2)}) collective-permute-start(bf16[4,128,128]{2,1,0:T(8,128)(2,1)S(1)} %adjoint1_pair_a.1.rest_0_), channel_id=1, source_target_pairs={{0,16},{8,24},{16,0},{24,8},{1,17},{9,25},{17,1},{25,9},{2,18},{10... | collective-permute-start | bytes 393224 | tf_op jit(solution)/shard_map/ppermute | solution.py:273
  37.5 0.6 collective-permute-start.3
  38.2 3.7 %collective-permute-done.1.rest_1_ = bf16[4,128,128]{2,1,0:T(8,128)(2,1)S(1)} collective-permute-done((bf16[4,128,128]{2,1,0:T(8,128)(2,1)S(1)}, bf16[4,128,128]{2,1,0:T(8,128)(2,1)S(1)}, u32[]{:S(2)}, u32[]{:S(2)}) %collective-permute-start.1) | collective-permute-done | bytes 131104 | tf_op jit(solution)/shard_map/ppermute | solution.py:273
  42.2 1.8 %collective-permute-done.3.rest_1_ = bf16[4,128,128]{2,1,0:T(8,128)(2,1)S(1)} collective-permute-done((bf16[4,128,128]{2,1,0:T(8,128)(2,1)S(1)}, bf16[4,128,128]{2,1,0:T(8,128)(2,1)S(1)}, u32[]{:S(2)}, u32[]{:S(2)}) %collective-permute-start.3) | collective-permute-done | bytes 131104 | tf_op jit(solution)/shard_map/ppermute | solution.py:273
  44.2 1.0 %forward2_early.1.early = f32[8,128,128]{2,1,0:T(8,128)S(1)} custom-call(bf16[2,1024,256]{2,1,0:T(8,128)(2,1)S(1)} %get-tuple-element.28.refs_0_.dense_own_a, bf16[2,1024,256]{2,1,0:T(8,128)(2,1)S(1)} %get-tuple-element.25.refs_0_.dense_own_b, bf16[2,1024,256]{2,1,0:T(8,128)(2,1)S(1)} %copy-done.2, bf16[4,128,128]{2,1,0:T(8,128)(2,1)S(1)} %get-tuple-element.36.own_a, ...), custom_call_target="tpu_custom_call" | custom-call | flops 402653184 | bytes 3145728 | tf_op jit(solution)/shard_map/forward2_early/pallas_call | solution.py:385
  45.2 0.3 collective-permute-done.4.mate_b
  45.5 0.4 forward2_late.1
  46.0 12.6 %all_to_all.21 = bf16[8,128,128]{2,1,0:T(8,128)(2,1)S(1)} all-to-all(bf16[8,128,128]{2,1,0:T(8,128)(2,1)S(1)} %forward2_late.1), channel_id=1, replica_groups=mesh['shot'=4,'band'=8] {'band'}, dimensions={0} | all-to-all | bytes 524288 | tf_op jit(solution)/shard_map/all_to_all | solution.py:278
  58.7 12.0 %all_to_all.22 = bf16[8,1,128,128]{3,2,1,0:T(8,128)(2,1)S(1)} all-to-all(bf16[8,1,128,128]{3,2,1,0:T(8,128)(2,1)S(1)} %get-tuple-element.39), channel_id=1, replica_groups=mesh['shot'=4,'band'=8] {'band'}, dimensions={0} | all-to-all | bytes 524288 | tf_op jit(solution)/shard_map/all_to_all | solution.py:278
  70.6 0.3 adjoint2_give_a.1
  71.0 0.4 adjoint2_keep_a.1
  71.5 0.6 collective-permute-start.8
  72.0 0.3 collective-permute-done.6.got_ref
  72.4 1.6 %collective-permute-start.7 = (bf16[4,128,128]{2,1,0:T(8,128)(2,1)S(1)}, bf16[4,128,128]{2,1,0:T(8,128)(2,1)S(1)}, u32[]{:S(2)}, u32[]{:S(2)}) collective-permute-start(bf16[4,128,128]{2,1,0:T(8,128)(2,1)S(1)} %adjoint2_pair_a.1.rest_0_), channel_id=1, source_target_pairs={{0,16},{8,24},{16,0},{24,8},{1,17},{9,25},{17,1},{25,9},{2,18},{10... | collective-permute-start | bytes 393224 | tf_op jit(solution)/shard_map/ppermute | solution.py:273
  74.3 0.6 collective-permute-start.9
  74.9 0.7 turn.1
  75.6 3.2 %collective-permute-done.7.rest_1_ = bf16[4,128,128]{2,1,0:T(8,128)(2,1)S(1)} collective-permute-done((bf16[4,128,128]{2,1,0:T(8,128)(2,1)S(1)}, bf16[4,128,128]{2,1,0:T(8,128)(2,1)S(1)}, u32[]{:S(2)}, u32[]{:S(2)}) %collective-permute-start.7) | collective-permute-done | bytes 131104 | tf_op jit(solution)/shard_map/ppermute | solution.py:273
  79.0 1.8 %collective-permute-done.9.rest_1_ = bf16[4,128,128]{2,1,0:T(8,128)(2,1)S(1)} collective-permute-done((bf16[4,128,128]{2,1,0:T(8,128)(2,1)S(1)}, bf16[4,128,128]{2,1,0:T(8,128)(2,1)S(1)}, u32[]{:S(2)}, u32[]{:S(2)}) %collective-permute-start.9) | collective-permute-done | bytes 131104 | tf_op jit(solution)/shard_map/ppermute | solution.py:273
  81.1 0.9 %new_state_early.1 = (f32[16,128,128]{2,1,0:T(8,128)}, f32[4,128,128]{2,1,0:T(8,128)S(1)}) custom-call(f32[16,128,128]{2,1,0:T(8,128)S(1)} %get-tuple-element.26.base, bf16[4,128,128]{2,1,0:T(8,128)(2,1)S(1)} %total_a.1.own_a, bf16[4,128,128]{2,1,0:T(8,128)(2,1)S(1)} %total_b.1.own_b, bf16[4,128,128]{2,1,0:T(8,128)(2,1)S(1)} %collective-permute-done.10.mate_a), custom_call_target="tpu_custom_call" | custom-call | bytes 3145728 | tf_op jit(solution)/shard_map/new_state_early/pallas_call | solution.py:427
  82.0 0.4 collective-permute-done.11.mate_b
  82.4 0.7 new_state_late.1
  (41 shorter events, 2.4 us)
Async XLA Ops:
  0.6 10.9 %copy-start.8 = (s32[64]{0:T(128)S(1)}, s32[64]{0:T(128)}, u32[]{:S(2)}) copy-start(s32[64]{0:T(128)} %bund.1) | copy-start | bytes 772
  0.6 10.9 %copy-start.9 = (s32[64]{0:T(128)S(1)}, s32[64]{0:T(128)}, u32[]{:S(2)}) copy-start(s32[64]{0:T(128)} %cblk.1) | copy-start | bytes 772
  4.3 16.2 %copy-start.6 = (f32[1,128]{1,0:T(1,128)S(1)}, f32[1,128]{1,0:T(1,128)}, u32[]{:S(2)}) copy-start(f32[1,128]{1,0:T(1,128)} %obs_ref.3) | copy-start | bytes 1540
  4.3 16.2 %copy-start.7 = (f32[1,128]{1,0:T(1,128)S(1)}, f32[1,128]{1,0:T(1,128)}, u32[]{:S(2)}) copy-start(f32[1,128]{1,0:T(1,128)} %wt_ref.3) | copy-start | bytes 1540
  4.3 16.2 %all-to-all-start = ((bf16[8,128,128]{2,1,0:T(8,128)(2,1)}), bf16[8,128,128]{2,1,0:T(8,128)(2,1)S(1)}, u32[]{:S(2)}, u32[]{:S(2)}) async-start(bf16[8,128,128]{2,1,0:T(8,128)(2,1)} %forward1.1), calls=%async_computation | async-start | bytes 524288 | tf_op jit(solution)/shard_map/all_to_all | solution.py:278
  11.6 1.6 %copy-start.3 = (bf16[64,128,128]{2,1,0:T(8,128)(2,1)S(1)}, bf16[64,128,128]{2,1,0:T(8,128)(2,1)}, u32[]{:S(2)}) copy-start(bf16[64,128,128]{2,1,0:T(8,128)(2,1)} %sens.1) | copy-start | bytes 6291460
  16.7 1.0 %copy-start = (bf16[2,1024,256]{2,1,0:T(8,128)(2,1)}, bf16[2,1024,256]{2,1,0:T(8,128)(2,1)S(1)}, u32[]{:S(2)}) copy-start(bf16[2,1024,256]{2,1,0:T(8,128)(2,1)S(1)} %get-tuple-element.31.refs_0_.dense_mate_a) | copy-start | bytes 3145732
  32.6 1.2 %copy-start.1 = (bf16[2,1024,256]{2,1,0:T(8,128)(2,1)S(1)}, bf16[2,1024,256]{2,1,0:T(8,128)(2,1)}, u32[]{:S(2)}) copy-start(bf16[2,1024,256]{2,1,0:T(8,128)(2,1)} %copy-done) | copy-start | bytes 3145732
  34.1 1.4 %collective-permute-start = (bf16[4,128,128]{2,1,0:T(8,128)(2,1)S(1)}, bf16[4,128,128]{2,1,0:T(8,128)(2,1)S(1)}, u32[]{:S(2)}, u32[]{:S(2)}) collective-permute-start(bf16[4,128,128]{2,1,0:T(8,128)(2,1)S(1)} %adjoint1_give_a.1), channel_id=1, source_target_pairs={{0,8},{8,0},{16,24},{24,16},{1,9},{9,1},{17,25},{25,17},{2,10},{10... | collective-permute-start | bytes 393224 | tf_op jit(solution)/shard_map/ppermute | solution.py:269
  34.2 3.9 %copy-start.4 = (f32[2048,128]{1,0:T(8,128)S(1)}, f32[2048,128]{1,0:T(8,128)}, u32[]{:S(2)}) copy-start(f32[2048,128]{1,0:T(8,128)} %param.10) | copy-start | bytes 3145732
  34.2 3.9 %copy-start.5 = (f32[2048,128]{1,0:T(8,128)S(1)}, f32[2048,128]{1,0:T(8,128)}, u32[]{:S(2)}) copy-start(f32[2048,128]{1,0:T(8,128)} %param.11) | copy-start | bytes 3145732
  34.7 2.8 %collective-permute-start.2 = (bf16[4,128,128]{2,1,0:T(8,128)(2,1)S(1)}, bf16[4,128,128]{2,1,0:T(8,128)(2,1)S(1)}, u32[]{:S(2)}, u32[]{:S(2)}) collective-permute-start(bf16[4,128,128]{2,1,0:T(8,128)(2,1)S(1)} %get-tuple-element.34), channel_id=1, source_target_pairs={{0,8},{8,0},{16,24},{24,16},{1,9},{9,1},{17,25},{25,17},{2,10},{10... | collective-permute-start | bytes 393224 | tf_op jit(solution)/shard_map/ppermute | solution.py:269
  35.5 6.4 %collective-permute-start.1 = (bf16[4,128,128]{2,1,0:T(8,128)(2,1)S(1)}, bf16[4,128,128]{2,1,0:T(8,128)(2,1)S(1)}, u32[]{:S(2)}, u32[]{:S(2)}) collective-permute-start(bf16[4,128,128]{2,1,0:T(8,128)(2,1)S(1)} %adjoint1_pair_a.1.rest_0_), channel_id=1, source_target_pairs={{0,16},{8,24},{16,0},{24,8},{1,17},{9,25},{17,1},{25,9},{2,18},{10... | collective-permute-start | bytes 393224 | tf_op jit(solution)/shard_map/ppermute | solution.py:273
  37.4 6.8 %copy-start.2 = (bf16[2,1024,256]{2,1,0:T(8,128)(2,1)S(1)}, bf16[2,1024,256]{2,1,0:T(8,128)(2,1)}, u32[]{:S(2)}) copy-start(bf16[2,1024,256]{2,1,0:T(8,128)(2,1)} %copy-done) | copy-start | bytes 3145732
  37.5 6.5 %collective-permute-start.3 = (bf16[4,128,128]{2,1,0:T(8,128)(2,1)S(1)}, bf16[4,128,128]{2,1,0:T(8,128)(2,1)S(1)}, u32[]{:S(2)}, u32[]{:S(2)}) collective-permute-start(bf16[4,128,128]{2,1,0:T(8,128)(2,1)S(1)} %adjoint1_pair_b.1.rest_0_), channel_id=1, source_target_pairs={{0,16},{8,24},{16,0},{24,8},{1,17},{9,25},{17,1},{25,9},{2,18},{10... | collective-permute-start | bytes 393224 | tf_op jit(solution)/shard_map/ppermute | solution.py:273
  42.1 2.1 %collective-permute-start.5 = (bf16[4,128,128]{2,1,0:T(8,128)(2,1)S(1)}, bf16[4,128,128]{2,1,0:T(8,128)(2,1)S(1)}, u32[]{:S(2)}, u32[]{:S(2)}) collective-permute-start(bf16[4,128,128]{2,1,0:T(8,128)(2,1)S(1)} %get-tuple-element.36.own_a), channel_id=1, source_target_pairs={{0,8},{8,0},{16,24},{24,16},{1,9},{9,1},{17,25},{25,17},{2,10},{10... | collective-permute-start | bytes 393224 | tf_op jit(solution)/shard_map/ppermute | solution.py:269
  44.1 1.4 %collective-permute-start.4 = (bf16[4,128,128]{2,1,0:T(8,128)(2,1)S(1)}, bf16[4,128,128]{2,1,0:T(8,128)(2,1)S(1)}, u32[]{:S(2)}, u32[]{:S(2)}) collective-permute-start(bf16[4,128,128]{2,1,0:T(8,128)(2,1)S(1)} %get-tuple-element.35.own_b), channel_id=1, source_target_pairs={{0,8},{8,0},{16,24},{24,16},{1,9},{9,1},{17,25},{25,17},{2,10},{10... | collective-permute-start | bytes 393224 | tf_op jit(solution)/shard_map/ppermute | solution.py:269
  71.0 1.4 %collective-permute-start.6 = (bf16[4,128,128]{2,1,0:T(8,128)(2,1)S(1)}, bf16[4,128,128]{2,1,0:T(8,128)(2,1)S(1)}, u32[]{:S(2)}, u32[]{:S(2)}) collective-permute-start(bf16[4,128,128]{2,1,0:T(8,128)(2,1)S(1)} %adjoint2_give_a.1), channel_id=1, source_target_pairs={{0,8},{8,0},{16,24},{24,16},{1,9},{9,1},{17,25},{25,17},{2,10},{10... | collective-permute-start | bytes 393224 | tf_op jit(solution)/shard_map/ppermute | solution.py:269
  71.5 2.8 %collective-permute-start.8 = (bf16[4,128,128]{2,1,0:T(8,128)(2,1)S(1)}, bf16[4,128,128]{2,1,0:T(8,128)(2,1)S(1)}, u32[]{:S(2)}, u32[]{:S(2)}) collective-permute-start(bf16[4,128,128]{2,1,0:T(8,128)(2,1)S(1)} %get-tuple-element.42), channel_id=1, source_target_pairs={{0,8},{8,0},{16,24},{24,16},{1,9},{9,1},{17,25},{25,17},{2,10},{10... | collective-permute-start | bytes 393224 | tf_op jit(solution)/shard_map/ppermute | solution.py:269
  72.4 6.4 %collective-permute-start.7 = (bf16[4,128,128]{2,1,0:T(8,128)(2,1)S(1)}, bf16[4,128,128]{2,1,0:T(8,128)(2,1)S(1)}, u32[]{:S(2)}, u32[]{:S(2)}) collective-permute-start(bf16[4,128,128]{2,1,0:T(8,128)(2,1)S(1)} %adjoint2_pair_a.1.rest_0_), channel_id=1, source_target_pairs={{0,16},{8,24},{16,0},{24,8},{1,17},{9,25},{17,1},{25,9},{2,18},{10... | collective-permute-start | bytes 393224 | tf_op jit(solution)/shard_map/ppermute | solution.py:273
  74.3 6.5 %collective-permute-start.9 = (bf16[4,128,128]{2,1,0:T(8,128)(2,1)S(1)}, bf16[4,128,128]{2,1,0:T(8,128)(2,1)S(1)}, u32[]{:S(2)}, u32[]{:S(2)}) collective-permute-start(bf16[4,128,128]{2,1,0:T(8,128)(2,1)S(1)} %adjoint2_pair_b.1.rest_0_), channel_id=1, source_target_pairs={{0,16},{8,24},{16,0},{24,8},{1,17},{9,25},{17,1},{25,9},{2,18},{10... | collective-permute-start | bytes 393224 | tf_op jit(solution)/shard_map/ppermute | solution.py:273
  78.9 2.1 %collective-permute-start.10 = (bf16[4,128,128]{2,1,0:T(8,128)(2,1)S(1)}, bf16[4,128,128]{2,1,0:T(8,128)(2,1)S(1)}, u32[]{:S(2)}, u32[]{:S(2)}) collective-permute-start(bf16[4,128,128]{2,1,0:T(8,128)(2,1)S(1)} %total_a.1.own_a), channel_id=1, source_target_pairs={{0,8},{8,0},{16,24},{24,16},{1,9},{9,1},{17,25},{25,17},{2,10},{10... | collective-permute-start | bytes 393224 | tf_op jit(solution)/shard_map/ppermute | solution.py:269
  81.0 1.4 %collective-permute-start.11 = (bf16[4,128,128]{2,1,0:T(8,128)(2,1)S(1)}, bf16[4,128,128]{2,1,0:T(8,128)(2,1)S(1)}, u32[]{:S(2)}, u32[]{:S(2)}) collective-permute-start(bf16[4,128,128]{2,1,0:T(8,128)(2,1)S(1)} %total_b.1.own_b), channel_id=1, source_target_pairs={{0,8},{8,0},{16,24},{24,16},{1,9},{9,1},{17,25},{25,17},{2,10},{10... | collective-permute-start | bytes 393224 | tf_op jit(solution)/shard_map/ppermute | solution.py:269

commit v9 on v8

--- a/solution.py
+++ b/solution.py
@@ -219,7 +219,8 @@
         out_ref[i] = (field_ref[i] - 0.25 * grad).astype(bf16)
 
 
-def total_kernel(ny, grad_ref, after_ref, *rest):
+def total_kernel(ny, after, grad_ref, *rest):
+    rest = rest[after:]
     part_refs, (out_ref, order) = rest[:ny], rest[ny:]
     for i in range(out_ref.shape[0]):
         grad2 = sum_over_y(lax.axis_index("shot") // 2, part_refs, order, i)
@@ -292,7 +293,7 @@
         if keep:
             outs += (arr((owned, samples, rays), f32),)
         copies, *resid = call(
-            residual_kernel, outs, [], [VMEM] * 3 + [ANY], name, bytes_accessed=64 << 20
+            residual_kernel, outs, [], [VMEM] * 3 + [ANY], name, bytes_accessed=1 << 20
         )(parts, observed, pick_weight, after)
         return resid, over_band(copies).reshape(bundles, samples, rays)
 
@@ -403,7 +404,7 @@
 
     (resid2_t,), resid_all2 = residual(part2, token, "residual2", True)
     *sums2, _ = adjoint(dense, resid_all2, "adjoint2")
-    resid2, after = call(
+    resid2, turned = call(
         turn_kernel,
         (arr((owned, rays, samples), f32), small_token),
         [],
@@ -411,17 +412,18 @@
         "turn",
         bytes_accessed=1 << 20,
     )(resid2_t)
-    own, mate = [], []
+    own, mate, after = [], [], [turned, dense[GIVE_A], dense[KEEP_A], dense[GIVE_B]]
     for grad, sums, part in zip(grad1, sums2, "ab"):
         total = call(
-            functools.partial(total_kernel, ny),
+            functools.partial(total_kernel, ny, len(after)),
             quarter_bf16,
             [order],
-            [VMEM, ANY] + [VMEM] * ny,
+            [VMEM] + [ANY] * len(after) + [VMEM] * ny,
             "total_" + part,
             bytes_accessed=1 << 19,
-        )(grad, after, *sums)
+        )(grad, *after, *sums)
         own.append(total)
+        after = []
         mate.append(other_core(total))
     whole = arr((cells, CBLK, samples), f32)
     so_far, rest = call(

time: 83.5 us -> 82.3 us (0.986)
  local copies, waits for them, and re-layouts: 3.82 us -> 2.59 us
    unnamed x20 -> x18, local copies, waits for them, and re-layouts: 3.82 us -> 2.59 us
where the time goes in v9:
time: 82.3 us; the launch traced here: 81.9 us
  blocking collectives  36.5 us (44%)
  waiting for transfers between devices  14.7 us (18%)
  Pallas kernels  14 us (17%)
  starting transfers between devices  13.1 us (16%)
  local copies, waits for them, and re-layouts  2.59 us (3%)
  between operations  0.95 us (1%)
    all_to_all x3, blocking collectives, over_band(): lax.all_to_all(array, 'band', split_axis=0, concat_axis=0, tiled=True)  36.5 us
    ppermute x4, waiting for transfers between devices, other_chips(): lax.ppermute(array, 'shot', [(i, i ^ 2 * d) for i in range(nshot)])  10.5 us
    all_to_all x1, starting transfers between devices, over_band(): lax.all_to_all(array, 'band', split_axis=0, concat_axis=0, tiled=True)  7.27 us
    ppermute x4, starting transfers between devices, other_chips(): lax.ppermute(array, 'shot', [(i, i ^ 2 * d) for i in range(nshot)])  4.32 us
    pallas_call x1, Pallas kernels, per_device(): call(first_forward_kernel, part_out, [pltpu.VMEM((bundles, rays, samples)...  3.63 us
    pallas_call x1, Pallas kernels, per_device(): call(dense_kernel, (arr(dense_shape, bf16),) * 4 + (small_token,), [pltpu...  3.48 us
    all_to_all x1, waiting for transfers between devices, over_band(): lax.all_to_all(array, 'band', split_axis=0, concat_axis=0, tiled=True)  2.85 us
    unnamed x18, local copies, waits for them, and re-layouts  2.59 us
  transfers between devices with their start and end apart: 13, of which 9 were waited for; matrix products, arithmetic and copies ran while one was open for 0% of the time, Pallas kernels for 10%

profile of v9, /device:TPU:0, one launch (start us, length us, event | category | flops | bytes accessed | tf_op | source)
XLA Modules:
  0.0 81.9 jit_solution(16825486923607712818)
XLA Ops:
  0.6 3.6 %forward1.1 = bf16[8,128,128]{2,1,0:T(8,128)(2,1)} custom-call(s32[64]{0:T(128)} %bund.1, s32[64]{0:T(128)} %cblk.1, bf16[64,128,128]{2,1,0:T(8,128)(2,1)} %sens.1, f32[16,128,128]{2,1,0:T(8,128)} %bitcast.7, f32[16,128,128]{2,1,0:T(8,128)} %bitcast.9), custom_call_target="tpu_custom_call" | custom-call | flops 268435456 | bytes 2097152 | tf_op jit(solution)/shard_map/forward1/pallas_call | solution.py:331
  4.3 7.3 %all-to-all-start = ((bf16[8,128,128]{2,1,0:T(8,128)(2,1)}), bf16[8,128,128]{2,1,0:T(8,128)(2,1)S(1)}, u32[]{:S(2)}, u32[]{:S(2)}) async-start(bf16[8,128,128]{2,1,0:T(8,128)(2,1)} %forward1.1), calls=%async_computation | async-start | bytes 524288 | tf_op jit(solution)/shard_map/all_to_all | solution.py:279
  11.6 1.6 %copy-done.2 = bf16[64,128,128]{2,1,0:T(8,128)(2,1)S(1)} copy-done((bf16[64,128,128]{2,1,0:T(8,128)(2,1)S(1)}, bf16[64,128,128]{2,1,0:T(8,128)(2,1)}, u32[]{:S(2)}) %copy-start.2) | copy-done | bytes 2097176
  13.2 3.5 %dense.1 = (bf16[2,1024,256]{2,1,0:T(8,128)(2,1)S(1)}, bf16[2,1024,256]{2,1,0:T(8,128)(2,1)S(1)}, bf16[2,1024,256]{2,1,0:T(8,128)(2,1)S(1)}, bf16[2,1024,256]{2,1,0:T(8,128)(2,1)S(1)}, f32[8,128]{1,0:T(8,128)S(1)}) custom-call(s32[64]{0:T(128)S(1)} %copy-done.7, s32[64]{0:T(128)S(1)} %copy-done.8, bf16[64,128,128]{2,1,0:T(8,128)(2,1)S(1)} %copy-done.2), custom_call_target="tpu_custom_call" | custom-call | bytes 16777216 | tf_op jit(solution)/shard_map/dense/pallas_call | solution.py:350
  16.7 1.0 %copy-done = bf16[2,1024,256]{2,1,0:T(8,128)(2,1)} copy-done((bf16[2,1024,256]{2,1,0:T(8,128)(2,1)}, bf16[2,1024,256]{2,1,0:T(8,128)(2,1)S(1)}, u32[]{:S(2)}) %copy-start) | copy-done | bytes 1048600
  17.6 2.9 %all-to-all-done = bf16[8,128,128]{2,1,0:T(8,128)(2,1)S(1)} async-done(((bf16[8,128,128]{2,1,0:T(8,128)(2,1)}), bf16[8,128,128]{2,1,0:T(8,128)(2,1)S(1)}, u32[]{:S(2)}, u32[]{:S(2)}) %all-to-all-start) | async-done | bytes 262176 | tf_op jit(solution)/shard_map/all_to_all | solution.py:279
  20.6 12.0 %all_to_all.20 = bf16[8,1,128,128]{3,2,1,0:T(8,128)(2,1)S(1)} all-to-all(bf16[8,1,128,128]{3,2,1,0:T(8,128)(2,1)S(1)} %residual1.1), channel_id=1, replica_groups=mesh['shot'=4,'band'=8] {'band'}, dimensions={0} | all-to-all | bytes 524288 | tf_op jit(solution)/shard_map/all_to_all | solution.py:279
  32.6 0.3 adjoint1_give_a.1
  33.0 0.4 adjoint1_keep_a.1
  33.4 0.5 collective-permute-start.2
  34.0 0.3 collective-permute-done.got_ref
  34.3 1.6 %collective-permute-start.1 = (bf16[4,128,128]{2,1,0:T(8,128)(2,1)S(1)}, bf16[4,128,128]{2,1,0:T(8,128)(2,1)S(1)}, u32[]{:S(2)}, u32[]{:S(2)}) collective-permute-start(bf16[4,128,128]{2,1,0:T(8,128)(2,1)S(1)} %adjoint1_pair_a.1.rest_0_), channel_id=1, source_target_pairs={{0,16},{8,24},{16,0},{24,8},{1,17},{9,25},{17,1},{25,9},{2,18},{10... | collective-permute-start | bytes 393224 | tf_op jit(solution)/shard_map/ppermute | solution.py:274
  36.3 0.6 collective-permute-start.3
  37.0 3.7 %collective-permute-done.1.rest_1_ = bf16[4,128,128]{2,1,0:T(8,128)(2,1)S(1)} collective-permute-done((bf16[4,128,128]{2,1,0:T(8,128)(2,1)S(1)}, bf16[4,128,128]{2,1,0:T(8,128)(2,1)S(1)}, u32[]{:S(2)}, u32[]{:S(2)}) %collective-permute-start.1) | collective-permute-done | bytes 131104 | tf_op jit(solution)/shard_map/ppermute | solution.py:274
  41.0 1.8 %collective-permute-done.3.rest_1_ = bf16[4,128,128]{2,1,0:T(8,128)(2,1)S(1)} collective-permute-done((bf16[4,128,128]{2,1,0:T(8,128)(2,1)S(1)}, bf16[4,128,128]{2,1,0:T(8,128)(2,1)S(1)}, u32[]{:S(2)}, u32[]{:S(2)}) %collective-permute-start.3) | collective-permute-done | bytes 131104 | tf_op jit(solution)/shard_map/ppermute | solution.py:274
  43.0 1.0 %forward2_early.1.early = f32[8,128,128]{2,1,0:T(8,128)S(1)} custom-call(bf16[2,1024,256]{2,1,0:T(8,128)(2,1)S(1)} %get-tuple-element.28.refs_0_.dense_own_a.rest_2_, bf16[2,1024,256]{2,1,0:T(8,128)(2,1)S(1)} %copy-done.1, bf16[2,1024,256]{2,1,0:T(8,128)(2,1)S(1)} %get-tuple-element.31.refs_0_.dense_mate_a.rest_1_, ...), custom_call_target="tpu_custom_call" | custom-call | flops 402653184 | bytes 3145728 | tf_op jit(solution)/shard_map/forward2_early/pallas_call | solution.py:386
  44.0 0.4 collective-permute-done.4.mate_b
  44.3 0.4 forward2_late.1
  44.7 12.6 %all_to_all.21 = bf16[8,128,128]{2,1,0:T(8,128)(2,1)S(1)} all-to-all(bf16[8,128,128]{2,1,0:T(8,128)(2,1)S(1)} %forward2_late.1), channel_id=1, replica_groups=mesh['shot'=4,'band'=8] {'band'}, dimensions={0} | all-to-all | bytes 524288 | tf_op jit(solution)/shard_map/all_to_all | solution.py:279
  57.5 12.0 %all_to_all.22 = bf16[8,1,128,128]{3,2,1,0:T(8,128)(2,1)S(1)} all-to-all(bf16[8,1,128,128]{3,2,1,0:T(8,128)(2,1)S(1)} %get-tuple-element.39), channel_id=1, replica_groups=mesh['shot'=4,'band'=8] {'band'}, dimensions={0} | all-to-all | bytes 524288 | tf_op jit(solution)/shard_map/all_to_all | solution.py:279
  69.4 0.3 adjoint2_give_a.1
  69.8 0.4 adjoint2_keep_a.1
  70.3 0.6 collective-permute-start.8
  70.8 0.3 collective-permute-done.6.got_ref
  71.2 1.6 %collective-permute-start.7 = (bf16[4,128,128]{2,1,0:T(8,128)(2,1)S(1)}, bf16[4,128,128]{2,1,0:T(8,128)(2,1)S(1)}, u32[]{:S(2)}, u32[]{:S(2)}) collective-permute-start(bf16[4,128,128]{2,1,0:T(8,128)(2,1)S(1)} %adjoint2_pair_a.1.rest_4_), channel_id=1, source_target_pairs={{0,16},{8,24},{16,0},{24,8},{1,17},{9,25},{17,1},{25,9},{2,18},{10... | collective-permute-start | bytes 393224 | tf_op jit(solution)/shard_map/ppermute | solution.py:274
  73.1 0.6 collective-permute-start.9
  73.7 0.7 turn.1
  74.4 3.2 %collective-permute-done.7.rest_5_ = bf16[4,128,128]{2,1,0:T(8,128)(2,1)S(1)} collective-permute-done((bf16[4,128,128]{2,1,0:T(8,128)(2,1)S(1)}, bf16[4,128,128]{2,1,0:T(8,128)(2,1)S(1)}, u32[]{:S(2)}, u32[]{:S(2)}) %collective-permute-start.7) | collective-permute-done | bytes 131104 | tf_op jit(solution)/shard_map/ppermute | solution.py:274
  77.8 1.8 %collective-permute-done.9.rest_1_ = bf16[4,128,128]{2,1,0:T(8,128)(2,1)S(1)} collective-permute-done((bf16[4,128,128]{2,1,0:T(8,128)(2,1)S(1)}, bf16[4,128,128]{2,1,0:T(8,128)(2,1)S(1)}, u32[]{:S(2)}, u32[]{:S(2)}) %collective-permute-start.9) | collective-permute-done | bytes 131104 | tf_op jit(solution)/shard_map/ppermute | solution.py:274
  79.8 0.9 %new_state_early.1 = (f32[16,128,128]{2,1,0:T(8,128)}, f32[4,128,128]{2,1,0:T(8,128)S(1)}) custom-call(f32[16,128,128]{2,1,0:T(8,128)S(1)} %get-tuple-element.26.base, bf16[4,128,128]{2,1,0:T(8,128)(2,1)S(1)} %total_a.1.own_a, bf16[4,128,128]{2,1,0:T(8,128)(2,1)S(1)} %total_b.1.own_b, bf16[4,128,128]{2,1,0:T(8,128)(2,1)S(1)} %collective-permute-done.10.mate_a), custom_call_target="tpu_custom_call" | custom-call | bytes 3145728 | tf_op jit(solution)/shard_map/new_state_early/pallas_call | solution.py:429
  80.8 0.4 collective-permute-done.11.mate_b
  81.2 0.7 new_state_late.1
  (39 shorter events, 2.1 us)
Async XLA Ops:
  0.6 10.9 %copy-start.7 = (s32[64]{0:T(128)S(1)}, s32[64]{0:T(128)}, u32[]{:S(2)}) copy-start(s32[64]{0:T(128)} %bund.1) | copy-start | bytes 772
  0.6 10.9 %copy-start.8 = (s32[64]{0:T(128)S(1)}, s32[64]{0:T(128)}, u32[]{:S(2)}) copy-start(s32[64]{0:T(128)} %cblk.1) | copy-start | bytes 772
  4.3 16.2 %copy-start.5 = (f32[1,128]{1,0:T(1,128)S(1)}, f32[1,128]{1,0:T(1,128)}, u32[]{:S(2)}) copy-start(f32[1,128]{1,0:T(1,128)} %obs_ref.3) | copy-start | bytes 1540
  4.3 16.2 %copy-start.6 = (f32[1,128]{1,0:T(1,128)S(1)}, f32[1,128]{1,0:T(1,128)}, u32[]{:S(2)}) copy-start(f32[1,128]{1,0:T(1,128)} %wt_ref.3) | copy-start | bytes 1540
  4.3 16.2 %all-to-all-start = ((bf16[8,128,128]{2,1,0:T(8,128)(2,1)}), bf16[8,128,128]{2,1,0:T(8,128)(2,1)S(1)}, u32[]{:S(2)}, u32[]{:S(2)}) async-start(bf16[8,128,128]{2,1,0:T(8,128)(2,1)} %forward1.1), calls=%async_computation | async-start | bytes 524288 | tf_op jit(solution)/shard_map/all_to_all | solution.py:279
  11.6 1.6 %copy-start.2 = (bf16[64,128,128]{2,1,0:T(8,128)(2,1)S(1)}, bf16[64,128,128]{2,1,0:T(8,128)(2,1)}, u32[]{:S(2)}) copy-start(bf16[64,128,128]{2,1,0:T(8,128)(2,1)} %sens.1) | copy-start | bytes 6291460
  16.7 1.0 %copy-start = (bf16[2,1024,256]{2,1,0:T(8,128)(2,1)}, bf16[2,1024,256]{2,1,0:T(8,128)(2,1)S(1)}, u32[]{:S(2)}) copy-start(bf16[2,1024,256]{2,1,0:T(8,128)(2,1)S(1)} %get-tuple-element.25.refs_0_.dense_own_b) | copy-start | bytes 3145732
  32.6 3.3 %copy-start.1 = (bf16[2,1024,256]{2,1,0:T(8,128)(2,1)S(1)}, bf16[2,1024,256]{2,1,0:T(8,128)(2,1)}, u32[]{:S(2)}) copy-start(bf16[2,1024,256]{2,1,0:T(8,128)(2,1)} %copy-done) | copy-start | bytes 3145732
  32.9 1.4 %collective-permute-start = (bf16[4,128,128]{2,1,0:T(8,128)(2,1)S(1)}, bf16[4,128,128]{2,1,0:T(8,128)(2,1)S(1)}, u32[]{:S(2)}, u32[]{:S(2)}) collective-permute-start(bf16[4,128,128]{2,1,0:T(8,128)(2,1)S(1)} %adjoint1_give_a.1), channel_id=1, source_target_pairs={{0,8},{8,0},{16,24},{24,16},{1,9},{9,1},{17,25},{25,17},{2,10},{10... | collective-permute-start | bytes 393224 | tf_op jit(solution)/shard_map/ppermute | solution.py:270
  33.0 3.9 %copy-start.3 = (f32[2048,128]{1,0:T(8,128)S(1)}, f32[2048,128]{1,0:T(8,128)}, u32[]{:S(2)}) copy-start(f32[2048,128]{1,0:T(8,128)} %param.10) | copy-start | bytes 3145732
  33.0 3.9 %copy-start.4 = (f32[2048,128]{1,0:T(8,128)S(1)}, f32[2048,128]{1,0:T(8,128)}, u32[]{:S(2)}) copy-start(f32[2048,128]{1,0:T(8,128)} %param.11) | copy-start | bytes 3145732
  33.4 2.8 %collective-permute-start.2 = (bf16[4,128,128]{2,1,0:T(8,128)(2,1)S(1)}, bf16[4,128,128]{2,1,0:T(8,128)(2,1)S(1)}, u32[]{:S(2)}, u32[]{:S(2)}) collective-permute-start(bf16[4,128,128]{2,1,0:T(8,128)(2,1)S(1)} %get-tuple-element.34), channel_id=1, source_target_pairs={{0,8},{8,0},{16,24},{24,16},{1,9},{9,1},{17,25},{25,17},{2,10},{10... | collective-permute-start | bytes 393224 | tf_op jit(solution)/shard_map/ppermute | solution.py:270
  34.3 6.4 %collective-permute-start.1 = (bf16[4,128,128]{2,1,0:T(8,128)(2,1)S(1)}, bf16[4,128,128]{2,1,0:T(8,128)(2,1)S(1)}, u32[]{:S(2)}, u32[]{:S(2)}) collective-permute-start(bf16[4,128,128]{2,1,0:T(8,128)(2,1)S(1)} %adjoint1_pair_a.1.rest_0_), channel_id=1, source_target_pairs={{0,16},{8,24},{16,0},{24,8},{1,17},{9,25},{17,1},{25,9},{2,18},{10... | collective-permute-start | bytes 393224 | tf_op jit(solution)/shard_map/ppermute | solution.py:274
  36.3 6.5 %collective-permute-start.3 = (bf16[4,128,128]{2,1,0:T(8,128)(2,1)S(1)}, bf16[4,128,128]{2,1,0:T(8,128)(2,1)S(1)}, u32[]{:S(2)}, u32[]{:S(2)}) collective-permute-start(bf16[4,128,128]{2,1,0:T(8,128)(2,1)S(1)} %adjoint1_pair_b.1.rest_0_), channel_id=1, source_target_pairs={{0,16},{8,24},{16,0},{24,8},{1,17},{9,25},{17,1},{25,9},{2,18},{10... | collective-permute-start | bytes 393224 | tf_op jit(solution)/shard_map/ppermute | solution.py:274
  40.9 2.1 %collective-permute-start.5 = (bf16[4,128,128]{2,1,0:T(8,128)(2,1)S(1)}, bf16[4,128,128]{2,1,0:T(8,128)(2,1)S(1)}, u32[]{:S(2)}, u32[]{:S(2)}) collective-permute-start(bf16[4,128,128]{2,1,0:T(8,128)(2,1)S(1)} %get-tuple-element.36.own_a), channel_id=1, source_target_pairs={{0,8},{8,0},{16,24},{24,16},{1,9},{9,1},{17,25},{25,17},{2,10},{10... | collective-permute-start | bytes 393224 | tf_op jit(solution)/shard_map/ppermute | solution.py:270
  42.9 1.4 %collective-permute-start.4 = (bf16[4,128,128]{2,1,0:T(8,128)(2,1)S(1)}, bf16[4,128,128]{2,1,0:T(8,128)(2,1)S(1)}, u32[]{:S(2)}, u32[]{:S(2)}) collective-permute-start(bf16[4,128,128]{2,1,0:T(8,128)(2,1)S(1)} %get-tuple-element.35.own_b), channel_id=1, source_target_pairs={{0,8},{8,0},{16,24},{24,16},{1,9},{9,1},{17,25},{25,17},{2,10},{10... | collective-permute-start | bytes 393224 | tf_op jit(solution)/shard_map/ppermute | solution.py:270
  69.7 1.4 %collective-permute-start.6 = (bf16[4,128,128]{2,1,0:T(8,128)(2,1)S(1)}, bf16[4,128,128]{2,1,0:T(8,128)(2,1)S(1)}, u32[]{:S(2)}, u32[]{:S(2)}) collective-permute-start(bf16[4,128,128]{2,1,0:T(8,128)(2,1)S(1)} %adjoint2_give_a.1), channel_id=1, source_target_pairs={{0,8},{8,0},{16,24},{24,16},{1,9},{9,1},{17,25},{25,17},{2,10},{10... | collective-permute-start | bytes 393224 | tf_op jit(solution)/shard_map/ppermute | solution.py:270
  70.3 2.8 %collective-permute-start.8 = (bf16[4,128,128]{2,1,0:T(8,128)(2,1)S(1)}, bf16[4,128,128]{2,1,0:T(8,128)(2,1)S(1)}, u32[]{:S(2)}, u32[]{:S(2)}) collective-permute-start(bf16[4,128,128]{2,1,0:T(8,128)(2,1)S(1)} %get-tuple-element.42), channel_id=1, source_target_pairs={{0,8},{8,0},{16,24},{24,16},{1,9},{9,1},{17,25},{25,17},{2,10},{10... | collective-permute-start | bytes 393224 | tf_op jit(solution)/shard_map/ppermute | solution.py:270
  71.2 6.4 %collective-permute-start.7 = (bf16[4,128,128]{2,1,0:T(8,128)(2,1)S(1)}, bf16[4,128,128]{2,1,0:T(8,128)(2,1)S(1)}, u32[]{:S(2)}, u32[]{:S(2)}) collective-permute-start(bf16[4,128,128]{2,1,0:T(8,128)(2,1)S(1)} %adjoint2_pair_a.1.rest_4_), channel_id=1, source_target_pairs={{0,16},{8,24},{16,0},{24,8},{1,17},{9,25},{17,1},{25,9},{2,18},{10... | collective-permute-start | bytes 393224 | tf_op jit(solution)/shard_map/ppermute | solution.py:274
  73.1 6.5 %collective-permute-start.9 = (bf16[4,128,128]{2,1,0:T(8,128)(2,1)S(1)}, bf16[4,128,128]{2,1,0:T(8,128)(2,1)S(1)}, u32[]{:S(2)}, u32[]{:S(2)}) collective-permute-start(bf16[4,128,128]{2,1,0:T(8,128)(2,1)S(1)} %adjoint2_pair_b.1.rest_0_), channel_id=1, source_target_pairs={{0,16},{8,24},{16,0},{24,8},{1,17},{9,25},{17,1},{25,9},{2,18},{10... | collective-permute-start | bytes 393224 | tf_op jit(solution)/shard_map/ppermute | solution.py:274
  77.7 2.1 %collective-permute-start.10 = (bf16[4,128,128]{2,1,0:T(8,128)(2,1)S(1)}, bf16[4,128,128]{2,1,0:T(8,128)(2,1)S(1)}, u32[]{:S(2)}, u32[]{:S(2)}) collective-permute-start(bf16[4,128,128]{2,1,0:T(8,128)(2,1)S(1)} %total_a.1.own_a), channel_id=1, source_target_pairs={{0,8},{8,0},{16,24},{24,16},{1,9},{9,1},{17,25},{25,17},{2,10},{10... | collective-permute-start | bytes 393224 | tf_op jit(solution)/shard_map/ppermute | solution.py:270
  79.8 1.4 %collective-permute-start.11 = (bf16[4,128,128]{2,1,0:T(8,128)(2,1)S(1)}, bf16[4,128,128]{2,1,0:T(8,128)(2,1)S(1)}, u32[]{:S(2)}, u32[]{:S(2)}) collective-permute-start(bf16[4,128,128]{2,1,0:T(8,128)(2,1)S(1)} %total_b.1.own_b), channel_id=1, source_target_pairs={{0,8},{8,0},{16,24},{24,16},{1,9},{9,1},{17,25},{25,17},{2,10},{10... | collective-permute-start | bytes 393224 | tf_op jit(solution)/shard_map/ppermute | solution.py:270

commit v10 on v9

--- a/solution.py
+++ b/solution.py
@@ -11,7 +11,6 @@
 GROUP = 32
 CHUNKS = 2
 FIRST_VMEM = 55 << 20
-GIVE_A, KEEP_A, GIVE_B, KEEP_B = range(4)
 
 VMEM = pl.BlockSpec(memory_space=pltpu.VMEM)
 SMEM = pl.BlockSpec(memory_space=pltpu.SMEM)
@@ -103,59 +102,68 @@
     out_ref[...] = acc[...].astype(bf16)
 
 
+def sizes_of(pairs):
+    return (pairs // 4,) * 4
+
+
 def dense_kernel(bund, cblk, sens, *rest):
-    out_refs, (token_ref, total) = rest[:4], rest[4:]
+    out_refs, (token_ref, total) = rest[:-2], rest[-2:]
     rays = sens.shape[1]
-    quarter = 2 * total.shape[1]
+    pairs = total.shape[1]
     core = lax.axis_index("shot") % 2
     total[...] = jnp.zeros_like(total)
 
     def place(k, carry):
-        cell = cblk[k]
-        kept = jnp.where(cell // (2 * quarter) == core, 1, 0)
-        part = 2 * (cell // quarter % 2) + kept
+        pair = cblk[k] // 2
+        kept = jnp.where(pair // pairs == core, 1, 0)
         rows = pl.ds(pl.multiple_of(bund[k] * rays, rays), rays)
-        lanes = pl.ds(pl.multiple_of(cell % 2 * CBLK, CBLK), CBLK)
-        total[part, cell % quarter // 2, rows, lanes] += sens[k].astype(f32)
+        lanes = pl.ds(pl.multiple_of(cblk[k] % 2 * CBLK, CBLK), CBLK)
+        total[kept, pair % pairs, rows, lanes] += sens[k].astype(f32)
         return carry
 
     lax.fori_loop(0, sens.shape[0], place, 0)
-    for part, out_ref in zip((KEEP_B, GIVE_A, KEEP_A, GIVE_B), out_refs):
-        out_ref[...] = total[part].astype(bf16)
+    at = 0
+    for p in range(len(out_refs) // 2):
+        size = out_refs[2 * p].shape[0]
+        for kept in range(2):
+            out_refs[2 * p + kept][...] = total[kept, at : at + size].astype(bf16)
+        at += size
     token_ref[...] = jnp.zeros_like(token_ref)
 
 
 def dense_forward(columns, store):
     step = 2 * CBLK
-    pairs = columns[0][0].shape[0]
     probe = jnp.concatenate(
-        [part[...].reshape(2 * CBLK * pairs, -1) for _, part in columns], axis=0
+        [part[...].reshape(CBLK * part.shape[0], -1) for _, part in columns], axis=0
     )
     for m in range(columns[0][0].shape[1] // step):
         rows = pl.ds(m * step, step)
         lhs = jnp.concatenate(
-            [dense[pair, rows, :] for dense, _ in columns for pair in range(pairs)], axis=1
+            [dense[pair, rows, :] for dense, _ in columns for pair in range(dense.shape[0])],
+            axis=1,
         )
         total = jnp.dot(lhs, probe, preferred_element_type=f32)
         store(pl.ds(2 * m, 2), total.reshape(2, CBLK, -1))
 
 
-def early_forward_kernel(dense_own_a, dense_own_b, dense_mate_a, own_a, own_b, mate_a, acc):
+def early_forward_kernel(*refs):
+    acc = refs[-1]
+    count = len(refs) // 2
+
     def store(rows, value):
         acc[rows] = value
 
-    columns = [(dense_own_a, own_a), (dense_own_b, own_b), (dense_mate_a, mate_a)]
-    dense_forward(columns, store)
-
-
-def late_forward_kernel(dense_mate_b, mate_b, early, out_ref):
+    dense_forward(list(zip(refs[:count], refs[count : 2 * count])), store)
+
+
+def late_forward_kernel(dense_last, mate_last, early, out_ref):
     def store(rows, value):
         out_ref[rows] = (early[rows] + value).astype(bf16)
 
-    dense_forward([(dense_mate_b, mate_b)], store)
-
-
-def adjoint_kernel(resid, *refs):
+    dense_forward([(dense_last, mate_last)], store)
+
+
+def adjoint_kernel(resid, after_ref, *refs):
     lhs = jnp.concatenate([resid[m] for m in range(resid.shape[0])], axis=1)
     count = len(refs) // 2
     for dense, out_ref in zip(refs[:count], refs[count:]):
@@ -166,7 +174,7 @@
             out_ref[2 * pair + 1] = both[:, CBLK:]
 
 
-def pair_kernel(keep_ref, got_ref, out_ref):
+def pair_kernel(keep_ref, got_ref, after_ref, out_ref):
     out_ref[...] = (keep_ref[...] + got_ref[...].astype(f32)).astype(bf16)
 
 
@@ -189,12 +197,13 @@
     token_ref[...] = jnp.zeros_like(token_ref)
 
 
-def prepare_kernel(state, prior, after_ref, field_a, field_b, base_ref):
-    quarter = field_a.shape[0]
-    own = lax.axis_index("shot") % 2 * (2 * quarter)
-    for at, field_ref in ((own, field_a), (own + quarter, field_b)):
-        part = pl.ds(at, quarter)
+def prepare_kernel(state, prior, after_ref, *rest):
+    field_refs, base_ref = rest[:-1], rest[-1]
+    at = lax.axis_index("shot") % 2 * (state.shape[0] // 2)
+    for field_ref in field_refs:
+        part = pl.ds(at, field_ref.shape[0])
         field_ref[...] = state[part] + prior[part]
+        at += field_ref.shape[0]
     base_ref[...] = state[...] + 0.5 * prior[...]
 
 
@@ -211,7 +220,7 @@
     return total.T
 
 
-def probe_kernel(ny, field_ref, *rest):
+def probe_kernel(ny, field_ref, after_ref, *rest):
     part_refs, (out_ref, grad_ref, order) = rest[:ny], rest[ny:]
     for i in range(out_ref.shape[0]):
         grad = sum_over_y(lax.axis_index("shot") // 2, part_refs, order, i)
@@ -227,27 +236,34 @@
         out_ref[i] = (grad_ref[i] + grad2).astype(bf16)
 
 
-def early_update_kernel(base, own_a, own_b, mate_a, out_hbm, rest_ref, new, sems):
-    quarter = own_a.shape[0]
+def early_update_kernel(parts, base, *refs):
+    part_refs, (out_hbm, rest_ref, new, sems) = refs[:-4], refs[-4:]
+    half = base.shape[0] // 2
     core = lax.axis_index("shot") % 2
-    own, mate = core * (2 * quarter), (1 - core) * (2 * quarter)
-    copies = []
-    for n, (at, part_ref) in enumerate(((own, own_a), (own + quarter, own_b), (mate, mate_a))):
-        new[n] = base[pl.ds(at, quarter)] - 0.125 * part_ref[...].astype(f32)
+    own, mate = core * half, (1 - core) * half
+    done, copies = 0, []
+    for n, part_ref in enumerate(part_refs):
+        size = part_ref.shape[0]
+        at = own + done if n < parts else mate + done - half
+        new[done : done + size] = base[pl.ds(at, size)] - 0.125 * part_ref[...].astype(f32)
         copies.append(
-            pltpu.make_async_copy(new.at[n], out_hbm.at[pl.ds(at, quarter)], sems.at[n])
+            pltpu.make_async_copy(
+                new.at[pl.ds(done, size)], out_hbm.at[pl.ds(at, size)], sems.at[n]
+            )
         )
         copies[-1].start()
-    rest_ref[...] = base[pl.ds(mate + quarter, quarter)]
+        done += size
+    rest_ref[...] = base[pl.ds(mate + done - half, rest_ref.shape[0])]
     for copy in copies:
         copy.wait()
 
 
-def late_update_kernel(rest_ref, mate_b, so_far_hbm, out_hbm, new, sem):
-    quarter = mate_b.shape[0]
-    at = (1 - lax.axis_index("shot") % 2) * (2 * quarter) + quarter
-    new[...] = rest_ref[...] - 0.125 * mate_b[...].astype(f32)
-    copy = pltpu.make_async_copy(new, out_hbm.at[pl.ds(at, quarter)], sem)
+def late_update_kernel(rest_ref, mate_last, so_far_hbm, out_hbm, new, sem):
+    size = mate_last.shape[0]
+    half = out_hbm.shape[0] // 2
+    at = (2 - lax.axis_index("shot") % 2) * half - size
+    new[...] = rest_ref[...] - 0.125 * mate_last[...].astype(f32)
+    copy = pltpu.make_async_copy(new, out_hbm.at[pl.ds(at, size)], sem)
     copy.start()
     copy.wait()
 
@@ -258,7 +274,8 @@
     owned, rays = observed.shape
     bundles = owned * nband
     cells = state.shape[0] // CBLK
-    quarter = cells // 4
+    sizes = sizes_of(cells // 4)
+    parts = len(sizes)
     ny = nshot // 2
     flops = 2 * nblk * rays * CBLK * samples
     sens_bytes = nblk * rays * CBLK * 2
@@ -279,12 +296,12 @@
         return lax.all_to_all(array, "band", split_axis=0, concat_axis=0, tiled=True)
 
     part_out = arr((bundles, rays, samples), bf16)
-    dense_shape = (quarter // 2, bundles * rays, 2 * CBLK)
+    dense_bf16 = [arr((size, bundles * rays, 2 * CBLK), bf16) for size in sizes]
     small_token = arr((8, CBLK), f32)
     dense_flops = 2 * bundles * rays * cells * CBLK * samples
     dense_bytes = 2 * bundles * rays * cells * CBLK
-    quarter_bf16 = arr((quarter, CBLK, samples), bf16)
-    quarter_f32 = arr((quarter, CBLK, samples), f32)
+    part_bf16 = [arr((2 * size, CBLK, samples), bf16) for size in sizes]
+    part_f32 = [arr((2 * size, CBLK, samples), f32) for size in sizes]
     order = pltpu.VMEM((ny, samples, CBLK), bf16)
 
     def residual(part, after, name, keep):
@@ -298,35 +315,38 @@
         return resid, over_band(copies).reshape(bundles, samples, rays)
 
     def adjoint(dense, resid_all, name):
-        def kernel(parts, part):
+        def kernel(picked, after):
+            share = sum(sizes[p // 2] for p in picked)
             return call(
                 adjoint_kernel,
-                tuple(quarter_f32 if p % 2 else quarter_bf16 for p in parts),
+                tuple(part_f32[p // 2] if p % 2 else part_bf16[p // 2] for p in picked),
                 [],
-                [VMEM] * (1 + len(parts)),
-                name + part,
-                dense_flops * len(parts) // 4,
-                dense_bytes * len(parts) // 4,
-            )(resid_all, *[dense[p] for p in parts])
-
-        def pair(keep, got, part):
-            return call(
+                [VMEM, ANY] + [VMEM] * len(picked),
+                name,
+                dense_flops * 2 * share // cells,
+                dense_bytes * 2 * share // cells,
+            )(resid_all, after, *[dense[p] for p in picked])
+
+        sums = []
+        (give,) = kernel((0,), token)
+        before = token
+        for part in range(parts):
+            got = other_core(give)
+            if part + 1 < parts:
+                keep, give = kernel((2 * part + 1, 2 * part + 2), before if part else give)
+            else:
+                (keep,) = kernel((2 * part + 1,), before)
+            pair = call(
                 pair_kernel,
-                quarter_bf16,
+                part_bf16[part],
                 [],
-                [VMEM] * 2,
-                name + "_pair" + part,
+                [VMEM, VMEM, ANY],
+                name + "_pair",
                 bytes_accessed=1 << 19,
-            )(keep, got)
-
-        (give_a,) = kernel((GIVE_A,), "_give_a")
-        got_a = other_core(give_a)
-        keep_a, give_b = kernel((KEEP_A, GIVE_B), "_keep_a")
-        got_b = other_core(give_b)
-        sums_a = other_chips(pair(keep_a, got_a, "_a"))
-        (keep_b,) = kernel((KEEP_B,), "_keep_b")
-        sums_b = other_chips(pair(keep_b, got_b, "_b"))
-        return sums_a, sums_b, keep_b
+            )(keep, got, before)
+            before = pair
+            sums.append(other_chips(pair))
+        return sums, keep
 
     part1 = call(
         first_forward_kernel,
@@ -347,38 +367,38 @@
         sens_bytes,
         vmem=FIRST_VMEM,
     )(bund, cblk, sens, state_b, prior_b)
-    dense_keep_b, *dense, token = call(
+    *dense, token = call(
         dense_kernel,
-        (arr(dense_shape, bf16),) * 4 + (small_token,),
-        [pltpu.VMEM((4,) + dense_shape, f32)],
+        tuple(d for d in dense_bf16 for _ in range(2)) + (small_token,),
+        [pltpu.VMEM((2, cells // 4, bundles * rays, 2 * CBLK), f32)],
         [SMEM, SMEM, VMEM],
         "dense",
         0,
         16 << 20,
         vmem=3 * dense_bytes + 2 * sens_bytes + (2 << 20),
     )(bund, cblk, sens)
-    dense.append(dense_keep_b)
     _, resid_all1 = residual(part1, token, "residual1", False)
-    *sums1, after = adjoint(dense, resid_all1, "adjoint1")
+    sums1, after = adjoint(dense, resid_all1, "adjoint1")
 
     *fields, base = call(
         prepare_kernel,
-        (quarter_f32, quarter_f32, arr((cells, CBLK, samples), f32)),
+        (*part_f32, arr((cells, CBLK, samples), f32)),
         [],
         [VMEM, VMEM, ANY],
         "prepare",
         bytes_accessed=4 << 20,
     )(state_b, prior_b, after)
-    own, grad1, mate = [], [], []
-    for field, sums, part in zip(fields, sums1, "ab"):
+    own, grad1, mate, before = [], [], [], token
+    for part, (field, sums) in enumerate(zip(fields, sums1)):
         probe, grad = call(
             functools.partial(probe_kernel, ny),
-            (quarter_bf16, quarter_f32),
+            (part_bf16[part], part_f32[part]),
             [order],
-            [VMEM] * (1 + ny),
-            "probe2_" + part,
+            [VMEM, ANY] + [VMEM] * ny,
+            "probe2",
             bytes_accessed=1 << 19,
-        )(field, *sums)
+        )(field, before, *sums)
+        before = probe
         own.append(probe)
         grad1.append(grad)
         mate.append(other_core(probe))
@@ -387,23 +407,23 @@
         early_forward_kernel,
         arr((bundles, rays, samples), f32),
         [],
-        [VMEM] * 6,
+        [VMEM] * (4 * parts - 2),
         "forward2_early",
-        dense_flops * 3 // 4,
-        dense_bytes * 3 // 4,
-    )(dense[KEEP_A], dense[KEEP_B], dense[GIVE_A], own[0], own[1], mate[0])
+        dense_flops * 7 // 8,
+        dense_bytes * 7 // 8,
+    )(*dense[1::2], *dense[0:-2:2], *own, *mate[:-1])
     part2 = call(
         late_forward_kernel,
         part_out,
         [],
         [VMEM] * 3,
         "forward2_late",
-        dense_flops // 4,
-        dense_bytes // 4,
-    )(dense[GIVE_B], mate[1], early)
+        dense_flops // 8,
+        dense_bytes // 8,
+    )(dense[-2], mate[-1], early)
 
     (resid2_t,), resid_all2 = residual(part2, token, "residual2", True)
-    *sums2, _ = adjoint(dense, resid_all2, "adjoint2")
+    sums2, _ = adjoint(dense, resid_all2, "adjoint2")
     resid2, turned = call(
         turn_kernel,
         (arr((owned, rays, samples), f32), small_token),
@@ -412,39 +432,43 @@
         "turn",
         bytes_accessed=1 << 20,
     )(resid2_t)
-    own, mate, after = [], [], [turned, dense[GIVE_A], dense[KEEP_A], dense[GIVE_B]]
-    for grad, sums, part in zip(grad1, sums2, "ab"):
+    own, mate, after = [], [], [turned, *dense[:-1]]
+    for part, (grad, sums) in enumerate(zip(grad1, sums2)):
         total = call(
             functools.partial(total_kernel, ny, len(after)),
-            quarter_bf16,
+            part_bf16[part],
             [order],
             [VMEM] + [ANY] * len(after) + [VMEM] * ny,
-            "total_" + part,
+            "total",
             bytes_accessed=1 << 19,
         )(grad, *after, *sums)
         own.append(total)
-        after = []
+        after = [total]
         mate.append(other_core(total))
     whole = arr((cells, CBLK, samples), f32)
+    last = 2 * sizes[-1]
     so_far, rest = call(
-        early_update_kernel,
-        (whole, quarter_f32),
-        [pltpu.VMEM((3, quarter, CBLK, samples), f32), pltpu.SemaphoreType.DMA((3,))],
-        [VMEM] * 4,
+        functools.partial(early_update_kernel, parts),
+        (whole, part_f32[-1]),
+        [
+            pltpu.VMEM((cells - last, CBLK, samples), f32),
+            pltpu.SemaphoreType.DMA((2 * parts - 1,)),
+        ],
+        [VMEM] * (2 * parts),
         "new_state_early",
         bytes_accessed=3 << 20,
         out_specs=(HBM, VMEM),
-    )(base, own[0], own[1], mate[0])
+    )(base, *own, *mate[:-1])
     new_state = call(
         late_update_kernel,
         whole,
-        [pltpu.VMEM((quarter, CBLK, samples), f32), pltpu.SemaphoreType.DMA],
+        [pltpu.VMEM((last, CBLK, samples), f32), pltpu.SemaphoreType.DMA],
         [VMEM, VMEM, HBM],
         "new_state_late",
         bytes_accessed=1 << 20,
         out_specs=HBM,
         input_output_aliases={2: 0},
-    )(rest, mate[1], so_far)
+    )(rest, mate[-1], so_far)
     return new_state.reshape(state.shape), resid2
 
 

time: 82.3 us -> 85 us (1.033)
  starting transfers between devices: 13.1 us -> 19.2 us
  waiting for transfers between devices: 14.7 us -> 9.85 us
    ppermute x4 -> x8, waiting for transfers between devices: 10.5 us -> 5.47 us  [other_chips(): lax.ppermute(array, 'shot', [(i, i ^ 2 * d) for i in range(nshot)])]
    ppermute x4 -> x8, starting transfers between devices: 4.32 us -> 8.36 us  [other_chips(): lax.ppermute(array, 'shot', [(i, i ^ 2 * d) for i in range(nshot)])]
    ppermute x8 -> x16, starting transfers between devices: 1.52 us -> 3.59 us  [other_core(): return lax.ppermute(array, 'shot', [(i, i ^ 1) for i in range(nshot)])]
    unnamed x18 -> x22, local copies, waits for them, and re-layouts: 2.59 us -> 3.21 us
    pallas_call x18 -> x30, Pallas kernels: 8.07 us -> 8.68 us  [the longest x1 3.1 us: per_device(): call(dense_kernel, tuple((d for d in dense_bf16 for _ in range(2))) + (sm...]
    ppermute x8 -> x16, waiting for transfers between devices: 1.38 us -> 1.78 us  [other_core(): return lax.ppermute(array, 'shot', [(i, i ^ 1) for i in range(nshot)])]
  transfers between devices with their start and end apart: 13 -> 25, of which waited for: 9 -> 11; matrix products, arithmetic and copies ran while one was open for 0% -> 0% of each run, Pallas kernels for 10% -> 11%
where the time goes in v10:
time: 85 us; the launch traced here: 84.6 us
  blocking collectives  36.5 us (43%)
  starting transfers between devices  19.2 us (23%)
  Pallas kernels  14.7 us (17%)
  waiting for transfers between devices  9.85 us (12%)
  local copies, waits for them, and re-layouts  3.21 us (4%)
  between operations  1.12 us (1%)
    all_to_all x3, blocking collectives, over_band(): lax.all_to_all(array, 'band', split_axis=0, concat_axis=0, tiled=True)  36.5 us
    ppermute x8, starting transfers between devices, other_chips(): lax.ppermute(array, 'shot', [(i, i ^ 2 * d) for i in range(nshot)])  8.36 us
    all_to_all x1, starting transfers between devices, over_band(): lax.all_to_all(array, 'band', split_axis=0, concat_axis=0, tiled=True)  7.27 us
    ppermute x8, waiting for transfers between devices, other_chips(): lax.ppermute(array, 'shot', [(i, i ^ 2 * d) for i in range(nshot)])  5.47 us
    pallas_call x1, Pallas kernels, per_device(): call(first_forward_kernel, part_out, [pltpu.VMEM((bundles, rays, samples)...  3.65 us
    ppermute x16, starting transfers between devices, other_core(): return lax.ppermute(array, 'shot', [(i, i ^ 1) for i in range(nshot)])  3.59 us
    unnamed x22, local copies, waits for them, and re-layouts  3.21 us
    pallas_call x1, Pallas kernels, per_device(): call(dense_kernel, tuple((d for d in dense_bf16 for _ in range(2))) + (sm...  3.1 us
  transfers between devices with their start and end apart: 25, of which 11 were waited for; matrix products, arithmetic and copies ran while one was open for 0% of the time, Pallas kernels for 11%

profile of v10, /device:TPU:0, one launch (start us, length us, event | category | flops | bytes accessed | tf_op | source)
XLA Modules:
  0.0 84.6 jit_solution(8557520788246561578)
XLA Ops:
  0.6 3.6 %forward1.1 = bf16[8,128,128]{2,1,0:T(8,128)(2,1)} custom-call(s32[64]{0:T(128)} %bund.1, s32[64]{0:T(128)} %cblk.1, bf16[64,128,128]{2,1,0:T(8,128)(2,1)} %sens.1, f32[16,128,128]{2,1,0:T(8,128)} %bitcast.17, f32[16,128,128]{2,1,0:T(8,128)} %bitcast.19), custom_call_target="tpu_custom_call" | custom-call | flops 268435456 | bytes 2097152 | tf_op jit(solution)/shard_map/forward1/pallas_call | solution.py:351
  4.3 7.3 %all-to-all-start = ((bf16[8,128,128]{2,1,0:T(8,128)(2,1)}), bf16[8,128,128]{2,1,0:T(8,128)(2,1)S(1)}, u32[]{:S(2)}, u32[]{:S(2)}) async-start(bf16[8,128,128]{2,1,0:T(8,128)(2,1)} %forward1.1), calls=%async_computation | async-start | bytes 524288 | tf_op jit(solution)/shard_map/all_to_all | solution.py:296
  11.6 1.6 %copy-done = bf16[64,128,128]{2,1,0:T(8,128)(2,1)S(1)} copy-done((bf16[64,128,128]{2,1,0:T(8,128)(2,1)S(1)}, bf16[64,128,128]{2,1,0:T(8,128)(2,1)}, u32[]{:S(2)}) %copy-start) | copy-done | bytes 2097176
  13.2 3.1 %dense.1 = (bf16[1,1024,256]{2,1,0:T(8,128)(2,1)S(1)}, bf16[1,1024,256]{2,1,0:T(8,128)(2,1)S(1)}, bf16[1,1024,256]{2,1,0:T(8,128)(2,1)S(1)}, bf16[1,1024,256]{2,...) custom-call(s32[64]{0:T(128)S(1)} %copy-done.9, ...), custom_call_target="tpu_custom_call" | custom-call | bytes 16777216 | tf_op jit(solution)/shard_map/dense/pallas_call | solution.py:370
  16.3 0.8 copy-done.1
  17.1 0.8 copy-done.3
  17.9 2.6 %all-to-all-done = bf16[8,128,128]{2,1,0:T(8,128)(2,1)S(1)} async-done(((bf16[8,128,128]{2,1,0:T(8,128)(2,1)}), bf16[8,128,128]{2,1,0:T(8,128)(2,1)S(1)}, u32[]{:S(2)}, u32[]{:S(2)}) %all-to-all-start) | async-done | bytes 262176 | tf_op jit(solution)/shard_map/all_to_all | solution.py:296
  20.6 12.0 %all_to_all.20 = bf16[8,1,128,128]{3,2,1,0:T(8,128)(2,1)S(1)} all-to-all(bf16[8,1,128,128]{3,2,1,0:T(8,128)(2,1)S(1)} %residual1.1), channel_id=1, replica_groups=mesh['shot'=4,'band'=8] {'band'}, dimensions={0} | all-to-all | bytes 524288 | tf_op jit(solution)/shard_map/all_to_all | solution.py:296
  33.2 0.6 collective-permute-start.1
  35.5 1.5 %collective-permute-start.3 = (bf16[2,128,128]{2,1,0:T(8,128)(2,1)S(1)}, bf16[2,128,128]{2,1,0:T(8,128)(2,1)S(1)}, u32[]{:S(2)}, u32[]{:S(2)}) collective-permute-start(bf16[2,128,128]{2,1,0:T(8,128)(2,1)S(1)} %adjoint1_pair.4.after_ref.rest_0_), channel_id=1, source_target_pairs={{0,16},{8,24},{16,0},{24,8},{1,17},{9,25},{17,1},{25,9},{2,18},{10... | collective-permute-start | bytes 196616 | tf_op jit(solution)/shard_map/ppermute | solution.py:291
  37.5 1.6 %collective-permute-start.5 = (bf16[2,128,128]{2,1,0:T(8,128)(2,1)S(1)}, bf16[2,128,128]{2,1,0:T(8,128)(2,1)S(1)}, u32[]{:S(2)}, u32[]{:S(2)}) collective-permute-start(bf16[2,128,128]{2,1,0:T(8,128)(2,1)S(1)} %adjoint1_pair.6.after_ref.rest_0_), channel_id=1, source_target_pairs={{0,16},{8,24},{16,0},{24,8},{1,17},{9,25},{17,1},{25,9},{2,18},{10... | collective-permute-start | bytes 196616 | tf_op jit(solution)/shard_map/ppermute | solution.py:291
  39.4 0.5 collective-permute-start.7
  40.4 1.7 %collective-permute-done.4.rest_1_ = bf16[2,128,128]{2,1,0:T(8,128)(2,1)S(1)} collective-permute-done((bf16[2,128,128]{2,1,0:T(8,128)(2,1)S(1)}, bf16[2,128,128]{2,1,0:T(8,128)(2,1)S(1)}, u32[]{:S(2)}, u32[]{:S(2)}) %collective-permute-start.4) | collective-permute-done | bytes 65568 | tf_op jit(solution)/shard_map/ppermute | solution.py:291
  42.2 1.1 %collective-permute-done.5.rest_1_ = bf16[2,128,128]{2,1,0:T(8,128)(2,1)S(1)} collective-permute-done((bf16[2,128,128]{2,1,0:T(8,128)(2,1)S(1)}, bf16[2,128,128]{2,1,0:T(8,128)(2,1)S(1)}, u32[]{:S(2)}, u32[]{:S(2)}) %collective-permute-start.5) | collective-permute-done | bytes 65568 | tf_op jit(solution)/shard_map/ppermute | solution.py:291
  43.5 0.5 collective-permute-done.7.rest_1_
  44.2 0.5 collective-permute-done.11.refs_13_
  44.7 1.1 %forward2_early.1.early = f32[8,128,128]{2,1,0:T(8,128)S(1)} custom-call(bf16[1,1024,256]{2,1,0:T(8,128)(2,1)S(1)} %get-tuple-element.44.refs_0_.rest_2_, bf16[1,1024,256]{2,1,0:T(8,128)(2,1)S(1)} %get-tuple-element.47.refs_0_.refs_1_.rest_4_, bf16[1,1024,256]{2,1,0:T(8,128)(2,1)S(1)} %get-tuple-element.51.refs_0_.refs_2_.rest_6_, ...), custom_call_target="tpu_custom_call" | custom-call | flops 469762048 | bytes 3670016 | tf_op jit(solution)/shard_map/forward2_early/pallas_call | solution.py:406
  46.1 12.6 %all_to_all.21 = bf16[8,128,128]{2,1,0:T(8,128)(2,1)S(1)} all-to-all(bf16[8,128,128]{2,1,0:T(8,128)(2,1)S(1)} %forward2_late.1), channel_id=1, replica_groups=mesh['shot'=4,'band'=8] {'band'}, dimensions={0} | all-to-all | bytes 524288 | tf_op jit(solution)/shard_map/all_to_all | solution.py:296
  58.9 12.0 %all_to_all.22 = bf16[8,1,128,128]{3,2,1,0:T(8,128)(2,1)S(1)} all-to-all(bf16[8,1,128,128]{3,2,1,0:T(8,128)(2,1)S(1)} %get-tuple-element.69), channel_id=1, replica_groups=mesh['shot'=4,'band'=8] {'band'}, dimensions={0} | all-to-all | bytes 524288 | tf_op jit(solution)/shard_map/all_to_all | solution.py:296
  71.4 0.6 collective-permute-start.14
  73.7 1.4 %collective-permute-start.15 = (bf16[2,128,128]{2,1,0:T(8,128)(2,1)S(1)}, bf16[2,128,128]{2,1,0:T(8,128)(2,1)S(1)}, u32[]{:S(2)}, u32[]{:S(2)}) collective-permute-start(bf16[2,128,128]{2,1,0:T(8,128)(2,1)S(1)} %adjoint2_pair.5.rest_1_.after_ref), channel_id=1, source_target_pairs={{0,16},{8,24},{16,0},{24,8},{1,17},{9,25},{17,1},{25,9},{2,18},{10... | collective-permute-start | bytes 196616 | tf_op jit(solution)/shard_map/ppermute | solution.py:291
  75.1 0.6 collective-permute-start.13
  75.7 1.5 %collective-permute-start.17 = (bf16[2,128,128]{2,1,0:T(8,128)(2,1)S(1)}, bf16[2,128,128]{2,1,0:T(8,128)(2,1)S(1)}, u32[]{:S(2)}, u32[]{:S(2)}) collective-permute-start(bf16[2,128,128]{2,1,0:T(8,128)(2,1)S(1)} %adjoint2_pair.6.rest_1_.after_ref), channel_id=1, source_target_pairs={{0,16},{8,24},{16,0},{24,8},{1,17},{9,25},{17,1},{25,9},{2,18},{10... | collective-permute-start | bytes 196616 | tf_op jit(solution)/shard_map/ppermute | solution.py:291
  77.5 0.7 collective-permute-start.19
  78.2 0.7 turn.1
  78.9 1.2 %collective-permute-done.13.rest_9_ = bf16[2,128,128]{2,1,0:T(8,128)(2,1)S(1)} collective-permute-done((bf16[2,128,128]{2,1,0:T(8,128)(2,1)S(1)}, bf16[2,128,128]{2,1,0:T(8,128)(2,1)S(1)}, u32[]{:S(2)}, u32[]{:S(2)}) %collective-permute-start.13) | collective-permute-done | bytes 65568 | tf_op jit(solution)/shard_map/ppermute | solution.py:291
  80.4 0.6 collective-permute-start.21
  80.9 0.5 collective-permute-done.17.rest_2_
  81.7 0.5 collective-permute-done.19.rest_2_
  82.4 0.5 collective-permute-done.22.refs_6_
  82.9 1.0 %new_state_early.1 = (f32[16,128,128]{2,1,0:T(8,128)}, f32[2,128,128]{2,1,0:T(8,128)S(1)}) custom-call(f32[16,128,128]{2,1,0:T(8,128)S(1)} %get-tuple-element.56.base, bf16[2,128,128]{2,1,0:T(8,128)(2,1)S(1)} %total.4.rest_0_.refs_0_, bf16[2,128,128]{2,1,0:T(8,128)(2,1)S(1)} %total.5.rest_0_.refs_1_, bf16[2,128,128]{2,1,0:T(8,128)(2,1)S(1)} %total.6.rest_0_.refs_2_, ...), custom_call_target="tpu_custom_call" | custom-call | bytes 3145728 | tf_op jit(solution)/shard_map/new_state_early/pallas_call | solution.py:450
  83.9 0.7 new_state_late.1
  (79 shorter events, 7.6 us)
Async XLA Ops:
  0.6 11.0 %copy-start.9 = (s32[64]{0:T(128)S(1)}, s32[64]{0:T(128)}, u32[]{:S(2)}) copy-start(s32[64]{0:T(128)} %bund.1) | copy-start | bytes 772
  0.6 11.0 %copy-start.10 = (s32[64]{0:T(128)S(1)}, s32[64]{0:T(128)}, u32[]{:S(2)}) copy-start(s32[64]{0:T(128)} %cblk.1) | copy-start | bytes 772
  4.3 16.2 %copy-start.7 = (f32[1,128]{1,0:T(1,128)S(1)}, f32[1,128]{1,0:T(1,128)}, u32[]{:S(2)}) copy-start(f32[1,128]{1,0:T(1,128)} %obs_ref.3) | copy-start | bytes 1540
  4.3 16.2 %copy-start.8 = (f32[1,128]{1,0:T(1,128)S(1)}, f32[1,128]{1,0:T(1,128)}, u32[]{:S(2)}) copy-start(f32[1,128]{1,0:T(1,128)} %wt_ref.3) | copy-start | bytes 1540
  4.3 16.2 %all-to-all-start = ((bf16[8,128,128]{2,1,0:T(8,128)(2,1)}), bf16[8,128,128]{2,1,0:T(8,128)(2,1)S(1)}, u32[]{:S(2)}, u32[]{:S(2)}) async-start(bf16[8,128,128]{2,1,0:T(8,128)(2,1)} %forward1.1), calls=%async_computation | async-start | bytes 524288 | tf_op jit(solution)/shard_map/all_to_all | solution.py:296
  32.8 1.3 %collective-permute-start = (bf16[2,128,128]{2,1,0:T(8,128)(2,1)S(1)}, bf16[2,128,128]{2,1,0:T(8,128)(2,1)S(1)}, u32[]{:S(2)}, u32[]{:S(2)}) collective-permute-start(bf16[2,128,128]{2,1,0:T(8,128)(2,1)S(1)} %adjoint1.5.after_ref), channel_id=1, source_target_pairs={{0,8},{8,0},{16,24},{24,16},{1,9},{9,1},{17,25},{25,17},{2,10},{10... | collective-permute-start | bytes 196616 | tf_op jit(solution)/shard_map/ppermute | solution.py:287
  33.2 5.9 %copy-start.4 = (bf16[1,1024,256]{2,1,0:T(8,128)(2,1)S(1)}, bf16[1,1024,256]{2,1,0:T(8,128)(2,1)}, u32[]{:S(2)}) copy-start(bf16[1,1024,256]{2,1,0:T(8,128)(2,1)} %copy-done.3) | copy-start | bytes 1572868
  33.2 1.5 %collective-permute-start.1 = (bf16[2,128,128]{2,1,0:T(8,128)(2,1)S(1)}, bf16[2,128,128]{2,1,0:T(8,128)(2,1)S(1)}, u32[]{:S(2)}, u32[]{:S(2)}) collective-permute-start(bf16[2,128,128]{2,1,0:T(8,128)(2,1)S(1)} %get-tuple-element.50), channel_id=1, source_target_pairs={{0,8},{8,0},{16,24},{24,16},{1,9},{9,1},{17,25},{25,17},{2,10},{10... | collective-permute-start | bytes 196616 | tf_op jit(solution)/shard_map/ppermute | solution.py:287
  34.2 5.8 %copy-start.5 = (f32[2048,128]{1,0:T(8,128)S(1)}, f32[2048,128]{1,0:T(8,128)}, u32[]{:S(2)}) copy-start(f32[2048,128]{1,0:T(8,128)} %param.10) | copy-start | bytes 3145732
  34.2 5.8 %copy-start.6 = (f32[2048,128]{1,0:T(8,128)S(1)}, f32[2048,128]{1,0:T(8,128)}, u32[]{:S(2)}) copy-start(f32[2048,128]{1,0:T(8,128)} %param.11) | copy-start | bytes 3145732
  34.5 3.0 %collective-permute-start.2 = (bf16[2,128,128]{2,1,0:T(8,128)(2,1)S(1)}, bf16[2,128,128]{2,1,0:T(8,128)(2,1)S(1)}, u32[]{:S(2)}, u32[]{:S(2)}) collective-permute-start(bf16[2,128,128]{2,1,0:T(8,128)(2,1)S(1)} %get-tuple-element.54), channel_id=1, source_target_pairs={{0,8},{8,0},{16,24},{24,16},{1,9},{9,1},{17,25},{25,17},{2,10},{10... | collective-permute-start | bytes 196616 | tf_op jit(solution)/shard_map/ppermute | solution.py:287
  35.1 4.3 %collective-permute-start.6 = (bf16[2,128,128]{2,1,0:T(8,128)(2,1)S(1)}, bf16[2,128,128]{2,1,0:T(8,128)(2,1)S(1)}, u32[]{:S(2)}, u32[]{:S(2)}) collective-permute-start(bf16[2,128,128]{2,1,0:T(8,128)(2,1)S(1)} %get-tuple-element.65), channel_id=1, source_target_pairs={{0,8},{8,0},{16,24},{24,16},{1,9},{9,1},{17,25},{25,17},{2,10},{10... | collective-permute-start | bytes 196616 | tf_op jit(solution)/shard_map/ppermute | solution.py:287
  35.5 4.7 %collective-permute-start.3 = (bf16[2,128,128]{2,1,0:T(8,128)(2,1)S(1)}, bf16[2,128,128]{2,1,0:T(8,128)(2,1)S(1)}, u32[]{:S(2)}, u32[]{:S(2)}) collective-permute-start(bf16[2,128,128]{2,1,0:T(8,128)(2,1)S(1)} %adjoint1_pair.4.after_ref.rest_0_), channel_id=1, source_target_pairs={{0,16},{8,24},{16,0},{24,8},{1,17},{9,25},{17,1},{25,9},{2,18},{10... | collective-permute-start | bytes 196616 | tf_op jit(solution)/shard_map/ppermute | solution.py:291
  37.0 5.0 %collective-permute-start.4 = (bf16[2,128,128]{2,1,0:T(8,128)(2,1)S(1)}, bf16[2,128,128]{2,1,0:T(8,128)(2,1)S(1)}, u32[]{:S(2)}, u32[]{:S(2)}) collective-permute-start(bf16[2,128,128]{2,1,0:T(8,128)(2,1)S(1)} %adjoint1_pair.5.after_ref.rest_0_), channel_id=1, source_target_pairs={{0,16},{8,24},{16,0},{24,8},{1,17},{9,25},{17,1},{25,9},{2,18},{10... | collective-permute-start | bytes 196616 | tf_op jit(solution)/shard_map/ppermute | solution.py:291
  37.5 5.7 %collective-permute-start.5 = (bf16[2,128,128]{2,1,0:T(8,128)(2,1)S(1)}, bf16[2,128,128]{2,1,0:T(8,128)(2,1)S(1)}, u32[]{:S(2)}, u32[]{:S(2)}) collective-permute-start(bf16[2,128,128]{2,1,0:T(8,128)(2,1)S(1)} %adjoint1_pair.6.after_ref.rest_0_), channel_id=1, source_target_pairs={{0,16},{8,24},{16,0},{24,8},{1,17},{9,25},{17,1},{25,9},{2,18},{10... | collective-permute-start | bytes 196616 | tf_op jit(solution)/shard_map/ppermute | solution.py:291
  39.4 4.5 %collective-permute-start.7 = (bf16[2,128,128]{2,1,0:T(8,128)(2,1)S(1)}, bf16[2,128,128]{2,1,0:T(8,128)(2,1)S(1)}, u32[]{:S(2)}, u32[]{:S(2)}) collective-permute-start(bf16[2,128,128]{2,1,0:T(8,128)(2,1)S(1)} %adjoint1_pair.7.rest_0_), channel_id=1, source_target_pairs={{0,16},{8,24},{16,0},{24,8},{1,17},{9,25},{17,1},{25,9},{2,18},{10... | collective-permute-start | bytes 196616 | tf_op jit(solution)/shard_map/ppermute | solution.py:291
  40.3 3.9 %collective-permute-start.9 = (bf16[2,128,128]{2,1,0:T(8,128)(2,1)S(1)}, bf16[2,128,128]{2,1,0:T(8,128)(2,1)S(1)}, u32[]{:S(2)}, u32[]{:S(2)}) collective-permute-start(bf16[2,128,128]{2,1,0:T(8,128)(2,1)S(1)} %get-tuple-element.62.after_ref.refs_7_), channel_id=1, source_target_pairs={{0,8},{8,0},{16,24},{24,16},{1,9},{9,1},{17,25},{25,17},{2,10},{10... | collective-permute-start | bytes 196616 | tf_op jit(solution)/shard_map/ppermute | solution.py:287
  42.1 2.0 %collective-permute-start.10 = (bf16[2,128,128]{2,1,0:T(8,128)(2,1)S(1)}, bf16[2,128,128]{2,1,0:T(8,128)(2,1)S(1)}, u32[]{:S(2)}, u32[]{:S(2)}) collective-permute-start(bf16[2,128,128]{2,1,0:T(8,128)(2,1)S(1)} %get-tuple-element.63.after_ref.refs_8_), channel_id=1, source_target_pairs={{0,8},{8,0},{16,24},{24,16},{1,9},{9,1},{17,25},{25,17},{2,10},{10... | collective-permute-start | bytes 196616 | tf_op jit(solution)/shard_map/ppermute | solution.py:287
  43.4 1.3 %collective-permute-start.11 = (bf16[2,128,128]{2,1,0:T(8,128)(2,1)S(1)}, bf16[2,128,128]{2,1,0:T(8,128)(2,1)S(1)}, u32[]{:S(2)}, u32[]{:S(2)}) collective-permute-start(bf16[2,128,128]{2,1,0:T(8,128)(2,1)S(1)} %get-tuple-element.64.after_ref.refs_9_), channel_id=1, source_target_pairs={{0,8},{8,0},{16,24},{24,16},{1,9},{9,1},{17,25},{25,17},{2,10},{10... | collective-permute-start | bytes 196616 | tf_op jit(solution)/shard_map/ppermute | solution.py:287
  44.1 1.7 %collective-permute-start.8 = (bf16[2,128,128]{2,1,0:T(8,128)(2,1)S(1)}, bf16[2,128,128]{2,1,0:T(8,128)(2,1)S(1)}, u32[]{:S(2)}, u32[]{:S(2)}) collective-permute-start(bf16[2,128,128]{2,1,0:T(8,128)(2,1)S(1)} %get-tuple-element.66.refs_10_), channel_id=1, source_target_pairs={{0,8},{8,0},{16,24},{24,16},{1,9},{9,1},{17,25},{25,17},{2,10},{10... | collective-permute-start | bytes 196616 | tf_op jit(solution)/shard_map/ppermute | solution.py:287
  71.1 1.3 %collective-permute-start.12 = (bf16[2,128,128]{2,1,0:T(8,128)(2,1)S(1)}, bf16[2,128,128]{2,1,0:T(8,128)(2,1)S(1)}, u32[]{:S(2)}, u32[]{:S(2)}) collective-permute-start(bf16[2,128,128]{2,1,0:T(8,128)(2,1)S(1)} %adjoint2.5.after_ref), channel_id=1, source_target_pairs={{0,8},{8,0},{16,24},{24,16},{1,9},{9,1},{17,25},{25,17},{2,10},{10... | collective-permute-start | bytes 196616 | tf_op jit(solution)/shard_map/ppermute | solution.py:287
  71.4 1.5 %collective-permute-start.14 = (bf16[2,128,128]{2,1,0:T(8,128)(2,1)S(1)}, bf16[2,128,128]{2,1,0:T(8,128)(2,1)S(1)}, u32[]{:S(2)}, u32[]{:S(2)}) collective-permute-start(bf16[2,128,128]{2,1,0:T(8,128)(2,1)S(1)} %get-tuple-element.73), channel_id=1, source_target_pairs={{0,8},{8,0},{16,24},{24,16},{1,9},{9,1},{17,25},{25,17},{2,10},{10... | collective-permute-start | bytes 196616 | tf_op jit(solution)/shard_map/ppermute | solution.py:287
  72.7 3.0 %collective-permute-start.16 = (bf16[2,128,128]{2,1,0:T(8,128)(2,1)S(1)}, bf16[2,128,128]{2,1,0:T(8,128)(2,1)S(1)}, u32[]{:S(2)}, u32[]{:S(2)}) collective-permute-start(bf16[2,128,128]{2,1,0:T(8,128)(2,1)S(1)} %get-tuple-element.76), channel_id=1, source_target_pairs={{0,8},{8,0},{16,24},{24,16},{1,9},{9,1},{17,25},{25,17},{2,10},{10... | collective-permute-start | bytes 196616 | tf_op jit(solution)/shard_map/ppermute | solution.py:287
  73.3 4.2 %collective-permute-start.18 = (bf16[2,128,128]{2,1,0:T(8,128)(2,1)S(1)}, bf16[2,128,128]{2,1,0:T(8,128)(2,1)S(1)}, u32[]{:S(2)}, u32[]{:S(2)}) collective-permute-start(bf16[2,128,128]{2,1,0:T(8,128)(2,1)S(1)} %get-tuple-element.78), channel_id=1, source_target_pairs={{0,8},{8,0},{16,24},{24,16},{1,9},{9,1},{17,25},{25,17},{2,10},{10... | collective-permute-start | bytes 196616 | tf_op jit(solution)/shard_map/ppermute | solution.py:287
  73.7 6.6 %collective-permute-start.15 = (bf16[2,128,128]{2,1,0:T(8,128)(2,1)S(1)}, bf16[2,128,128]{2,1,0:T(8,128)(2,1)S(1)}, u32[]{:S(2)}, u32[]{:S(2)}) collective-permute-start(bf16[2,128,128]{2,1,0:T(8,128)(2,1)S(1)} %adjoint2_pair.5.rest_1_.after_ref), channel_id=1, source_target_pairs={{0,16},{8,24},{16,0},{24,8},{1,17},{9,25},{17,1},{25,9},{2,18},{10... | collective-permute-start | bytes 196616 | tf_op jit(solution)/shard_map/ppermute | solution.py:291
  75.1 5.0 %collective-permute-start.13 = (bf16[2,128,128]{2,1,0:T(8,128)(2,1)S(1)}, bf16[2,128,128]{2,1,0:T(8,128)(2,1)S(1)}, u32[]{:S(2)}, u32[]{:S(2)}) collective-permute-start(bf16[2,128,128]{2,1,0:T(8,128)(2,1)S(1)} %adjoint2_pair.4.rest_8_.after_ref), channel_id=1, source_target_pairs={{0,16},{8,24},{16,0},{24,8},{1,17},{9,25},{17,1},{25,9},{2,18},{10... | collective-permute-start | bytes 196616 | tf_op jit(solution)/shard_map/ppermute | solution.py:291
  75.7 5.7 %collective-permute-start.17 = (bf16[2,128,128]{2,1,0:T(8,128)(2,1)S(1)}, bf16[2,128,128]{2,1,0:T(8,128)(2,1)S(1)}, u32[]{:S(2)}, u32[]{:S(2)}) collective-permute-start(bf16[2,128,128]{2,1,0:T(8,128)(2,1)S(1)} %adjoint2_pair.6.rest_1_.after_ref), channel_id=1, source_target_pairs={{0,16},{8,24},{16,0},{24,8},{1,17},{9,25},{17,1},{25,9},{2,18},{10... | collective-permute-start | bytes 196616 | tf_op jit(solution)/shard_map/ppermute | solution.py:291
  77.5 4.7 %collective-permute-start.19 = (bf16[2,128,128]{2,1,0:T(8,128)(2,1)S(1)}, bf16[2,128,128]{2,1,0:T(8,128)(2,1)S(1)}, u32[]{:S(2)}, u32[]{:S(2)}) collective-permute-start(bf16[2,128,128]{2,1,0:T(8,128)(2,1)S(1)} %adjoint2_pair.7.rest_1_), channel_id=1, source_target_pairs={{0,16},{8,24},{16,0},{24,8},{1,17},{9,25},{17,1},{25,9},{2,18},{10... | collective-permute-start | bytes 196616 | tf_op jit(solution)/shard_map/ppermute | solution.py:291
  80.2 2.2 %collective-permute-start.20 = (bf16[2,128,128]{2,1,0:T(8,128)(2,1)S(1)}, bf16[2,128,128]{2,1,0:T(8,128)(2,1)S(1)}, u32[]{:S(2)}, u32[]{:S(2)}) collective-permute-start(bf16[2,128,128]{2,1,0:T(8,128)(2,1)S(1)} %total.4.rest_0_.refs_0_), channel_id=1, source_target_pairs={{0,8},{8,0},{16,24},{24,16},{1,9},{9,1},{17,25},{25,17},{2,10},{10... | collective-permute-start | bytes 196616 | tf_op jit(solution)/shard_map/ppermute | solution.py:287
  80.4 2.0 %collective-permute-start.21 = (bf16[2,128,128]{2,1,0:T(8,128)(2,1)S(1)}, bf16[2,128,128]{2,1,0:T(8,128)(2,1)S(1)}, u32[]{:S(2)}, u32[]{:S(2)}) collective-permute-start(bf16[2,128,128]{2,1,0:T(8,128)(2,1)S(1)} %total.5.rest_0_.refs_1_), channel_id=1, source_target_pairs={{0,8},{8,0},{16,24},{24,16},{1,9},{9,1},{17,25},{25,17},{2,10},{10... | collective-permute-start | bytes 196616 | tf_op jit(solution)/shard_map/ppermute | solution.py:287
  81.6 1.3 %collective-permute-start.22 = (bf16[2,128,128]{2,1,0:T(8,128)(2,1)S(1)}, bf16[2,128,128]{2,1,0:T(8,128)(2,1)S(1)}, u32[]{:S(2)}, u32[]{:S(2)}) collective-permute-start(bf16[2,128,128]{2,1,0:T(8,128)(2,1)S(1)} %total.6.rest_0_.refs_2_), channel_id=1, source_target_pairs={{0,8},{8,0},{16,24},{24,16},{1,9},{9,1},{17,25},{25,17},{2,10},{10... | collective-permute-start | bytes 196616 | tf_op jit(solution)/shard_map/ppermute | solution.py:287
  82.3 1.6 %collective-permute-start.23 = (bf16[2,128,128]{2,1,0:T(8,128)(2,1)S(1)}, bf16[2,128,128]{2,1,0:T(8,128)(2,1)S(1)}, u32[]{:S(2)}, u32[]{:S(2)}) collective-permute-start(bf16[2,128,128]{2,1,0:T(8,128)(2,1)S(1)} %total.7.refs_3_), channel_id=1, source_target_pairs={{0,8},{8,0},{16,24},{24,16},{1,9},{9,1},{17,25},{25,17},{2,10},{10... | collective-permute-start | bytes 196616 | tf_op jit(solution)/shard_map/ppermute | solution.py:287
  (4 other events, 5.4 us)

commit v11 on v10

--- a/solution.py
+++ b/solution.py
@@ -75,7 +75,7 @@
         part = pl.ds(c * step, step)
         return pltpu.make_async_copy(sens_hbm.at[part], sens.at[part], sems.at[6 + c])
 
-    for copy in small + fields[0] + fields[1] + [block_copy(c) for c in range(CHUNKS)]:
+    for copy in small + fields[0] + fields[1] + [block_copy(0)]:
         copy.start()
     acc[...] = jnp.zeros_like(acc)
 
@@ -83,6 +83,9 @@
         part = pl.ds(h * half, half)
         for copy in fields[h]:
             copy.wait()
+        if h == 0:
+            for c in range(1, CHUNKS):
+                block_copy(c).start()
         probe[part] = (state[part] + 0.5 * prior[part]).astype(bf16)
     for copy in small:
         copy.wait()
@@ -103,7 +106,7 @@
 
 
 def sizes_of(pairs):
-    return (pairs // 4,) * 4
+    return (pairs - 2 * (pairs // 4), pairs // 4, pairs // 4)
 
 
 def dense_kernel(bund, cblk, sens, *rest):
@@ -327,26 +330,23 @@
                 dense_bytes * 2 * share // cells,
             )(resid_all, after, *[dense[p] for p in picked])
 
-        sums = []
         (give,) = kernel((0,), token)
-        before = token
+        got = [other_core(give)]
+        first, *gives = kernel((1,) + tuple(range(2, 2 * parts, 2)), give)
+        got += [other_core(give) for give in gives]
+        keeps = [first, *kernel(tuple(range(3, 2 * parts, 2)), first)]
+        sums, before = [], token
         for part in range(parts):
-            got = other_core(give)
-            if part + 1 < parts:
-                keep, give = kernel((2 * part + 1, 2 * part + 2), before if part else give)
-            else:
-                (keep,) = kernel((2 * part + 1,), before)
-            pair = call(
+            before = call(
                 pair_kernel,
                 part_bf16[part],
                 [],
                 [VMEM, VMEM, ANY],
                 name + "_pair",
                 bytes_accessed=1 << 19,
-            )(keep, got, before)
-            before = pair
-            sums.append(other_chips(pair))
-        return sums, keep
+            )(keeps[part], got[part], before)
+            sums.append(other_chips(before))
+        return sums, keeps[-1]
 
     part1 = call(
         first_forward_kernel,
@@ -388,7 +388,7 @@
         "prepare",
         bytes_accessed=4 << 20,
     )(state_b, prior_b, after)
-    own, grad1, mate, before = [], [], [], token
+    own, grad1, mate, before = [], [], [], sums1[-1][0]
     for part, (field, sums) in enumerate(zip(fields, sums1)):
         probe, grad = call(
             functools.partial(probe_kernel, ny),
@@ -432,7 +432,7 @@
         "turn",
         bytes_accessed=1 << 20,
     )(resid2_t)
-    own, mate, after = [], [], [turned, *dense[:-1]]
+    own, mate, after = [], [], [turned, sums2[-1][0], *dense[:-1]]
     for part, (grad, sums) in enumerate(zip(grad1, sums2)):
         total = call(
             functools.partial(total_kernel, ny, len(after)),

time: 85 us -> 86.1 us (1.013)
  waiting for transfers between devices: 9.85 us -> 12.6 us
  starting transfers between devices: 19.2 us -> 17.4 us
    ppermute x8 -> x6, waiting for transfers between devices: 5.47 us -> 7.39 us  [other_chips(): lax.ppermute(array, 'shot', [(i, i ^ 2 * d) for i in range(nshot)])]
    ppermute x16 -> x12, starting transfers between devices: 3.59 us -> 1.75 us  [other_core(): return lax.ppermute(array, 'shot', [(i, i ^ 1) for i in range(nshot)])]
    ppermute x16 -> x12, waiting for transfers between devices: 1.78 us -> 2.64 us  [other_core(): return lax.ppermute(array, 'shot', [(i, i ^ 1) for i in range(nshot)])]
    pallas_call x10 -> x6, Pallas kernels: 2.79 us -> 2.11 us  [kernel(): call(adjoint_kernel, tuple((part_f32[p // 2] if p % 2 else part_bf16[p //...]
    ppermute x8 -> x6, starting transfers between devices: 8.36 us -> 8.43 us  [other_chips(): lax.ppermute(array, 'shot', [(i, i ^ 2 * d) for i in range(nshot)])]
  transfers between devices with their start and end apart: 25 -> 19, of which waited for: 11 -> 11; matrix products, arithmetic and copies ran while one was open for 0% -> 0% of each run, Pallas kernels for 11% -> 10%
where the time goes in v11:
time: 86.1 us; the launch traced here: 85.7 us
  blocking collectives  37.3 us (43%)
  starting transfers between devices  17.4 us (20%)
  Pallas kernels  14.1 us (16%)
  waiting for transfers between devices  12.6 us (15%)
  local copies, waits for them, and re-layouts  3.19 us (4%)
  between operations  1.01 us (1%)
    all_to_all x3, blocking collectives, over_band(): lax.all_to_all(array, 'band', split_axis=0, concat_axis=0, tiled=True)  37.3 us
    ppermute x6, starting transfers between devices, other_chips(): lax.ppermute(array, 'shot', [(i, i ^ 2 * d) for i in range(nshot)])  8.43 us
    ppermute x6, waiting for transfers between devices, other_chips(): lax.ppermute(array, 'shot', [(i, i ^ 2 * d) for i in range(nshot)])  7.39 us
    all_to_all x1, starting transfers between devices, over_band(): lax.all_to_all(array, 'band', split_axis=0, concat_axis=0, tiled=True)  7.26 us
    pallas_call x1, Pallas kernels, per_device(): call(first_forward_kernel, part_out, [pltpu.VMEM((bundles, rays, samples)...  3.88 us
    unnamed x22, local copies, waits for them, and re-layouts  3.19 us
    pallas_call x1, Pallas kernels, per_device(): call(dense_kernel, tuple((d for d in dense_bf16 for _ in range(2))) + (sm...  3.1 us
    ppermute x12, waiting for transfers between devices, other_core(): return lax.ppermute(array, 'shot', [(i, i ^ 1) for i in range(nshot)])  2.64 us
  transfers between devices with their start and end apart: 19, of which 11 were waited for; matrix products, arithmetic and copies ran while one was open for 0% of the time, Pallas kernels for 10%

profile of v11, /device:TPU:0, one launch (start us, length us, event | category | flops | bytes accessed | tf_op | source)
XLA Modules:
  0.0 85.7 jit_solution(15037539631498422646)
XLA Ops:
  0.6 3.9 %forward1.1 = bf16[8,128,128]{2,1,0:T(8,128)(2,1)} custom-call(s32[64]{0:T(128)} %bund.1, s32[64]{0:T(128)} %cblk.1, bf16[64,128,128]{2,1,0:T(8,128)(2,1)} %sens.1, f32[16,128,128]{2,1,0:T(8,128)} %bitcast.7, f32[16,128,128]{2,1,0:T(8,128)} %bitcast.9), custom_call_target="tpu_custom_call" | custom-call | flops 268435456 | bytes 2097152 | tf_op jit(solution)/shard_map/forward1/pallas_call | solution.py:351
  4.6 7.3 %all-to-all-start = ((bf16[8,128,128]{2,1,0:T(8,128)(2,1)}), bf16[8,128,128]{2,1,0:T(8,128)(2,1)S(1)}, u32[]{:S(2)}, u32[]{:S(2)}) async-start(bf16[8,128,128]{2,1,0:T(8,128)(2,1)} %forward1.1), calls=%async_computation | async-start | bytes 524288 | tf_op jit(solution)/shard_map/all_to_all | solution.py:299
  11.8 1.6 %copy-done.2 = bf16[64,128,128]{2,1,0:T(8,128)(2,1)S(1)} copy-done((bf16[64,128,128]{2,1,0:T(8,128)(2,1)S(1)}, bf16[64,128,128]{2,1,0:T(8,128)(2,1)}, u32[]{:S(2)}) %copy-start.2) | copy-done | bytes 2097176
  13.4 3.1 %dense.1 = (bf16[2,1024,256]{2,1,0:T(8,128)(2,1)S(1)}, bf16[2,1024,256]{2,1,0:T(8,128)(2,1)S(1)}, bf16[1,1024,256]{2,1,0:T(8,128)(2,1)S(1)}, bf16[1,1024,256]{2,...) custom-call(s32[64]{0:T(128)S(1)} %copy-done.9, ...), custom_call_target="tpu_custom_call" | custom-call | bytes 16777216 | tf_op jit(solution)/shard_map/dense/pallas_call | solution.py:370
  16.6 0.8 copy-done
  17.3 0.8 copy-done.3
  18.1 2.6 %all-to-all-done = bf16[8,128,128]{2,1,0:T(8,128)(2,1)S(1)} async-done(((bf16[8,128,128]{2,1,0:T(8,128)(2,1)}), bf16[8,128,128]{2,1,0:T(8,128)(2,1)S(1)}, u32[]{:S(2)}, u32[]{:S(2)}) %all-to-all-start) | async-done | bytes 262176 | tf_op jit(solution)/shard_map/all_to_all | solution.py:299
  20.9 12.1 %all_to_all.20 = bf16[8,1,128,128]{3,2,1,0:T(8,128)(2,1)S(1)} all-to-all(bf16[8,1,128,128]{3,2,1,0:T(8,128)(2,1)S(1)} %residual1.1), channel_id=1, replica_groups=mesh['shot'=4,'band'=8] {'band'}, dimensions={0} | all-to-all | bytes 524288 | tf_op jit(solution)/shard_map/all_to_all | solution.py:299
  32.9 0.3 adjoint1.3.after_ref
  33.4 0.4 adjoint1.4
  33.8 0.8 collective-permute-done.2.got_ref
  34.7 1.6 %collective-permute-start.3 = (bf16[4,128,128]{2,1,0:T(8,128)(2,1)S(1)}, bf16[4,128,128]{2,1,0:T(8,128)(2,1)S(1)}, u32[]{:S(2)}, u32[]{:S(2)}) collective-permute-start(bf16[4,128,128]{2,1,0:T(8,128)(2,1)S(1)} %adjoint1_pair.3.after_ref.rest_0_), channel_id=1, source_target_pairs={{0,16},{8,24},{16,0},{24,8},{1,17},{9,25},{17,1},{25,9},{2,18},{10... | collective-permute-start | bytes 393224 | tf_op jit(solution)/shard_map/ppermute | solution.py:294
  36.3 0.5 collective-permute-start
  37.6 0.6 collective-permute-start.4
  38.2 2.2 %collective-permute-done.3.rest_1_ = bf16[4,128,128]{2,1,0:T(8,128)(2,1)S(1)} collective-permute-done((bf16[4,128,128]{2,1,0:T(8,128)(2,1)S(1)}, bf16[4,128,128]{2,1,0:T(8,128)(2,1)S(1)}, u32[]{:S(2)}, u32[]{:S(2)}) %collective-permute-start.3) | collective-permute-done | bytes 131104 | tf_op jit(solution)/shard_map/ppermute | solution.py:294
  40.5 2.3 %collective-permute-start.5 = (bf16[2,128,128]{2,1,0:T(8,128)(2,1)S(1)}, bf16[2,128,128]{2,1,0:T(8,128)(2,1)S(1)}, u32[]{:S(2)}, u32[]{:S(2)}) collective-permute-start(bf16[2,128,128]{2,1,0:T(8,128)(2,1)S(1)} %adjoint1_pair.5.after_ref.rest_0_), channel_id=1, source_target_pairs={{0,16},{8,24},{16,0},{24,8},{1,17},{9,25},{17,1},{25,9},{2,18},{10... | collective-permute-start | bytes 196616 | tf_op jit(solution)/shard_map/ppermute | solution.py:294
  43.2 2.3 %collective-permute-done.5.rest_1_ = bf16[2,128,128]{2,1,0:T(8,128)(2,1)S(1)} collective-permute-done((bf16[2,128,128]{2,1,0:T(8,128)(2,1)S(1)}, bf16[2,128,128]{2,1,0:T(8,128)(2,1)S(1)}, u32[]{:S(2)}, u32[]{:S(2)}) %collective-permute-start.5) | collective-permute-done | bytes 65568 | tf_op jit(solution)/shard_map/ppermute | solution.py:294
  45.7 1.1 %forward2_early.1.early = f32[8,128,128]{2,1,0:T(8,128)S(1)} custom-call(bf16[2,1024,256]{2,1,0:T(8,128)(2,1)S(1)} %get-tuple-element.37.refs_0_.rest_3_, bf16[1,1024,256]{2,1,0:T(8,128)(2,1)S(1)} %get-tuple-element.41.refs_0_.refs_1_.rest_5_, bf16[1,1024,256]{2,1,0:T(8,128)(2,1)S(1)} %copy-done.4, ...), custom_call_target="tpu_custom_call" | custom-call | flops 469762048 | bytes 3670016 | tf_op jit(solution)/shard_map/forward2_early/pallas_call | solution.py:406
  47.2 12.9 %all_to_all.21 = bf16[8,128,128]{2,1,0:T(8,128)(2,1)S(1)} all-to-all(bf16[8,128,128]{2,1,0:T(8,128)(2,1)S(1)} %forward2_late.1), channel_id=1, replica_groups=mesh['shot'=4,'band'=8] {'band'}, dimensions={0} | all-to-all | bytes 524288 | tf_op jit(solution)/shard_map/all_to_all | solution.py:299
  60.2 12.4 %all_to_all.22 = bf16[8,1,128,128]{3,2,1,0:T(8,128)(2,1)S(1)} all-to-all(bf16[8,1,128,128]{3,2,1,0:T(8,128)(2,1)S(1)} %get-tuple-element.57), channel_id=1, replica_groups=mesh['shot'=4,'band'=8] {'band'}, dimensions={0} | all-to-all | bytes 524288 | tf_op jit(solution)/shard_map/all_to_all | solution.py:299
  73.0 0.4 adjoint2.4
  73.5 0.9 %collective-permute-done.11.got_ref = bf16[4,128,128]{2,1,0:T(8,128)(2,1)S(1)} collective-permute-done((bf16[4,128,128]{2,1,0:T(8,128)(2,1)S(1)}, bf16[4,128,128]{2,1,0:T(8,128)(2,1)S(1)}, u32[]{:S(2)}, u32[]{:S(2)}) %collective-permute-start.11) | collective-permute-done | bytes 131104 | tf_op jit(solution)/shard_map/ppermute | solution.py:290
  74.4 1.8 %collective-permute-start.12 = (bf16[4,128,128]{2,1,0:T(8,128)(2,1)S(1)}, bf16[4,128,128]{2,1,0:T(8,128)(2,1)S(1)}, u32[]{:S(2)}, u32[]{:S(2)}) collective-permute-start(bf16[4,128,128]{2,1,0:T(8,128)(2,1)S(1)} %adjoint2_pair.3.after_ref.rest_7_), channel_id=1, source_target_pairs={{0,16},{8,24},{16,0},{24,8},{1,17},{9,25},{17,1},{25,9},{2,18},{10... | collective-permute-start | bytes 393224 | tf_op jit(solution)/shard_map/ppermute | solution.py:294
  76.2 0.5 collective-permute-start.9
  76.7 0.7 turn.1
  77.8 0.3 collective-permute-start.13
  78.1 1.8 %collective-permute-start.14 = (bf16[2,128,128]{2,1,0:T(8,128)(2,1)S(1)}, bf16[2,128,128]{2,1,0:T(8,128)(2,1)S(1)}, u32[]{:S(2)}, u32[]{:S(2)}) collective-permute-start(bf16[2,128,128]{2,1,0:T(8,128)(2,1)S(1)} %adjoint2_pair.5.rest_1_), channel_id=1, source_target_pairs={{0,16},{8,24},{16,0},{24,8},{1,17},{9,25},{17,1},{25,9},{2,18},{10... | collective-permute-start | bytes 196616 | tf_op jit(solution)/shard_map/ppermute | solution.py:294
  80.3 2.3 %collective-permute-done.13.rest_2_ = bf16[2,128,128]{2,1,0:T(8,128)(2,1)S(1)} collective-permute-done((bf16[2,128,128]{2,1,0:T(8,128)(2,1)S(1)}, bf16[2,128,128]{2,1,0:T(8,128)(2,1)S(1)}, u32[]{:S(2)}, u32[]{:S(2)}) %collective-permute-start.13) | collective-permute-done | bytes 65568 | tf_op jit(solution)/shard_map/ppermute | solution.py:294
  82.7 0.5 collective-permute-done.14.rest_2_
  83.4 0.5 collective-permute-done.16.refs_4_
  84.0 1.0 %new_state_early.1 = (f32[16,128,128]{2,1,0:T(8,128)}, f32[2,128,128]{2,1,0:T(8,128)S(1)}) custom-call(f32[16,128,128]{2,1,0:T(8,128)S(1)} %get-tuple-element.44.base, bf16[4,128,128]{2,1,0:T(8,128)(2,1)S(1)} %total.3.rest_0_.refs_0_, bf16[2,128,128]{2,1,0:T(8,128)(2,1)S(1)} %total.4.rest_0_.refs_1_, bf16[2,128,128]{2,1,0:T(8,128)(2,1)S(1)} %total.5.refs_2_, ...), custom_call_target="tpu_custom_call" | custom-call | bytes 3145728 | tf_op jit(solution)/shard_map/new_state_early/pallas_call | solution.py:450
  85.0 0.7 new_state_late.1
  (59 shorter events, 3.6 us)
Async XLA Ops:
  0.6 11.2 %copy-start.9 = (s32[64]{0:T(128)S(1)}, s32[64]{0:T(128)}, u32[]{:S(2)}) copy-start(s32[64]{0:T(128)} %bund.1) | copy-start | bytes 772
  0.6 11.2 %copy-start.10 = (s32[64]{0:T(128)S(1)}, s32[64]{0:T(128)}, u32[]{:S(2)}) copy-start(s32[64]{0:T(128)} %cblk.1) | copy-start | bytes 772
  4.5 16.2 %copy-start.7 = (f32[1,128]{1,0:T(1,128)S(1)}, f32[1,128]{1,0:T(1,128)}, u32[]{:S(2)}) copy-start(f32[1,128]{1,0:T(1,128)} %obs_ref.3) | copy-start | bytes 1540
  4.5 16.2 %copy-start.8 = (f32[1,128]{1,0:T(1,128)S(1)}, f32[1,128]{1,0:T(1,128)}, u32[]{:S(2)}) copy-start(f32[1,128]{1,0:T(1,128)} %wt_ref.3) | copy-start | bytes 1540
  4.6 16.2 %all-to-all-start = ((bf16[8,128,128]{2,1,0:T(8,128)(2,1)}), bf16[8,128,128]{2,1,0:T(8,128)(2,1)S(1)}, u32[]{:S(2)}, u32[]{:S(2)}) async-start(bf16[8,128,128]{2,1,0:T(8,128)(2,1)} %forward1.1), calls=%async_computation | async-start | bytes 524288 | tf_op jit(solution)/shard_map/all_to_all | solution.py:299
  11.8 1.6 %copy-start.2 = (bf16[64,128,128]{2,1,0:T(8,128)(2,1)S(1)}, bf16[64,128,128]{2,1,0:T(8,128)(2,1)}, u32[]{:S(2)}) copy-start(bf16[64,128,128]{2,1,0:T(8,128)(2,1)} %sens.1) | copy-start | bytes 6291460
  16.5 0.8 copy-start
  17.3 0.8 copy-start.3
  20.7 12.6 %copy-start.1 = (bf16[1,1024,256]{2,1,0:T(8,128)(2,1)S(1)}, bf16[1,1024,256]{2,1,0:T(8,128)(2,1)}, u32[]{:S(2)}) copy-start(bf16[1,1024,256]{2,1,0:T(8,128)(2,1)} %copy-done) | copy-start | bytes 1572868
  32.9 3.9 %copy-start.4 = (bf16[1,1024,256]{2,1,0:T(8,128)(2,1)S(1)}, bf16[1,1024,256]{2,1,0:T(8,128)(2,1)}, u32[]{:S(2)}) copy-start(bf16[1,1024,256]{2,1,0:T(8,128)(2,1)} %copy-done.3) | copy-start | bytes 1572868
  33.3 1.4 %collective-permute-start.2 = (bf16[4,128,128]{2,1,0:T(8,128)(2,1)S(1)}, bf16[4,128,128]{2,1,0:T(8,128)(2,1)S(1)}, u32[]{:S(2)}, u32[]{:S(2)}) collective-permute-start(bf16[4,128,128]{2,1,0:T(8,128)(2,1)S(1)} %adjoint1.3.after_ref), channel_id=1, source_target_pairs={{0,8},{8,0},{16,24},{24,16},{1,9},{9,1},{17,25},{25,17},{2,10},{10... | collective-permute-start | bytes 393224 | tf_op jit(solution)/shard_map/ppermute | solution.py:290
  33.3 3.8 %copy-start.5 = (f32[2048,128]{1,0:T(8,128)S(1)}, f32[2048,128]{1,0:T(8,128)}, u32[]{:S(2)}) copy-start(f32[2048,128]{1,0:T(8,128)} %param.10) | copy-start | bytes 3145732
  33.4 3.8 %copy-start.6 = (f32[2048,128]{1,0:T(8,128)S(1)}, f32[2048,128]{1,0:T(8,128)}, u32[]{:S(2)}) copy-start(f32[2048,128]{1,0:T(8,128)} %param.11) | copy-start | bytes 3145732
  34.7 5.6 %collective-permute-start.3 = (bf16[4,128,128]{2,1,0:T(8,128)(2,1)S(1)}, bf16[4,128,128]{2,1,0:T(8,128)(2,1)S(1)}, u32[]{:S(2)}, u32[]{:S(2)}) collective-permute-start(bf16[4,128,128]{2,1,0:T(8,128)(2,1)S(1)} %adjoint1_pair.3.after_ref.rest_0_), channel_id=1, source_target_pairs={{0,16},{8,24},{16,0},{24,8},{1,17},{9,25},{17,1},{25,9},{2,18},{10... | collective-permute-start | bytes 393224 | tf_op jit(solution)/shard_map/ppermute | solution.py:294
  36.3 1.3 %collective-permute-start.1 = (bf16[2,128,128]{2,1,0:T(8,128)(2,1)S(1)}, bf16[2,128,128]{2,1,0:T(8,128)(2,1)S(1)}, u32[]{:S(2)}, u32[]{:S(2)}) collective-permute-start(bf16[2,128,128]{2,1,0:T(8,128)(2,1)S(1)} %get-tuple-element.48), channel_id=1, source_target_pairs={{0,8},{8,0},{16,24},{24,16},{1,9},{9,1},{17,25},{25,17},{2,10},{10... | collective-permute-start | bytes 196616 | tf_op jit(solution)/shard_map/ppermute | solution.py:290
  36.3 1.8 %collective-permute-start = (bf16[2,128,128]{2,1,0:T(8,128)(2,1)S(1)}, bf16[2,128,128]{2,1,0:T(8,128)(2,1)S(1)}, u32[]{:S(2)}, u32[]{:S(2)}) collective-permute-start(bf16[2,128,128]{2,1,0:T(8,128)(2,1)S(1)} %get-tuple-element.46), channel_id=1, source_target_pairs={{0,8},{8,0},{16,24},{24,16},{1,9},{9,1},{17,25},{25,17},{2,10},{10... | collective-permute-start | bytes 196616 | tf_op jit(solution)/shard_map/ppermute | solution.py:290
  37.6 5.3 %collective-permute-start.4 = (bf16[2,128,128]{2,1,0:T(8,128)(2,1)S(1)}, bf16[2,128,128]{2,1,0:T(8,128)(2,1)S(1)}, u32[]{:S(2)}, u32[]{:S(2)}) collective-permute-start(bf16[2,128,128]{2,1,0:T(8,128)(2,1)S(1)} %adjoint1_pair.4.after_ref.rest_0_), channel_id=1, source_target_pairs={{0,16},{8,24},{16,0},{24,8},{1,17},{9,25},{17,1},{25,9},{2,18},{10... | collective-permute-start | bytes 196616 | tf_op jit(solution)/shard_map/ppermute | solution.py:294
  40.5 5.3 %collective-permute-start.7 = (bf16[4,128,128]{2,1,0:T(8,128)(2,1)S(1)}, bf16[4,128,128]{2,1,0:T(8,128)(2,1)S(1)}, u32[]{:S(2)}, u32[]{:S(2)}) collective-permute-start(bf16[4,128,128]{2,1,0:T(8,128)(2,1)S(1)} %get-tuple-element.52.after_ref.refs_5_), channel_id=1, source_target_pairs={{0,8},{8,0},{16,24},{24,16},{1,9},{9,1},{17,25},{25,17},{2,10},{10... | collective-permute-start | bytes 393224 | tf_op jit(solution)/shard_map/ppermute | solution.py:290
  40.5 5.0 %collective-permute-start.5 = (bf16[2,128,128]{2,1,0:T(8,128)(2,1)S(1)}, bf16[2,128,128]{2,1,0:T(8,128)(2,1)S(1)}, u32[]{:S(2)}, u32[]{:S(2)}) collective-permute-start(bf16[2,128,128]{2,1,0:T(8,128)(2,1)S(1)} %adjoint1_pair.5.after_ref.rest_0_), channel_id=1, source_target_pairs={{0,16},{8,24},{16,0},{24,8},{1,17},{9,25},{17,1},{25,9},{2,18},{10... | collective-permute-start | bytes 196616 | tf_op jit(solution)/shard_map/ppermute | solution.py:294
  43.0 2.8 %collective-permute-start.8 = (bf16[2,128,128]{2,1,0:T(8,128)(2,1)S(1)}, bf16[2,128,128]{2,1,0:T(8,128)(2,1)S(1)}, u32[]{:S(2)}, u32[]{:S(2)}) collective-permute-start(bf16[2,128,128]{2,1,0:T(8,128)(2,1)S(1)} %get-tuple-element.53.after_ref.refs_6_), channel_id=1, source_target_pairs={{0,8},{8,0},{16,24},{24,16},{1,9},{9,1},{17,25},{25,17},{2,10},{10... | collective-permute-start | bytes 196616 | tf_op jit(solution)/shard_map/ppermute | solution.py:290
  45.6 1.3 %collective-permute-start.6 = (bf16[2,128,128]{2,1,0:T(8,128)(2,1)S(1)}, bf16[2,128,128]{2,1,0:T(8,128)(2,1)S(1)}, u32[]{:S(2)}, u32[]{:S(2)}) collective-permute-start(bf16[2,128,128]{2,1,0:T(8,128)(2,1)S(1)} %get-tuple-element.54.refs_7_), channel_id=1, source_target_pairs={{0,8},{8,0},{16,24},{24,16},{1,9},{9,1},{17,25},{25,17},{2,10},{10... | collective-permute-start | bytes 196616 | tf_op jit(solution)/shard_map/ppermute | solution.py:290
  72.9 1.4 %collective-permute-start.11 = (bf16[4,128,128]{2,1,0:T(8,128)(2,1)S(1)}, bf16[4,128,128]{2,1,0:T(8,128)(2,1)S(1)}, u32[]{:S(2)}, u32[]{:S(2)}) collective-permute-start(bf16[4,128,128]{2,1,0:T(8,128)(2,1)S(1)} %adjoint2.3.after_ref), channel_id=1, source_target_pairs={{0,8},{8,0},{16,24},{24,16},{1,9},{9,1},{17,25},{25,17},{2,10},{10... | collective-permute-start | bytes 393224 | tf_op jit(solution)/shard_map/ppermute | solution.py:290
  74.4 5.7 %collective-permute-start.12 = (bf16[4,128,128]{2,1,0:T(8,128)(2,1)S(1)}, bf16[4,128,128]{2,1,0:T(8,128)(2,1)S(1)}, u32[]{:S(2)}, u32[]{:S(2)}) collective-permute-start(bf16[4,128,128]{2,1,0:T(8,128)(2,1)S(1)} %adjoint2_pair.3.after_ref.rest_7_), channel_id=1, source_target_pairs={{0,16},{8,24},{16,0},{24,8},{1,17},{9,25},{17,1},{25,9},{2,18},{10... | collective-permute-start | bytes 393224 | tf_op jit(solution)/shard_map/ppermute | solution.py:294
  76.2 1.6 %collective-permute-start.10 = (bf16[2,128,128]{2,1,0:T(8,128)(2,1)S(1)}, bf16[2,128,128]{2,1,0:T(8,128)(2,1)S(1)}, u32[]{:S(2)}, u32[]{:S(2)}) collective-permute-start(bf16[2,128,128]{2,1,0:T(8,128)(2,1)S(1)} %get-tuple-element.62), channel_id=1, source_target_pairs={{0,8},{8,0},{16,24},{24,16},{1,9},{9,1},{17,25},{25,17},{2,10},{10... | collective-permute-start | bytes 196616 | tf_op jit(solution)/shard_map/ppermute | solution.py:290
  76.2 1.9 %collective-permute-start.9 = (bf16[2,128,128]{2,1,0:T(8,128)(2,1)S(1)}, bf16[2,128,128]{2,1,0:T(8,128)(2,1)S(1)}, u32[]{:S(2)}, u32[]{:S(2)}) collective-permute-start(bf16[2,128,128]{2,1,0:T(8,128)(2,1)S(1)} %get-tuple-element.60), channel_id=1, source_target_pairs={{0,8},{8,0},{16,24},{24,16},{1,9},{9,1},{17,25},{25,17},{2,10},{10... | collective-permute-start | bytes 196616 | tf_op jit(solution)/shard_map/ppermute | solution.py:290
  77.8 4.8 %collective-permute-start.13 = (bf16[2,128,128]{2,1,0:T(8,128)(2,1)S(1)}, bf16[2,128,128]{2,1,0:T(8,128)(2,1)S(1)}, u32[]{:S(2)}, u32[]{:S(2)}) collective-permute-start(bf16[2,128,128]{2,1,0:T(8,128)(2,1)S(1)} %adjoint2_pair.4.after_ref.rest_1_), channel_id=1, source_target_pairs={{0,16},{8,24},{16,0},{24,8},{1,17},{9,25},{17,1},{25,9},{2,18},{10... | collective-permute-start | bytes 196616 | tf_op jit(solution)/shard_map/ppermute | solution.py:294
  78.1 5.1 %collective-permute-start.14 = (bf16[2,128,128]{2,1,0:T(8,128)(2,1)S(1)}, bf16[2,128,128]{2,1,0:T(8,128)(2,1)S(1)}, u32[]{:S(2)}, u32[]{:S(2)}) collective-permute-start(bf16[2,128,128]{2,1,0:T(8,128)(2,1)S(1)} %adjoint2_pair.5.rest_1_), channel_id=1, source_target_pairs={{0,16},{8,24},{16,0},{24,8},{1,17},{9,25},{17,1},{25,9},{2,18},{10... | collective-permute-start | bytes 196616 | tf_op jit(solution)/shard_map/ppermute | solution.py:294
  80.2 3.8 %collective-permute-start.15 = (bf16[4,128,128]{2,1,0:T(8,128)(2,1)S(1)}, bf16[4,128,128]{2,1,0:T(8,128)(2,1)S(1)}, u32[]{:S(2)}, u32[]{:S(2)}) collective-permute-start(bf16[4,128,128]{2,1,0:T(8,128)(2,1)S(1)} %total.3.rest_0_.refs_0_), channel_id=1, source_target_pairs={{0,8},{8,0},{16,24},{24,16},{1,9},{9,1},{17,25},{25,17},{2,10},{10... | collective-permute-start | bytes 393224 | tf_op jit(solution)/shard_map/ppermute | solution.py:290
  82.7 1.3 %collective-permute-start.16 = (bf16[2,128,128]{2,1,0:T(8,128)(2,1)S(1)}, bf16[2,128,128]{2,1,0:T(8,128)(2,1)S(1)}, u32[]{:S(2)}, u32[]{:S(2)}) collective-permute-start(bf16[2,128,128]{2,1,0:T(8,128)(2,1)S(1)} %total.4.rest_0_.refs_1_), channel_id=1, source_target_pairs={{0,8},{8,0},{16,24},{24,16},{1,9},{9,1},{17,25},{25,17},{2,10},{10... | collective-permute-start | bytes 196616 | tf_op jit(solution)/shard_map/ppermute | solution.py:290
  83.4 1.6 %collective-permute-start.17 = (bf16[2,128,128]{2,1,0:T(8,128)(2,1)S(1)}, bf16[2,128,128]{2,1,0:T(8,128)(2,1)S(1)}, u32[]{:S(2)}, u32[]{:S(2)}) collective-permute-start(bf16[2,128,128]{2,1,0:T(8,128)(2,1)S(1)} %total.5.refs_2_), channel_id=1, source_target_pairs={{0,8},{8,0},{16,24},{24,16},{1,9},{9,1},{17,25},{25,17},{2,10},{10... | collective-permute-start | bytes 196616 | tf_op jit(solution)/shard_map/ppermute | solution.py:290

commit v12 on v9

--- a/solution.py
+++ b/solution.py
@@ -10,6 +10,7 @@
 CBLK = 128
 GROUP = 32
 CHUNKS = 2
+FIELDS = 4
 FIRST_VMEM = 55 << 20
 GIVE_A, KEEP_A, GIVE_B, KEEP_B = range(4)
 
@@ -57,14 +58,14 @@
     nblk = sens.shape[0]
     step = nblk // CHUNKS
     cells = state.shape[0]
-    half = cells // 2
+    share = cells // FIELDS
     small = [
         pltpu.make_async_copy(bund_hbm, bund, sems.at[0]),
         pltpu.make_async_copy(cblk_hbm, cblk, sems.at[1]),
     ]
     fields = []
-    for h in range(2):
-        part = pl.ds(h * half, half)
+    for h in range(FIELDS):
+        part = pl.ds(h * share, share)
         fields.append(
             [
                 pltpu.make_async_copy(state_hbm.at[part], state.at[part], sems.at[2 + 2 * h]),
@@ -72,16 +73,24 @@
             ]
         )
 
-    def block_copy(c):
-        part = pl.ds(c * step, step)
-        return pltpu.make_async_copy(sens_hbm.at[part], sens.at[part], sems.at[6 + c])
-
-    for copy in small + fields[0] + fields[1] + [block_copy(c) for c in range(CHUNKS)]:
+    def block_copies(c):
+        size = step // 2
+        copies = []
+        for h in range(2):
+            part = pl.ds(c * step + h * size, size)
+            sem = sems.at[2 + 2 * FIELDS + 2 * c + h]
+            copies.append(pltpu.make_async_copy(sens_hbm.at[part], sens.at[part], sem))
+        return copies
+
+    for copy in small + [copy for field in fields for copy in field]:
         copy.start()
+    for c in range(CHUNKS):
+        for copy in block_copies(c):
+            copy.start()
     acc[...] = jnp.zeros_like(acc)
 
-    for h in range(2):
-        part = pl.ds(h * half, half)
+    for h in range(FIELDS):
+        part = pl.ds(h * share, share)
         for copy in fields[h]:
             copy.wait()
         probe[part] = (state[part] + 0.5 * prior[part]).astype(bf16)
@@ -89,7 +98,8 @@
         copy.wait()
 
     def chunk(c, carry):
-        block_copy(c).wait()
+        for copy in block_copies(c):
+            copy.wait()
         for g in range(step // GROUP):
             ks = [c * step + g * GROUP + j for j in range(GROUP)]
             prods = [
@@ -339,7 +349,7 @@
             pltpu.VMEM(sens.shape, bf16),
             pltpu.VMEM(state_b.shape, f32),
             pltpu.VMEM(state_b.shape, f32),
-            pltpu.SemaphoreType.DMA((6 + CHUNKS,)),
+            pltpu.SemaphoreType.DMA((2 + 2 * FIELDS + 2 * CHUNKS,)),
         ],
         [HBM] * 5,
         "forward1",

time: 82.3 us -> 82.3 us (level)
  no operation moved by 1% of the time
where the time goes in v12:
time: 82.3 us; the launch traced here: 81.9 us
  blocking collectives  36.5 us (44%)
  waiting for transfers between devices  14.7 us (18%)
  Pallas kernels  14.1 us (17%)
  starting transfers between devices  13.1 us (16%)
  local copies, waits for them, and re-layouts  2.59 us (3%)
  between operations  0.95 us (1%)
    all_to_all x3, blocking collectives, over_band(): lax.all_to_all(array, 'band', split_axis=0, concat_axis=0, tiled=True)  36.5 us
    ppermute x4, waiting for transfers between devices, other_chips(): lax.ppermute(array, 'shot', [(i, i ^ 2 * d) for i in range(nshot)])  10.5 us
    all_to_all x1, starting transfers between devices, over_band(): lax.all_to_all(array, 'band', split_axis=0, concat_axis=0, tiled=True)  7.27 us
    ppermute x4, starting transfers between devices, other_chips(): lax.ppermute(array, 'shot', [(i, i ^ 2 * d) for i in range(nshot)])  4.31 us
    pallas_call x1, Pallas kernels, per_device(): call(first_forward_kernel, part_out, [pltpu.VMEM((bundles, rays, samples)...  3.65 us
    pallas_call x1, Pallas kernels, per_device(): call(dense_kernel, (arr(dense_shape, bf16),) * 4 + (small_token,), [pltpu...  3.48 us
    all_to_all x1, waiting for transfers between devices, over_band(): lax.all_to_all(array, 'band', split_axis=0, concat_axis=0, tiled=True)  2.85 us
    unnamed x18, local copies, waits for them, and re-layouts  2.59 us
  transfers between devices with their start and end apart: 13, of which 9 were waited for; matrix products, arithmetic and copies ran while one was open for 0% of the time, Pallas kernels for 10%

profile of v12, /device:TPU:0, one launch (start us, length us, event | category | flops | bytes accessed | tf_op | source)
XLA Modules:
  0.0 81.9 jit_solution(421849754784068963)
XLA Ops:
  0.6 3.7 %forward1.1 = bf16[8,128,128]{2,1,0:T(8,128)(2,1)} custom-call(s32[64]{0:T(128)} %bund.1, s32[64]{0:T(128)} %cblk.1, bf16[64,128,128]{2,1,0:T(8,128)(2,1)} %sens.1, f32[16,128,128]{2,1,0:T(8,128)} %bitcast.7, f32[16,128,128]{2,1,0:T(8,128)} %bitcast.9), custom_call_target="tpu_custom_call" | custom-call | flops 268435456 | bytes 2097152 | tf_op jit(solution)/shard_map/forward1/pallas_call | solution.py:341
  4.3 7.3 %all-to-all-start = ((bf16[8,128,128]{2,1,0:T(8,128)(2,1)}), bf16[8,128,128]{2,1,0:T(8,128)(2,1)S(1)}, u32[]{:S(2)}, u32[]{:S(2)}) async-start(bf16[8,128,128]{2,1,0:T(8,128)(2,1)} %forward1.1), calls=%async_computation | async-start | bytes 524288 | tf_op jit(solution)/shard_map/all_to_all | solution.py:289
  11.6 1.6 %copy-done.2 = bf16[64,128,128]{2,1,0:T(8,128)(2,1)S(1)} copy-done((bf16[64,128,128]{2,1,0:T(8,128)(2,1)S(1)}, bf16[64,128,128]{2,1,0:T(8,128)(2,1)}, u32[]{:S(2)}) %copy-start.2) | copy-done | bytes 2097176
  13.2 3.5 %dense.1 = (bf16[2,1024,256]{2,1,0:T(8,128)(2,1)S(1)}, bf16[2,1024,256]{2,1,0:T(8,128)(2,1)S(1)}, bf16[2,1024,256]{2,1,0:T(8,128)(2,1)S(1)}, bf16[2,1024,256]{2,1,0:T(8,128)(2,1)S(1)}, f32[8,128]{1,0:T(8,128)S(1)}) custom-call(s32[64]{0:T(128)S(1)} %copy-done.7, s32[64]{0:T(128)S(1)} %copy-done.8, bf16[64,128,128]{2,1,0:T(8,128)(2,1)S(1)} %copy-done.2), custom_call_target="tpu_custom_call" | custom-call | bytes 16777216 | tf_op jit(solution)/shard_map/dense/pallas_call | solution.py:360
  16.7 1.0 %copy-done = bf16[2,1024,256]{2,1,0:T(8,128)(2,1)} copy-done((bf16[2,1024,256]{2,1,0:T(8,128)(2,1)}, bf16[2,1024,256]{2,1,0:T(8,128)(2,1)S(1)}, u32[]{:S(2)}) %copy-start) | copy-done | bytes 1048600
  17.7 2.8 %all-to-all-done = bf16[8,128,128]{2,1,0:T(8,128)(2,1)S(1)} async-done(((bf16[8,128,128]{2,1,0:T(8,128)(2,1)}), bf16[8,128,128]{2,1,0:T(8,128)(2,1)S(1)}, u32[]{:S(2)}, u32[]{:S(2)}) %all-to-all-start) | async-done | bytes 262176 | tf_op jit(solution)/shard_map/all_to_all | solution.py:289
  20.6 12.0 %all_to_all.20 = bf16[8,1,128,128]{3,2,1,0:T(8,128)(2,1)S(1)} all-to-all(bf16[8,1,128,128]{3,2,1,0:T(8,128)(2,1)S(1)} %residual1.1), channel_id=1, replica_groups=mesh['shot'=4,'band'=8] {'band'}, dimensions={0} | all-to-all | bytes 524288 | tf_op jit(solution)/shard_map/all_to_all | solution.py:289
  32.6 0.3 adjoint1_give_a.1
  33.0 0.4 adjoint1_keep_a.1
  33.5 0.5 collective-permute-start.2
  34.0 0.3 collective-permute-done.got_ref
  34.4 1.6 %collective-permute-start.1 = (bf16[4,128,128]{2,1,0:T(8,128)(2,1)S(1)}, bf16[4,128,128]{2,1,0:T(8,128)(2,1)S(1)}, u32[]{:S(2)}, u32[]{:S(2)}) collective-permute-start(bf16[4,128,128]{2,1,0:T(8,128)(2,1)S(1)} %adjoint1_pair_a.1.rest_0_), channel_id=1, source_target_pairs={{0,16},{8,24},{16,0},{24,8},{1,17},{9,25},{17,1},{25,9},{2,18},{10... | collective-permute-start | bytes 393224 | tf_op jit(solution)/shard_map/ppermute | solution.py:284
  36.3 0.6 collective-permute-start.3
  37.0 3.7 %collective-permute-done.1.rest_1_ = bf16[4,128,128]{2,1,0:T(8,128)(2,1)S(1)} collective-permute-done((bf16[4,128,128]{2,1,0:T(8,128)(2,1)S(1)}, bf16[4,128,128]{2,1,0:T(8,128)(2,1)S(1)}, u32[]{:S(2)}, u32[]{:S(2)}) %collective-permute-start.1) | collective-permute-done | bytes 131104 | tf_op jit(solution)/shard_map/ppermute | solution.py:284
  41.0 1.8 %collective-permute-done.3.rest_1_ = bf16[4,128,128]{2,1,0:T(8,128)(2,1)S(1)} collective-permute-done((bf16[4,128,128]{2,1,0:T(8,128)(2,1)S(1)}, bf16[4,128,128]{2,1,0:T(8,128)(2,1)S(1)}, u32[]{:S(2)}, u32[]{:S(2)}) %collective-permute-start.3) | collective-permute-done | bytes 131104 | tf_op jit(solution)/shard_map/ppermute | solution.py:284
  43.0 1.0 %forward2_early.1.early = f32[8,128,128]{2,1,0:T(8,128)S(1)} custom-call(bf16[2,1024,256]{2,1,0:T(8,128)(2,1)S(1)} %get-tuple-element.28.refs_0_.dense_own_a.rest_2_, bf16[2,1024,256]{2,1,0:T(8,128)(2,1)S(1)} %copy-done.1, bf16[2,1024,256]{2,1,0:T(8,128)(2,1)S(1)} %get-tuple-element.31.refs_0_.dense_mate_a.rest_1_, ...), custom_call_target="tpu_custom_call" | custom-call | flops 402653184 | bytes 3145728 | tf_op jit(solution)/shard_map/forward2_early/pallas_call | solution.py:396
  44.0 0.4 collective-permute-done.4.mate_b
  44.3 0.4 forward2_late.1
  44.8 12.6 %all_to_all.21 = bf16[8,128,128]{2,1,0:T(8,128)(2,1)S(1)} all-to-all(bf16[8,128,128]{2,1,0:T(8,128)(2,1)S(1)} %forward2_late.1), channel_id=1, replica_groups=mesh['shot'=4,'band'=8] {'band'}, dimensions={0} | all-to-all | bytes 524288 | tf_op jit(solution)/shard_map/all_to_all | solution.py:289
  57.5 12.0 %all_to_all.22 = bf16[8,1,128,128]{3,2,1,0:T(8,128)(2,1)S(1)} all-to-all(bf16[8,1,128,128]{3,2,1,0:T(8,128)(2,1)S(1)} %get-tuple-element.39), channel_id=1, replica_groups=mesh['shot'=4,'band'=8] {'band'}, dimensions={0} | all-to-all | bytes 524288 | tf_op jit(solution)/shard_map/all_to_all | solution.py:289
  69.4 0.3 adjoint2_give_a.1
  69.8 0.4 adjoint2_keep_a.1
  70.3 0.6 collective-permute-start.8
  70.8 0.3 collective-permute-done.6.got_ref
  71.2 1.6 %collective-permute-start.7 = (bf16[4,128,128]{2,1,0:T(8,128)(2,1)S(1)}, bf16[4,128,128]{2,1,0:T(8,128)(2,1)S(1)}, u32[]{:S(2)}, u32[]{:S(2)}) collective-permute-start(bf16[4,128,128]{2,1,0:T(8,128)(2,1)S(1)} %adjoint2_pair_a.1.rest_4_), channel_id=1, source_target_pairs={{0,16},{8,24},{16,0},{24,8},{1,17},{9,25},{17,1},{25,9},{2,18},{10... | collective-permute-start | bytes 393224 | tf_op jit(solution)/shard_map/ppermute | solution.py:284
  73.2 0.6 collective-permute-start.9
  73.7 0.7 turn.1
  74.4 3.2 %collective-permute-done.7.rest_5_ = bf16[4,128,128]{2,1,0:T(8,128)(2,1)S(1)} collective-permute-done((bf16[4,128,128]{2,1,0:T(8,128)(2,1)S(1)}, bf16[4,128,128]{2,1,0:T(8,128)(2,1)S(1)}, u32[]{:S(2)}, u32[]{:S(2)}) %collective-permute-start.7) | collective-permute-done | bytes 131104 | tf_op jit(solution)/shard_map/ppermute | solution.py:284
  77.8 1.8 %collective-permute-done.9.rest_1_ = bf16[4,128,128]{2,1,0:T(8,128)(2,1)S(1)} collective-permute-done((bf16[4,128,128]{2,1,0:T(8,128)(2,1)S(1)}, bf16[4,128,128]{2,1,0:T(8,128)(2,1)S(1)}, u32[]{:S(2)}, u32[]{:S(2)}) %collective-permute-start.9) | collective-permute-done | bytes 131104 | tf_op jit(solution)/shard_map/ppermute | solution.py:284
  79.9 0.9 %new_state_early.1 = (f32[16,128,128]{2,1,0:T(8,128)}, f32[4,128,128]{2,1,0:T(8,128)S(1)}) custom-call(f32[16,128,128]{2,1,0:T(8,128)S(1)} %get-tuple-element.26.base, bf16[4,128,128]{2,1,0:T(8,128)(2,1)S(1)} %total_a.1.own_a, bf16[4,128,128]{2,1,0:T(8,128)(2,1)S(1)} %total_b.1.own_b, bf16[4,128,128]{2,1,0:T(8,128)(2,1)S(1)} %collective-permute-done.10.mate_a), custom_call_target="tpu_custom_call" | custom-call | bytes 3145728 | tf_op jit(solution)/shard_map/new_state_early/pallas_call | solution.py:439
  80.8 0.4 collective-permute-done.11.mate_b
  81.2 0.7 new_state_late.1
  (39 shorter events, 2.1 us)
Async XLA Ops:
  0.6 11.0 %copy-start.7 = (s32[64]{0:T(128)S(1)}, s32[64]{0:T(128)}, u32[]{:S(2)}) copy-start(s32[64]{0:T(128)} %bund.1) | copy-start | bytes 772
  0.6 11.0 %copy-start.8 = (s32[64]{0:T(128)S(1)}, s32[64]{0:T(128)}, u32[]{:S(2)}) copy-start(s32[64]{0:T(128)} %cblk.1) | copy-start | bytes 772
  4.3 16.2 %copy-start.5 = (f32[1,128]{1,0:T(1,128)S(1)}, f32[1,128]{1,0:T(1,128)}, u32[]{:S(2)}) copy-start(f32[1,128]{1,0:T(1,128)} %obs_ref.3) | copy-start | bytes 1540
  4.3 16.2 %copy-start.6 = (f32[1,128]{1,0:T(1,128)S(1)}, f32[1,128]{1,0:T(1,128)}, u32[]{:S(2)}) copy-start(f32[1,128]{1,0:T(1,128)} %wt_ref.3) | copy-start | bytes 1540
  4.3 16.2 %all-to-all-start = ((bf16[8,128,128]{2,1,0:T(8,128)(2,1)}), bf16[8,128,128]{2,1,0:T(8,128)(2,1)S(1)}, u32[]{:S(2)}, u32[]{:S(2)}) async-start(bf16[8,128,128]{2,1,0:T(8,128)(2,1)} %forward1.1), calls=%async_computation | async-start | bytes 524288 | tf_op jit(solution)/shard_map/all_to_all | solution.py:289
  11.6 1.6 %copy-start.2 = (bf16[64,128,128]{2,1,0:T(8,128)(2,1)S(1)}, bf16[64,128,128]{2,1,0:T(8,128)(2,1)}, u32[]{:S(2)}) copy-start(bf16[64,128,128]{2,1,0:T(8,128)(2,1)} %sens.1) | copy-start | bytes 6291460
  16.7 1.0 %copy-start = (bf16[2,1024,256]{2,1,0:T(8,128)(2,1)}, bf16[2,1024,256]{2,1,0:T(8,128)(2,1)S(1)}, u32[]{:S(2)}) copy-start(bf16[2,1024,256]{2,1,0:T(8,128)(2,1)S(1)} %get-tuple-element.25.refs_0_.dense_own_b) | copy-start | bytes 3145732
  32.6 3.4 %copy-start.1 = (bf16[2,1024,256]{2,1,0:T(8,128)(2,1)S(1)}, bf16[2,1024,256]{2,1,0:T(8,128)(2,1)}, u32[]{:S(2)}) copy-start(bf16[2,1024,256]{2,1,0:T(8,128)(2,1)} %copy-done) | copy-start | bytes 3145732
  32.9 1.4 %collective-permute-start = (bf16[4,128,128]{2,1,0:T(8,128)(2,1)S(1)}, bf16[4,128,128]{2,1,0:T(8,128)(2,1)S(1)}, u32[]{:S(2)}, u32[]{:S(2)}) collective-permute-start(bf16[4,128,128]{2,1,0:T(8,128)(2,1)S(1)} %adjoint1_give_a.1), channel_id=1, source_target_pairs={{0,8},{8,0},{16,24},{24,16},{1,9},{9,1},{17,25},{25,17},{2,10},{10... | collective-permute-start | bytes 393224 | tf_op jit(solution)/shard_map/ppermute | solution.py:280
  33.0 3.9 %copy-start.3 = (f32[2048,128]{1,0:T(8,128)S(1)}, f32[2048,128]{1,0:T(8,128)}, u32[]{:S(2)}) copy-start(f32[2048,128]{1,0:T(8,128)} %param.10) | copy-start | bytes 3145732
  33.0 3.9 %copy-start.4 = (f32[2048,128]{1,0:T(8,128)S(1)}, f32[2048,128]{1,0:T(8,128)}, u32[]{:S(2)}) copy-start(f32[2048,128]{1,0:T(8,128)} %param.11) | copy-start | bytes 3145732
  33.5 2.8 %collective-permute-start.2 = (bf16[4,128,128]{2,1,0:T(8,128)(2,1)S(1)}, bf16[4,128,128]{2,1,0:T(8,128)(2,1)S(1)}, u32[]{:S(2)}, u32[]{:S(2)}) collective-permute-start(bf16[4,128,128]{2,1,0:T(8,128)(2,1)S(1)} %get-tuple-element.34), channel_id=1, source_target_pairs={{0,8},{8,0},{16,24},{24,16},{1,9},{9,1},{17,25},{25,17},{2,10},{10... | collective-permute-start | bytes 393224 | tf_op jit(solution)/shard_map/ppermute | solution.py:280
  34.4 6.4 %collective-permute-start.1 = (bf16[4,128,128]{2,1,0:T(8,128)(2,1)S(1)}, bf16[4,128,128]{2,1,0:T(8,128)(2,1)S(1)}, u32[]{:S(2)}, u32[]{:S(2)}) collective-permute-start(bf16[4,128,128]{2,1,0:T(8,128)(2,1)S(1)} %adjoint1_pair_a.1.rest_0_), channel_id=1, source_target_pairs={{0,16},{8,24},{16,0},{24,8},{1,17},{9,25},{17,1},{25,9},{2,18},{10... | collective-permute-start | bytes 393224 | tf_op jit(solution)/shard_map/ppermute | solution.py:284
  36.3 6.5 %collective-permute-start.3 = (bf16[4,128,128]{2,1,0:T(8,128)(2,1)S(1)}, bf16[4,128,128]{2,1,0:T(8,128)(2,1)S(1)}, u32[]{:S(2)}, u32[]{:S(2)}) collective-permute-start(bf16[4,128,128]{2,1,0:T(8,128)(2,1)S(1)} %adjoint1_pair_b.1.rest_0_), channel_id=1, source_target_pairs={{0,16},{8,24},{16,0},{24,8},{1,17},{9,25},{17,1},{25,9},{2,18},{10... | collective-permute-start | bytes 393224 | tf_op jit(solution)/shard_map/ppermute | solution.py:284
  40.9 2.1 %collective-permute-start.5 = (bf16[4,128,128]{2,1,0:T(8,128)(2,1)S(1)}, bf16[4,128,128]{2,1,0:T(8,128)(2,1)S(1)}, u32[]{:S(2)}, u32[]{:S(2)}) collective-permute-start(bf16[4,128,128]{2,1,0:T(8,128)(2,1)S(1)} %get-tuple-element.36.own_a), channel_id=1, source_target_pairs={{0,8},{8,0},{16,24},{24,16},{1,9},{9,1},{17,25},{25,17},{2,10},{10... | collective-permute-start | bytes 393224 | tf_op jit(solution)/shard_map/ppermute | solution.py:280
  42.9 1.4 %collective-permute-start.4 = (bf16[4,128,128]{2,1,0:T(8,128)(2,1)S(1)}, bf16[4,128,128]{2,1,0:T(8,128)(2,1)S(1)}, u32[]{:S(2)}, u32[]{:S(2)}) collective-permute-start(bf16[4,128,128]{2,1,0:T(8,128)(2,1)S(1)} %get-tuple-element.35.own_b), channel_id=1, source_target_pairs={{0,8},{8,0},{16,24},{24,16},{1,9},{9,1},{17,25},{25,17},{2,10},{10... | collective-permute-start | bytes 393224 | tf_op jit(solution)/shard_map/ppermute | solution.py:280
  69.8 1.4 %collective-permute-start.6 = (bf16[4,128,128]{2,1,0:T(8,128)(2,1)S(1)}, bf16[4,128,128]{2,1,0:T(8,128)(2,1)S(1)}, u32[]{:S(2)}, u32[]{:S(2)}) collective-permute-start(bf16[4,128,128]{2,1,0:T(8,128)(2,1)S(1)} %adjoint2_give_a.1), channel_id=1, source_target_pairs={{0,8},{8,0},{16,24},{24,16},{1,9},{9,1},{17,25},{25,17},{2,10},{10... | collective-permute-start | bytes 393224 | tf_op jit(solution)/shard_map/ppermute | solution.py:280
  70.3 2.8 %collective-permute-start.8 = (bf16[4,128,128]{2,1,0:T(8,128)(2,1)S(1)}, bf16[4,128,128]{2,1,0:T(8,128)(2,1)S(1)}, u32[]{:S(2)}, u32[]{:S(2)}) collective-permute-start(bf16[4,128,128]{2,1,0:T(8,128)(2,1)S(1)} %get-tuple-element.42), channel_id=1, source_target_pairs={{0,8},{8,0},{16,24},{24,16},{1,9},{9,1},{17,25},{25,17},{2,10},{10... | collective-permute-start | bytes 393224 | tf_op jit(solution)/shard_map/ppermute | solution.py:280
  71.2 6.4 %collective-permute-start.7 = (bf16[4,128,128]{2,1,0:T(8,128)(2,1)S(1)}, bf16[4,128,128]{2,1,0:T(8,128)(2,1)S(1)}, u32[]{:S(2)}, u32[]{:S(2)}) collective-permute-start(bf16[4,128,128]{2,1,0:T(8,128)(2,1)S(1)} %adjoint2_pair_a.1.rest_4_), channel_id=1, source_target_pairs={{0,16},{8,24},{16,0},{24,8},{1,17},{9,25},{17,1},{25,9},{2,18},{10... | collective-permute-start | bytes 393224 | tf_op jit(solution)/shard_map/ppermute | solution.py:284
  73.2 6.5 %collective-permute-start.9 = (bf16[4,128,128]{2,1,0:T(8,128)(2,1)S(1)}, bf16[4,128,128]{2,1,0:T(8,128)(2,1)S(1)}, u32[]{:S(2)}, u32[]{:S(2)}) collective-permute-start(bf16[4,128,128]{2,1,0:T(8,128)(2,1)S(1)} %adjoint2_pair_b.1.rest_0_), channel_id=1, source_target_pairs={{0,16},{8,24},{16,0},{24,8},{1,17},{9,25},{17,1},{25,9},{2,18},{10... | collective-permute-start | bytes 393224 | tf_op jit(solution)/shard_map/ppermute | solution.py:284
  77.8 2.1 %collective-permute-start.10 = (bf16[4,128,128]{2,1,0:T(8,128)(2,1)S(1)}, bf16[4,128,128]{2,1,0:T(8,128)(2,1)S(1)}, u32[]{:S(2)}, u32[]{:S(2)}) collective-permute-start(bf16[4,128,128]{2,1,0:T(8,128)(2,1)S(1)} %total_a.1.own_a), channel_id=1, source_target_pairs={{0,8},{8,0},{16,24},{24,16},{1,9},{9,1},{17,25},{25,17},{2,10},{10... | collective-permute-start | bytes 393224 | tf_op jit(solution)/shard_map/ppermute | solution.py:280
  79.8 1.4 %collective-permute-start.11 = (bf16[4,128,128]{2,1,0:T(8,128)(2,1)S(1)}, bf16[4,128,128]{2,1,0:T(8,128)(2,1)S(1)}, u32[]{:S(2)}, u32[]{:S(2)}) collective-permute-start(bf16[4,128,128]{2,1,0:T(8,128)(2,1)S(1)} %total_b.1.own_b), channel_id=1, source_target_pairs={{0,8},{8,0},{16,24},{24,16},{1,9},{9,1},{17,25},{25,17},{2,10},{10... | collective-permute-start | bytes 393224 | tf_op jit(solution)/shard_map/ppermute | solution.py:280

commit v13 on v12

--- a/solution.py
+++ b/solution.py
@@ -47,6 +47,7 @@
     prior_hbm,
     out_ref,
     acc,
+    acc_odd,
     probe,
     bund,
     cblk,
@@ -87,7 +88,9 @@
     for c in range(CHUNKS):
         for copy in block_copies(c):
             copy.start()
-    acc[...] = jnp.zeros_like(acc)
+    accs = (acc, acc_odd)
+    for ref in accs:
+        ref[...] = jnp.zeros_like(ref)
 
     for h in range(FIELDS):
         part = pl.ds(h * share, share)
@@ -105,12 +108,12 @@
             prods = [
                 jnp.dot(sens[k], probe[cblk[k]], preferred_element_type=f32) for k in ks
             ]
-            for k, prod in zip(ks, prods):
-                acc[bund[k]] += prod
+            for j, (k, prod) in enumerate(zip(ks, prods)):
+                accs[j % 2][bund[k]] += prod
         return carry
 
     lax.fori_loop(0, CHUNKS, chunk, 0)
-    out_ref[...] = acc[...].astype(bf16)
+    out_ref[...] = (acc[...] + acc_odd[...]).astype(bf16)
 
 
 def dense_kernel(bund, cblk, sens, *rest):
@@ -342,6 +345,7 @@
         first_forward_kernel,
         part_out,
         [
+            pltpu.VMEM((bundles, rays, samples), f32),
             pltpu.VMEM((bundles, rays, samples), f32),
             pltpu.VMEM((cells, CBLK, samples), bf16),
             pltpu.SMEM((nblk,), i32),

time: 82.3 us -> 82.3 us (level)
  no operation moved by 1% of the time
where the time goes in v13:
time: 82.3 us; the launch traced here: 81.9 us
  blocking collectives  36.5 us (44%)
  waiting for transfers between devices  14.7 us (18%)
  Pallas kernels  14.1 us (17%)
  starting transfers between devices  13.1 us (16%)
  local copies, waits for them, and re-layouts  2.59 us (3%)
  between operations  0.95 us (1%)
    all_to_all x3, blocking collectives, over_band(): lax.all_to_all(array, 'band', split_axis=0, concat_axis=0, tiled=True)  36.5 us
    ppermute x4, waiting for transfers between devices, other_chips(): lax.ppermute(array, 'shot', [(i, i ^ 2 * d) for i in range(nshot)])  10.5 us
    all_to_all x1, starting transfers between devices, over_band(): lax.all_to_all(array, 'band', split_axis=0, concat_axis=0, tiled=True)  7.26 us
    ppermute x4, starting transfers between devices, other_chips(): lax.ppermute(array, 'shot', [(i, i ^ 2 * d) for i in range(nshot)])  4.31 us
    pallas_call x1, Pallas kernels, per_device(): call(first_forward_kernel, part_out, [pltpu.VMEM((bundles, rays, samples)...  3.69 us
    pallas_call x1, Pallas kernels, per_device(): call(dense_kernel, (arr(dense_shape, bf16),) * 4 + (small_token,), [pltpu...  3.48 us
    all_to_all x1, waiting for transfers between devices, over_band(): lax.all_to_all(array, 'band', split_axis=0, concat_axis=0, tiled=True)  2.84 us
    unnamed x18, local copies, waits for them, and re-layouts  2.59 us
  transfers between devices with their start and end apart: 13, of which 9 were waited for; matrix products, arithmetic and copies ran while one was open for 0% of the time, Pallas kernels for 10%

profile of v13, /device:TPU:0, one launch (start us, length us, event | category | flops | bytes accessed | tf_op | source)
XLA Modules:
  0.0 81.9 jit_solution(676134711762799313)
XLA Ops:
  0.6 3.7 %forward1.1 = bf16[8,128,128]{2,1,0:T(8,128)(2,1)} custom-call(s32[64]{0:T(128)} %bund.1, s32[64]{0:T(128)} %cblk.1, bf16[64,128,128]{2,1,0:T(8,128)(2,1)} %sens.1, f32[16,128,128]{2,1,0:T(8,128)} %bitcast.7, f32[16,128,128]{2,1,0:T(8,128)} %bitcast.9), custom_call_target="tpu_custom_call" | custom-call | flops 268435456 | bytes 2097152 | tf_op jit(solution)/shard_map/forward1/pallas_call | solution.py:344
  4.4 7.3 %all-to-all-start = ((bf16[8,128,128]{2,1,0:T(8,128)(2,1)}), bf16[8,128,128]{2,1,0:T(8,128)(2,1)S(1)}, u32[]{:S(2)}, u32[]{:S(2)}) async-start(bf16[8,128,128]{2,1,0:T(8,128)(2,1)} %forward1.1), calls=%async_computation | async-start | bytes 524288 | tf_op jit(solution)/shard_map/all_to_all | solution.py:292
  11.7 1.6 %copy-done.2 = bf16[64,128,128]{2,1,0:T(8,128)(2,1)S(1)} copy-done((bf16[64,128,128]{2,1,0:T(8,128)(2,1)S(1)}, bf16[64,128,128]{2,1,0:T(8,128)(2,1)}, u32[]{:S(2)}) %copy-start.2) | copy-done | bytes 2097176
  13.2 3.5 %dense.1 = (bf16[2,1024,256]{2,1,0:T(8,128)(2,1)S(1)}, bf16[2,1024,256]{2,1,0:T(8,128)(2,1)S(1)}, bf16[2,1024,256]{2,1,0:T(8,128)(2,1)S(1)}, bf16[2,1024,256]{2,1,0:T(8,128)(2,1)S(1)}, f32[8,128]{1,0:T(8,128)S(1)}) custom-call(s32[64]{0:T(128)S(1)} %copy-done.7, s32[64]{0:T(128)S(1)} %copy-done.8, bf16[64,128,128]{2,1,0:T(8,128)(2,1)S(1)} %copy-done.2), custom_call_target="tpu_custom_call" | custom-call | bytes 16777216 | tf_op jit(solution)/shard_map/dense/pallas_call | solution.py:364
  16.7 1.0 %copy-done = bf16[2,1024,256]{2,1,0:T(8,128)(2,1)} copy-done((bf16[2,1024,256]{2,1,0:T(8,128)(2,1)}, bf16[2,1024,256]{2,1,0:T(8,128)(2,1)S(1)}, u32[]{:S(2)}) %copy-start) | copy-done | bytes 1048600
  17.7 2.8 %all-to-all-done = bf16[8,128,128]{2,1,0:T(8,128)(2,1)S(1)} async-done(((bf16[8,128,128]{2,1,0:T(8,128)(2,1)}), bf16[8,128,128]{2,1,0:T(8,128)(2,1)S(1)}, u32[]{:S(2)}, u32[]{:S(2)}) %all-to-all-start) | async-done | bytes 262176 | tf_op jit(solution)/shard_map/all_to_all | solution.py:292
  20.7 12.0 %all_to_all.20 = bf16[8,1,128,128]{3,2,1,0:T(8,128)(2,1)S(1)} all-to-all(bf16[8,1,128,128]{3,2,1,0:T(8,128)(2,1)S(1)} %residual1.1), channel_id=1, replica_groups=mesh['shot'=4,'band'=8] {'band'}, dimensions={0} | all-to-all | bytes 524288 | tf_op jit(solution)/shard_map/all_to_all | solution.py:292
  32.6 0.3 adjoint1_give_a.1
  33.0 0.4 adjoint1_keep_a.1
  33.5 0.5 collective-permute-start.2
  34.0 0.3 collective-permute-done.got_ref
  34.4 1.6 %collective-permute-start.1 = (bf16[4,128,128]{2,1,0:T(8,128)(2,1)S(1)}, bf16[4,128,128]{2,1,0:T(8,128)(2,1)S(1)}, u32[]{:S(2)}, u32[]{:S(2)}) collective-permute-start(bf16[4,128,128]{2,1,0:T(8,128)(2,1)S(1)} %adjoint1_pair_a.1.rest_0_), channel_id=1, source_target_pairs={{0,16},{8,24},{16,0},{24,8},{1,17},{9,25},{17,1},{25,9},{2,18},{10... | collective-permute-start | bytes 393224 | tf_op jit(solution)/shard_map/ppermute | solution.py:287
  36.3 0.6 collective-permute-start.3
  37.1 3.7 %collective-permute-done.1.rest_1_ = bf16[4,128,128]{2,1,0:T(8,128)(2,1)S(1)} collective-permute-done((bf16[4,128,128]{2,1,0:T(8,128)(2,1)S(1)}, bf16[4,128,128]{2,1,0:T(8,128)(2,1)S(1)}, u32[]{:S(2)}, u32[]{:S(2)}) %collective-permute-start.1) | collective-permute-done | bytes 131104 | tf_op jit(solution)/shard_map/ppermute | solution.py:287
  41.0 1.8 %collective-permute-done.3.rest_1_ = bf16[4,128,128]{2,1,0:T(8,128)(2,1)S(1)} collective-permute-done((bf16[4,128,128]{2,1,0:T(8,128)(2,1)S(1)}, bf16[4,128,128]{2,1,0:T(8,128)(2,1)S(1)}, u32[]{:S(2)}, u32[]{:S(2)}) %collective-permute-start.3) | collective-permute-done | bytes 131104 | tf_op jit(solution)/shard_map/ppermute | solution.py:287
  43.0 1.0 %forward2_early.1.early = f32[8,128,128]{2,1,0:T(8,128)S(1)} custom-call(bf16[2,1024,256]{2,1,0:T(8,128)(2,1)S(1)} %get-tuple-element.28.refs_0_.dense_own_a.rest_2_, bf16[2,1024,256]{2,1,0:T(8,128)(2,1)S(1)} %copy-done.1, bf16[2,1024,256]{2,1,0:T(8,128)(2,1)S(1)} %get-tuple-element.31.refs_0_.dense_mate_a.rest_1_, ...), custom_call_target="tpu_custom_call" | custom-call | flops 402653184 | bytes 3145728 | tf_op jit(solution)/shard_map/forward2_early/pallas_call | solution.py:400
  44.0 0.4 collective-permute-done.4.mate_b
  44.4 0.4 forward2_late.1
  44.8 12.6 %all_to_all.21 = bf16[8,128,128]{2,1,0:T(8,128)(2,1)S(1)} all-to-all(bf16[8,128,128]{2,1,0:T(8,128)(2,1)S(1)} %forward2_late.1), channel_id=1, replica_groups=mesh['shot'=4,'band'=8] {'band'}, dimensions={0} | all-to-all | bytes 524288 | tf_op jit(solution)/shard_map/all_to_all | solution.py:292
  57.5 12.0 %all_to_all.22 = bf16[8,1,128,128]{3,2,1,0:T(8,128)(2,1)S(1)} all-to-all(bf16[8,1,128,128]{3,2,1,0:T(8,128)(2,1)S(1)} %get-tuple-element.39), channel_id=1, replica_groups=mesh['shot'=4,'band'=8] {'band'}, dimensions={0} | all-to-all | bytes 524288 | tf_op jit(solution)/shard_map/all_to_all | solution.py:292
  69.5 0.3 adjoint2_give_a.1
  69.9 0.4 adjoint2_keep_a.1
  70.3 0.6 collective-permute-start.8
  70.9 0.3 collective-permute-done.6.got_ref
  71.2 1.6 %collective-permute-start.7 = (bf16[4,128,128]{2,1,0:T(8,128)(2,1)S(1)}, bf16[4,128,128]{2,1,0:T(8,128)(2,1)S(1)}, u32[]{:S(2)}, u32[]{:S(2)}) collective-permute-start(bf16[4,128,128]{2,1,0:T(8,128)(2,1)S(1)} %adjoint2_pair_a.1.rest_4_), channel_id=1, source_target_pairs={{0,16},{8,24},{16,0},{24,8},{1,17},{9,25},{17,1},{25,9},{2,18},{10... | collective-permute-start | bytes 393224 | tf_op jit(solution)/shard_map/ppermute | solution.py:287
  73.2 0.6 collective-permute-start.9
  73.7 0.7 turn.1
  74.5 3.2 %collective-permute-done.7.rest_5_ = bf16[4,128,128]{2,1,0:T(8,128)(2,1)S(1)} collective-permute-done((bf16[4,128,128]{2,1,0:T(8,128)(2,1)S(1)}, bf16[4,128,128]{2,1,0:T(8,128)(2,1)S(1)}, u32[]{:S(2)}, u32[]{:S(2)}) %collective-permute-start.7) | collective-permute-done | bytes 131104 | tf_op jit(solution)/shard_map/ppermute | solution.py:287
  77.9 1.8 %collective-permute-done.9.rest_1_ = bf16[4,128,128]{2,1,0:T(8,128)(2,1)S(1)} collective-permute-done((bf16[4,128,128]{2,1,0:T(8,128)(2,1)S(1)}, bf16[4,128,128]{2,1,0:T(8,128)(2,1)S(1)}, u32[]{:S(2)}, u32[]{:S(2)}) %collective-permute-start.9) | collective-permute-done | bytes 131104 | tf_op jit(solution)/shard_map/ppermute | solution.py:287
  79.9 0.9 %new_state_early.1 = (f32[16,128,128]{2,1,0:T(8,128)}, f32[4,128,128]{2,1,0:T(8,128)S(1)}) custom-call(f32[16,128,128]{2,1,0:T(8,128)S(1)} %get-tuple-element.26.base, bf16[4,128,128]{2,1,0:T(8,128)(2,1)S(1)} %total_a.1.own_a, bf16[4,128,128]{2,1,0:T(8,128)(2,1)S(1)} %total_b.1.own_b, bf16[4,128,128]{2,1,0:T(8,128)(2,1)S(1)} %collective-permute-done.10.mate_a), custom_call_target="tpu_custom_call" | custom-call | bytes 3145728 | tf_op jit(solution)/shard_map/new_state_early/pallas_call | solution.py:443
  80.8 0.4 collective-permute-done.11.mate_b
  81.2 0.7 new_state_late.1
  (39 shorter events, 2.1 us)
Async XLA Ops:
  0.6 11.0 %copy-start.7 = (s32[64]{0:T(128)S(1)}, s32[64]{0:T(128)}, u32[]{:S(2)}) copy-start(s32[64]{0:T(128)} %bund.1) | copy-start | bytes 772
  0.6 11.0 %copy-start.8 = (s32[64]{0:T(128)S(1)}, s32[64]{0:T(128)}, u32[]{:S(2)}) copy-start(s32[64]{0:T(128)} %cblk.1) | copy-start | bytes 772
  4.3 16.2 %copy-start.5 = (f32[1,128]{1,0:T(1,128)S(1)}, f32[1,128]{1,0:T(1,128)}, u32[]{:S(2)}) copy-start(f32[1,128]{1,0:T(1,128)} %obs_ref.3) | copy-start | bytes 1540
  4.4 16.2 %copy-start.6 = (f32[1,128]{1,0:T(1,128)S(1)}, f32[1,128]{1,0:T(1,128)}, u32[]{:S(2)}) copy-start(f32[1,128]{1,0:T(1,128)} %wt_ref.3) | copy-start | bytes 1540
  4.4 16.2 %all-to-all-start = ((bf16[8,128,128]{2,1,0:T(8,128)(2,1)}), bf16[8,128,128]{2,1,0:T(8,128)(2,1)S(1)}, u32[]{:S(2)}, u32[]{:S(2)}) async-start(bf16[8,128,128]{2,1,0:T(8,128)(2,1)} %forward1.1), calls=%async_computation | async-start | bytes 524288 | tf_op jit(solution)/shard_map/all_to_all | solution.py:292
  11.6 1.6 %copy-start.2 = (bf16[64,128,128]{2,1,0:T(8,128)(2,1)S(1)}, bf16[64,128,128]{2,1,0:T(8,128)(2,1)}, u32[]{:S(2)}) copy-start(bf16[64,128,128]{2,1,0:T(8,128)(2,1)} %sens.1) | copy-start | bytes 6291460
  16.7 1.0 %copy-start = (bf16[2,1024,256]{2,1,0:T(8,128)(2,1)}, bf16[2,1024,256]{2,1,0:T(8,128)(2,1)S(1)}, u32[]{:S(2)}) copy-start(bf16[2,1024,256]{2,1,0:T(8,128)(2,1)S(1)} %get-tuple-element.25.refs_0_.dense_own_b) | copy-start | bytes 3145732
  32.6 3.4 %copy-start.1 = (bf16[2,1024,256]{2,1,0:T(8,128)(2,1)S(1)}, bf16[2,1024,256]{2,1,0:T(8,128)(2,1)}, u32[]{:S(2)}) copy-start(bf16[2,1024,256]{2,1,0:T(8,128)(2,1)} %copy-done) | copy-start | bytes 3145732
  32.9 1.4 %collective-permute-start = (bf16[4,128,128]{2,1,0:T(8,128)(2,1)S(1)}, bf16[4,128,128]{2,1,0:T(8,128)(2,1)S(1)}, u32[]{:S(2)}, u32[]{:S(2)}) collective-permute-start(bf16[4,128,128]{2,1,0:T(8,128)(2,1)S(1)} %adjoint1_give_a.1), channel_id=1, source_target_pairs={{0,8},{8,0},{16,24},{24,16},{1,9},{9,1},{17,25},{25,17},{2,10},{10... | collective-permute-start | bytes 393224 | tf_op jit(solution)/shard_map/ppermute | solution.py:283
  33.0 3.9 %copy-start.3 = (f32[2048,128]{1,0:T(8,128)S(1)}, f32[2048,128]{1,0:T(8,128)}, u32[]{:S(2)}) copy-start(f32[2048,128]{1,0:T(8,128)} %param.10) | copy-start | bytes 3145732
  33.0 3.9 %copy-start.4 = (f32[2048,128]{1,0:T(8,128)S(1)}, f32[2048,128]{1,0:T(8,128)}, u32[]{:S(2)}) copy-start(f32[2048,128]{1,0:T(8,128)} %param.11) | copy-start | bytes 3145732
  33.5 2.8 %collective-permute-start.2 = (bf16[4,128,128]{2,1,0:T(8,128)(2,1)S(1)}, bf16[4,128,128]{2,1,0:T(8,128)(2,1)S(1)}, u32[]{:S(2)}, u32[]{:S(2)}) collective-permute-start(bf16[4,128,128]{2,1,0:T(8,128)(2,1)S(1)} %get-tuple-element.34), channel_id=1, source_target_pairs={{0,8},{8,0},{16,24},{24,16},{1,9},{9,1},{17,25},{25,17},{2,10},{10... | collective-permute-start | bytes 393224 | tf_op jit(solution)/shard_map/ppermute | solution.py:283
  34.4 6.4 %collective-permute-start.1 = (bf16[4,128,128]{2,1,0:T(8,128)(2,1)S(1)}, bf16[4,128,128]{2,1,0:T(8,128)(2,1)S(1)}, u32[]{:S(2)}, u32[]{:S(2)}) collective-permute-start(bf16[4,128,128]{2,1,0:T(8,128)(2,1)S(1)} %adjoint1_pair_a.1.rest_0_), channel_id=1, source_target_pairs={{0,16},{8,24},{16,0},{24,8},{1,17},{9,25},{17,1},{25,9},{2,18},{10... | collective-permute-start | bytes 393224 | tf_op jit(solution)/shard_map/ppermute | solution.py:287
  36.3 6.5 %collective-permute-start.3 = (bf16[4,128,128]{2,1,0:T(8,128)(2,1)S(1)}, bf16[4,128,128]{2,1,0:T(8,128)(2,1)S(1)}, u32[]{:S(2)}, u32[]{:S(2)}) collective-permute-start(bf16[4,128,128]{2,1,0:T(8,128)(2,1)S(1)} %adjoint1_pair_b.1.rest_0_), channel_id=1, source_target_pairs={{0,16},{8,24},{16,0},{24,8},{1,17},{9,25},{17,1},{25,9},{2,18},{10... | collective-permute-start | bytes 393224 | tf_op jit(solution)/shard_map/ppermute | solution.py:287
  40.9 2.1 %collective-permute-start.5 = (bf16[4,128,128]{2,1,0:T(8,128)(2,1)S(1)}, bf16[4,128,128]{2,1,0:T(8,128)(2,1)S(1)}, u32[]{:S(2)}, u32[]{:S(2)}) collective-permute-start(bf16[4,128,128]{2,1,0:T(8,128)(2,1)S(1)} %get-tuple-element.36.own_a), channel_id=1, source_target_pairs={{0,8},{8,0},{16,24},{24,16},{1,9},{9,1},{17,25},{25,17},{2,10},{10... | collective-permute-start | bytes 393224 | tf_op jit(solution)/shard_map/ppermute | solution.py:283
  42.9 1.4 %collective-permute-start.4 = (bf16[4,128,128]{2,1,0:T(8,128)(2,1)S(1)}, bf16[4,128,128]{2,1,0:T(8,128)(2,1)S(1)}, u32[]{:S(2)}, u32[]{:S(2)}) collective-permute-start(bf16[4,128,128]{2,1,0:T(8,128)(2,1)S(1)} %get-tuple-element.35.own_b), channel_id=1, source_target_pairs={{0,8},{8,0},{16,24},{24,16},{1,9},{9,1},{17,25},{25,17},{2,10},{10... | collective-permute-start | bytes 393224 | tf_op jit(solution)/shard_map/ppermute | solution.py:283
  69.8 1.4 %collective-permute-start.6 = (bf16[4,128,128]{2,1,0:T(8,128)(2,1)S(1)}, bf16[4,128,128]{2,1,0:T(8,128)(2,1)S(1)}, u32[]{:S(2)}, u32[]{:S(2)}) collective-permute-start(bf16[4,128,128]{2,1,0:T(8,128)(2,1)S(1)} %adjoint2_give_a.1), channel_id=1, source_target_pairs={{0,8},{8,0},{16,24},{24,16},{1,9},{9,1},{17,25},{25,17},{2,10},{10... | collective-permute-start | bytes 393224 | tf_op jit(solution)/shard_map/ppermute | solution.py:283
  70.3 2.8 %collective-permute-start.8 = (bf16[4,128,128]{2,1,0:T(8,128)(2,1)S(1)}, bf16[4,128,128]{2,1,0:T(8,128)(2,1)S(1)}, u32[]{:S(2)}, u32[]{:S(2)}) collective-permute-start(bf16[4,128,128]{2,1,0:T(8,128)(2,1)S(1)} %get-tuple-element.42), channel_id=1, source_target_pairs={{0,8},{8,0},{16,24},{24,16},{1,9},{9,1},{17,25},{25,17},{2,10},{10... | collective-permute-start | bytes 393224 | tf_op jit(solution)/shard_map/ppermute | solution.py:283
  71.2 6.4 %collective-permute-start.7 = (bf16[4,128,128]{2,1,0:T(8,128)(2,1)S(1)}, bf16[4,128,128]{2,1,0:T(8,128)(2,1)S(1)}, u32[]{:S(2)}, u32[]{:S(2)}) collective-permute-start(bf16[4,128,128]{2,1,0:T(8,128)(2,1)S(1)} %adjoint2_pair_a.1.rest_4_), channel_id=1, source_target_pairs={{0,16},{8,24},{16,0},{24,8},{1,17},{9,25},{17,1},{25,9},{2,18},{10... | collective-permute-start | bytes 393224 | tf_op jit(solution)/shard_map/ppermute | solution.py:287
  73.2 6.5 %collective-permute-start.9 = (bf16[4,128,128]{2,1,0:T(8,128)(2,1)S(1)}, bf16[4,128,128]{2,1,0:T(8,128)(2,1)S(1)}, u32[]{:S(2)}, u32[]{:S(2)}) collective-permute-start(bf16[4,128,128]{2,1,0:T(8,128)(2,1)S(1)} %adjoint2_pair_b.1.rest_0_), channel_id=1, source_target_pairs={{0,16},{8,24},{16,0},{24,8},{1,17},{9,25},{17,1},{25,9},{2,18},{10... | collective-permute-start | bytes 393224 | tf_op jit(solution)/shard_map/ppermute | solution.py:287
  77.8 2.1 %collective-permute-start.10 = (bf16[4,128,128]{2,1,0:T(8,128)(2,1)S(1)}, bf16[4,128,128]{2,1,0:T(8,128)(2,1)S(1)}, u32[]{:S(2)}, u32[]{:S(2)}) collective-permute-start(bf16[4,128,128]{2,1,0:T(8,128)(2,1)S(1)} %total_a.1.own_a), channel_id=1, source_target_pairs={{0,8},{8,0},{16,24},{24,16},{1,9},{9,1},{17,25},{25,17},{2,10},{10... | collective-permute-start | bytes 393224 | tf_op jit(solution)/shard_map/ppermute | solution.py:283
  79.8 1.4 %collective-permute-start.11 = (bf16[4,128,128]{2,1,0:T(8,128)(2,1)S(1)}, bf16[4,128,128]{2,1,0:T(8,128)(2,1)S(1)}, u32[]{:S(2)}, u32[]{:S(2)}) collective-permute-start(bf16[4,128,128]{2,1,0:T(8,128)(2,1)S(1)} %total_b.1.own_b), channel_id=1, source_target_pairs={{0,8},{8,0},{16,24},{24,16},{1,9},{9,1},{17,25},{25,17},{2,10},{10... | collective-permute-start | bytes 393224 | tf_op jit(solution)/shard_map/ppermute | solution.py:283

commit v14 on v12

--- a/solution.py
+++ b/solution.py
@@ -97,16 +97,29 @@
     for copy in small:
         copy.wait()
 
+    samples = acc.shape[2]
+    none = jnp.zeros(probe.shape[1:], bf16)
+
+    def two_products(k1, k2):
+        rhs = jnp.concatenate(
+            [
+                jnp.concatenate([probe[cblk[k1]], none], axis=1),
+                jnp.concatenate([none, probe[cblk[k2]]], axis=1),
+            ],
+            axis=0,
+        )
+        lhs = jnp.concatenate([sens[k1], sens[k2]], axis=1)
+        return jnp.dot(lhs, rhs, preferred_element_type=f32)
+
     def chunk(c, carry):
         for copy in block_copies(c):
             copy.wait()
         for g in range(step // GROUP):
             ks = [c * step + g * GROUP + j for j in range(GROUP)]
-            prods = [
-                jnp.dot(sens[k], probe[cblk[k]], preferred_element_type=f32) for k in ks
-            ]
-            for k, prod in zip(ks, prods):
-                acc[bund[k]] += prod
+            prods = [two_products(k1, k2) for k1, k2 in zip(ks[0::2], ks[1::2])]
+            for j, k in enumerate(ks):
+                lanes = slice(j % 2 * samples, (j % 2 + 1) * samples)
+                acc[bund[k]] += prods[j // 2][:, lanes]
         return carry
 
     lax.fori_loop(0, CHUNKS, chunk, 0)

time: 82.3 us -> 82.3 us (level)
  no operation moved by 1% of the time
where the time goes in v14:
time: 82.3 us; the launch traced here: 82 us
  blocking collectives  36.5 us (44%)
  waiting for transfers between devices  14.7 us (18%)
  Pallas kernels  14.1 us (17%)
  starting transfers between devices  13.1 us (16%)
  local copies, waits for them, and re-layouts  2.59 us (3%)
  between operations  0.95 us (1%)
    all_to_all x3, blocking collectives, over_band(): lax.all_to_all(array, 'band', split_axis=0, concat_axis=0, tiled=True)  36.5 us
    ppermute x4, waiting for transfers between devices, other_chips(): lax.ppermute(array, 'shot', [(i, i ^ 2 * d) for i in range(nshot)])  10.5 us
    all_to_all x1, starting transfers between devices, over_band(): lax.all_to_all(array, 'band', split_axis=0, concat_axis=0, tiled=True)  7.26 us
    ppermute x4, starting transfers between devices, other_chips(): lax.ppermute(array, 'shot', [(i, i ^ 2 * d) for i in range(nshot)])  4.32 us
    pallas_call x1, Pallas kernels, per_device(): call(first_forward_kernel, part_out, [pltpu.VMEM((bundles, rays, samples)...  3.69 us
    pallas_call x1, Pallas kernels, per_device(): call(dense_kernel, (arr(dense_shape, bf16),) * 4 + (small_token,), [pltpu...  3.48 us
    all_to_all x1, waiting for transfers between devices, over_band(): lax.all_to_all(array, 'band', split_axis=0, concat_axis=0, tiled=True)  2.85 us
    unnamed x18, local copies, waits for them, and re-layouts  2.59 us
  transfers between devices with their start and end apart: 13, of which 9 were waited for; matrix products, arithmetic and copies ran while one was open for 0% of the time, Pallas kernels for 10%

profile of v14, /device:TPU:0, one launch (start us, length us, event | category | flops | bytes accessed | tf_op | source)
XLA Modules:
  0.0 82.0 jit_solution(2721622648011155624)
XLA Ops:
  0.6 3.7 %forward1.1 = bf16[8,128,128]{2,1,0:T(8,128)(2,1)} custom-call(s32[64]{0:T(128)} %bund.1, s32[64]{0:T(128)} %cblk.1, bf16[64,128,128]{2,1,0:T(8,128)(2,1)} %sens.1, f32[16,128,128]{2,1,0:T(8,128)} %bitcast.7, f32[16,128,128]{2,1,0:T(8,128)} %bitcast.9), custom_call_target="tpu_custom_call" | custom-call | flops 268435456 | bytes 2097152 | tf_op jit(solution)/shard_map/forward1/pallas_call | solution.py:354
  4.4 7.3 %all-to-all-start = ((bf16[8,128,128]{2,1,0:T(8,128)(2,1)}), bf16[8,128,128]{2,1,0:T(8,128)(2,1)S(1)}, u32[]{:S(2)}, u32[]{:S(2)}) async-start(bf16[8,128,128]{2,1,0:T(8,128)(2,1)} %forward1.1), calls=%async_computation | async-start | bytes 524288 | tf_op jit(solution)/shard_map/all_to_all | solution.py:302
  11.7 1.6 %copy-done.2 = bf16[64,128,128]{2,1,0:T(8,128)(2,1)S(1)} copy-done((bf16[64,128,128]{2,1,0:T(8,128)(2,1)S(1)}, bf16[64,128,128]{2,1,0:T(8,128)(2,1)}, u32[]{:S(2)}) %copy-start.2) | copy-done | bytes 2097176
  13.2 3.5 %dense.1 = (bf16[2,1024,256]{2,1,0:T(8,128)(2,1)S(1)}, bf16[2,1024,256]{2,1,0:T(8,128)(2,1)S(1)}, bf16[2,1024,256]{2,1,0:T(8,128)(2,1)S(1)}, bf16[2,1024,256]{2,1,0:T(8,128)(2,1)S(1)}, f32[8,128]{1,0:T(8,128)S(1)}) custom-call(s32[64]{0:T(128)S(1)} %copy-done.7, s32[64]{0:T(128)S(1)} %copy-done.8, bf16[64,128,128]{2,1,0:T(8,128)(2,1)S(1)} %copy-done.2), custom_call_target="tpu_custom_call" | custom-call | bytes 16777216 | tf_op jit(solution)/shard_map/dense/pallas_call | solution.py:373
  16.7 1.0 %copy-done = bf16[2,1024,256]{2,1,0:T(8,128)(2,1)} copy-done((bf16[2,1024,256]{2,1,0:T(8,128)(2,1)}, bf16[2,1024,256]{2,1,0:T(8,128)(2,1)S(1)}, u32[]{:S(2)}) %copy-start) | copy-done | bytes 1048600
  17.7 2.9 %all-to-all-done = bf16[8,128,128]{2,1,0:T(8,128)(2,1)S(1)} async-done(((bf16[8,128,128]{2,1,0:T(8,128)(2,1)}), bf16[8,128,128]{2,1,0:T(8,128)(2,1)S(1)}, u32[]{:S(2)}, u32[]{:S(2)}) %all-to-all-start) | async-done | bytes 262176 | tf_op jit(solution)/shard_map/all_to_all | solution.py:302
  20.7 12.0 %all_to_all.20 = bf16[8,1,128,128]{3,2,1,0:T(8,128)(2,1)S(1)} all-to-all(bf16[8,1,128,128]{3,2,1,0:T(8,128)(2,1)S(1)} %residual1.1), channel_id=1, replica_groups=mesh['shot'=4,'band'=8] {'band'}, dimensions={0} | all-to-all | bytes 524288 | tf_op jit(solution)/shard_map/all_to_all | solution.py:302
  32.6 0.3 adjoint1_give_a.1
  33.0 0.4 adjoint1_keep_a.1
  33.5 0.5 collective-permute-start.2
  34.0 0.3 collective-permute-done.got_ref
  34.4 1.6 %collective-permute-start.1 = (bf16[4,128,128]{2,1,0:T(8,128)(2,1)S(1)}, bf16[4,128,128]{2,1,0:T(8,128)(2,1)S(1)}, u32[]{:S(2)}, u32[]{:S(2)}) collective-permute-start(bf16[4,128,128]{2,1,0:T(8,128)(2,1)S(1)} %adjoint1_pair_a.1.rest_0_), channel_id=1, source_target_pairs={{0,16},{8,24},{16,0},{24,8},{1,17},{9,25},{17,1},{25,9},{2,18},{10... | collective-permute-start | bytes 393224 | tf_op jit(solution)/shard_map/ppermute | solution.py:297
  36.3 0.6 collective-permute-start.3
  37.1 3.7 %collective-permute-done.1.rest_1_ = bf16[4,128,128]{2,1,0:T(8,128)(2,1)S(1)} collective-permute-done((bf16[4,128,128]{2,1,0:T(8,128)(2,1)S(1)}, bf16[4,128,128]{2,1,0:T(8,128)(2,1)S(1)}, u32[]{:S(2)}, u32[]{:S(2)}) %collective-permute-start.1) | collective-permute-done | bytes 131104 | tf_op jit(solution)/shard_map/ppermute | solution.py:297
  41.0 1.8 %collective-permute-done.3.rest_1_ = bf16[4,128,128]{2,1,0:T(8,128)(2,1)S(1)} collective-permute-done((bf16[4,128,128]{2,1,0:T(8,128)(2,1)S(1)}, bf16[4,128,128]{2,1,0:T(8,128)(2,1)S(1)}, u32[]{:S(2)}, u32[]{:S(2)}) %collective-permute-start.3) | collective-permute-done | bytes 131104 | tf_op jit(solution)/shard_map/ppermute | solution.py:297
  43.0 1.0 %forward2_early.1.early = f32[8,128,128]{2,1,0:T(8,128)S(1)} custom-call(bf16[2,1024,256]{2,1,0:T(8,128)(2,1)S(1)} %get-tuple-element.28.refs_0_.dense_own_a.rest_2_, bf16[2,1024,256]{2,1,0:T(8,128)(2,1)S(1)} %copy-done.1, bf16[2,1024,256]{2,1,0:T(8,128)(2,1)S(1)} %get-tuple-element.31.refs_0_.dense_mate_a.rest_1_, ...), custom_call_target="tpu_custom_call" | custom-call | flops 402653184 | bytes 3145728 | tf_op jit(solution)/shard_map/forward2_early/pallas_call | solution.py:409
  44.0 0.4 collective-permute-done.4.mate_b
  44.4 0.4 forward2_late.1
  44.8 12.6 %all_to_all.21 = bf16[8,128,128]{2,1,0:T(8,128)(2,1)S(1)} all-to-all(bf16[8,128,128]{2,1,0:T(8,128)(2,1)S(1)} %forward2_late.1), channel_id=1, replica_groups=mesh['shot'=4,'band'=8] {'band'}, dimensions={0} | all-to-all | bytes 524288 | tf_op jit(solution)/shard_map/all_to_all | solution.py:302
  57.5 12.0 %all_to_all.22 = bf16[8,1,128,128]{3,2,1,0:T(8,128)(2,1)S(1)} all-to-all(bf16[8,1,128,128]{3,2,1,0:T(8,128)(2,1)S(1)} %get-tuple-element.39), channel_id=1, replica_groups=mesh['shot'=4,'band'=8] {'band'}, dimensions={0} | all-to-all | bytes 524288 | tf_op jit(solution)/shard_map/all_to_all | solution.py:302
  69.5 0.3 adjoint2_give_a.1
  69.9 0.4 adjoint2_keep_a.1
  70.3 0.6 collective-permute-start.8
  70.9 0.3 collective-permute-done.6.got_ref
  71.2 1.6 %collective-permute-start.7 = (bf16[4,128,128]{2,1,0:T(8,128)(2,1)S(1)}, bf16[4,128,128]{2,1,0:T(8,128)(2,1)S(1)}, u32[]{:S(2)}, u32[]{:S(2)}) collective-permute-start(bf16[4,128,128]{2,1,0:T(8,128)(2,1)S(1)} %adjoint2_pair_a.1.rest_4_), channel_id=1, source_target_pairs={{0,16},{8,24},{16,0},{24,8},{1,17},{9,25},{17,1},{25,9},{2,18},{10... | collective-permute-start | bytes 393224 | tf_op jit(solution)/shard_map/ppermute | solution.py:297
  73.2 0.6 collective-permute-start.9
  73.8 0.7 turn.1
  74.5 3.2 %collective-permute-done.7.rest_5_ = bf16[4,128,128]{2,1,0:T(8,128)(2,1)S(1)} collective-permute-done((bf16[4,128,128]{2,1,0:T(8,128)(2,1)S(1)}, bf16[4,128,128]{2,1,0:T(8,128)(2,1)S(1)}, u32[]{:S(2)}, u32[]{:S(2)}) %collective-permute-start.7) | collective-permute-done | bytes 131104 | tf_op jit(solution)/shard_map/ppermute | solution.py:297
  77.9 1.8 %collective-permute-done.9.rest_1_ = bf16[4,128,128]{2,1,0:T(8,128)(2,1)S(1)} collective-permute-done((bf16[4,128,128]{2,1,0:T(8,128)(2,1)S(1)}, bf16[4,128,128]{2,1,0:T(8,128)(2,1)S(1)}, u32[]{:S(2)}, u32[]{:S(2)}) %collective-permute-start.9) | collective-permute-done | bytes 131104 | tf_op jit(solution)/shard_map/ppermute | solution.py:297
  79.9 0.9 %new_state_early.1 = (f32[16,128,128]{2,1,0:T(8,128)}, f32[4,128,128]{2,1,0:T(8,128)S(1)}) custom-call(f32[16,128,128]{2,1,0:T(8,128)S(1)} %get-tuple-element.26.base, bf16[4,128,128]{2,1,0:T(8,128)(2,1)S(1)} %total_a.1.own_a, bf16[4,128,128]{2,1,0:T(8,128)(2,1)S(1)} %total_b.1.own_b, bf16[4,128,128]{2,1,0:T(8,128)(2,1)S(1)} %collective-permute-done.10.mate_a), custom_call_target="tpu_custom_call" | custom-call | bytes 3145728 | tf_op jit(solution)/shard_map/new_state_early/pallas_call | solution.py:452
  80.8 0.4 collective-permute-done.11.mate_b
  81.2 0.7 new_state_late.1
  (39 shorter events, 2.1 us)
Async XLA Ops:
  0.6 11.0 %copy-start.7 = (s32[64]{0:T(128)S(1)}, s32[64]{0:T(128)}, u32[]{:S(2)}) copy-start(s32[64]{0:T(128)} %bund.1) | copy-start | bytes 772
  0.6 11.0 %copy-start.8 = (s32[64]{0:T(128)S(1)}, s32[64]{0:T(128)}, u32[]{:S(2)}) copy-start(s32[64]{0:T(128)} %cblk.1) | copy-start | bytes 772
  4.3 16.2 %copy-start.5 = (f32[1,128]{1,0:T(1,128)S(1)}, f32[1,128]{1,0:T(1,128)}, u32[]{:S(2)}) copy-start(f32[1,128]{1,0:T(1,128)} %obs_ref.3) | copy-start | bytes 1540
  4.4 16.2 %copy-start.6 = (f32[1,128]{1,0:T(1,128)S(1)}, f32[1,128]{1,0:T(1,128)}, u32[]{:S(2)}) copy-start(f32[1,128]{1,0:T(1,128)} %wt_ref.3) | copy-start | bytes 1540
  4.4 16.2 %all-to-all-start = ((bf16[8,128,128]{2,1,0:T(8,128)(2,1)}), bf16[8,128,128]{2,1,0:T(8,128)(2,1)S(1)}, u32[]{:S(2)}, u32[]{:S(2)}) async-start(bf16[8,128,128]{2,1,0:T(8,128)(2,1)} %forward1.1), calls=%async_computation | async-start | bytes 524288 | tf_op jit(solution)/shard_map/all_to_all | solution.py:302
  11.6 1.6 %copy-start.2 = (bf16[64,128,128]{2,1,0:T(8,128)(2,1)S(1)}, bf16[64,128,128]{2,1,0:T(8,128)(2,1)}, u32[]{:S(2)}) copy-start(bf16[64,128,128]{2,1,0:T(8,128)(2,1)} %sens.1) | copy-start | bytes 6291460
  16.7 1.0 %copy-start = (bf16[2,1024,256]{2,1,0:T(8,128)(2,1)}, bf16[2,1024,256]{2,1,0:T(8,128)(2,1)S(1)}, u32[]{:S(2)}) copy-start(bf16[2,1024,256]{2,1,0:T(8,128)(2,1)S(1)} %get-tuple-element.25.refs_0_.dense_own_b) | copy-start | bytes 3145732
  32.6 3.4 %copy-start.1 = (bf16[2,1024,256]{2,1,0:T(8,128)(2,1)S(1)}, bf16[2,1024,256]{2,1,0:T(8,128)(2,1)}, u32[]{:S(2)}) copy-start(bf16[2,1024,256]{2,1,0:T(8,128)(2,1)} %copy-done) | copy-start | bytes 3145732
  32.9 1.4 %collective-permute-start = (bf16[4,128,128]{2,1,0:T(8,128)(2,1)S(1)}, bf16[4,128,128]{2,1,0:T(8,128)(2,1)S(1)}, u32[]{:S(2)}, u32[]{:S(2)}) collective-permute-start(bf16[4,128,128]{2,1,0:T(8,128)(2,1)S(1)} %adjoint1_give_a.1), channel_id=1, source_target_pairs={{0,8},{8,0},{16,24},{24,16},{1,9},{9,1},{17,25},{25,17},{2,10},{10... | collective-permute-start | bytes 393224 | tf_op jit(solution)/shard_map/ppermute | solution.py:293
  33.0 3.9 %copy-start.3 = (f32[2048,128]{1,0:T(8,128)S(1)}, f32[2048,128]{1,0:T(8,128)}, u32[]{:S(2)}) copy-start(f32[2048,128]{1,0:T(8,128)} %param.10) | copy-start | bytes 3145732
  33.0 3.9 %copy-start.4 = (f32[2048,128]{1,0:T(8,128)S(1)}, f32[2048,128]{1,0:T(8,128)}, u32[]{:S(2)}) copy-start(f32[2048,128]{1,0:T(8,128)} %param.11) | copy-start | bytes 3145732
  33.5 2.8 %collective-permute-start.2 = (bf16[4,128,128]{2,1,0:T(8,128)(2,1)S(1)}, bf16[4,128,128]{2,1,0:T(8,128)(2,1)S(1)}, u32[]{:S(2)}, u32[]{:S(2)}) collective-permute-start(bf16[4,128,128]{2,1,0:T(8,128)(2,1)S(1)} %get-tuple-element.34), channel_id=1, source_target_pairs={{0,8},{8,0},{16,24},{24,16},{1,9},{9,1},{17,25},{25,17},{2,10},{10... | collective-permute-start | bytes 393224 | tf_op jit(solution)/shard_map/ppermute | solution.py:293
  34.4 6.4 %collective-permute-start.1 = (bf16[4,128,128]{2,1,0:T(8,128)(2,1)S(1)}, bf16[4,128,128]{2,1,0:T(8,128)(2,1)S(1)}, u32[]{:S(2)}, u32[]{:S(2)}) collective-permute-start(bf16[4,128,128]{2,1,0:T(8,128)(2,1)S(1)} %adjoint1_pair_a.1.rest_0_), channel_id=1, source_target_pairs={{0,16},{8,24},{16,0},{24,8},{1,17},{9,25},{17,1},{25,9},{2,18},{10... | collective-permute-start | bytes 393224 | tf_op jit(solution)/shard_map/ppermute | solution.py:297
  36.3 6.5 %collective-permute-start.3 = (bf16[4,128,128]{2,1,0:T(8,128)(2,1)S(1)}, bf16[4,128,128]{2,1,0:T(8,128)(2,1)S(1)}, u32[]{:S(2)}, u32[]{:S(2)}) collective-permute-start(bf16[4,128,128]{2,1,0:T(8,128)(2,1)S(1)} %adjoint1_pair_b.1.rest_0_), channel_id=1, source_target_pairs={{0,16},{8,24},{16,0},{24,8},{1,17},{9,25},{17,1},{25,9},{2,18},{10... | collective-permute-start | bytes 393224 | tf_op jit(solution)/shard_map/ppermute | solution.py:297
  40.9 2.1 %collective-permute-start.5 = (bf16[4,128,128]{2,1,0:T(8,128)(2,1)S(1)}, bf16[4,128,128]{2,1,0:T(8,128)(2,1)S(1)}, u32[]{:S(2)}, u32[]{:S(2)}) collective-permute-start(bf16[4,128,128]{2,1,0:T(8,128)(2,1)S(1)} %get-tuple-element.36.own_a), channel_id=1, source_target_pairs={{0,8},{8,0},{16,24},{24,16},{1,9},{9,1},{17,25},{25,17},{2,10},{10... | collective-permute-start | bytes 393224 | tf_op jit(solution)/shard_map/ppermute | solution.py:293
  42.9 1.4 %collective-permute-start.4 = (bf16[4,128,128]{2,1,0:T(8,128)(2,1)S(1)}, bf16[4,128,128]{2,1,0:T(8,128)(2,1)S(1)}, u32[]{:S(2)}, u32[]{:S(2)}) collective-permute-start(bf16[4,128,128]{2,1,0:T(8,128)(2,1)S(1)} %get-tuple-element.35.own_b), channel_id=1, source_target_pairs={{0,8},{8,0},{16,24},{24,16},{1,9},{9,1},{17,25},{25,17},{2,10},{10... | collective-permute-start | bytes 393224 | tf_op jit(solution)/shard_map/ppermute | solution.py:293
  69.8 1.4 %collective-permute-start.6 = (bf16[4,128,128]{2,1,0:T(8,128)(2,1)S(1)}, bf16[4,128,128]{2,1,0:T(8,128)(2,1)S(1)}, u32[]{:S(2)}, u32[]{:S(2)}) collective-permute-start(bf16[4,128,128]{2,1,0:T(8,128)(2,1)S(1)} %adjoint2_give_a.1), channel_id=1, source_target_pairs={{0,8},{8,0},{16,24},{24,16},{1,9},{9,1},{17,25},{25,17},{2,10},{10... | collective-permute-start | bytes 393224 | tf_op jit(solution)/shard_map/ppermute | solution.py:293
  70.3 2.8 %collective-permute-start.8 = (bf16[4,128,128]{2,1,0:T(8,128)(2,1)S(1)}, bf16[4,128,128]{2,1,0:T(8,128)(2,1)S(1)}, u32[]{:S(2)}, u32[]{:S(2)}) collective-permute-start(bf16[4,128,128]{2,1,0:T(8,128)(2,1)S(1)} %get-tuple-element.42), channel_id=1, source_target_pairs={{0,8},{8,0},{16,24},{24,16},{1,9},{9,1},{17,25},{25,17},{2,10},{10... | collective-permute-start | bytes 393224 | tf_op jit(solution)/shard_map/ppermute | solution.py:293
  71.2 6.4 %collective-permute-start.7 = (bf16[4,128,128]{2,1,0:T(8,128)(2,1)S(1)}, bf16[4,128,128]{2,1,0:T(8,128)(2,1)S(1)}, u32[]{:S(2)}, u32[]{:S(2)}) collective-permute-start(bf16[4,128,128]{2,1,0:T(8,128)(2,1)S(1)} %adjoint2_pair_a.1.rest_4_), channel_id=1, source_target_pairs={{0,16},{8,24},{16,0},{24,8},{1,17},{9,25},{17,1},{25,9},{2,18},{10... | collective-permute-start | bytes 393224 | tf_op jit(solution)/shard_map/ppermute | solution.py:297
  73.2 6.5 %collective-permute-start.9 = (bf16[4,128,128]{2,1,0:T(8,128)(2,1)S(1)}, bf16[4,128,128]{2,1,0:T(8,128)(2,1)S(1)}, u32[]{:S(2)}, u32[]{:S(2)}) collective-permute-start(bf16[4,128,128]{2,1,0:T(8,128)(2,1)S(1)} %adjoint2_pair_b.1.rest_0_), channel_id=1, source_target_pairs={{0,16},{8,24},{16,0},{24,8},{1,17},{9,25},{17,1},{25,9},{2,18},{10... | collective-permute-start | bytes 393224 | tf_op jit(solution)/shard_map/ppermute | solution.py:297
  77.8 2.1 %collective-permute-start.10 = (bf16[4,128,128]{2,1,0:T(8,128)(2,1)S(1)}, bf16[4,128,128]{2,1,0:T(8,128)(2,1)S(1)}, u32[]{:S(2)}, u32[]{:S(2)}) collective-permute-start(bf16[4,128,128]{2,1,0:T(8,128)(2,1)S(1)} %total_a.1.own_a), channel_id=1, source_target_pairs={{0,8},{8,0},{16,24},{24,16},{1,9},{9,1},{17,25},{25,17},{2,10},{10... | collective-permute-start | bytes 393224 | tf_op jit(solution)/shard_map/ppermute | solution.py:293
  79.8 1.4 %collective-permute-start.11 = (bf16[4,128,128]{2,1,0:T(8,128)(2,1)S(1)}, bf16[4,128,128]{2,1,0:T(8,128)(2,1)S(1)}, u32[]{:S(2)}, u32[]{:S(2)}) collective-permute-start(bf16[4,128,128]{2,1,0:T(8,128)(2,1)S(1)} %total_b.1.own_b), channel_id=1, source_target_pairs={{0,8},{8,0},{16,24},{24,16},{1,9},{9,1},{17,25},{25,17},{2,10},{10... | collective-permute-start | bytes 393224 | tf_op jit(solution)/shard_map/ppermute | solution.py:293

commit v15 on v12

--- a/solution.py
+++ b/solution.py
@@ -11,6 +11,7 @@
 GROUP = 32
 CHUNKS = 2
 FIELDS = 4
+WRITES = 4
 FIRST_VMEM = 55 << 20
 GIVE_A, KEEP_A, GIVE_B, KEEP_B = range(4)
 
@@ -45,7 +46,7 @@
     sens_hbm,
     state_hbm,
     prior_hbm,
-    out_ref,
+    out_hbm,
     acc,
     probe,
     bund,
@@ -54,6 +55,8 @@
     state,
     prior,
     sems,
+    out,
+    out_sems,
 ):
     nblk = sens.shape[0]
     step = nblk // CHUNKS
@@ -110,7 +113,15 @@
         return carry
 
     lax.fori_loop(0, CHUNKS, chunk, 0)
-    out_ref[...] = acc[...].astype(bf16)
+    share = out_hbm.shape[0] // WRITES
+    writes = []
+    for n in range(WRITES):
+        part = pl.ds(n * share, share)
+        out[part] = acc[part].astype(bf16)
+        writes.append(pltpu.make_async_copy(out.at[part], out_hbm.at[part], out_sems.at[n]))
+        writes[-1].start()
+    for copy in writes:
+        copy.wait()
 
 
 def dense_kernel(bund, cblk, sens, *rest):
@@ -253,13 +264,16 @@
         copy.wait()
 
 
-def late_update_kernel(rest_ref, mate_b, so_far_hbm, out_hbm, new, sem):
+def late_update_kernel(rest_ref, mate_b, so_far_hbm, out_hbm, new, sems):
     quarter = mate_b.shape[0]
     at = (1 - lax.axis_index("shot") % 2) * (2 * quarter) + quarter
-    new[...] = rest_ref[...] - 0.125 * mate_b[...].astype(f32)
-    copy = pltpu.make_async_copy(new, out_hbm.at[pl.ds(at, quarter)], sem)
-    copy.start()
-    copy.wait()
+    copies = []
+    for n in range(quarter):
+        new[n] = rest_ref[n] - 0.125 * mate_b[n].astype(f32)
+        copies.append(pltpu.make_async_copy(new.at[n], out_hbm.at[at + n], sems.at[n]))
+        copies[-1].start()
+    for copy in copies:
+        copy.wait()
 
 
 def per_device(nshot, nband, sens, bund, cblk, state, prior, observed, pick_weight):
@@ -350,12 +364,15 @@
             pltpu.VMEM(state_b.shape, f32),
             pltpu.VMEM(state_b.shape, f32),
             pltpu.SemaphoreType.DMA((2 + 2 * FIELDS + 2 * CHUNKS,)),
+            pltpu.VMEM((bundles, rays, samples), bf16),
+            pltpu.SemaphoreType.DMA((WRITES,)),
         ],
         [HBM] * 5,
         "forward1",
         flops,
         sens_bytes,
         vmem=FIRST_VMEM,
+        out_specs=HBM,
     )(bund, cblk, sens, state_b, prior_b)
     dense_keep_b, *dense, token = call(
         dense_kernel,
@@ -448,7 +465,7 @@
     new_state = call(
         late_update_kernel,
         whole,
-        [pltpu.VMEM((quarter, CBLK, samples), f32), pltpu.SemaphoreType.DMA],
+        [pltpu.VMEM((quarter, CBLK, samples), f32), pltpu.SemaphoreType.DMA((quarter,))],
         [VMEM, VMEM, HBM],
         "new_state_late",
         bytes_accessed=1 << 20,

time: 82.3 us -> 82.3 us (level)
  no operation moved by 1% of the time
where the time goes in v15:
time: 82.3 us; the launch traced here: 81.9 us
  blocking collectives  36.5 us (44%)
  waiting for transfers between devices  14.7 us (18%)
  Pallas kernels  14.1 us (17%)
  starting transfers between devices  13.1 us (16%)
  local copies, waits for them, and re-layouts  2.59 us (3%)
  between operations  0.95 us (1%)
    all_to_all x3, blocking collectives, over_band(): lax.all_to_all(array, 'band', split_axis=0, concat_axis=0, tiled=True)  36.5 us
    ppermute x4, waiting for transfers between devices, other_chips(): lax.ppermute(array, 'shot', [(i, i ^ 2 * d) for i in range(nshot)])  10.5 us
    all_to_all x1, starting transfers between devices, over_band(): lax.all_to_all(array, 'band', split_axis=0, concat_axis=0, tiled=True)  7.27 us
    ppermute x4, starting transfers between devices, other_chips(): lax.ppermute(array, 'shot', [(i, i ^ 2 * d) for i in range(nshot)])  4.31 us
    pallas_call x1, Pallas kernels, per_device(): call(first_forward_kernel, part_out, [pltpu.VMEM((bundles, rays, samples)...  3.67 us
    pallas_call x1, Pallas kernels, per_device(): call(dense_kernel, (arr(dense_shape, bf16),) * 4 + (small_token,), [pltpu...  3.48 us
    all_to_all x1, waiting for transfers between devices, over_band(): lax.all_to_all(array, 'band', split_axis=0, concat_axis=0, tiled=True)  2.85 us
    unnamed x18, local copies, waits for them, and re-layouts  2.59 us
  transfers between devices with their start and end apart: 13, of which 9 were waited for; matrix products, arithmetic and copies ran while one was open for 0% of the time, Pallas kernels for 10%

profile of v15, /device:TPU:0, one launch (start us, length us, event | category | flops | bytes accessed | tf_op | source)
XLA Modules:
  0.0 81.9 jit_solution(1867843733143580834)
XLA Ops:
  0.6 3.7 %forward1.1 = bf16[8,128,128]{2,1,0:T(8,128)(2,1)} custom-call(s32[64]{0:T(128)} %bund.1, s32[64]{0:T(128)} %cblk.1, bf16[64,128,128]{2,1,0:T(8,128)(2,1)} %sens.1, f32[16,128,128]{2,1,0:T(8,128)} %bitcast.7, f32[16,128,128]{2,1,0:T(8,128)} %bitcast.9), custom_call_target="tpu_custom_call" | custom-call | flops 268435456 | bytes 2097152 | tf_op jit(solution)/shard_map/forward1/pallas_call | solution.py:355
  4.3 7.3 %all-to-all-start = ((bf16[8,128,128]{2,1,0:T(8,128)(2,1)}), bf16[8,128,128]{2,1,0:T(8,128)(2,1)S(1)}, u32[]{:S(2)}, u32[]{:S(2)}) async-start(bf16[8,128,128]{2,1,0:T(8,128)(2,1)} %forward1.1), calls=%async_computation | async-start | bytes 524288 | tf_op jit(solution)/shard_map/all_to_all | solution.py:303
  11.6 1.6 %copy-done.2 = bf16[64,128,128]{2,1,0:T(8,128)(2,1)S(1)} copy-done((bf16[64,128,128]{2,1,0:T(8,128)(2,1)S(1)}, bf16[64,128,128]{2,1,0:T(8,128)(2,1)}, u32[]{:S(2)}) %copy-start.2) | copy-done | bytes 2097176
  13.2 3.5 %dense.1 = (bf16[2,1024,256]{2,1,0:T(8,128)(2,1)S(1)}, bf16[2,1024,256]{2,1,0:T(8,128)(2,1)S(1)}, bf16[2,1024,256]{2,1,0:T(8,128)(2,1)S(1)}, bf16[2,1024,256]{2,1,0:T(8,128)(2,1)S(1)}, f32[8,128]{1,0:T(8,128)S(1)}) custom-call(s32[64]{0:T(128)S(1)} %copy-done.7, s32[64]{0:T(128)S(1)} %copy-done.8, bf16[64,128,128]{2,1,0:T(8,128)(2,1)S(1)} %copy-done.2), custom_call_target="tpu_custom_call" | custom-call | bytes 16777216 | tf_op jit(solution)/shard_map/dense/pallas_call | solution.py:377
  16.7 1.0 %copy-done = bf16[2,1024,256]{2,1,0:T(8,128)(2,1)} copy-done((bf16[2,1024,256]{2,1,0:T(8,128)(2,1)}, bf16[2,1024,256]{2,1,0:T(8,128)(2,1)S(1)}, u32[]{:S(2)}) %copy-start) | copy-done | bytes 1048600
  17.7 2.8 %all-to-all-done = bf16[8,128,128]{2,1,0:T(8,128)(2,1)S(1)} async-done(((bf16[8,128,128]{2,1,0:T(8,128)(2,1)}), bf16[8,128,128]{2,1,0:T(8,128)(2,1)S(1)}, u32[]{:S(2)}, u32[]{:S(2)}) %all-to-all-start) | async-done | bytes 262176 | tf_op jit(solution)/shard_map/all_to_all | solution.py:303
  20.7 12.0 %all_to_all.20 = bf16[8,1,128,128]{3,2,1,0:T(8,128)(2,1)S(1)} all-to-all(bf16[8,1,128,128]{3,2,1,0:T(8,128)(2,1)S(1)} %residual1.1), channel_id=1, replica_groups=mesh['shot'=4,'band'=8] {'band'}, dimensions={0} | all-to-all | bytes 524288 | tf_op jit(solution)/shard_map/all_to_all | solution.py:303
  32.6 0.3 adjoint1_give_a.1
  33.0 0.4 adjoint1_keep_a.1
  33.5 0.5 collective-permute-start.2
  34.0 0.3 collective-permute-done.got_ref
  34.4 1.6 %collective-permute-start.1 = (bf16[4,128,128]{2,1,0:T(8,128)(2,1)S(1)}, bf16[4,128,128]{2,1,0:T(8,128)(2,1)S(1)}, u32[]{:S(2)}, u32[]{:S(2)}) collective-permute-start(bf16[4,128,128]{2,1,0:T(8,128)(2,1)S(1)} %adjoint1_pair_a.1.rest_0_), channel_id=1, source_target_pairs={{0,16},{8,24},{16,0},{24,8},{1,17},{9,25},{17,1},{25,9},{2,18},{10... | collective-permute-start | bytes 393224 | tf_op jit(solution)/shard_map/ppermute | solution.py:298
  36.3 0.6 collective-permute-start.3
  37.1 3.7 %collective-permute-done.1.rest_1_ = bf16[4,128,128]{2,1,0:T(8,128)(2,1)S(1)} collective-permute-done((bf16[4,128,128]{2,1,0:T(8,128)(2,1)S(1)}, bf16[4,128,128]{2,1,0:T(8,128)(2,1)S(1)}, u32[]{:S(2)}, u32[]{:S(2)}) %collective-permute-start.1) | collective-permute-done | bytes 131104 | tf_op jit(solution)/shard_map/ppermute | solution.py:298
  41.0 1.8 %collective-permute-done.3.rest_1_ = bf16[4,128,128]{2,1,0:T(8,128)(2,1)S(1)} collective-permute-done((bf16[4,128,128]{2,1,0:T(8,128)(2,1)S(1)}, bf16[4,128,128]{2,1,0:T(8,128)(2,1)S(1)}, u32[]{:S(2)}, u32[]{:S(2)}) %collective-permute-start.3) | collective-permute-done | bytes 131104 | tf_op jit(solution)/shard_map/ppermute | solution.py:298
  43.0 1.0 %forward2_early.1.early = f32[8,128,128]{2,1,0:T(8,128)S(1)} custom-call(bf16[2,1024,256]{2,1,0:T(8,128)(2,1)S(1)} %get-tuple-element.28.refs_0_.dense_own_a.rest_2_, bf16[2,1024,256]{2,1,0:T(8,128)(2,1)S(1)} %copy-done.1, bf16[2,1024,256]{2,1,0:T(8,128)(2,1)S(1)} %get-tuple-element.31.refs_0_.dense_mate_a.rest_1_, ...), custom_call_target="tpu_custom_call" | custom-call | flops 402653184 | bytes 3145728 | tf_op jit(solution)/shard_map/forward2_early/pallas_call | solution.py:413
  44.0 0.4 collective-permute-done.4.mate_b
  44.3 0.4 forward2_late.1
  44.8 12.6 %all_to_all.21 = bf16[8,128,128]{2,1,0:T(8,128)(2,1)S(1)} all-to-all(bf16[8,128,128]{2,1,0:T(8,128)(2,1)S(1)} %forward2_late.1), channel_id=1, replica_groups=mesh['shot'=4,'band'=8] {'band'}, dimensions={0} | all-to-all | bytes 524288 | tf_op jit(solution)/shard_map/all_to_all | solution.py:303
  57.5 12.0 %all_to_all.22 = bf16[8,1,128,128]{3,2,1,0:T(8,128)(2,1)S(1)} all-to-all(bf16[8,1,128,128]{3,2,1,0:T(8,128)(2,1)S(1)} %get-tuple-element.39), channel_id=1, replica_groups=mesh['shot'=4,'band'=8] {'band'}, dimensions={0} | all-to-all | bytes 524288 | tf_op jit(solution)/shard_map/all_to_all | solution.py:303
  69.5 0.3 adjoint2_give_a.1
  69.9 0.4 adjoint2_keep_a.1
  70.3 0.6 collective-permute-start.8
  70.9 0.3 collective-permute-done.6.got_ref
  71.2 1.6 %collective-permute-start.7 = (bf16[4,128,128]{2,1,0:T(8,128)(2,1)S(1)}, bf16[4,128,128]{2,1,0:T(8,128)(2,1)S(1)}, u32[]{:S(2)}, u32[]{:S(2)}) collective-permute-start(bf16[4,128,128]{2,1,0:T(8,128)(2,1)S(1)} %adjoint2_pair_a.1.rest_4_), channel_id=1, source_target_pairs={{0,16},{8,24},{16,0},{24,8},{1,17},{9,25},{17,1},{25,9},{2,18},{10... | collective-permute-start | bytes 393224 | tf_op jit(solution)/shard_map/ppermute | solution.py:298
  73.2 0.6 collective-permute-start.9
  73.7 0.7 turn.1
  74.5 3.2 %collective-permute-done.7.rest_5_ = bf16[4,128,128]{2,1,0:T(8,128)(2,1)S(1)} collective-permute-done((bf16[4,128,128]{2,1,0:T(8,128)(2,1)S(1)}, bf16[4,128,128]{2,1,0:T(8,128)(2,1)S(1)}, u32[]{:S(2)}, u32[]{:S(2)}) %collective-permute-start.7) | collective-permute-done | bytes 131104 | tf_op jit(solution)/shard_map/ppermute | solution.py:298
  77.8 1.8 %collective-permute-done.9.rest_1_ = bf16[4,128,128]{2,1,0:T(8,128)(2,1)S(1)} collective-permute-done((bf16[4,128,128]{2,1,0:T(8,128)(2,1)S(1)}, bf16[4,128,128]{2,1,0:T(8,128)(2,1)S(1)}, u32[]{:S(2)}, u32[]{:S(2)}) %collective-permute-start.9) | collective-permute-done | bytes 131104 | tf_op jit(solution)/shard_map/ppermute | solution.py:298
  79.9 0.9 %new_state_early.1 = (f32[16,128,128]{2,1,0:T(8,128)}, f32[4,128,128]{2,1,0:T(8,128)S(1)}) custom-call(f32[16,128,128]{2,1,0:T(8,128)S(1)} %get-tuple-element.26.base, bf16[4,128,128]{2,1,0:T(8,128)(2,1)S(1)} %total_a.1.own_a, bf16[4,128,128]{2,1,0:T(8,128)(2,1)S(1)} %total_b.1.own_b, bf16[4,128,128]{2,1,0:T(8,128)(2,1)S(1)} %collective-permute-done.10.mate_a), custom_call_target="tpu_custom_call" | custom-call | bytes 3145728 | tf_op jit(solution)/shard_map/new_state_early/pallas_call | solution.py:456
  80.8 0.4 collective-permute-done.11.mate_b
  81.2 0.7 new_state_late.1
  (39 shorter events, 2.1 us)
Async XLA Ops:
  0.6 11.0 %copy-start.7 = (s32[64]{0:T(128)S(1)}, s32[64]{0:T(128)}, u32[]{:S(2)}) copy-start(s32[64]{0:T(128)} %bund.1) | copy-start | bytes 772
  0.6 11.0 %copy-start.8 = (s32[64]{0:T(128)S(1)}, s32[64]{0:T(128)}, u32[]{:S(2)}) copy-start(s32[64]{0:T(128)} %cblk.1) | copy-start | bytes 772
  4.3 16.2 %copy-start.5 = (f32[1,128]{1,0:T(1,128)S(1)}, f32[1,128]{1,0:T(1,128)}, u32[]{:S(2)}) copy-start(f32[1,128]{1,0:T(1,128)} %obs_ref.3) | copy-start | bytes 1540
  4.3 16.2 %copy-start.6 = (f32[1,128]{1,0:T(1,128)S(1)}, f32[1,128]{1,0:T(1,128)}, u32[]{:S(2)}) copy-start(f32[1,128]{1,0:T(1,128)} %wt_ref.3) | copy-start | bytes 1540
  4.3 16.2 %all-to-all-start = ((bf16[8,128,128]{2,1,0:T(8,128)(2,1)}), bf16[8,128,128]{2,1,0:T(8,128)(2,1)S(1)}, u32[]{:S(2)}, u32[]{:S(2)}) async-start(bf16[8,128,128]{2,1,0:T(8,128)(2,1)} %forward1.1), calls=%async_computation | async-start | bytes 524288 | tf_op jit(solution)/shard_map/all_to_all | solution.py:303
  11.6 1.6 %copy-start.2 = (bf16[64,128,128]{2,1,0:T(8,128)(2,1)S(1)}, bf16[64,128,128]{2,1,0:T(8,128)(2,1)}, u32[]{:S(2)}) copy-start(bf16[64,128,128]{2,1,0:T(8,128)(2,1)} %sens.1) | copy-start | bytes 6291460
  16.7 1.0 %copy-start = (bf16[2,1024,256]{2,1,0:T(8,128)(2,1)}, bf16[2,1024,256]{2,1,0:T(8,128)(2,1)S(1)}, u32[]{:S(2)}) copy-start(bf16[2,1024,256]{2,1,0:T(8,128)(2,1)S(1)} %get-tuple-element.25.refs_0_.dense_own_b) | copy-start | bytes 3145732
  32.6 3.4 %copy-start.1 = (bf16[2,1024,256]{2,1,0:T(8,128)(2,1)S(1)}, bf16[2,1024,256]{2,1,0:T(8,128)(2,1)}, u32[]{:S(2)}) copy-start(bf16[2,1024,256]{2,1,0:T(8,128)(2,1)} %copy-done) | copy-start | bytes 3145732
  32.9 1.4 %collective-permute-start = (bf16[4,128,128]{2,1,0:T(8,128)(2,1)S(1)}, bf16[4,128,128]{2,1,0:T(8,128)(2,1)S(1)}, u32[]{:S(2)}, u32[]{:S(2)}) collective-permute-start(bf16[4,128,128]{2,1,0:T(8,128)(2,1)S(1)} %adjoint1_give_a.1), channel_id=1, source_target_pairs={{0,8},{8,0},{16,24},{24,16},{1,9},{9,1},{17,25},{25,17},{2,10},{10... | collective-permute-start | bytes 393224 | tf_op jit(solution)/shard_map/ppermute | solution.py:294
  33.0 3.9 %copy-start.3 = (f32[2048,128]{1,0:T(8,128)S(1)}, f32[2048,128]{1,0:T(8,128)}, u32[]{:S(2)}) copy-start(f32[2048,128]{1,0:T(8,128)} %param.10) | copy-start | bytes 3145732
  33.0 3.9 %copy-start.4 = (f32[2048,128]{1,0:T(8,128)S(1)}, f32[2048,128]{1,0:T(8,128)}, u32[]{:S(2)}) copy-start(f32[2048,128]{1,0:T(8,128)} %param.11) | copy-start | bytes 3145732
  33.5 2.8 %collective-permute-start.2 = (bf16[4,128,128]{2,1,0:T(8,128)(2,1)S(1)}, bf16[4,128,128]{2,1,0:T(8,128)(2,1)S(1)}, u32[]{:S(2)}, u32[]{:S(2)}) collective-permute-start(bf16[4,128,128]{2,1,0:T(8,128)(2,1)S(1)} %get-tuple-element.34), channel_id=1, source_target_pairs={{0,8},{8,0},{16,24},{24,16},{1,9},{9,1},{17,25},{25,17},{2,10},{10... | collective-permute-start | bytes 393224 | tf_op jit(solution)/shard_map/ppermute | solution.py:294
  34.4 6.4 %collective-permute-start.1 = (bf16[4,128,128]{2,1,0:T(8,128)(2,1)S(1)}, bf16[4,128,128]{2,1,0:T(8,128)(2,1)S(1)}, u32[]{:S(2)}, u32[]{:S(2)}) collective-permute-start(bf16[4,128,128]{2,1,0:T(8,128)(2,1)S(1)} %adjoint1_pair_a.1.rest_0_), channel_id=1, source_target_pairs={{0,16},{8,24},{16,0},{24,8},{1,17},{9,25},{17,1},{25,9},{2,18},{10... | collective-permute-start | bytes 393224 | tf_op jit(solution)/shard_map/ppermute | solution.py:298
  36.3 6.5 %collective-permute-start.3 = (bf16[4,128,128]{2,1,0:T(8,128)(2,1)S(1)}, bf16[4,128,128]{2,1,0:T(8,128)(2,1)S(1)}, u32[]{:S(2)}, u32[]{:S(2)}) collective-permute-start(bf16[4,128,128]{2,1,0:T(8,128)(2,1)S(1)} %adjoint1_pair_b.1.rest_0_), channel_id=1, source_target_pairs={{0,16},{8,24},{16,0},{24,8},{1,17},{9,25},{17,1},{25,9},{2,18},{10... | collective-permute-start | bytes 393224 | tf_op jit(solution)/shard_map/ppermute | solution.py:298
  40.9 2.1 %collective-permute-start.5 = (bf16[4,128,128]{2,1,0:T(8,128)(2,1)S(1)}, bf16[4,128,128]{2,1,0:T(8,128)(2,1)S(1)}, u32[]{:S(2)}, u32[]{:S(2)}) collective-permute-start(bf16[4,128,128]{2,1,0:T(8,128)(2,1)S(1)} %get-tuple-element.36.own_a), channel_id=1, source_target_pairs={{0,8},{8,0},{16,24},{24,16},{1,9},{9,1},{17,25},{25,17},{2,10},{10... | collective-permute-start | bytes 393224 | tf_op jit(solution)/shard_map/ppermute | solution.py:294
  42.9 1.4 %collective-permute-start.4 = (bf16[4,128,128]{2,1,0:T(8,128)(2,1)S(1)}, bf16[4,128,128]{2,1,0:T(8,128)(2,1)S(1)}, u32[]{:S(2)}, u32[]{:S(2)}) collective-permute-start(bf16[4,128,128]{2,1,0:T(8,128)(2,1)S(1)} %get-tuple-element.35.own_b), channel_id=1, source_target_pairs={{0,8},{8,0},{16,24},{24,16},{1,9},{9,1},{17,25},{25,17},{2,10},{10... | collective-permute-start | bytes 393224 | tf_op jit(solution)/shard_map/ppermute | solution.py:294
  69.8 1.4 %collective-permute-start.6 = (bf16[4,128,128]{2,1,0:T(8,128)(2,1)S(1)}, bf16[4,128,128]{2,1,0:T(8,128)(2,1)S(1)}, u32[]{:S(2)}, u32[]{:S(2)}) collective-permute-start(bf16[4,128,128]{2,1,0:T(8,128)(2,1)S(1)} %adjoint2_give_a.1), channel_id=1, source_target_pairs={{0,8},{8,0},{16,24},{24,16},{1,9},{9,1},{17,25},{25,17},{2,10},{10... | collective-permute-start | bytes 393224 | tf_op jit(solution)/shard_map/ppermute | solution.py:294
  70.3 2.8 %collective-permute-start.8 = (bf16[4,128,128]{2,1,0:T(8,128)(2,1)S(1)}, bf16[4,128,128]{2,1,0:T(8,128)(2,1)S(1)}, u32[]{:S(2)}, u32[]{:S(2)}) collective-permute-start(bf16[4,128,128]{2,1,0:T(8,128)(2,1)S(1)} %get-tuple-element.42), channel_id=1, source_target_pairs={{0,8},{8,0},{16,24},{24,16},{1,9},{9,1},{17,25},{25,17},{2,10},{10... | collective-permute-start | bytes 393224 | tf_op jit(solution)/shard_map/ppermute | solution.py:294
  71.2 6.4 %collective-permute-start.7 = (bf16[4,128,128]{2,1,0:T(8,128)(2,1)S(1)}, bf16[4,128,128]{2,1,0:T(8,128)(2,1)S(1)}, u32[]{:S(2)}, u32[]{:S(2)}) collective-permute-start(bf16[4,128,128]{2,1,0:T(8,128)(2,1)S(1)} %adjoint2_pair_a.1.rest_4_), channel_id=1, source_target_pairs={{0,16},{8,24},{16,0},{24,8},{1,17},{9,25},{17,1},{25,9},{2,18},{10... | collective-permute-start | bytes 393224 | tf_op jit(solution)/shard_map/ppermute | solution.py:298
  73.2 6.5 %collective-permute-start.9 = (bf16[4,128,128]{2,1,0:T(8,128)(2,1)S(1)}, bf16[4,128,128]{2,1,0:T(8,128)(2,1)S(1)}, u32[]{:S(2)}, u32[]{:S(2)}) collective-permute-start(bf16[4,128,128]{2,1,0:T(8,128)(2,1)S(1)} %adjoint2_pair_b.1.rest_0_), channel_id=1, source_target_pairs={{0,16},{8,24},{16,0},{24,8},{1,17},{9,25},{17,1},{25,9},{2,18},{10... | collective-permute-start | bytes 393224 | tf_op jit(solution)/shard_map/ppermute | solution.py:298
  77.8 2.1 %collective-permute-start.10 = (bf16[4,128,128]{2,1,0:T(8,128)(2,1)S(1)}, bf16[4,128,128]{2,1,0:T(8,128)(2,1)S(1)}, u32[]{:S(2)}, u32[]{:S(2)}) collective-permute-start(bf16[4,128,128]{2,1,0:T(8,128)(2,1)S(1)} %total_a.1.own_a), channel_id=1, source_target_pairs={{0,8},{8,0},{16,24},{24,16},{1,9},{9,1},{17,25},{25,17},{2,10},{10... | collective-permute-start | bytes 393224 | tf_op jit(solution)/shard_map/ppermute | solution.py:294
  79.8 1.4 %collective-permute-start.11 = (bf16[4,128,128]{2,1,0:T(8,128)(2,1)S(1)}, bf16[4,128,128]{2,1,0:T(8,128)(2,1)S(1)}, u32[]{:S(2)}, u32[]{:S(2)}) collective-permute-start(bf16[4,128,128]{2,1,0:T(8,128)(2,1)S(1)} %total_b.1.own_b), channel_id=1, source_target_pairs={{0,8},{8,0},{16,24},{24,16},{1,9},{9,1},{17,25},{25,17},{2,10},{10... | collective-permute-start | bytes 393224 | tf_op jit(solution)/shard_map/ppermute | solution.py:294

commit v16 on v12

--- a/solution.py
+++ b/solution.py
@@ -177,7 +177,8 @@
 
 
 def pair_kernel(keep_ref, got_ref, out_ref):
-    out_ref[...] = (keep_ref[...] + got_ref[...].astype(f32)).astype(bf16)
+    for i in range(out_ref.shape[0]):
+        out_ref[i] = (keep_ref[i] + got_ref[i].astype(f32)).T.astype(bf16)
 
 
 def residual_kernel(parts_ref, obs_ref, wt_ref, after_ref, out_ref, *resid_ref):
@@ -218,7 +219,7 @@
     total = parts[0].astype(f32)
     for part in parts[1:]:
         total += part.astype(f32)
-    return total.T
+    return total
 
 
 def probe_kernel(ny, field_ref, *rest):

time: 82.3 us -> 82.3 us (level)
  no operation moved by 1% of the time
where the time goes in v16:
time: 82.3 us; the launch traced here: 81.9 us
  blocking collectives  36.5 us (44%)
  waiting for transfers between devices  14.7 us (18%)
  Pallas kernels  14 us (17%)
  starting transfers between devices  13.1 us (16%)
  local copies, waits for them, and re-layouts  2.59 us (3%)
  between operations  0.94 us (1%)
    all_to_all x3, blocking collectives, over_band(): lax.all_to_all(array, 'band', split_axis=0, concat_axis=0, tiled=True)  36.5 us
    ppermute x4, waiting for transfers between devices, other_chips(): lax.ppermute(array, 'shot', [(i, i ^ 2 * d) for i in range(nshot)])  10.5 us
    all_to_all x1, starting transfers between devices, over_band(): lax.all_to_all(array, 'band', split_axis=0, concat_axis=0, tiled=True)  7.27 us
    ppermute x4, starting transfers between devices, other_chips(): lax.ppermute(array, 'shot', [(i, i ^ 2 * d) for i in range(nshot)])  4.31 us
    pallas_call x1, Pallas kernels, per_device(): call(first_forward_kernel, part_out, [pltpu.VMEM((bundles, rays, samples)...  3.65 us
    pallas_call x1, Pallas kernels, per_device(): call(dense_kernel, (arr(dense_shape, bf16),) * 4 + (small_token,), [pltpu...  3.48 us
    all_to_all x1, waiting for transfers between devices, over_band(): lax.all_to_all(array, 'band', split_axis=0, concat_axis=0, tiled=True)  2.85 us
    unnamed x18, local copies, waits for them, and re-layouts  2.59 us
  transfers between devices with their start and end apart: 13, of which 9 were waited for; matrix products, arithmetic and copies ran while one was open for 0% of the time, Pallas kernels for 10%

profile of v16, /device:TPU:0, one launch (start us, length us, event | category | flops | bytes accessed | tf_op | source)
XLA Modules:
  0.0 81.9 jit_solution(13363862018434836812)
XLA Ops:
  0.6 3.7 %forward1.1 = bf16[8,128,128]{2,1,0:T(8,128)(2,1)} custom-call(s32[64]{0:T(128)} %bund.1, s32[64]{0:T(128)} %cblk.1, bf16[64,128,128]{2,1,0:T(8,128)(2,1)} %sens.1, f32[16,128,128]{2,1,0:T(8,128)} %bitcast.7, f32[16,128,128]{2,1,0:T(8,128)} %bitcast.9), custom_call_target="tpu_custom_call" | custom-call | flops 268435456 | bytes 2097152 | tf_op jit(solution)/shard_map/forward1/pallas_call | solution.py:342
  4.3 7.3 %all-to-all-start = ((bf16[8,128,128]{2,1,0:T(8,128)(2,1)}), bf16[8,128,128]{2,1,0:T(8,128)(2,1)S(1)}, u32[]{:S(2)}, u32[]{:S(2)}) async-start(bf16[8,128,128]{2,1,0:T(8,128)(2,1)} %forward1.1), calls=%async_computation | async-start | bytes 524288 | tf_op jit(solution)/shard_map/all_to_all | solution.py:290
  11.6 1.6 %copy-done.2 = bf16[64,128,128]{2,1,0:T(8,128)(2,1)S(1)} copy-done((bf16[64,128,128]{2,1,0:T(8,128)(2,1)S(1)}, bf16[64,128,128]{2,1,0:T(8,128)(2,1)}, u32[]{:S(2)}) %copy-start.2) | copy-done | bytes 2097176
  13.2 3.5 %dense.1 = (bf16[2,1024,256]{2,1,0:T(8,128)(2,1)S(1)}, bf16[2,1024,256]{2,1,0:T(8,128)(2,1)S(1)}, bf16[2,1024,256]{2,1,0:T(8,128)(2,1)S(1)}, bf16[2,1024,256]{2,1,0:T(8,128)(2,1)S(1)}, f32[8,128]{1,0:T(8,128)S(1)}) custom-call(s32[64]{0:T(128)S(1)} %copy-done.7, s32[64]{0:T(128)S(1)} %copy-done.8, bf16[64,128,128]{2,1,0:T(8,128)(2,1)S(1)} %copy-done.2), custom_call_target="tpu_custom_call" | custom-call | bytes 16777216 | tf_op jit(solution)/shard_map/dense/pallas_call | solution.py:361
  16.7 1.0 %copy-done = bf16[2,1024,256]{2,1,0:T(8,128)(2,1)} copy-done((bf16[2,1024,256]{2,1,0:T(8,128)(2,1)}, bf16[2,1024,256]{2,1,0:T(8,128)(2,1)S(1)}, u32[]{:S(2)}) %copy-start) | copy-done | bytes 1048600
  17.7 2.8 %all-to-all-done = bf16[8,128,128]{2,1,0:T(8,128)(2,1)S(1)} async-done(((bf16[8,128,128]{2,1,0:T(8,128)(2,1)}), bf16[8,128,128]{2,1,0:T(8,128)(2,1)S(1)}, u32[]{:S(2)}, u32[]{:S(2)}) %all-to-all-start) | async-done | bytes 262176 | tf_op jit(solution)/shard_map/all_to_all | solution.py:290
  20.6 12.0 %all_to_all.20 = bf16[8,1,128,128]{3,2,1,0:T(8,128)(2,1)S(1)} all-to-all(bf16[8,1,128,128]{3,2,1,0:T(8,128)(2,1)S(1)} %residual1.1), channel_id=1, replica_groups=mesh['shot'=4,'band'=8] {'band'}, dimensions={0} | all-to-all | bytes 524288 | tf_op jit(solution)/shard_map/all_to_all | solution.py:290
  32.6 0.3 adjoint1_give_a.1
  33.0 0.4 adjoint1_keep_a.1
  33.5 0.5 collective-permute-start.2
  34.0 0.3 collective-permute-done.got_ref
  34.4 1.6 %collective-permute-start.1 = (bf16[4,128,128]{2,1,0:T(8,128)(2,1)S(1)}, bf16[4,128,128]{2,1,0:T(8,128)(2,1)S(1)}, u32[]{:S(2)}, u32[]{:S(2)}) collective-permute-start(bf16[4,128,128]{2,1,0:T(8,128)(2,1)S(1)} %adjoint1_pair_a.1.rest_0_), channel_id=1, source_target_pairs={{0,16},{8,24},{16,0},{24,8},{1,17},{9,25},{17,1},{25,9},{2,18},{10... | collective-permute-start | bytes 393224 | tf_op jit(solution)/shard_map/ppermute | solution.py:285
  36.5 0.6 collective-permute-start.3
  37.2 3.6 %collective-permute-done.1.rest_1_ = bf16[4,128,128]{2,1,0:T(8,128)(2,1)S(1)} collective-permute-done((bf16[4,128,128]{2,1,0:T(8,128)(2,1)S(1)}, bf16[4,128,128]{2,1,0:T(8,128)(2,1)S(1)}, u32[]{:S(2)}, u32[]{:S(2)}) %collective-permute-start.1) | collective-permute-done | bytes 131104 | tf_op jit(solution)/shard_map/ppermute | solution.py:285
  41.0 1.9 %collective-permute-done.3.rest_1_ = bf16[4,128,128]{2,1,0:T(8,128)(2,1)S(1)} collective-permute-done((bf16[4,128,128]{2,1,0:T(8,128)(2,1)S(1)}, bf16[4,128,128]{2,1,0:T(8,128)(2,1)S(1)}, u32[]{:S(2)}, u32[]{:S(2)}) %collective-permute-start.3) | collective-permute-done | bytes 131104 | tf_op jit(solution)/shard_map/ppermute | solution.py:285
  43.0 1.0 %forward2_early.1.early = f32[8,128,128]{2,1,0:T(8,128)S(1)} custom-call(bf16[2,1024,256]{2,1,0:T(8,128)(2,1)S(1)} %get-tuple-element.28.refs_0_.dense_own_a.rest_2_, bf16[2,1024,256]{2,1,0:T(8,128)(2,1)S(1)} %copy-done.1, bf16[2,1024,256]{2,1,0:T(8,128)(2,1)S(1)} %get-tuple-element.31.refs_0_.dense_mate_a.rest_1_, ...), custom_call_target="tpu_custom_call" | custom-call | flops 402653184 | bytes 3145728 | tf_op jit(solution)/shard_map/forward2_early/pallas_call | solution.py:397
  44.0 0.4 collective-permute-done.4.mate_b
  44.3 0.4 forward2_late.1
  44.8 12.6 %all_to_all.21 = bf16[8,128,128]{2,1,0:T(8,128)(2,1)S(1)} all-to-all(bf16[8,128,128]{2,1,0:T(8,128)(2,1)S(1)} %forward2_late.1), channel_id=1, replica_groups=mesh['shot'=4,'band'=8] {'band'}, dimensions={0} | all-to-all | bytes 524288 | tf_op jit(solution)/shard_map/all_to_all | solution.py:290
  57.5 12.0 %all_to_all.22 = bf16[8,1,128,128]{3,2,1,0:T(8,128)(2,1)S(1)} all-to-all(bf16[8,1,128,128]{3,2,1,0:T(8,128)(2,1)S(1)} %get-tuple-element.39), channel_id=1, replica_groups=mesh['shot'=4,'band'=8] {'band'}, dimensions={0} | all-to-all | bytes 524288 | tf_op jit(solution)/shard_map/all_to_all | solution.py:290
  69.4 0.3 adjoint2_give_a.1
  69.8 0.4 adjoint2_keep_a.1
  70.3 0.6 collective-permute-start.8
  70.8 0.3 collective-permute-done.6.got_ref
  71.3 1.6 %collective-permute-start.7 = (bf16[4,128,128]{2,1,0:T(8,128)(2,1)S(1)}, bf16[4,128,128]{2,1,0:T(8,128)(2,1)S(1)}, u32[]{:S(2)}, u32[]{:S(2)}) collective-permute-start(bf16[4,128,128]{2,1,0:T(8,128)(2,1)S(1)} %adjoint2_pair_a.1.rest_4_), channel_id=1, source_target_pairs={{0,16},{8,24},{16,0},{24,8},{1,17},{9,25},{17,1},{25,9},{2,18},{10... | collective-permute-start | bytes 393224 | tf_op jit(solution)/shard_map/ppermute | solution.py:285
  73.3 0.6 collective-permute-start.9
  73.9 0.7 turn.1
  74.6 3.1 %collective-permute-done.7.rest_5_ = bf16[4,128,128]{2,1,0:T(8,128)(2,1)S(1)} collective-permute-done((bf16[4,128,128]{2,1,0:T(8,128)(2,1)S(1)}, bf16[4,128,128]{2,1,0:T(8,128)(2,1)S(1)}, u32[]{:S(2)}, u32[]{:S(2)}) %collective-permute-start.7) | collective-permute-done | bytes 131104 | tf_op jit(solution)/shard_map/ppermute | solution.py:285
  77.8 1.9 %collective-permute-done.9.rest_1_ = bf16[4,128,128]{2,1,0:T(8,128)(2,1)S(1)} collective-permute-done((bf16[4,128,128]{2,1,0:T(8,128)(2,1)S(1)}, bf16[4,128,128]{2,1,0:T(8,128)(2,1)S(1)}, u32[]{:S(2)}, u32[]{:S(2)}) %collective-permute-start.9) | collective-permute-done | bytes 131104 | tf_op jit(solution)/shard_map/ppermute | solution.py:285
  79.8 0.9 %new_state_early.1 = (f32[16,128,128]{2,1,0:T(8,128)}, f32[4,128,128]{2,1,0:T(8,128)S(1)}) custom-call(f32[16,128,128]{2,1,0:T(8,128)S(1)} %get-tuple-element.26.base, bf16[4,128,128]{2,1,0:T(8,128)(2,1)S(1)} %total_a.1.own_a, bf16[4,128,128]{2,1,0:T(8,128)(2,1)S(1)} %total_b.1.own_b, bf16[4,128,128]{2,1,0:T(8,128)(2,1)S(1)} %collective-permute-done.10.mate_a), custom_call_target="tpu_custom_call" | custom-call | bytes 3145728 | tf_op jit(solution)/shard_map/new_state_early/pallas_call | solution.py:440
  80.8 0.4 collective-permute-done.11.mate_b
  81.2 0.7 new_state_late.1
  (39 shorter events, 2.1 us)
Async XLA Ops:
  0.6 11.0 %copy-start.7 = (s32[64]{0:T(128)S(1)}, s32[64]{0:T(128)}, u32[]{:S(2)}) copy-start(s32[64]{0:T(128)} %bund.1) | copy-start | bytes 772
  0.6 11.0 %copy-start.8 = (s32[64]{0:T(128)S(1)}, s32[64]{0:T(128)}, u32[]{:S(2)}) copy-start(s32[64]{0:T(128)} %cblk.1) | copy-start | bytes 772
  4.3 16.2 %copy-start.5 = (f32[1,128]{1,0:T(1,128)S(1)}, f32[1,128]{1,0:T(1,128)}, u32[]{:S(2)}) copy-start(f32[1,128]{1,0:T(1,128)} %obs_ref.3) | copy-start | bytes 1540
  4.3 16.2 %copy-start.6 = (f32[1,128]{1,0:T(1,128)S(1)}, f32[1,128]{1,0:T(1,128)}, u32[]{:S(2)}) copy-start(f32[1,128]{1,0:T(1,128)} %wt_ref.3) | copy-start | bytes 1540
  4.3 16.2 %all-to-all-start = ((bf16[8,128,128]{2,1,0:T(8,128)(2,1)}), bf16[8,128,128]{2,1,0:T(8,128)(2,1)S(1)}, u32[]{:S(2)}, u32[]{:S(2)}) async-start(bf16[8,128,128]{2,1,0:T(8,128)(2,1)} %forward1.1), calls=%async_computation | async-start | bytes 524288 | tf_op jit(solution)/shard_map/all_to_all | solution.py:290
  11.6 1.6 %copy-start.2 = (bf16[64,128,128]{2,1,0:T(8,128)(2,1)S(1)}, bf16[64,128,128]{2,1,0:T(8,128)(2,1)}, u32[]{:S(2)}) copy-start(bf16[64,128,128]{2,1,0:T(8,128)(2,1)} %sens.1) | copy-start | bytes 6291460
  16.7 1.0 %copy-start = (bf16[2,1024,256]{2,1,0:T(8,128)(2,1)}, bf16[2,1024,256]{2,1,0:T(8,128)(2,1)S(1)}, u32[]{:S(2)}) copy-start(bf16[2,1024,256]{2,1,0:T(8,128)(2,1)S(1)} %get-tuple-element.25.refs_0_.dense_own_b) | copy-start | bytes 3145732
  32.6 3.4 %copy-start.1 = (bf16[2,1024,256]{2,1,0:T(8,128)(2,1)S(1)}, bf16[2,1024,256]{2,1,0:T(8,128)(2,1)}, u32[]{:S(2)}) copy-start(bf16[2,1024,256]{2,1,0:T(8,128)(2,1)} %copy-done) | copy-start | bytes 3145732
  32.9 1.4 %collective-permute-start = (bf16[4,128,128]{2,1,0:T(8,128)(2,1)S(1)}, bf16[4,128,128]{2,1,0:T(8,128)(2,1)S(1)}, u32[]{:S(2)}, u32[]{:S(2)}) collective-permute-start(bf16[4,128,128]{2,1,0:T(8,128)(2,1)S(1)} %adjoint1_give_a.1), channel_id=1, source_target_pairs={{0,8},{8,0},{16,24},{24,16},{1,9},{9,1},{17,25},{25,17},{2,10},{10... | collective-permute-start | bytes 393224 | tf_op jit(solution)/shard_map/ppermute | solution.py:281
  33.0 4.0 %copy-start.3 = (f32[2048,128]{1,0:T(8,128)S(1)}, f32[2048,128]{1,0:T(8,128)}, u32[]{:S(2)}) copy-start(f32[2048,128]{1,0:T(8,128)} %param.10) | copy-start | bytes 3145732
  33.0 4.0 %copy-start.4 = (f32[2048,128]{1,0:T(8,128)S(1)}, f32[2048,128]{1,0:T(8,128)}, u32[]{:S(2)}) copy-start(f32[2048,128]{1,0:T(8,128)} %param.11) | copy-start | bytes 3145732
  33.5 2.9 %collective-permute-start.2 = (bf16[4,128,128]{2,1,0:T(8,128)(2,1)S(1)}, bf16[4,128,128]{2,1,0:T(8,128)(2,1)S(1)}, u32[]{:S(2)}, u32[]{:S(2)}) collective-permute-start(bf16[4,128,128]{2,1,0:T(8,128)(2,1)S(1)} %get-tuple-element.34), channel_id=1, source_target_pairs={{0,8},{8,0},{16,24},{24,16},{1,9},{9,1},{17,25},{25,17},{2,10},{10... | collective-permute-start | bytes 393224 | tf_op jit(solution)/shard_map/ppermute | solution.py:281
  34.4 6.4 %collective-permute-start.1 = (bf16[4,128,128]{2,1,0:T(8,128)(2,1)S(1)}, bf16[4,128,128]{2,1,0:T(8,128)(2,1)S(1)}, u32[]{:S(2)}, u32[]{:S(2)}) collective-permute-start(bf16[4,128,128]{2,1,0:T(8,128)(2,1)S(1)} %adjoint1_pair_a.1.rest_0_), channel_id=1, source_target_pairs={{0,16},{8,24},{16,0},{24,8},{1,17},{9,25},{17,1},{25,9},{2,18},{10... | collective-permute-start | bytes 393224 | tf_op jit(solution)/shard_map/ppermute | solution.py:285
  36.5 6.4 %collective-permute-start.3 = (bf16[4,128,128]{2,1,0:T(8,128)(2,1)S(1)}, bf16[4,128,128]{2,1,0:T(8,128)(2,1)S(1)}, u32[]{:S(2)}, u32[]{:S(2)}) collective-permute-start(bf16[4,128,128]{2,1,0:T(8,128)(2,1)S(1)} %adjoint1_pair_b.1.rest_0_), channel_id=1, source_target_pairs={{0,16},{8,24},{16,0},{24,8},{1,17},{9,25},{17,1},{25,9},{2,18},{10... | collective-permute-start | bytes 393224 | tf_op jit(solution)/shard_map/ppermute | solution.py:285
  40.9 2.1 %collective-permute-start.5 = (bf16[4,128,128]{2,1,0:T(8,128)(2,1)S(1)}, bf16[4,128,128]{2,1,0:T(8,128)(2,1)S(1)}, u32[]{:S(2)}, u32[]{:S(2)}) collective-permute-start(bf16[4,128,128]{2,1,0:T(8,128)(2,1)S(1)} %get-tuple-element.36.own_a), channel_id=1, source_target_pairs={{0,8},{8,0},{16,24},{24,16},{1,9},{9,1},{17,25},{25,17},{2,10},{10... | collective-permute-start | bytes 393224 | tf_op jit(solution)/shard_map/ppermute | solution.py:281
  42.9 1.4 %collective-permute-start.4 = (bf16[4,128,128]{2,1,0:T(8,128)(2,1)S(1)}, bf16[4,128,128]{2,1,0:T(8,128)(2,1)S(1)}, u32[]{:S(2)}, u32[]{:S(2)}) collective-permute-start(bf16[4,128,128]{2,1,0:T(8,128)(2,1)S(1)} %get-tuple-element.35.own_b), channel_id=1, source_target_pairs={{0,8},{8,0},{16,24},{24,16},{1,9},{9,1},{17,25},{25,17},{2,10},{10... | collective-permute-start | bytes 393224 | tf_op jit(solution)/shard_map/ppermute | solution.py:281
  69.8 1.4 %collective-permute-start.6 = (bf16[4,128,128]{2,1,0:T(8,128)(2,1)S(1)}, bf16[4,128,128]{2,1,0:T(8,128)(2,1)S(1)}, u32[]{:S(2)}, u32[]{:S(2)}) collective-permute-start(bf16[4,128,128]{2,1,0:T(8,128)(2,1)S(1)} %adjoint2_give_a.1), channel_id=1, source_target_pairs={{0,8},{8,0},{16,24},{24,16},{1,9},{9,1},{17,25},{25,17},{2,10},{10... | collective-permute-start | bytes 393224 | tf_op jit(solution)/shard_map/ppermute | solution.py:281
  70.3 2.9 %collective-permute-start.8 = (bf16[4,128,128]{2,1,0:T(8,128)(2,1)S(1)}, bf16[4,128,128]{2,1,0:T(8,128)(2,1)S(1)}, u32[]{:S(2)}, u32[]{:S(2)}) collective-permute-start(bf16[4,128,128]{2,1,0:T(8,128)(2,1)S(1)} %get-tuple-element.42), channel_id=1, source_target_pairs={{0,8},{8,0},{16,24},{24,16},{1,9},{9,1},{17,25},{25,17},{2,10},{10... | collective-permute-start | bytes 393224 | tf_op jit(solution)/shard_map/ppermute | solution.py:281
  71.3 6.4 %collective-permute-start.7 = (bf16[4,128,128]{2,1,0:T(8,128)(2,1)S(1)}, bf16[4,128,128]{2,1,0:T(8,128)(2,1)S(1)}, u32[]{:S(2)}, u32[]{:S(2)}) collective-permute-start(bf16[4,128,128]{2,1,0:T(8,128)(2,1)S(1)} %adjoint2_pair_a.1.rest_4_), channel_id=1, source_target_pairs={{0,16},{8,24},{16,0},{24,8},{1,17},{9,25},{17,1},{25,9},{2,18},{10... | collective-permute-start | bytes 393224 | tf_op jit(solution)/shard_map/ppermute | solution.py:285
  73.3 6.4 %collective-permute-start.9 = (bf16[4,128,128]{2,1,0:T(8,128)(2,1)S(1)}, bf16[4,128,128]{2,1,0:T(8,128)(2,1)S(1)}, u32[]{:S(2)}, u32[]{:S(2)}) collective-permute-start(bf16[4,128,128]{2,1,0:T(8,128)(2,1)S(1)} %adjoint2_pair_b.1.rest_0_), channel_id=1, source_target_pairs={{0,16},{8,24},{16,0},{24,8},{1,17},{9,25},{17,1},{25,9},{2,18},{10... | collective-permute-start | bytes 393224 | tf_op jit(solution)/shard_map/ppermute | solution.py:285
  77.7 2.1 %collective-permute-start.10 = (bf16[4,128,128]{2,1,0:T(8,128)(2,1)S(1)}, bf16[4,128,128]{2,1,0:T(8,128)(2,1)S(1)}, u32[]{:S(2)}, u32[]{:S(2)}) collective-permute-start(bf16[4,128,128]{2,1,0:T(8,128)(2,1)S(1)} %total_a.1.own_a), channel_id=1, source_target_pairs={{0,8},{8,0},{16,24},{24,16},{1,9},{9,1},{17,25},{25,17},{2,10},{10... | collective-permute-start | bytes 393224 | tf_op jit(solution)/shard_map/ppermute | solution.py:281
  79.8 1.4 %collective-permute-start.11 = (bf16[4,128,128]{2,1,0:T(8,128)(2,1)S(1)}, bf16[4,128,128]{2,1,0:T(8,128)(2,1)S(1)}, u32[]{:S(2)}, u32[]{:S(2)}) collective-permute-start(bf16[4,128,128]{2,1,0:T(8,128)(2,1)S(1)} %total_b.1.own_b), channel_id=1, source_target_pairs={{0,8},{8,0},{16,24},{24,16},{1,9},{9,1},{17,25},{25,17},{2,10},{10... | collective-permute-start | bytes 393224 | tf_op jit(solution)/shard_map/ppermute | solution.py:281

commit v17 on v12

--- a/solution.py
+++ b/solution.py
@@ -136,7 +136,7 @@
 
 
 def dense_forward(columns, store):
-    step = 2 * CBLK
+    step = 4 * CBLK
     pairs = columns[0][0].shape[0]
     probe = jnp.concatenate(
         [part[...].reshape(2 * CBLK * pairs, -1) for _, part in columns], axis=0
@@ -147,7 +147,7 @@
             [dense[pair, rows, :] for dense, _ in columns for pair in range(pairs)], axis=1
         )
         total = jnp.dot(lhs, probe, preferred_element_type=f32)
-        store(pl.ds(2 * m, 2), total.reshape(2, CBLK, -1))
+        store(pl.ds(4 * m, 4), total.reshape(4, CBLK, -1))
 
 
 def early_forward_kernel(dense_own_a, dense_own_b, dense_mate_a, own_a, own_b, mate_a, acc):

time: 82.3 us -> 82.3 us (level)
  no operation moved by 1% of the time
where the time goes in v17:
time: 82.3 us; the launch traced here: 81.9 us
  blocking collectives  36.5 us (44%)
  waiting for transfers between devices  14.7 us (18%)
  Pallas kernels  14.1 us (17%)
  starting transfers between devices  13.1 us (16%)
  local copies, waits for them, and re-layouts  2.59 us (3%)
  between operations  0.95 us (1%)
    all_to_all x3, blocking collectives, over_band(): lax.all_to_all(array, 'band', split_axis=0, concat_axis=0, tiled=True)  36.5 us
    ppermute x4, waiting for transfers between devices, other_chips(): lax.ppermute(array, 'shot', [(i, i ^ 2 * d) for i in range(nshot)])  10.5 us
    all_to_all x1, starting transfers between devices, over_band(): lax.all_to_all(array, 'band', split_axis=0, concat_axis=0, tiled=True)  7.27 us
    ppermute x4, starting transfers between devices, other_chips(): lax.ppermute(array, 'shot', [(i, i ^ 2 * d) for i in range(nshot)])  4.31 us
    pallas_call x1, Pallas kernels, per_device(): call(first_forward_kernel, part_out, [pltpu.VMEM((bundles, rays, samples)...  3.65 us
    pallas_call x1, Pallas kernels, per_device(): call(dense_kernel, (arr(dense_shape, bf16),) * 4 + (small_token,), [pltpu...  3.48 us
    all_to_all x1, waiting for transfers between devices, over_band(): lax.all_to_all(array, 'band', split_axis=0, concat_axis=0, tiled=True)  2.85 us
    unnamed x18, local copies, waits for them, and re-layouts  2.59 us
  transfers between devices with their start and end apart: 13, of which 9 were waited for; matrix products, arithmetic and copies ran while one was open for 0% of the time, Pallas kernels for 10%

profile of v17, /device:TPU:0, one launch (start us, length us, event | category | flops | bytes accessed | tf_op | source)
XLA Modules:
  0.0 81.9 jit_solution(12826407617828259106)
XLA Ops:
  0.6 3.7 %forward1.1 = bf16[8,128,128]{2,1,0:T(8,128)(2,1)} custom-call(s32[64]{0:T(128)} %bund.1, s32[64]{0:T(128)} %cblk.1, bf16[64,128,128]{2,1,0:T(8,128)(2,1)} %sens.1, f32[16,128,128]{2,1,0:T(8,128)} %bitcast.7, f32[16,128,128]{2,1,0:T(8,128)} %bitcast.9), custom_call_target="tpu_custom_call" | custom-call | flops 268435456 | bytes 2097152 | tf_op jit(solution)/shard_map/forward1/pallas_call | solution.py:341
  4.3 7.3 %all-to-all-start = ((bf16[8,128,128]{2,1,0:T(8,128)(2,1)}), bf16[8,128,128]{2,1,0:T(8,128)(2,1)S(1)}, u32[]{:S(2)}, u32[]{:S(2)}) async-start(bf16[8,128,128]{2,1,0:T(8,128)(2,1)} %forward1.1), calls=%async_computation | async-start | bytes 524288 | tf_op jit(solution)/shard_map/all_to_all | solution.py:289
  11.6 1.6 %copy-done.2 = bf16[64,128,128]{2,1,0:T(8,128)(2,1)S(1)} copy-done((bf16[64,128,128]{2,1,0:T(8,128)(2,1)S(1)}, bf16[64,128,128]{2,1,0:T(8,128)(2,1)}, u32[]{:S(2)}) %copy-start.2) | copy-done | bytes 2097176
  13.2 3.5 %dense.1 = (bf16[2,1024,256]{2,1,0:T(8,128)(2,1)S(1)}, bf16[2,1024,256]{2,1,0:T(8,128)(2,1)S(1)}, bf16[2,1024,256]{2,1,0:T(8,128)(2,1)S(1)}, bf16[2,1024,256]{2,1,0:T(8,128)(2,1)S(1)}, f32[8,128]{1,0:T(8,128)S(1)}) custom-call(s32[64]{0:T(128)S(1)} %copy-done.7, s32[64]{0:T(128)S(1)} %copy-done.8, bf16[64,128,128]{2,1,0:T(8,128)(2,1)S(1)} %copy-done.2), custom_call_target="tpu_custom_call" | custom-call | bytes 16777216 | tf_op jit(solution)/shard_map/dense/pallas_call | solution.py:360
  16.7 1.0 %copy-done = bf16[2,1024,256]{2,1,0:T(8,128)(2,1)} copy-done((bf16[2,1024,256]{2,1,0:T(8,128)(2,1)}, bf16[2,1024,256]{2,1,0:T(8,128)(2,1)S(1)}, u32[]{:S(2)}) %copy-start) | copy-done | bytes 1048600
  17.7 2.8 %all-to-all-done = bf16[8,128,128]{2,1,0:T(8,128)(2,1)S(1)} async-done(((bf16[8,128,128]{2,1,0:T(8,128)(2,1)}), bf16[8,128,128]{2,1,0:T(8,128)(2,1)S(1)}, u32[]{:S(2)}, u32[]{:S(2)}) %all-to-all-start) | async-done | bytes 262176 | tf_op jit(solution)/shard_map/all_to_all | solution.py:289
  20.6 12.0 %all_to_all.20 = bf16[8,1,128,128]{3,2,1,0:T(8,128)(2,1)S(1)} all-to-all(bf16[8,1,128,128]{3,2,1,0:T(8,128)(2,1)S(1)} %residual1.1), channel_id=1, replica_groups=mesh['shot'=4,'band'=8] {'band'}, dimensions={0} | all-to-all | bytes 524288 | tf_op jit(solution)/shard_map/all_to_all | solution.py:289
  32.6 0.3 adjoint1_give_a.1
  33.0 0.4 adjoint1_keep_a.1
  33.5 0.5 collective-permute-start.2
  34.0 0.3 collective-permute-done.got_ref
  34.4 1.6 %collective-permute-start.1 = (bf16[4,128,128]{2,1,0:T(8,128)(2,1)S(1)}, bf16[4,128,128]{2,1,0:T(8,128)(2,1)S(1)}, u32[]{:S(2)}, u32[]{:S(2)}) collective-permute-start(bf16[4,128,128]{2,1,0:T(8,128)(2,1)S(1)} %adjoint1_pair_a.1.rest_0_), channel_id=1, source_target_pairs={{0,16},{8,24},{16,0},{24,8},{1,17},{9,25},{17,1},{25,9},{2,18},{10... | collective-permute-start | bytes 393224 | tf_op jit(solution)/shard_map/ppermute | solution.py:284
  36.3 0.6 collective-permute-start.3
  37.0 3.7 %collective-permute-done.1.rest_1_ = bf16[4,128,128]{2,1,0:T(8,128)(2,1)S(1)} collective-permute-done((bf16[4,128,128]{2,1,0:T(8,128)(2,1)S(1)}, bf16[4,128,128]{2,1,0:T(8,128)(2,1)S(1)}, u32[]{:S(2)}, u32[]{:S(2)}) %collective-permute-start.1) | collective-permute-done | bytes 131104 | tf_op jit(solution)/shard_map/ppermute | solution.py:284
  41.0 1.8 %collective-permute-done.3.rest_1_ = bf16[4,128,128]{2,1,0:T(8,128)(2,1)S(1)} collective-permute-done((bf16[4,128,128]{2,1,0:T(8,128)(2,1)S(1)}, bf16[4,128,128]{2,1,0:T(8,128)(2,1)S(1)}, u32[]{:S(2)}, u32[]{:S(2)}) %collective-permute-start.3) | collective-permute-done | bytes 131104 | tf_op jit(solution)/shard_map/ppermute | solution.py:284
  43.0 1.0 %forward2_early.1.early = f32[8,128,128]{2,1,0:T(8,128)S(1)} custom-call(bf16[2,1024,256]{2,1,0:T(8,128)(2,1)S(1)} %get-tuple-element.28.refs_0_.dense_own_a.rest_2_, bf16[2,1024,256]{2,1,0:T(8,128)(2,1)S(1)} %copy-done.1, bf16[2,1024,256]{2,1,0:T(8,128)(2,1)S(1)} %get-tuple-element.31.refs_0_.dense_mate_a.rest_1_, ...), custom_call_target="tpu_custom_call" | custom-call | flops 402653184 | bytes 3145728 | tf_op jit(solution)/shard_map/forward2_early/pallas_call | solution.py:396
  44.0 0.4 collective-permute-done.4.mate_b
  44.3 0.4 forward2_late.1
  44.8 12.6 %all_to_all.21 = bf16[8,128,128]{2,1,0:T(8,128)(2,1)S(1)} all-to-all(bf16[8,128,128]{2,1,0:T(8,128)(2,1)S(1)} %forward2_late.1), channel_id=1, replica_groups=mesh['shot'=4,'band'=8] {'band'}, dimensions={0} | all-to-all | bytes 524288 | tf_op jit(solution)/shard_map/all_to_all | solution.py:289
  57.5 12.0 %all_to_all.22 = bf16[8,1,128,128]{3,2,1,0:T(8,128)(2,1)S(1)} all-to-all(bf16[8,1,128,128]{3,2,1,0:T(8,128)(2,1)S(1)} %get-tuple-element.39), channel_id=1, replica_groups=mesh['shot'=4,'band'=8] {'band'}, dimensions={0} | all-to-all | bytes 524288 | tf_op jit(solution)/shard_map/all_to_all | solution.py:289
  69.5 0.3 adjoint2_give_a.1
  69.9 0.4 adjoint2_keep_a.1
  70.3 0.6 collective-permute-start.8
  70.9 0.3 collective-permute-done.6.got_ref
  71.2 1.6 %collective-permute-start.7 = (bf16[4,128,128]{2,1,0:T(8,128)(2,1)S(1)}, bf16[4,128,128]{2,1,0:T(8,128)(2,1)S(1)}, u32[]{:S(2)}, u32[]{:S(2)}) collective-permute-start(bf16[4,128,128]{2,1,0:T(8,128)(2,1)S(1)} %adjoint2_pair_a.1.rest_4_), channel_id=1, source_target_pairs={{0,16},{8,24},{16,0},{24,8},{1,17},{9,25},{17,1},{25,9},{2,18},{10... | collective-permute-start | bytes 393224 | tf_op jit(solution)/shard_map/ppermute | solution.py:284
  73.2 0.6 collective-permute-start.9
  73.7 0.7 turn.1
  74.5 3.2 %collective-permute-done.7.rest_5_ = bf16[4,128,128]{2,1,0:T(8,128)(2,1)S(1)} collective-permute-done((bf16[4,128,128]{2,1,0:T(8,128)(2,1)S(1)}, bf16[4,128,128]{2,1,0:T(8,128)(2,1)S(1)}, u32[]{:S(2)}, u32[]{:S(2)}) %collective-permute-start.7) | collective-permute-done | bytes 131104 | tf_op jit(solution)/shard_map/ppermute | solution.py:284
  77.8 1.8 %collective-permute-done.9.rest_1_ = bf16[4,128,128]{2,1,0:T(8,128)(2,1)S(1)} collective-permute-done((bf16[4,128,128]{2,1,0:T(8,128)(2,1)S(1)}, bf16[4,128,128]{2,1,0:T(8,128)(2,1)S(1)}, u32[]{:S(2)}, u32[]{:S(2)}) %collective-permute-start.9) | collective-permute-done | bytes 131104 | tf_op jit(solution)/shard_map/ppermute | solution.py:284
  79.9 0.9 %new_state_early.1 = (f32[16,128,128]{2,1,0:T(8,128)}, f32[4,128,128]{2,1,0:T(8,128)S(1)}) custom-call(f32[16,128,128]{2,1,0:T(8,128)S(1)} %get-tuple-element.26.base, bf16[4,128,128]{2,1,0:T(8,128)(2,1)S(1)} %total_a.1.own_a, bf16[4,128,128]{2,1,0:T(8,128)(2,1)S(1)} %total_b.1.own_b, bf16[4,128,128]{2,1,0:T(8,128)(2,1)S(1)} %collective-permute-done.10.mate_a), custom_call_target="tpu_custom_call" | custom-call | bytes 3145728 | tf_op jit(solution)/shard_map/new_state_early/pallas_call | solution.py:439
  80.8 0.4 collective-permute-done.11.mate_b
  81.2 0.7 new_state_late.1
  (39 shorter events, 2.1 us)
Async XLA Ops:
  0.6 11.0 %copy-start.7 = (s32[64]{0:T(128)S(1)}, s32[64]{0:T(128)}, u32[]{:S(2)}) copy-start(s32[64]{0:T(128)} %bund.1) | copy-start | bytes 772
  0.6 11.0 %copy-start.8 = (s32[64]{0:T(128)S(1)}, s32[64]{0:T(128)}, u32[]{:S(2)}) copy-start(s32[64]{0:T(128)} %cblk.1) | copy-start | bytes 772
  4.3 16.2 %copy-start.5 = (f32[1,128]{1,0:T(1,128)S(1)}, f32[1,128]{1,0:T(1,128)}, u32[]{:S(2)}) copy-start(f32[1,128]{1,0:T(1,128)} %obs_ref.3) | copy-start | bytes 1540
  4.3 16.2 %copy-start.6 = (f32[1,128]{1,0:T(1,128)S(1)}, f32[1,128]{1,0:T(1,128)}, u32[]{:S(2)}) copy-start(f32[1,128]{1,0:T(1,128)} %wt_ref.3) | copy-start | bytes 1540
  4.3 16.2 %all-to-all-start = ((bf16[8,128,128]{2,1,0:T(8,128)(2,1)}), bf16[8,128,128]{2,1,0:T(8,128)(2,1)S(1)}, u32[]{:S(2)}, u32[]{:S(2)}) async-start(bf16[8,128,128]{2,1,0:T(8,128)(2,1)} %forward1.1), calls=%async_computation | async-start | bytes 524288 | tf_op jit(solution)/shard_map/all_to_all | solution.py:289
  11.6 1.6 %copy-start.2 = (bf16[64,128,128]{2,1,0:T(8,128)(2,1)S(1)}, bf16[64,128,128]{2,1,0:T(8,128)(2,1)}, u32[]{:S(2)}) copy-start(bf16[64,128,128]{2,1,0:T(8,128)(2,1)} %sens.1) | copy-start | bytes 6291460
  16.7 1.0 %copy-start = (bf16[2,1024,256]{2,1,0:T(8,128)(2,1)}, bf16[2,1024,256]{2,1,0:T(8,128)(2,1)S(1)}, u32[]{:S(2)}) copy-start(bf16[2,1024,256]{2,1,0:T(8,128)(2,1)S(1)} %get-tuple-element.25.refs_0_.dense_own_b) | copy-start | bytes 3145732
  32.6 3.4 %copy-start.1 = (bf16[2,1024,256]{2,1,0:T(8,128)(2,1)S(1)}, bf16[2,1024,256]{2,1,0:T(8,128)(2,1)}, u32[]{:S(2)}) copy-start(bf16[2,1024,256]{2,1,0:T(8,128)(2,1)} %copy-done) | copy-start | bytes 3145732
  32.9 1.4 %collective-permute-start = (bf16[4,128,128]{2,1,0:T(8,128)(2,1)S(1)}, bf16[4,128,128]{2,1,0:T(8,128)(2,1)S(1)}, u32[]{:S(2)}, u32[]{:S(2)}) collective-permute-start(bf16[4,128,128]{2,1,0:T(8,128)(2,1)S(1)} %adjoint1_give_a.1), channel_id=1, source_target_pairs={{0,8},{8,0},{16,24},{24,16},{1,9},{9,1},{17,25},{25,17},{2,10},{10... | collective-permute-start | bytes 393224 | tf_op jit(solution)/shard_map/ppermute | solution.py:280
  33.0 3.9 %copy-start.3 = (f32[2048,128]{1,0:T(8,128)S(1)}, f32[2048,128]{1,0:T(8,128)}, u32[]{:S(2)}) copy-start(f32[2048,128]{1,0:T(8,128)} %param.10) | copy-start | bytes 3145732
  33.0 3.9 %copy-start.4 = (f32[2048,128]{1,0:T(8,128)S(1)}, f32[2048,128]{1,0:T(8,128)}, u32[]{:S(2)}) copy-start(f32[2048,128]{1,0:T(8,128)} %param.11) | copy-start | bytes 3145732
  33.5 2.8 %collective-permute-start.2 = (bf16[4,128,128]{2,1,0:T(8,128)(2,1)S(1)}, bf16[4,128,128]{2,1,0:T(8,128)(2,1)S(1)}, u32[]{:S(2)}, u32[]{:S(2)}) collective-permute-start(bf16[4,128,128]{2,1,0:T(8,128)(2,1)S(1)} %get-tuple-element.34), channel_id=1, source_target_pairs={{0,8},{8,0},{16,24},{24,16},{1,9},{9,1},{17,25},{25,17},{2,10},{10... | collective-permute-start | bytes 393224 | tf_op jit(solution)/shard_map/ppermute | solution.py:280
  34.4 6.4 %collective-permute-start.1 = (bf16[4,128,128]{2,1,0:T(8,128)(2,1)S(1)}, bf16[4,128,128]{2,1,0:T(8,128)(2,1)S(1)}, u32[]{:S(2)}, u32[]{:S(2)}) collective-permute-start(bf16[4,128,128]{2,1,0:T(8,128)(2,1)S(1)} %adjoint1_pair_a.1.rest_0_), channel_id=1, source_target_pairs={{0,16},{8,24},{16,0},{24,8},{1,17},{9,25},{17,1},{25,9},{2,18},{10... | collective-permute-start | bytes 393224 | tf_op jit(solution)/shard_map/ppermute | solution.py:284
  36.3 6.5 %collective-permute-start.3 = (bf16[4,128,128]{2,1,0:T(8,128)(2,1)S(1)}, bf16[4,128,128]{2,1,0:T(8,128)(2,1)S(1)}, u32[]{:S(2)}, u32[]{:S(2)}) collective-permute-start(bf16[4,128,128]{2,1,0:T(8,128)(2,1)S(1)} %adjoint1_pair_b.1.rest_0_), channel_id=1, source_target_pairs={{0,16},{8,24},{16,0},{24,8},{1,17},{9,25},{17,1},{25,9},{2,18},{10... | collective-permute-start | bytes 393224 | tf_op jit(solution)/shard_map/ppermute | solution.py:284
  40.9 2.1 %collective-permute-start.5 = (bf16[4,128,128]{2,1,0:T(8,128)(2,1)S(1)}, bf16[4,128,128]{2,1,0:T(8,128)(2,1)S(1)}, u32[]{:S(2)}, u32[]{:S(2)}) collective-permute-start(bf16[4,128,128]{2,1,0:T(8,128)(2,1)S(1)} %get-tuple-element.36.own_a), channel_id=1, source_target_pairs={{0,8},{8,0},{16,24},{24,16},{1,9},{9,1},{17,25},{25,17},{2,10},{10... | collective-permute-start | bytes 393224 | tf_op jit(solution)/shard_map/ppermute | solution.py:280
  42.9 1.4 %collective-permute-start.4 = (bf16[4,128,128]{2,1,0:T(8,128)(2,1)S(1)}, bf16[4,128,128]{2,1,0:T(8,128)(2,1)S(1)}, u32[]{:S(2)}, u32[]{:S(2)}) collective-permute-start(bf16[4,128,128]{2,1,0:T(8,128)(2,1)S(1)} %get-tuple-element.35.own_b), channel_id=1, source_target_pairs={{0,8},{8,0},{16,24},{24,16},{1,9},{9,1},{17,25},{25,17},{2,10},{10... | collective-permute-start | bytes 393224 | tf_op jit(solution)/shard_map/ppermute | solution.py:280
  69.8 1.4 %collective-permute-start.6 = (bf16[4,128,128]{2,1,0:T(8,128)(2,1)S(1)}, bf16[4,128,128]{2,1,0:T(8,128)(2,1)S(1)}, u32[]{:S(2)}, u32[]{:S(2)}) collective-permute-start(bf16[4,128,128]{2,1,0:T(8,128)(2,1)S(1)} %adjoint2_give_a.1), channel_id=1, source_target_pairs={{0,8},{8,0},{16,24},{24,16},{1,9},{9,1},{17,25},{25,17},{2,10},{10... | collective-permute-start | bytes 393224 | tf_op jit(solution)/shard_map/ppermute | solution.py:280
  70.3 2.8 %collective-permute-start.8 = (bf16[4,128,128]{2,1,0:T(8,128)(2,1)S(1)}, bf16[4,128,128]{2,1,0:T(8,128)(2,1)S(1)}, u32[]{:S(2)}, u32[]{:S(2)}) collective-permute-start(bf16[4,128,128]{2,1,0:T(8,128)(2,1)S(1)} %get-tuple-element.42), channel_id=1, source_target_pairs={{0,8},{8,0},{16,24},{24,16},{1,9},{9,1},{17,25},{25,17},{2,10},{10... | collective-permute-start | bytes 393224 | tf_op jit(solution)/shard_map/ppermute | solution.py:280
  71.2 6.4 %collective-permute-start.7 = (bf16[4,128,128]{2,1,0:T(8,128)(2,1)S(1)}, bf16[4,128,128]{2,1,0:T(8,128)(2,1)S(1)}, u32[]{:S(2)}, u32[]{:S(2)}) collective-permute-start(bf16[4,128,128]{2,1,0:T(8,128)(2,1)S(1)} %adjoint2_pair_a.1.rest_4_), channel_id=1, source_target_pairs={{0,16},{8,24},{16,0},{24,8},{1,17},{9,25},{17,1},{25,9},{2,18},{10... | collective-permute-start | bytes 393224 | tf_op jit(solution)/shard_map/ppermute | solution.py:284
  73.2 6.5 %collective-permute-start.9 = (bf16[4,128,128]{2,1,0:T(8,128)(2,1)S(1)}, bf16[4,128,128]{2,1,0:T(8,128)(2,1)S(1)}, u32[]{:S(2)}, u32[]{:S(2)}) collective-permute-start(bf16[4,128,128]{2,1,0:T(8,128)(2,1)S(1)} %adjoint2_pair_b.1.rest_0_), channel_id=1, source_target_pairs={{0,16},{8,24},{16,0},{24,8},{1,17},{9,25},{17,1},{25,9},{2,18},{10... | collective-permute-start | bytes 393224 | tf_op jit(solution)/shard_map/ppermute | solution.py:284
  77.8 2.1 %collective-permute-start.10 = (bf16[4,128,128]{2,1,0:T(8,128)(2,1)S(1)}, bf16[4,128,128]{2,1,0:T(8,128)(2,1)S(1)}, u32[]{:S(2)}, u32[]{:S(2)}) collective-permute-start(bf16[4,128,128]{2,1,0:T(8,128)(2,1)S(1)} %total_a.1.own_a), channel_id=1, source_target_pairs={{0,8},{8,0},{16,24},{24,16},{1,9},{9,1},{17,25},{25,17},{2,10},{10... | collective-permute-start | bytes 393224 | tf_op jit(solution)/shard_map/ppermute | solution.py:280
  79.8 1.4 %collective-permute-start.11 = (bf16[4,128,128]{2,1,0:T(8,128)(2,1)S(1)}, bf16[4,128,128]{2,1,0:T(8,128)(2,1)S(1)}, u32[]{:S(2)}, u32[]{:S(2)}) collective-permute-start(bf16[4,128,128]{2,1,0:T(8,128)(2,1)S(1)} %total_b.1.own_b), channel_id=1, source_target_pairs={{0,8},{8,0},{16,24},{24,16},{1,9},{9,1},{17,25},{25,17},{2,10},{10... | collective-permute-start | bytes 393224 | tf_op jit(solution)/shard_map/ppermute | solution.py:280
